TPU v7x, 32 devices: a whole 2x2x4 slice. The times are simulated.
32 devices in a mesh: dp: 8 (over z, x), seq: 4 (over y, core).
Axes of the slice: x: 2, y: 2, z: 4, core: 2. Of those that a mesh axis runs over, the one named last changes fastest.
Arguments:
- patches: float32 [8192, 768], P(('dp', 'seq')), may hold values from -6 to 6
- specials: float32 [64, 768], P(('dp', 'seq')), may hold values from -6 to 6
- lengths: int32 [8, 4], P('dp'), may hold values from 232 to 280, as said below
- keep_mask: int32 [8, 4, 4], P('dp'), may hold values 0 or 1
- norm1_gain: bfloat16 [2, 768], P(None, 'dp'), may hold values from 0.099609375 to 1.8984375
- norm1_bias: bfloat16 [2, 768], P(None, 'dp'), may hold values from -4 to 4
- qkv_weight: bfloat16 [2, 768, 2304], P(None, 'dp'), may hold values from -0.21875 to 0.21875
- query_bias: bfloat16 [2, 768], P(None, 'dp'), may hold values from -4 to 4
- value_bias: bfloat16 [2, 768], P(None, 'dp'), may hold values from -4 to 4
- proj_weight: bfloat16 [2, 768, 768], P(None, 'dp'), may hold values from -1.25 to 1.25
- proj_bias: bfloat16 [2, 768], P(None, 'dp'), may hold values from -4 to 4
- norm2_gain: bfloat16 [2, 768], P(None, 'dp'), may hold values from 0.099609375 to 1.8984375
- norm2_bias: bfloat16 [2, 768], P(None, 'dp'), may hold values from -4 to 4
- fc1_weight: bfloat16 [2, 768, 3072], P(None, 'dp'), may hold values from -0.21875 to 0.21875
- fc1_bias: bfloat16 [2, 3072], P(None, 'dp'), may hold values from -6 to 6
- fc2_weight: bfloat16 [2, 3072, 768], P(None, 'dp'), may hold values from -0.21875 to 0.21875
- fc2_bias: bfloat16 [2, 768], P(None, 'dp'), may hold values from -4 to 4
- cot_patches: float32 [8192, 768], P(('dp', 'seq')), may hold values from -6 to 6
- cot_specials: float32 [64, 768], P(('dp', 'seq')), may hold values from -6 to 6
Outputs:
- out_patches: float32 [8192, 768], P(('dp', 'seq'))
- out_specials: float32 [64, 768], P(('dp', 'seq'))
- grad_patches: float32 [8192, 768], P(('dp', 'seq'))
- grad_specials: float32 [64, 768], P(('dp', 'seq'))
- grad_norm1_gain: float32 [2, 768], P(None, 'dp')
- grad_norm1_bias: float32 [2, 768], P(None, 'dp')
- grad_qkv_weight: float32 [2, 768, 2304], P(None, 'dp', 'seq')
- grad_query_bias: float32 [2, 768], P(None, 'dp')
- grad_value_bias: float32 [2, 768], P(None, 'dp')
- grad_proj_weight: float32 [2, 768, 768], P(None, 'dp', 'seq')
- grad_proj_bias: float32 [2, 768], P(None, 'dp')
- grad_norm2_gain: float32 [2, 768], P(None, 'dp')
- grad_norm2_bias: float32 [2, 768], P(None, 'dp')
- grad_fc1_weight: float32 [2, 768, 3072], P(None, 'dp', 'seq')
- grad_fc1_bias: float32 [2, 3072], P(None, 'dp')
- grad_fc2_weight: float32 [2, 3072, 768], P(None, 'dp', 'seq')
- grad_fc2_bias: float32 [2, 768], P(None, 'dp')
Inputs may be any that keep to these rules, and one draw needn't show every extreme that they name: `lengths`: each row holds the patch counts of the 4 images of one group in packing order; they sum to 1024, one image of each row has exactly 280 patches and one exactly 232. `keep_mask`: last index 2 l is layer l's attention branch, 2 l + 1 its feed-forward branch.
All inputs are finite; a program needn't handle non-finite values. No bound on the sum of `keep_mask` on one device may be relied on, other than what follows from the above.
Results may differ from a plain program's by a relative error of at most 0.014.
Values may be sent and summed in bfloat16 or wider, within the bound.
No kernel may reach another device: no remote copies, remote signals or barrier semaphores. Data moves between devices by JAX's collectives and lax.ppermute only.
A program may use at most 256 MiB of HBM per device.

v0:
```python
from functools import partial

import jax
import jax.numpy as jnp
from jax import lax
from jax.sharding import PartitionSpec as P

HD = 64
LAYERS = 2


KEEP_RATE = 0.9
EPSILON = 1e-06
MASKED = -1e30


def layer_norm(values, gain_vector, shift_vector):
    center = values - jnp.mean(values, axis=-1, keepdims=True)
    spread = jnp.mean(center * center, axis=-1, keepdims=True)
    return center * lax.rsqrt(spread + EPSILON) * gain_vector + shift_vector


def exact_gelu(values):
    return jax.nn.gelu(values, approximate=False)


def contract_rows(left_side, right_side):
    return lax.dot_general(
        left_side, right_side, (((0,), (0,)), ((), ())), preferred_element_type=jnp.float32
    )


def contract_cols(left_side, right_side):
    return lax.dot_general(
        left_side, right_side, (((1,), (1,)), ((), ())), preferred_element_type=jnp.float32
    )


def block_scores(queries, query_image, heads_kv):
    key_patch, key_spec, value_patch, value_spec, patch_image, spec_image = heads_kv
    score_patch = (
        jnp.einsum("qhd,khd->hqk", queries, key_patch, preferred_element_type=jnp.float32) * 0.125
    )
    score_spec = (
        jnp.einsum("qhd,khd->hqk", queries, key_spec, preferred_element_type=jnp.float32) * 0.125
    )
    score_patch = jnp.where(
        (query_image[:, None] == patch_image[None, :])[None], score_patch, MASKED
    )
    score_spec = jnp.where((query_image[:, None] == spec_image[None, :])[None], score_spec, MASKED)
    return (score_patch, score_spec)


def attend_block(inputs_block, heads_kv):
    queries, query_image = inputs_block
    value_patch, value_spec = (heads_kv[2], heads_kv[3])
    score_patch, score_spec = block_scores(queries, query_image, heads_kv)
    row_max = jnp.maximum(jnp.max(score_patch, axis=2), jnp.max(score_spec, axis=2))
    exp_patch = jnp.exp(score_patch - row_max[:, :, None])
    exp_spec = jnp.exp(score_spec - row_max[:, :, None])
    row_total = jnp.sum(exp_patch, axis=2) + jnp.sum(exp_spec, axis=2)
    prob_patch = (exp_patch / row_total[:, :, None]).astype(jnp.bfloat16)
    prob_spec = (exp_spec / row_total[:, :, None]).astype(jnp.bfloat16)
    output = jnp.einsum("hqk,khd->qhd", prob_patch, value_patch, preferred_element_type=jnp.float32)
    output = output + jnp.einsum(
        "hqk,khd->qhd", prob_spec, value_spec, preferred_element_type=jnp.float32
    )
    return (output.reshape(queries.shape[0], -1), row_max + jnp.log(row_total))


def attend_back(totals, inputs_block, heads_kv):
    queries, query_image, log_total, grad_out = inputs_block
    key_patch, key_spec, value_patch, value_spec = (
        heads_kv[0],
        heads_kv[1],
        heads_kv[2],
        heads_kv[3],
    )
    score_patch, score_spec = block_scores(queries, query_image, heads_kv)
    prob_patch = jnp.exp(score_patch - log_total[:, :, None])
    prob_spec = jnp.exp(score_spec - log_total[:, :, None])
    grad_prob_patch = jnp.einsum(
        "qhd,khd->hqk", grad_out, value_patch, preferred_element_type=jnp.float32
    )
    grad_prob_spec = jnp.einsum(
        "qhd,khd->hqk", grad_out, value_spec, preferred_element_type=jnp.float32
    )
    inner_sum = jnp.sum(prob_patch * grad_prob_patch, axis=2) + jnp.sum(
        prob_spec * grad_prob_spec, axis=2
    )
    grad_score_patch = (prob_patch * (grad_prob_patch - inner_sum[:, :, None])).astype(jnp.bfloat16)
    grad_score_spec = (prob_spec * (grad_prob_spec - inner_sum[:, :, None])).astype(jnp.bfloat16)
    grad_query = jnp.einsum(
        "hqk,khd->qhd", grad_score_patch, key_patch, preferred_element_type=jnp.float32
    )
    grad_query = (
        grad_query
        + jnp.einsum("hqk,khd->qhd", grad_score_spec, key_spec, preferred_element_type=jnp.float32)
    ) * 0.125
    grad_key_patch, grad_key_spec, grad_value_patch, grad_value_spec = totals
    grad_key_patch = (
        grad_key_patch
        + jnp.einsum("hqk,qhd->khd", grad_score_patch, queries, preferred_element_type=jnp.float32)
        * 0.125
    )
    grad_key_spec = (
        grad_key_spec
        + jnp.einsum("hqk,qhd->khd", grad_score_spec, queries, preferred_element_type=jnp.float32)
        * 0.125
    )
    grad_value_patch = grad_value_patch + jnp.einsum(
        "hqk,qhd->khd",
        prob_patch.astype(jnp.bfloat16),
        grad_out,
        preferred_element_type=jnp.float32,
    )
    grad_value_spec = grad_value_spec + jnp.einsum(
        "hqk,qhd->khd", prob_spec.astype(jnp.bfloat16), grad_out, preferred_element_type=jnp.float32
    )
    return ((grad_key_patch, grad_key_spec, grad_value_patch, grad_value_spec), grad_query)


def split_heads(heads_patch, heads_spec, patch_image, spec_image):
    total_rows = heads_patch.shape[0]
    local_heads = heads_patch.shape[2] // HD
    split_patch = heads_patch.reshape(total_rows, 3, local_heads, HD)
    split_spec = heads_spec.reshape(heads_spec.shape[0], 3, local_heads, HD)
    heads_kv = (
        split_patch[:, 1],
        split_spec[:, 1],
        split_patch[:, 2],
        split_spec[:, 2],
        patch_image,
        spec_image,
    )
    block_rows = min(512, total_rows)
    block_count = total_rows // block_rows
    query_blocks = split_patch[:, 0].reshape(block_count, block_rows, local_heads, HD)
    image_blocks = patch_image.reshape(block_count, block_rows)
    return (split_spec[:, 0], heads_kv, query_blocks, image_blocks)


def attention(heads_patch, heads_spec, patch_image, spec_image):
    spec_queries, heads_kv, query_blocks, image_blocks = split_heads(
        heads_patch, heads_spec, patch_image, spec_image
    )
    out_blocks, log_patch = lax.map(
        partial(attend_block, heads_kv=heads_kv), (query_blocks, image_blocks)
    )
    out_spec, log_spec = attend_block((spec_queries, spec_image), heads_kv)
    return (out_blocks.reshape(heads_patch.shape[0], -1), out_spec, log_patch, log_spec)


def attention_back(
    heads_patch, heads_spec, patch_image, spec_image, log_patch, log_spec, grad_patch, grad_spec
):
    spec_queries, heads_kv, query_blocks, image_blocks = split_heads(
        heads_patch, heads_spec, patch_image, spec_image
    )
    total_rows = heads_patch.shape[0]
    local_heads = heads_patch.shape[2] // HD
    grad_blocks = grad_patch.reshape(query_blocks.shape)
    grad_spec_heads = grad_spec.reshape(grad_spec.shape[0], local_heads, HD)
    zero_totals = (
        jnp.zeros(heads_kv[0].shape, jnp.float32),
        jnp.zeros(heads_kv[1].shape, jnp.float32),
        jnp.zeros(heads_kv[2].shape, jnp.float32),
        jnp.zeros(heads_kv[3].shape, jnp.float32),
    )
    totals, grad_query_blocks = lax.scan(
        partial(attend_back, heads_kv=heads_kv),
        zero_totals,
        (query_blocks, image_blocks, log_patch, grad_blocks),
    )
    totals, grad_query_spec = attend_back(
        totals, (spec_queries, spec_image, log_spec, grad_spec_heads), heads_kv
    )
    grad_key_patch, grad_key_spec, grad_value_patch, grad_value_spec = totals
    grad_query_patch = grad_query_blocks.reshape(total_rows, local_heads, HD)
    mixed_patch = jnp.stack([grad_query_patch, grad_key_patch, grad_value_patch], axis=1)
    mixed_spec = jnp.stack([grad_query_spec, grad_key_spec, grad_value_spec], axis=1)
    mixed_patch = mixed_patch.astype(jnp.bfloat16).reshape(total_rows, 3, local_heads * HD)
    mixed_spec = mixed_spec.astype(jnp.bfloat16).reshape(mixed_spec.shape[0], 3, local_heads * HD)
    return (mixed_patch, mixed_spec)


def layer_forward(stream, params, keep_pair, patch_count, patch_image, spec_image):
    (
        gain_one,
        shift_one,
        w_mixed,
        bias_query,
        bias_value,
        w_proj,
        bias_proj,
        gain_two,
        shift_two,
        w_up,
        bias_up,
        w_down,
        bias_down,
    ) = params
    width = stream.shape[1]
    normed_one = layer_norm(
        stream, gain_one.astype(jnp.float32), shift_one.astype(jnp.float32)
    ).astype(jnp.bfloat16)
    bias_mixed = jnp.concatenate([bias_query, jnp.zeros_like(bias_query), bias_value]).astype(
        jnp.float32
    )
    mixed = (jnp.dot(normed_one, w_mixed, preferred_element_type=jnp.float32) + bias_mixed).astype(
        jnp.bfloat16
    )
    mixed = mixed.reshape(stream.shape[0], 3, width)
    heads_patch, heads_spec = (
        lax.all_to_all(mixed[:patch_count], "seq", split_axis=2, concat_axis=0, tiled=True),
        lax.all_to_all(mixed[patch_count:], "seq", split_axis=2, concat_axis=0, tiled=True),
    )
    out_patch, out_spec, log_patch, log_spec = attention(
        heads_patch, heads_spec, patch_image, spec_image
    )
    back_patch, back_spec = (
        lax.all_to_all(
            out_patch.astype(jnp.bfloat16), "seq", split_axis=0, concat_axis=1, tiled=True
        ),
        lax.all_to_all(
            out_spec.astype(jnp.bfloat16), "seq", split_axis=0, concat_axis=1, tiled=True
        ),
    )
    attended = jnp.concatenate([back_patch, back_spec])
    branch_one = jnp.dot(attended, w_proj, preferred_element_type=jnp.float32) + bias_proj.astype(
        jnp.float32
    )
    middle = stream + keep_pair[:, 0:1] * branch_one / KEEP_RATE
    normed_two = layer_norm(
        middle, gain_two.astype(jnp.float32), shift_two.astype(jnp.float32)
    ).astype(jnp.bfloat16)
    hidden_pre = jnp.dot(normed_two, w_up, preferred_element_type=jnp.float32) + bias_up.astype(
        jnp.float32
    )
    hidden = exact_gelu(hidden_pre).astype(jnp.bfloat16)
    branch_two = jnp.dot(hidden, w_down, preferred_element_type=jnp.float32) + bias_down.astype(
        jnp.float32
    )
    output = middle + keep_pair[:, 1:2] * branch_two / KEEP_RATE
    kept = (
        normed_one,
        heads_patch,
        heads_spec,
        log_patch,
        log_spec,
        attended,
        middle,
        normed_two,
        hidden_pre,
        hidden,
    )
    return (output, kept)


def layer_back(grad_stream, stream, params, keep_pair, patch_count, patch_image, spec_image):
    (
        gain_one,
        shift_one,
        w_mixed,
        bias_query,
        bias_value,
        w_proj,
        bias_proj,
        gain_two,
        shift_two,
        w_up,
        bias_up,
        w_down,
        bias_down,
    ) = params
    width = stream.shape[1]
    unused, kept = layer_forward(stream, params, keep_pair, patch_count, patch_image, spec_image)
    (
        normed_one,
        heads_patch,
        heads_spec,
        log_patch,
        log_spec,
        attended,
        middle,
        normed_two,
        hidden_pre,
        hidden,
    ) = kept
    grad_branch_two = (keep_pair[:, 1:2] * grad_stream / KEEP_RATE).astype(jnp.bfloat16)
    grad_bias_down = jnp.sum(grad_branch_two, axis=0, dtype=jnp.float32)
    grad_w_down = contract_rows(hidden, grad_branch_two)
    grad_hidden = contract_cols(grad_branch_two, w_down)
    grad_pre = jax.vjp(exact_gelu, hidden_pre)[1](grad_hidden)[0].astype(jnp.bfloat16)
    grad_bias_up = jnp.sum(grad_pre, axis=0, dtype=jnp.float32)
    grad_w_up = contract_rows(normed_two, grad_pre)
    grad_normed_two = contract_cols(grad_pre, w_up)
    norm_pull = jax.vjp(
        layer_norm, middle, gain_two.astype(jnp.float32), shift_two.astype(jnp.float32)
    )[1]
    grad_from_norm, grad_gain_two, grad_shift_two = norm_pull(grad_normed_two)
    grad_middle = grad_stream + grad_from_norm
    grad_branch_one = (keep_pair[:, 0:1] * grad_middle / KEEP_RATE).astype(jnp.bfloat16)
    grad_bias_proj = jnp.sum(grad_branch_one, axis=0, dtype=jnp.float32)
    grad_w_proj = contract_rows(attended, grad_branch_one)
    grad_attended = contract_cols(grad_branch_one, w_proj).astype(jnp.bfloat16)
    grad_patch, grad_spec = (
        lax.all_to_all(grad_attended[:patch_count], "seq", split_axis=1, concat_axis=0, tiled=True),
        lax.all_to_all(grad_attended[patch_count:], "seq", split_axis=1, concat_axis=0, tiled=True),
    )
    mixed_patch, mixed_spec = attention_back(
        heads_patch, heads_spec, patch_image, spec_image, log_patch, log_spec, grad_patch, grad_spec
    )
    back_patch, back_spec = (
        lax.all_to_all(mixed_patch, "seq", split_axis=0, concat_axis=2, tiled=True),
        lax.all_to_all(mixed_spec, "seq", split_axis=0, concat_axis=2, tiled=True),
    )
    grad_mixed = jnp.concatenate([back_patch, back_spec]).reshape(stream.shape[0], 3 * width)
    grad_w_mixed = contract_rows(normed_one, grad_mixed)
    column_sums = jnp.sum(grad_mixed, axis=0, dtype=jnp.float32)
    grad_normed_one = contract_cols(grad_mixed, w_mixed)
    first_pull = jax.vjp(
        layer_norm, stream, gain_one.astype(jnp.float32), shift_one.astype(jnp.float32)
    )[1]
    grad_from_first, grad_gain_one, grad_shift_one = first_pull(grad_normed_one)
    grad_input = grad_middle + grad_from_first
    partials = (
        grad_gain_one,
        grad_shift_one,
        grad_w_mixed,
        column_sums[:width],
        column_sums[2 * width :],
        grad_w_proj,
        grad_bias_proj,
        grad_gain_two,
        grad_shift_two,
        grad_w_up,
        grad_bias_up,
        grad_w_down,
        grad_bias_down,
    )
    return (grad_input, partials)


def assemble(matrices, vectors):
    return [
        vectors[0],
        vectors[1],
        matrices[0],
        vectors[2],
        vectors[3],
        matrices[1],
        vectors[4],
        vectors[5],
        vectors[6],
        matrices[2],
        vectors[7],
        matrices[3],
        vectors[8],
    ]


def local(
    patches,
    specials,
    lengths,
    keep_mask,
    norm1_gain,
    norm1_bias,
    qkv_weight,
    query_bias,
    value_bias,
    proj_weight,
    proj_bias,
    norm2_gain,
    norm2_bias,
    fc1_weight,
    fc1_bias,
    fc2_weight,
    fc2_bias,
    cot_patches,
    cot_specials,
):
    seq_index = lax.axis_index("seq")
    seq_count = lax.axis_size("seq")
    patch_count = patches.shape[0]
    spec_count = specials.shape[0]
    image_count = lengths.shape[1]
    image_ends = jnp.cumsum(lengths[0])
    all_positions = jnp.arange(patch_count * seq_count, dtype=jnp.int32)
    patch_image = jnp.sum((all_positions[:, None] >= image_ends[None, :]).astype(jnp.int32), axis=1)
    spec_image = jnp.arange(spec_count * seq_count, dtype=jnp.int32) // 2
    own_patch = lax.dynamic_slice_in_dim(patch_image, seq_index * patch_count, patch_count)
    own_spec = seq_index * (spec_count // 2) + jnp.arange(spec_count, dtype=jnp.int32) // 2
    own_image = jnp.concatenate([own_patch, own_spec])
    onehot_table = (own_image[:, None] == jnp.arange(image_count, dtype=jnp.int32)[None, :]).astype(
        jnp.float32
    )
    keep_rows = jnp.dot(onehot_table, keep_mask[0].astype(jnp.float32))
    stream = jnp.concatenate([patches, specials])
    layer_inputs = []
    gathered_all = []
    for layer_index in range(LAYERS):
        gathered = (
            lax.all_gather(norm1_gain[layer_index], "dp", axis=0, tiled=True),
            lax.all_gather(norm1_bias[layer_index], "dp", axis=0, tiled=True),
            lax.all_gather(qkv_weight[layer_index], "dp", axis=0, tiled=True),
            lax.all_gather(query_bias[layer_index], "dp", axis=0, tiled=True),
            lax.all_gather(value_bias[layer_index], "dp", axis=0, tiled=True),
            lax.all_gather(proj_weight[layer_index], "dp", axis=0, tiled=True),
            lax.all_gather(proj_bias[layer_index], "dp", axis=0, tiled=True),
            lax.all_gather(norm2_gain[layer_index], "dp", axis=0, tiled=True),
            lax.all_gather(norm2_bias[layer_index], "dp", axis=0, tiled=True),
            lax.all_gather(fc1_weight[layer_index], "dp", axis=0, tiled=True),
            lax.all_gather(fc1_bias[layer_index], "dp", axis=0, tiled=True),
            lax.all_gather(fc2_weight[layer_index], "dp", axis=0, tiled=True),
            lax.all_gather(fc2_bias[layer_index], "dp", axis=0, tiled=True),
        )
        gathered_all.append(gathered)
        layer_inputs.append(stream)
        stream, unused = layer_forward(
            stream,
            gathered,
            keep_rows[:, 2 * layer_index : 2 * layer_index + 2],
            patch_count,
            patch_image,
            spec_image,
        )
    out_patches = stream[:patch_count]
    out_specials = stream[patch_count:]
    grad_stream = jnp.concatenate([cot_patches, cot_specials])
    layer_shares = [None] * LAYERS
    for layer_index in reversed(range(LAYERS)):
        gathered = (
            lax.all_gather(norm1_gain[layer_index], "dp", axis=0, tiled=True),
            lax.all_gather(norm1_bias[layer_index], "dp", axis=0, tiled=True),
            lax.all_gather(qkv_weight[layer_index], "dp", axis=0, tiled=True),
            lax.all_gather(query_bias[layer_index], "dp", axis=0, tiled=True),
            lax.all_gather(value_bias[layer_index], "dp", axis=0, tiled=True),
            lax.all_gather(proj_weight[layer_index], "dp", axis=0, tiled=True),
            lax.all_gather(proj_bias[layer_index], "dp", axis=0, tiled=True),
            lax.all_gather(norm2_gain[layer_index], "dp", axis=0, tiled=True),
            lax.all_gather(norm2_bias[layer_index], "dp", axis=0, tiled=True),
            lax.all_gather(fc1_weight[layer_index], "dp", axis=0, tiled=True),
            lax.all_gather(fc1_bias[layer_index], "dp", axis=0, tiled=True),
            lax.all_gather(fc2_weight[layer_index], "dp", axis=0, tiled=True),
            lax.all_gather(fc2_bias[layer_index], "dp", axis=0, tiled=True),
        )
        grad_stream, partials = layer_back(
            grad_stream,
            layer_inputs[layer_index],
            gathered,
            keep_rows[:, 2 * layer_index : 2 * layer_index + 2],
            patch_count,
            patch_image,
            spec_image,
        )
        shares = (
            lax.psum_scatter(partials[0], "dp", scatter_dimension=0, tiled=True),
            lax.psum_scatter(partials[1], "dp", scatter_dimension=0, tiled=True),
            lax.psum_scatter(partials[2], "dp", scatter_dimension=0, tiled=True),
            lax.psum_scatter(partials[3], "dp", scatter_dimension=0, tiled=True),
            lax.psum_scatter(partials[4], "dp", scatter_dimension=0, tiled=True),
            lax.psum_scatter(partials[5], "dp", scatter_dimension=0, tiled=True),
            lax.psum_scatter(partials[6], "dp", scatter_dimension=0, tiled=True),
            lax.psum_scatter(partials[7], "dp", scatter_dimension=0, tiled=True),
            lax.psum_scatter(partials[8], "dp", scatter_dimension=0, tiled=True),
            lax.psum_scatter(partials[9], "dp", scatter_dimension=0, tiled=True),
            lax.psum_scatter(partials[10], "dp", scatter_dimension=0, tiled=True),
            lax.psum_scatter(partials[11], "dp", scatter_dimension=0, tiled=True),
            lax.psum_scatter(partials[12], "dp", scatter_dimension=0, tiled=True),
        )
        matrices = (
            lax.psum_scatter(
                shares[2].astype(jnp.bfloat16), "seq", scatter_dimension=1, tiled=True
            ).astype(jnp.float32),
            lax.psum_scatter(
                shares[5].astype(jnp.bfloat16), "seq", scatter_dimension=1, tiled=True
            ).astype(jnp.float32),
            lax.psum_scatter(
                shares[9].astype(jnp.bfloat16), "seq", scatter_dimension=1, tiled=True
            ).astype(jnp.float32),
            lax.psum_scatter(
                shares[11].astype(jnp.bfloat16), "seq", scatter_dimension=1, tiled=True
            ).astype(jnp.float32),
        )
        vectors = lax.psum(
            (
                shares[0],
                shares[1],
                shares[3],
                shares[4],
                shares[6],
                shares[7],
                shares[8],
                shares[10],
                shares[12],
            ),
            "seq",
        )
        layer_shares[layer_index] = assemble(matrices, vectors)
    results = [
        jnp.stack([layer_shares[layer_index][member] for layer_index in range(LAYERS)])
        for member in range(13)
    ]
    return (
        out_patches,
        out_specials,
        grad_stream[:patch_count],
        grad_stream[patch_count:],
        results[0],
        results[1],
        results[2],
        results[3],
        results[4],
        results[5],
        results[6],
        results[7],
        results[8],
        results[9],
        results[10],
        results[11],
        results[12],
    )


def solution(mesh):
    in_specs = (
        P(("dp", "seq"), None),
        P(("dp", "seq"), None),
        P("dp", None),
        P("dp", None, None),
        P(None, "dp"),
        P(None, "dp"),
        P(None, "dp", None),
        P(None, "dp"),
        P(None, "dp"),
        P(None, "dp", None),
        P(None, "dp"),
        P(None, "dp"),
        P(None, "dp"),
        P(None, "dp", None),
        P(None, "dp"),
        P(None, "dp", None),
        P(None, "dp"),
        P(("dp", "seq"), None),
        P(("dp", "seq"), None),
    )
    out_specs = (
        P(("dp", "seq"), None),
        P(("dp", "seq"), None),
        P(("dp", "seq"), None),
        P(("dp", "seq"), None),
        P(None, "dp"),
        P(None, "dp"),
        P(None, "dp", "seq"),
        P(None, "dp"),
        P(None, "dp"),
        P(None, "dp", "seq"),
        P(None, "dp"),
        P(None, "dp"),
        P(None, "dp"),
        P(None, "dp", "seq"),
        P(None, "dp"),
        P(None, "dp", "seq"),
        P(None, "dp"),
    )
    return jax.shard_map(local, mesh=mesh, in_specs=in_specs, out_specs=out_specs, check_vma=False)
```

profile of v0, /device:TPU:0, one launch (start us, length us, event | category | flops | bytes accessed | tf_op | source)
XLA Modules:
  0.0 2017.2 jit_solution(5170374144437964900)
XLA Ops:
  21.3 39.7 %all-reduce.36 = (bf16[768]{0:T(1024)(128)(2,1)S(1)}, bf16[768]{0:T(1024)(128)(2,1)S(1)}, bf16[768]{0:T(1024)(128)(2,1)S(1)}, bf16[768]{0:T(1024)(128)(2,1)S(1)}...) all-reduce(bf16[768]{0:T(1024)(128)(2,1)S(1)} %dynamic-update-slice, ...), channel_id=6, replica_groups=mesh['dp'=8,'seq'=4] {'dp'}, use_global_device_ids=true, to_apply=%add.3 | all-reduce | flops 12288 | bytes 49152 | tf_op jit(solution)/shard_map/all_gather | solution.py:409
  88.1 25.9 %all-gather.10 = bf16[1,3072]{1,0:T(2,128)(2,1)S(1)} all-gather(bf16[1,384]{1,0:T(2,128)(2,1)S(1)} %get-tuple-element.1314), channel_id=12, replica_groups=mesh['dp'=8,'seq'=4] {'dp'}, dimensions={1}, use_global_device_ids=true | all-gather | bytes 6912 | tf_op jit(solution)/shard_map/all_gather | solution.py:415
  163.1 21.3 %while.86 = (s32[]{:T(128)}, bf16[2,512,192]{1,2,0:T(8,128)(2,1)}, s32[2,512]{1,0:T(2,128)S(1)}, s32[1024]{0:T(1024)S(1)}, bf16[2,512,3,64]{1,3,2,0:T(8,128)(2,1...) while((s32[]{:T(128)}, bf16[2,512,192]{1,2,0:T(8,128)(2,1)}, ...), condition=%wide.region_9.10_spmd.clone, body=%wide.region_4.9_spmd.clone.sunk | while | flops 425493568 | bytes 26948852 | solution.py:147
  203.2 80.7 %all-gather.39.cloned.1.call-done = bf16[1,768,3072]{2,1,0:T(8,128)(2,1)} async-done(((bf16[1,96,3072]{2,1,0:T(8,128)(2,1)}), bf16[1,768,3072]{2,1,0:T(8,128)(2,1)}) %all-gather.39.cloned.1.call-update) | async-done | bytes 4718608 | tf_op jit(solution)/shard_map/all_gather | solution.py:414
  297.8 52.0 %all-gather.43.cloned.1.call-done = bf16[1,768,2304]{2,1,0:T(8,128)(2,1)} async-done(((bf16[1,96,2304]{2,1,0:T(8,128)(2,1)}), bf16[1,768,2304]{2,1,0:T(8,128)(2,1)}) %all-gather.43.cloned.1.call-update) | async-done | bytes 3538960 | tf_op jit(solution)/shard_map/all_gather | solution.py:407
  361.4 26.0 %all-gather.23 = bf16[1,3072]{1,0:T(2,128)(2,1)S(1)} all-gather(bf16[1,384]{1,0:T(2,128)(2,1)S(1)} %get-tuple-element.1313), channel_id=25, replica_groups=mesh['dp'=8,'seq'=4] {'dp'}, dimensions={1}, use_global_device_ids=true | all-gather | bytes 6912 | tf_op jit(solution)/shard_map/all_gather | solution.py:415
  440.8 22.5 %while.88 = (s32[]{:T(128)}, bf16[2,512,192]{1,2,0:T(8,128)(2,1)}, f32[2,3,512]{2,1,0:T(4,128)}, s32[2,512]{1,0:T(2,128)S(1)}, s32[1024]{0:T(1024)S(1)}, /*index...) while((s32[]{:T(128)}, bf16[2,512,192]{1,2,0:T(8,128)(2,1)}, ...), condition=%wide.region_35.36_spmd.clone, body=%wide.region_30.35_spmd.clone.sunk | while | flops 425495104 | bytes 26963200 | solution.py:147
  489.0 64.4 %all-gather.49.cloned.1.call-done = bf16[1,3072,768]{2,1,0:T(8,128)(2,1)} async-done(((bf16[1,384,768]{2,1,0:T(8,128)(2,1)}), bf16[1,3072,768]{2,1,0:T(8,128)(2,1)}) %all-gather.49.cloned.1.call-update) | async-done | bytes 4718608 | tf_op jit(solution)/shard_map/all_gather | solution.py:416
  591.1 50.4 %while.90 = (s32[]{:T(128)}, f32[1024,3,64]{0,2,1:T(8,128)}, f32[8,3,64]{2,0,1:T(8,128)}, f32[1024,3,64]{0,2,1:T(8,128)}, f32[8,3,64]{2,0,1:T(8,128)}, /*index=5...) while((s32[]{:T(128)}, f32[1024,3,64]{0,2,1:T(8,128)}, ...), condition=%wide.region_43.44_spmd.clone, body=%wide.region_40.43_spmd.clone.sunk | while | flops 1039915072 | bytes 115015256 | solution.py:170
  738.0 50.5 %while.91 = (s32[]{:T(128)}, f32[1024,3,64]{0,2,1:T(8,128)}, f32[8,3,64]{2,0,1:T(8,128)}, f32[1024,3,64]{0,2,1:T(8,128)}, f32[8,3,64]{2,0,1:T(8,128)}, /*index=5...) while((s32[]{:T(128)}, f32[1024,3,64]{0,2,1:T(8,128)}, ...), condition=%wide.region_61.62_spmd.clone, body=%wide.region_58.61_spmd.clone.sunk | while | flops 1039915072 | bytes 115015256 | solution.py:170
  807.3 24.5 %all-to-all-done.16 = bf16[1024,3,192]{2,1,0:T(4,128)(2,1)S(1)} async-done(((bf16[1024,3,192]{2,1,0:T(4,128)(2,1)}), bf16[1024,3,192]{2,1,0:T(4,128)(2,1)S(1)}, u32[]{:S(2)}, u32[]{:S(2)}) %all-to-all-start.16) | async-done | bytes 1179680 | tf_op jit(solution)/shard_map/all_to_all | solution.py:315
  897.9 41.6 %reduce-scatter.31.cloned.1.call-done = f32[96,2304]{1,0:T(8,128)} async-done(((f32[768,2304]{1,0:T(8,128)}), f32[96,2304]{1,0:T(8,128)}) %reduce-scatter.31.cloned.1.call-update) | async-done | bytes 884752 | tf_op jit(solution)/shard_map/reduce_scatter | solution.py:461
  968.5 103.1 %reduce-scatter.29.cloned.1.call-done = f32[96,2304]{1,0:T(8,128)} async-done(((f32[768,2304]{1,0:T(8,128)}), f32[96,2304]{1,0:T(8,128)}) %reduce-scatter.29.cloned.1.call-update) | async-done | bytes 884752 | tf_op jit(solution)/shard_map/reduce_scatter | solution.py:461
  1076.9 160.8 %reduce-scatter.47.cloned.1.call-done = f32[384,768]{1,0:T(8,128)} async-done(((f32[3072,768]{1,0:T(8,128)}), f32[384,768]{1,0:T(8,128)}) %reduce-scatter.47.cloned.1.call-update) | async-done | bytes 1179664 | tf_op jit(solution)/shard_map/reduce_scatter | solution.py:470
  1256.6 147.2 %reduce-scatter.45.cloned.1.call-done = f32[384,768]{1,0:T(8,128)} async-done(((f32[3072,768]{1,0:T(8,128)}), f32[384,768]{1,0:T(8,128)}) %reduce-scatter.45.cloned.1.call-update) | async-done | bytes 1179664 | tf_op jit(solution)/shard_map/reduce_scatter | solution.py:470
  1408.1 76.3 %all-reduce.39.cloned.1.call-done = (f32[768]{0:T(1024)}, f32[768]{0:T(1024)}, f32[768]{0:T(1024)}, f32[768]{0:T(1024)}, f32[768]{0:T(1024)}, /*index=5*/f32[768...) async-done(((f32[768]{0:T(1024)}, f32[768]{0:T(1024)}, ...) | async-done | bytes 73744
  1490.4 160.3 %reduce-scatter.41.cloned.1.call-done = f32[96,3072]{1,0:T(8,128)} async-done(((f32[768,3072]{1,0:T(8,128)}), f32[96,3072]{1,0:T(8,128)}) %reduce-scatter.41.cloned.1.call-update) | async-done | bytes 1179664 | tf_op jit(solution)/shard_map/reduce_scatter | solution.py:468
  1672.8 143.9 %reduce-scatter.37.cloned.1.call-done = f32[96,3072]{1,0:T(8,128)} async-done(((f32[768,3072]{1,0:T(8,128)}), f32[96,3072]{1,0:T(8,128)}) %reduce-scatter.37.cloned.1.call-update) | async-done | bytes 1179664 | tf_op jit(solution)/shard_map/reduce_scatter | solution.py:468
  1861.7 23.4 %reduce-scatter.51.cloned.1.call-done = bf16[576,96]{1,0:T(8,128)(2,1)} async-done(((bf16[2304,96]{1,0:T(8,128)(2,1)}), bf16[576,96]{1,0:T(8,128)(2,1)}) %reduce-scatter.51.cloned.1.call-update) | async-done | bytes 110608
  1886.2 24.1 %reduce-scatter.49.cloned.1.call-done = bf16[576,96]{1,0:T(8,128)(2,1)} async-done(((bf16[2304,96]{1,0:T(8,128)(2,1)}), bf16[576,96]{1,0:T(8,128)(2,1)}) %reduce-scatter.49.cloned.1.call-update) | async-done | bytes 110608
  1912.2 22.7 %reduce-scatter.59.cloned.1.call-done = bf16[192,384]{1,0:T(8,128)(2,1)} async-done(((bf16[768,384]{1,0:T(8,128)(2,1)}), bf16[192,384]{1,0:T(8,128)(2,1)}) %reduce-scatter.59.cloned.1.call-update) | async-done | bytes 147472
  1936.0 23.6 %reduce-scatter.57.cloned.1.call-done = bf16[192,384]{1,0:T(8,128)(2,1)} async-done(((bf16[768,384]{1,0:T(8,128)(2,1)}), bf16[192,384]{1,0:T(8,128)(2,1)}) %reduce-scatter.57.cloned.1.call-update) | async-done | bytes 147472
  1961.8 22.2 %reduce-scatter.43.cloned.1.call-done = bf16[96,768]{1,0:T(8,128)(2,1)} async-done(((bf16[96,3072]{1,0:T(8,128)(2,1)}), bf16[96,768]{1,0:T(8,128)(2,1)}) %reduce-scatter.43.cloned.1.call-update) | async-done | bytes 147472 | tf_op jit(solution)/shard_map/reduce_scatter | solution.py:480
  1984.0 24.6 %reduce-scatter.39.cloned.1.call-done = bf16[96,768]{1,0:T(8,128)(2,1)} async-done(((bf16[96,3072]{1,0:T(8,128)(2,1)}), bf16[96,768]{1,0:T(8,128)(2,1)}) %reduce-scatter.39.cloned.1.call-update) | async-done | bytes 147472 | tf_op jit(solution)/shard_map/reduce_scatter | solution.py:480
  (1065 shorter events, 750.2 us)
Async XLA Ops:
  9.5 182.1 %all-gather.37.cloned.1.call-start = ((), (), s32[]{:S(2)}) async-start(), calls=%async_computation.45 | async-start | bytes 1327104 | tf_op jit(solution)/shard_map/all_gather | solution.py:410
  11.3 191.8 %all-gather.41.cloned.1.call-start = ((), (), s32[]{:S(2)}) async-start(), calls=%async_computation.47 | async-start | bytes 5308416 | tf_op jit(solution)/shard_map/all_gather | solution.py:416
  12.6 271.3 %all-gather.39.cloned.1.call-start = ((), (), s32[]{:S(2)}) async-start(), calls=%async_computation.46 | async-start | bytes 5308416 | tf_op jit(solution)/shard_map/all_gather | solution.py:414
  13.8 336.1 %all-gather.43.cloned.1.call-start = ((), (), s32[]{:S(2)}) async-start(), calls=%async_computation.48 | async-start | bytes 3981312 | tf_op jit(solution)/shard_map/all_gather | solution.py:407
  14.4 462.0 %all-gather.45.cloned.1.call-start = ((), (), s32[]{:S(2)}) async-start(), calls=%async_computation.49 | async-start | bytes 1327104 | tf_op jit(solution)/shard_map/all_gather | solution.py:410
  15.0 468.4 %all-gather.47.cloned.1.call-start = ((), (), s32[]{:S(2)}) async-start(), calls=%async_computation.50 | async-start | bytes 5308416 | tf_op jit(solution)/shard_map/all_gather | solution.py:414
  15.7 537.7 %all-gather.49.cloned.1.call-start = ((), (), s32[]{:S(2)}) async-start(), calls=%async_computation.51 | async-start | bytes 5308416 | tf_op jit(solution)/shard_map/all_gather | solution.py:416
  659.3 234.4 %reduce-scatter.35.cloned.1.call-start = ((), (), s32[]{:S(2)}) async-start(), calls=%async_computation.37 | async-start | bytes 2654208 | tf_op jit(solution)/shard_map/reduce_scatter | solution.py:464
  668.5 227.1 %reduce-scatter.33.cloned.1.call-start = ((), (), s32[]{:S(2)}) async-start(), calls=%async_computation.36 | async-start | bytes 2654208 | tf_op jit(solution)/shard_map/reduce_scatter | solution.py:464
  718.3 221.2 %reduce-scatter.31.cloned.1.call-start = ((), (), s32[]{:S(2)}) async-start(), calls=%async_computation.35 | async-start | bytes 7962624 | tf_op jit(solution)/shard_map/reduce_scatter | solution.py:461
  806.1 265.5 %reduce-scatter.29.cloned.1.call-start = ((), (), s32[]{:S(2)}) async-start(), calls=%async_computation.34 | async-start | bytes 7962624 | tf_op jit(solution)/shard_map/reduce_scatter | solution.py:461
  841.2 396.5 %reduce-scatter.47.cloned.1.call-start = ((), (), s32[]{:S(2)}) async-start(), calls=%async_computation.43 | async-start | bytes 10616832 | tf_op jit(solution)/shard_map/reduce_scatter | solution.py:470
  855.0 548.8 %reduce-scatter.45.cloned.1.call-start = ((), (), s32[]{:S(2)}) async-start(), calls=%async_computation.42 | async-start | bytes 10616832 | tf_op jit(solution)/shard_map/reduce_scatter | solution.py:470
  868.8 615.6 %all-reduce.39.cloned.1.call-start = ((), (), s32[]{:S(2)}) async-start(), calls=%async_computation.58 | async-start | bytes 180224
  879.6 771.1 %reduce-scatter.41.cloned.1.call-start = ((), (), s32[]{:S(2)}) async-start(), calls=%async_computation.40 | async-start | bytes 10616832 | tf_op jit(solution)/shard_map/reduce_scatter | solution.py:468
  886.5 930.2 %reduce-scatter.37.cloned.1.call-start = ((), (), s32[]{:S(2)}) async-start(), calls=%async_computation.38 | async-start | bytes 10616832 | tf_op jit(solution)/shard_map/reduce_scatter | solution.py:468
  893.6 944.3 %reduce-scatter.55.cloned.1.call-start = ((), (), s32[]{:S(2)}) async-start(), calls=%async_computation.55 | async-start | bytes 245760
  895.6 964.5 %reduce-scatter.53.cloned.1.call-start = ((), (), s32[]{:S(2)}) async-start(), calls=%async_computation.54 | async-start | bytes 245760
  897.4 987.7 %reduce-scatter.51.cloned.1.call-start = ((), (), s32[]{:S(2)}) async-start(), calls=%async_computation.53 | async-start | bytes 737280
  967.1 943.2 %reduce-scatter.49.cloned.1.call-start = ((), (), s32[]{:S(2)}) async-start(), calls=%async_computation.52 | async-start | bytes 737280
  1073.9 861.0 %reduce-scatter.59.cloned.1.call-start = ((), (), s32[]{:S(2)}) async-start(), calls=%async_computation.57 | async-start | bytes 737280
  1240.2 719.4 %reduce-scatter.57.cloned.1.call-start = ((), (), s32[]{:S(2)}) async-start(), calls=%async_computation.56 | async-start | bytes 737280
  1406.2 577.8 %reduce-scatter.43.cloned.1.call-start = ((), (), s32[]{:S(2)}) async-start(), calls=%async_computation.41 | async-start | bytes 737280 | tf_op jit(solution)/shard_map/reduce_scatter | solution.py:480
  1652.9 355.7 %reduce-scatter.39.cloned.1.call-start = ((), (), s32[]{:S(2)}) async-start(), calls=%async_computation.39 | async-start | bytes 737280 | tf_op jit(solution)/shard_map/reduce_scatter | solution.py:480
  (235 other events, 7301.4 us)
Sparse Core Ops, SparseCore 0:
  10.8 68.4 all-gather.34
  82.0 39.7 all-gather.36
  124.5 78.5 all-gather.40
  205.8 78.0 all-gather.38
  286.5 63.3 all-gather.42
  351.9 39.5 all-gather.44
  393.7 78.6 all-gather.46
  475.1 78.2 all-gather.48
  668.6 67.6 reduce-scatter.34
  739.6 68.0 reduce-scatter.32
  811.4 128.0 reduce-scatter.30
  943.5 128.0 reduce-scatter.28
  1075.2 162.4 reduce-scatter.46
  1241.2 162.5 reduce-scatter.44
  1409.3 75.0 all-reduce.38
  1487.8 162.8 reduce-scatter.40
  1654.1 162.5 reduce-scatter.36
  1840.3 19.7 reduce-scatter.52
  1863.0 22.0 reduce-scatter.50
  1888.2 22.0 reduce-scatter.48
  1912.8 22.0 reduce-scatter.58
  1937.4 22.0 reduce-scatter.56
  1961.9 22.0 reduce-scatter.42
  1986.5 22.0 reduce-scatter.38
  (1 shorter events, 18.8 us)
where the time goes:
time: 2030 us; the launch traced here: 2020 us
  waiting for transfers between devices  1310 us (65%)
  matrix products  307 us (15%)
  local copies, waits for them, and re-layouts  139 us (7%)
  blocking collectives  103 us (5%)
  other arithmetic  72 us (4%)
  starting transfers between devices  68.7 us (3%)
    reduce_scatter x2, waiting for transfers between devices, local(): lax.psum_scatter(partials[11], 'dp', scatter_dimension=0, tiled=True)  308 us
    reduce_scatter x2, waiting for transfers between devices, local(): lax.psum_scatter(partials[9], 'dp', scatter_dimension=0, tiled=True)  304 us
    unnamed x32, waiting for transfers between devices  209 us
    reduce_scatter x2, waiting for transfers between devices, local(): lax.psum_scatter(partials[2], 'dp', scatter_dimension=0, tiled=True)  145 us
    all_gather x2, waiting for transfers between devices, local(): lax.all_gather(fc1_weight[layer_index], 'dp', axis=0, tiled=True)  80.8 us
    all_gather x2, waiting for transfers between devices, local(): lax.all_gather(qkv_weight[layer_index], 'dp', axis=0, tiled=True)  68 us
    all_gather x2, waiting for transfers between devices, local(): lax.all_gather(fc2_weight[layer_index], 'dp', axis=0, tiled=True)  67.3 us
    dot_general x8, matrix products, contract_rows(): lax.dot_general(left_side, right_side, (((0,), (0,)), ((), ())), preferre...  54.2 us
  transfers between devices with their start and end apart: 43, of which 28 were waited for; matrix products, arithmetic and copies ran while one was open for 21% of the time, Pallas kernels for 0%

commit v1 on v0

v1 whole, which is shorter than its diff:
```python
from functools import partial

import jax
import jax.numpy as jnp
from jax import lax
from jax.sharding import PartitionSpec as P

HD = 64
LAYERS = 2
MOST = 280
KEEP_RATE = 0.9
EPSILON = 1e-06
MASKED = -1e30
ROOT_HALF = 0.7071067811865476
ROOT_TWO_PI = 0.3989422804014327
BF = jnp.bfloat16
F32 = jnp.float32


def dot_nn(left, right):
    return lax.dot_general(left, right, (((1,), (0,)), ((), ())), preferred_element_type=F32)


def dot_nt(left, right):
    return lax.dot_general(left, right, (((1,), (1,)), ((), ())), preferred_element_type=F32)


def dot_tn(left, right):
    return lax.dot_general(left, right, (((0,), (0,)), ((), ())), preferred_element_type=F32)


class Place:
    def __init__(self):
        self.n_dp = lax.axis_size("dp")
        self.n_seq = lax.axis_size("seq")
        self.walked = self.n_dp == 8 and self.n_seq == 4
        self.dp = lax.axis_index("dp")
        self.seq = lax.axis_index("seq")
        if self.walked:
            self.core = self.seq % 2
            self.y = self.seq // 2
            self.x = self.dp % 2
            self.z = self.dp // 2
            self.nz = self.n_dp // 2

    def swap_seq(self, values, mask):
        return lax.ppermute(values, "seq", [(i, i ^ mask) for i in range(self.n_seq)])

    def swap_x(self, values):
        return lax.ppermute(values, "dp", [(i, i ^ 1) for i in range(self.n_dp)])

    def ring_z(self, values):
        return lax.ppermute(values, "dp", [(i, (i + 2) % self.n_dp) for i in range(self.n_dp)])

    def own_half(self, values, which, axis):
        low, high = jnp.split(values, 2, axis=axis)
        return jnp.where(which == 0, low, high)

    def in_order(self, which, mine, other, axis):
        return jnp.where(
            which == 0,
            jnp.concatenate([mine, other], axis=axis),
            jnp.concatenate([other, mine], axis=axis),
        )


def gather_matrix(place, shard):
    if not place.walked:
        whole = lax.all_gather(shard, "dp", axis=0, tiled=True)
        half = whole.shape[1] // 2
        return (whole[:, :half], whole[:, half:])
    rows, columns = shard.shape
    blocks = [place.own_half(shard, place.core, 1)]
    for _ in range(place.nz - 1):
        blocks.append(place.ring_z(blocks[-1]))
    halves = [place.own_half(block, place.y, 0) for block in blocks]
    first = place.swap_x(halves[0])
    rest = place.swap_x(jnp.stack(halves[1:]))
    first_back = place.swap_seq(first, 2)
    rest_back = place.swap_seq(rest, 2)
    crossed = [place.in_order(place.y, first, first_back, 0)]
    rest_all = place.in_order(place.y, rest, rest_back, 1)
    crossed += [rest_all[i] for i in range(place.nz - 1)]
    mine = jnp.zeros((place.nz, 2, rows, columns // 2), shard.dtype)
    for step in range(place.nz):
        at = (place.z - step) % place.nz
        mine = lax.dynamic_update_slice(mine, blocks[step][None, None], (at, place.x, 0, 0))
        mine = lax.dynamic_update_slice(mine, crossed[step][None, None], (at, 1 - place.x, 0, 0))
    mine = mine.reshape(place.n_dp * rows, columns // 2)
    return (mine, place.swap_seq(mine, 1))


def times(place, values, halves):
    low = dot_nn(values, halves[0])
    high = dot_nn(values, halves[1])
    if not place.walked:
        return jnp.concatenate([low, high], axis=1)
    return place.in_order(place.core, low, high, 1)


def times_back(place, values, halves):
    if not place.walked:
        low, high = jnp.split(values, 2, axis=1)
    else:
        low = place.own_half(values, place.core, 1)
        high = place.own_half(values, 1 - place.core, 1)
    return dot_nt(low, halves[0]) + dot_nt(high, halves[1])


def quarter(place, values, y, core):
    pieces = jnp.split(values, 4, axis=1)
    low = jnp.where(core == 0, pieces[0], pieces[1])
    high = jnp.where(core == 0, pieces[2], pieces[3])
    return jnp.where(y == 0, low, high)


def reduce_matrix(place, acts, grads):
    if not place.walked:
        part = dot_tn(acts, grads).astype(BF)
        part = lax.psum_scatter(part, "dp", scatter_dimension=0, tiled=True)
        return lax.psum_scatter(part, "seq", scatter_dimension=1, tiled=True).astype(F32)
    y, core, nz = place.y, place.core, place.nz
    rows = acts.shape[1] // place.n_dp
    wide = grads.shape[1] // 4
    sent = jnp.concatenate([quarter(place, grads, y, 1 - core), quarter(place, grads, 1 - y, 1 - core)], 1)
    kept = jnp.concatenate([quarter(place, grads, y, core), quarter(place, grads, 1 - y, core)], 1)
    got = place.swap_seq(dot_tn(acts, sent).astype(BF), 1)
    pair = (dot_tn(acts, kept) + got).astype(BF).reshape(nz, 2, rows, 2 * wide)
    near = lax.dynamic_index_in_dim(pair, place.x, 1, keepdims=False)
    far = lax.dynamic_index_in_dim(pair, 1 - place.x, 1, keepdims=False)
    got = place.swap_seq(far[:, :, wide:], 2)
    far = (far[:, :, :wide].astype(F32) + got).astype(BF)
    got = place.swap_x(far)
    near = jnp.concatenate(
        [(near[:, :, :wide].astype(F32) + got).astype(BF), near[:, :, wide:]], axis=2
    )

    def block(step):
        return lax.dynamic_index_in_dim(near, (place.z - step) % nz, 0, keepdims=False)

    total = block(1)
    for step in range(2, nz + 1):
        total = (place.ring_z(total).astype(F32) + block(step)).astype(BF)
    got = place.swap_seq(total[:, wide:], 2)
    return total[:, :wide].astype(F32) + got


def reduce_vectors(place, vectors):
    packed = jnp.concatenate(
        [vector.reshape(place.n_dp, vector.shape[0] // place.n_dp) for vector in vectors], axis=1
    )
    mask = 1
    while mask < place.n_seq:
        packed = packed + place.swap_seq(packed, mask)
        mask *= 2
    packed = lax.all_to_all(packed, "dp", split_axis=0, concat_axis=0, tiled=True)
    total = jnp.sum(packed, axis=0)
    results, at = [], 0
    for vector in vectors:
        width = vector.shape[0] // place.n_dp
        results.append(total[at : at + width])
        at += width
    return results


def gather_vectors(place, shards):
    widths = [shard.shape[1] for shard in shards]
    packed = jnp.concatenate(shards, axis=1)
    rows = packed.shape[0]
    spread = jnp.broadcast_to(packed[None], (place.n_dp,) + packed.shape)
    spread = lax.all_to_all(spread, "dp", split_axis=0, concat_axis=0, tiled=True)
    results, at = [], 0
    for width in widths:
        piece = spread[:, :, at : at + width]
        results.append(jnp.transpose(piece, (1, 0, 2)).reshape(rows, place.n_dp * width).astype(F32))
        at += width
    return results


def normalize(values):
    center = values - jnp.mean(values, axis=-1, keepdims=True)
    spread = jnp.mean(center * center, axis=-1, keepdims=True)
    scale = lax.rsqrt(spread + EPSILON)
    return (center * scale, scale)


def normalize_back(hat, scale, gain, grad):
    scaled = grad * gain
    first = jnp.mean(scaled, axis=-1, keepdims=True)
    second = jnp.mean(scaled * hat, axis=-1, keepdims=True)
    back = scale * (scaled - first - hat * second)
    return (back, jnp.sum(grad * hat, axis=0), jnp.sum(grad, axis=0))


def heads_of(mixed):
    rows = mixed.shape[0]
    width = mixed.shape[1] // 3
    split = mixed.reshape(rows, 3, width // HD, HD)
    return (split[:, 0], split[:, 1], split[:, 2])


def attend(mixed, key_ok):
    queries, keys, values = heads_of(mixed)
    scores = jnp.einsum("qhd,khd->hqk", queries, keys, preferred_element_type=F32) * 0.125
    scores = jnp.where(key_ok[None, None, :], scores, MASKED)
    top = jnp.max(scores, axis=2, keepdims=True)
    powers = jnp.exp(scores - top)
    probs = powers / jnp.sum(powers, axis=2, keepdims=True)
    out = jnp.einsum("hqk,khd->qhd", probs.astype(BF), values, preferred_element_type=F32)
    return (out.reshape(mixed.shape[0], -1).astype(BF), probs)


def attend_back(mixed, probs, grad_out):
    queries, keys, values = heads_of(mixed)
    rows = mixed.shape[0]
    grads = grad_out.reshape(queries.shape)
    grad_probs = jnp.einsum("qhd,khd->hqk", grads, values, preferred_element_type=F32)
    inner = jnp.sum(probs * grad_probs, axis=2, keepdims=True)
    grad_scores = (probs * (grad_probs - inner)).astype(BF)
    grad_values = jnp.einsum("hqk,qhd->khd", probs.astype(BF), grads, preferred_element_type=F32)
    grad_queries = (
        jnp.einsum("hqk,khd->qhd", grad_scores, keys, preferred_element_type=F32) * 0.125
    )
    grad_keys = (
        jnp.einsum("hqk,qhd->khd", grad_scores, queries, preferred_element_type=F32) * 0.125
    )
    return jnp.concatenate(
        [grad.reshape(rows, -1).astype(BF) for grad in (grad_queries, grad_keys, grad_values)], axis=1
    )


def layer_forward(place, stream, vectors, matrices, keeps, key_ok):
    gain_one, shift_one, bias_query, bias_value, bias_proj, gain_two, shift_two, bias_down, bias_up = vectors
    w_mixed, w_proj, w_up, w_down = matrices
    hat_one, scale_one = normalize(stream)
    normed_one = (hat_one * gain_one + shift_one).astype(BF)
    bias_mixed = jnp.concatenate([bias_query, jnp.zeros_like(bias_query), bias_value])
    mixed = (times(place, normed_one, w_mixed) + bias_mixed).astype(BF)
    attended, probs = attend(mixed, key_ok)
    middle = stream + keeps[0] * (times(place, attended, w_proj) + bias_proj) / KEEP_RATE
    hat_two, scale_two = normalize(middle)
    normed_two = (hat_two * gain_two + shift_two).astype(BF)
    hidden_pre = times(place, normed_two, w_up) + bias_up
    share = 0.5 * (1.0 + lax.erf(hidden_pre * ROOT_HALF))
    hidden = (hidden_pre * share).astype(BF)
    slope = share + hidden_pre * jnp.exp(-0.5 * hidden_pre * hidden_pre) * ROOT_TWO_PI
    output = middle + keeps[1] * (times(place, hidden, w_down) + bias_down) / KEEP_RATE
    saved = (hat_one, scale_one, normed_one, mixed, probs, attended, hat_two, scale_two, normed_two, hidden, slope)
    return (output, saved)


def layer_back(place, grad_stream, saved, vectors, matrices, keeps):
    hat_one, scale_one, normed_one, mixed, probs, attended, hat_two, scale_two, normed_two, hidden, slope = saved
    gain_one, gain_two = (vectors[0], vectors[5])
    w_mixed, w_proj, w_up, w_down = matrices
    width = grad_stream.shape[1]
    grad_down = (keeps[1] * grad_stream / KEEP_RATE).astype(BF)
    total_down = reduce_matrix(place, hidden, grad_down)
    grad_up = (times_back(place, grad_down, w_down) * slope).astype(BF)
    total_up = reduce_matrix(place, normed_two, grad_up)
    back_two, grad_gain_two, grad_shift_two = normalize_back(
        hat_two, scale_two, gain_two, times_back(place, grad_up, w_up)
    )
    grad_middle = grad_stream + back_two
    grad_proj = (keeps[0] * grad_middle / KEEP_RATE).astype(BF)
    total_proj = reduce_matrix(place, attended, grad_proj)
    grad_attended = times_back(place, grad_proj, w_proj).astype(BF)
    grad_mixed = attend_back(mixed, probs, grad_attended)
    total_mixed = reduce_matrix(place, normed_one, grad_mixed)
    back_one, grad_gain_one, grad_shift_one = normalize_back(
        hat_one, scale_one, gain_one, times_back(place, grad_mixed, w_mixed)
    )
    grad_input = grad_middle + back_one
    sum_mixed = jnp.sum(grad_mixed, axis=0, dtype=F32)
    totals = reduce_vectors(
        place,
        (
            grad_gain_one,
            grad_shift_one,
            sum_mixed[:width],
            sum_mixed[2 * width :],
            jnp.sum(grad_proj, axis=0, dtype=F32),
            grad_gain_two,
            grad_shift_two,
            jnp.sum(grad_down, axis=0, dtype=F32),
            jnp.sum(grad_up, axis=0, dtype=F32),
        ),
    )
    return (grad_input, totals, (total_mixed, total_proj, total_up, total_down))


def shift_seq(place, values, by):
    count = place.n_seq
    return lax.ppermute(values, "seq", [(i, i + by) for i in range(count) if 0 <= i + by < count])


def to_image(place, patches, specials, halo, start, length, rows):
    count, width = patches.shape
    before = shift_seq(place, patches[count - halo :], 1)
    after = shift_seq(place, patches[:halo], -1)
    spare = jnp.zeros((MOST + 2 * halo - count - 2 * halo, width), patches.dtype)
    window = jnp.concatenate([before, patches, after, spare])
    image = lax.dynamic_slice_in_dim(window, start, MOST)
    inside = jnp.arange(MOST, dtype=jnp.int32)[:, None] < length
    image = jnp.where(inside, image, 0.0)
    spare = jnp.zeros((rows - MOST - specials.shape[0], width), patches.dtype)
    return jnp.concatenate([image, specials, spare])


def from_image(place, stream, halo, start, length, count, specials):
    width = stream.shape[1]
    inside = jnp.arange(MOST, dtype=jnp.int32)[:, None] < length
    image = jnp.where(inside, stream[:MOST], 0.0)
    window = jnp.zeros((MOST + 2 * halo, width), stream.dtype)
    window = lax.dynamic_update_slice_in_dim(window, image, start, 0)
    own = window[halo : halo + count]
    from_before = shift_seq(place, window[halo + count : count + 2 * halo], 1)
    from_after = shift_seq(place, window[:halo], -1)
    blank = jnp.zeros((count - halo, width), stream.dtype)
    own = own + jnp.concatenate([from_before, blank]) + jnp.concatenate([blank, from_after])
    return (own, stream[MOST : MOST + specials])


def local(
    patches,
    specials,
    lengths,
    keep_mask,
    norm1_gain,
    norm1_bias,
    qkv_weight,
    query_bias,
    value_bias,
    proj_weight,
    proj_bias,
    norm2_gain,
    norm2_bias,
    fc1_weight,
    fc1_bias,
    fc2_weight,
    fc2_bias,
    cot_patches,
    cot_specials,
):
    place = Place()
    count = patches.shape[0]
    special_count = specials.shape[0]
    images = lengths.shape[1]
    halo = (MOST - count) * (images // 2)
    rows = -(-(MOST + special_count) // 16) * 16
    before = jnp.sum(jnp.where(jnp.arange(images) < place.seq, lengths[0], 0))
    length = lax.dynamic_index_in_dim(lengths[0], place.seq, 0, keepdims=False)
    start = before - place.seq * count + halo
    keeps = lax.dynamic_index_in_dim(keep_mask[0], place.seq, 0, keepdims=False).astype(F32)
    row_ids = jnp.arange(rows, dtype=jnp.int32)
    key_ok = (row_ids < length) | ((row_ids >= MOST) & (row_ids < MOST + special_count))

    shards = (norm1_gain, norm1_bias, query_bias, value_bias, proj_bias, norm2_gain, norm2_bias, fc2_bias, fc1_bias)
    vectors_all = gather_vectors(place, shards)
    stream = to_image(place, patches, specials, halo, start, length, rows)
    matrices = []
    for layer in range(LAYERS):
        matrices.append(
            tuple(
                gather_matrix(place, shard[layer])
                for shard in (qkv_weight, proj_weight, fc1_weight, fc2_weight)
            )
        )
    vectors = [tuple(vector[layer] for vector in vectors_all) for layer in range(LAYERS)]
    saved = []
    for layer in range(LAYERS):
        stream, kept = layer_forward(
            place, stream, vectors[layer], matrices[layer], keeps[2 * layer : 2 * layer + 2], key_ok
        )
        saved.append(kept)
    out_patches, out_specials = from_image(place, stream, halo, start, length, count, special_count)
    grad = to_image(place, cot_patches, cot_specials, halo, start, length, rows)
    vector_totals, matrix_totals = ([None] * LAYERS, [None] * LAYERS)
    for layer in reversed(range(LAYERS)):
        grad, vector_totals[layer], matrix_totals[layer] = layer_back(
            place, grad, saved[layer], vectors[layer], matrices[layer], keeps[2 * layer : 2 * layer + 2]
        )
    grad_patches, grad_specials = from_image(place, grad, halo, start, length, count, special_count)
    vector_out = [jnp.stack([vector_totals[layer][i] for layer in range(LAYERS)]) for i in range(9)]
    matrix_out = [jnp.stack([matrix_totals[layer][i] for layer in range(LAYERS)]) for i in range(4)]
    g1, s1, bq, bv, bp, g2, s2, bd, bu = vector_out
    wm, wp, wu, wd = matrix_out
    return (
        out_patches,
        out_specials,
        grad_patches,
        grad_specials,
        g1,
        s1,
        wm,
        bq,
        bv,
        wp,
        bp,
        g2,
        s2,
        wu,
        bu,
        wd,
        bd,
    )


def solution(mesh):
    in_specs = (
        P(("dp", "seq"), None),
        P(("dp", "seq"), None),
        P("dp", None),
        P("dp", None, None),
        P(None, "dp"),
        P(None, "dp"),
        P(None, "dp", None),
        P(None, "dp"),
        P(None, "dp"),
        P(None, "dp", None),
        P(None, "dp"),
        P(None, "dp"),
        P(None, "dp"),
        P(None, "dp", None),
        P(None, "dp"),
        P(None, "dp", None),
        P(None, "dp"),
        P(("dp", "seq"), None),
        P(("dp", "seq"), None),
    )
    out_specs = (
        P(("dp", "seq"), None),
        P(("dp", "seq"), None),
        P(("dp", "seq"), None),
        P(("dp", "seq"), None),
        P(None, "dp"),
        P(None, "dp"),
        P(None, "dp", "seq"),
        P(None, "dp"),
        P(None, "dp"),
        P(None, "dp", "seq"),
        P(None, "dp"),
        P(None, "dp"),
        P(None, "dp"),
        P(None, "dp", "seq"),
        P(None, "dp"),
        P(None, "dp", "seq"),
        P(None, "dp"),
    )
    return jax.shard_map(local, mesh=mesh, in_specs=in_specs, out_specs=out_specs, check_vma=False)
```

time: 2030 us -> 830 us (0.41)
  waiting for transfers between devices: 1310 us -> 316 us
  matrix products: 307 us -> 144 us
  blocking collectives: 103 us -> 0 us
  starting transfers between devices: 68.7 us -> 133 us
  other arithmetic: 72 us -> 106 us
  local copies, waits for them, and re-layouts: 139 us -> 114 us
    reduce_scatter x10 -> x0, waiting for transfers between devices: 804 us -> none  [the longest x2 308 us: local(): lax.psum_scatter(partials[11], 'dp', scatter_dimension=0, tiled=True)]
    ppermute x0 -> x132, waiting for transfers between devices: none -> 306 us  [the longest x48 181 us: ring_z(): lax.ppermute(values, 'dp', [(i, (i + 2) % self.n_dp) for i in range(self....]
    all_gather x8 -> x0, waiting for transfers between devices: 216 us -> none  [the longest x2 80.8 us: local(): lax.all_gather(fc1_weight[layer_index], 'dp', axis=0, tiled=True)]
    unnamed x32 -> x0, waiting for transfers between devices: 209 us -> none
    dot_general x123 -> x60, matrix products: 307 us -> 144 us  [the longest x16 45.2 us: dot_nt(): lax.dot_general(left, right, (((1,), (1,)), ((), ())), preferred_element_...]
    ppermute x0 -> x132, starting transfers between devices: none -> 117 us  [the longest x52 40.8 us: swap_seq(): lax.ppermute(values, 'seq', [(i, i ^ mask) for i in range(self.n_seq)])]
    all_gather x3 -> x0, blocking collectives: 91.7 us -> none  [the longest x2 52 us: local(): lax.all_gather(fc1_bias[layer_index], 'dp', axis=0, tiled=True)]
    all_to_all x18 -> x3, waiting for transfers between devices: 77.7 us -> 10.2 us  [the longest x2 10.2 us: reduce_vectors(): lax.all_to_all(packed, 'dp', split_axis=0, concat_axis=0, tiled=True)]
  transfers between devices with their start and end apart: 43 -> 135, of which waited for: 28 -> 70; matrix products, arithmetic and copies ran while one was open for 21% -> 31% of each run, Pallas kernels for 0% -> 0%
where the time goes in v1:
time: 830 us; the launch traced here: 818 us
  waiting for transfers between devices  316 us (38%)
  matrix products  144 us (17%)
  starting transfers between devices  133 us (16%)
  local copies, waits for them, and re-layouts  114 us (14%)
  other arithmetic  106 us (13%)
    ppermute x48, waiting for transfers between devices, ring_z(): lax.ppermute(values, 'dp', [(i, (i + 2) % self.n_dp) for i in range(self....  181 us
    ppermute x52, waiting for transfers between devices, swap_seq(): lax.ppermute(values, 'seq', [(i, i ^ mask) for i in range(self.n_seq)])  84.9 us
    dot_general x16, matrix products, dot_nt(): lax.dot_general(left, right, (((1,), (1,)), ((), ())), preferred_element_...  45.2 us
    dot_general x16, matrix products, dot_tn(): lax.dot_general(left, right, (((0,), (0,)), ((), ())), preferred_element_...  41.5 us
    ppermute x52, starting transfers between devices, swap_seq(): lax.ppermute(values, 'seq', [(i, i ^ mask) for i in range(self.n_seq)])  40.8 us
    ppermute x24, waiting for transfers between devices, swap_x(): return lax.ppermute(values, 'dp', [(i, i ^ 1) for i in range(self.n_dp)])  40.2 us
    ppermute x48, starting transfers between devices, ring_z(): lax.ppermute(values, 'dp', [(i, (i + 2) % self.n_dp) for i in range(self....  38.8 us
    dot_general x16, matrix products, dot_nn(): lax.dot_general(left, right, (((1,), (0,)), ((), ())), preferred_element_...  36.1 us
  transfers between devices with their start and end apart: 135, of which 70 were waited for; matrix products, arithmetic and copies ran while one was open for 31% of the time, Pallas kernels for 0%

profile of v1, /device:TPU:0, one launch (start us, length us, event | category | flops | bytes accessed | tf_op | source)
XLA Modules:
  0.0 818.3 jit_solution(9179164200350312879)
XLA Ops:
  90.3 6.8 collective-permute-done.45
  208.1 6.2 collective-permute-done.30
  214.3 11.6 %collective-permute-start.62 = (bf16[384,384]{1,0:T(8,128)(2,1)S(1)}, bf16[384,384]{1,0:T(8,128)(2,1)S(1)}, u32[]{:S(2)}, u32[]{:S(2)}) collective-permute-start(bf16[384,384]{1,0:T(8,128)(2,1)S(1)} %collective-permute-done.61), channel_id=1, source_target_pairs={{0,8},{4,12},{8,16},{12,20},{16,24},{20,28},{24,0},{28,4},{1,9},{5... | collective-permute-start | bytes 884744 | tf_op jit(solution)/shard_map/ppermute | solution.py:53
  228.3 6.2 collective-permute-done.62
  237.8 6.2 collective-permute-done.7
  249.3 7.6 collective-permute-done.8
  281.5 7.6 collective-permute-done.64
  508.2 7.5 all-to-all-start.1
  526.3 6.5 all-to-all-done.2
  558.0 6.2 collective-permute-done.98
  582.0 6.2 collective-permute-done.100
  623.8 9.6 %collective-permute-done.77 = bf16[4,96,576]{2,1,0:T(8,128)(2,1)S(1)} collective-permute-done((bf16[4,96,576]{2,1,0:T(8,128)(2,1)S(1)}, bf16[4,96,576]{2,1,0:T(8,128)(2,1)S(1)}, u32[]{:S(2)}, u32[]{:S(2)}) %collective-permute-start.77) | collective-permute-done | bytes 442400 | tf_op jit(solution)/shard_map/ppermute | solution.py:47
  635.5 7.7 collective-permute-done.84
  687.0 6.4 collective-permute-done.79
  693.6 7.6 collective-permute-done.86
  712.1 9.5 %collective-permute-done.81 = bf16[96,1152]{1,0:T(8,128)(2,1)S(1)} collective-permute-done((bf16[96,1152]{1,0:T(8,128)(2,1)S(1)}, bf16[96,1152]{1,0:T(8,128)(2,1)S(1)}, u32[]{:S(2)}, u32[]{:S(2)}) %collective-permute-start.81) | collective-permute-done | bytes 221216 | tf_op jit(solution)/shard_map/ppermute | solution.py:53
  721.8 7.5 collective-permute-done.88
  744.0 6.4 collective-permute-done.113
  760.3 6.2 collective-permute-done.114
  766.6 6.2 collective-permute-done.122
  772.9 6.2 collective-permute-done.129
  779.3 6.2 collective-permute-done.108
  785.6 6.2 collective-permute-done.115
  791.9 6.2 collective-permute-done.123
  (1023 shorter events, 642.9 us)
Async XLA Ops:
  3.3 63.5 %collective-permute-start.44 = (bf16[96,384]{1,0:T(8,128)(2,1)}, bf16[96,384]{1,0:T(8,128)(2,1)S(1)}, u32[]{:S(2)}, u32[]{:S(2)}) collective-permute-start(bf16[96,384]{1,0:T(8,128)(2,1)} %get-tuple-element.73), channel_id=1, source_target_pairs={{0,8},{4,12},{8,16},{12,20},{16,24},{20,28},{24,0},{28,4},{1,9},{5... | collective-permute-start | bytes 221192 | tf_op jit(solution)/shard_map/ppermute | solution.py:53
  7.8 43.1 %collective-permute-start.42 = (bf16[48,384]{1,0:T(8,128)(2,1)}, bf16[48,384]{1,0:T(8,128)(2,1)}, u32[]{:S(2)}, u32[]{:S(2)}) collective-permute-start(bf16[48,384]{1,0:T(8,128)(2,1)} %slice_select_fusion.37), channel_id=1, source_target_pairs={{0,4},{4,0},{8,12},{12,8},{16,20},{20,16},{24,28},{28,24},{1,5},{5... | collective-permute-start | bytes 110600 | tf_op jit(solution)/shard_map/ppermute | solution.py:50
  12.8 101.9 %collective-permute-start.36 = (bf16[96,1152]{1,0:T(8,128)(2,1)}, bf16[96,1152]{1,0:T(8,128)(2,1)}, u32[]{:S(2)}, u32[]{:S(2)}) collective-permute-start(bf16[96,1152]{1,0:T(8,128)(2,1)} %get-tuple-element.75), channel_id=1, source_target_pairs={{0,8},{4,12},{8,16},{12,20},{16,24},{20,28},{24,0},{28,4},{1,9},{5... | collective-permute-start | bytes 663560 | tf_op jit(solution)/shard_map/ppermute | solution.py:53
  15.9 60.8 %collective-permute-start.12 = (bf16[96,384]{1,0:T(8,128)(2,1)}, bf16[96,384]{1,0:T(8,128)(2,1)S(1)}, u32[]{:S(2)}, u32[]{:S(2)}) collective-permute-start(bf16[96,384]{1,0:T(8,128)(2,1)} %get-tuple-element.85), channel_id=1, source_target_pairs={{0,8},{4,12},{8,16},{12,20},{16,24},{20,28},{24,0},{28,4},{1,9},{5... | collective-permute-start | bytes 221192 | tf_op jit(solution)/shard_map/ppermute | solution.py:53
  18.9 46.5 %collective-permute-start.10 = (bf16[48,384]{1,0:T(8,128)(2,1)}, bf16[48,384]{1,0:T(8,128)(2,1)}, u32[]{:S(2)}, u32[]{:S(2)}) collective-permute-start(bf16[48,384]{1,0:T(8,128)(2,1)} %slice_select_fusion.41), channel_id=1, source_target_pairs={{0,4},{4,0},{8,12},{12,8},{16,20},{20,16},{24,28},{28,24},{1,5},{5... | collective-permute-start | bytes 110600 | tf_op jit(solution)/shard_map/ppermute | solution.py:50
  78.7 88.8 %collective-permute-start.28 = (bf16[384,384]{1,0:T(8,128)(2,1)S(1)}, bf16[384,384]{1,0:T(8,128)(2,1)}, u32[]{:S(2)}, u32[]{:S(2)}) collective-permute-start(bf16[384,384]{1,0:T(8,128)(2,1)S(1)} %copy-done.61), channel_id=1, source_target_pairs={{0,8},{4,12},{8,16},{12,20},{16,24},{20,28},{24,0},{28,4},{1,9},{5... | collective-permute-start | bytes 884744 | tf_op jit(solution)/shard_map/ppermute | solution.py:53
  80.9 69.9 %collective-permute-start.20 = (bf16[96,1536]{1,0:T(8,128)(2,1)}, bf16[96,1536]{1,0:T(8,128)(2,1)}, u32[]{:S(2)}, u32[]{:S(2)}) collective-permute-start(bf16[96,1536]{1,0:T(8,128)(2,1)} %copy-done.62), channel_id=1, source_target_pairs={{0,8},{4,12},{8,16},{12,20},{16,24},{20,28},{24,0},{28,4},{1,9},{5... | collective-permute-start | bytes 884744 | tf_op jit(solution)/shard_map/ppermute | solution.py:53
  98.4 41.1 %collective-permute-start.4 = (bf16[96,1152]{1,0:T(8,128)(2,1)}, bf16[96,1152]{1,0:T(8,128)(2,1)}, u32[]{:S(2)}, u32[]{:S(2)}) collective-permute-start(bf16[96,1152]{1,0:T(8,128)(2,1)} %get-tuple-element.87), channel_id=1, source_target_pairs={{0,8},{4,12},{8,16},{12,20},{16,24},{20,28},{24,0},{28,4},{1,9},{5... | collective-permute-start | bytes 663560 | tf_op jit(solution)/shard_map/ppermute | solution.py:53
  114.6 46.1 %collective-permute-start.52 = (bf16[96,1536]{1,0:T(8,128)(2,1)}, bf16[96,1536]{1,0:T(8,128)(2,1)S(1)}, u32[]{:S(2)}, u32[]{:S(2)}) collective-permute-start(bf16[96,1536]{1,0:T(8,128)(2,1)} %copy-done.63), channel_id=1, source_target_pairs={{0,8},{4,12},{8,16},{12,20},{16,24},{20,28},{24,0},{28,4},{1,9},{5... | collective-permute-start | bytes 884744 | tf_op jit(solution)/shard_map/ppermute | solution.py:53
  187.5 168.8 %collective-permute-start.49 = (bf16[768,384]{1,0:T(8,128)(2,1)}, bf16[768,384]{1,0:T(8,128)(2,1)}, u32[]{:S(2)}, u32[]{:S(2)}) collective-permute-start(bf16[768,384]{1,0:T(8,128)(2,1)} %bitcast.111), channel_id=1, source_target_pairs={{0,1},{1,0},{2,3},{3,2},{4,5},{5,4},{6,7},{7,6},{8,9},{9,8},{10,11... | collective-permute-start | bytes 1769480 | tf_op jit(solution)/shard_map/ppermute | solution.py:47
  189.6 127.9 %collective-permute-start.17 = (bf16[768,384]{1,0:T(8,128)(2,1)}, bf16[768,384]{1,0:T(8,128)(2,1)}, u32[]{:S(2)}, u32[]{:S(2)}) collective-permute-start(bf16[768,384]{1,0:T(8,128)(2,1)} %bitcast.40), channel_id=1, source_target_pairs={{0,1},{1,0},{2,3},{3,2},{4,5},{5,4},{6,7},{7,6},{8,9},{9,8},{10,11... | collective-permute-start | bytes 1769480 | tf_op jit(solution)/shard_map/ppermute | solution.py:47
  281.5 56.9 %collective-permute-start.41 = (bf16[768,1152]{1,0:T(8,128)(2,1)}, bf16[768,1152]{1,0:T(8,128)(2,1)}, u32[]{:S(2)}, u32[]{:S(2)}) collective-permute-start(bf16[768,1152]{1,0:T(8,128)(2,1)} %bitcast.91), channel_id=1, source_target_pairs={{0,1},{1,0},{2,3},{3,2},{4,5},{5,4},{6,7},{7,6},{8,9},{9,8},{10,11... | collective-permute-start | bytes 5308424 | tf_op jit(solution)/shard_map/ppermute | solution.py:47
  317.5 44.4 %collective-permute-start.57 = (bf16[768,1536]{1,0:T(8,128)(2,1)}, bf16[768,1536]{1,0:T(8,128)(2,1)}, u32[]{:S(2)}, u32[]{:S(2)}) collective-permute-start(bf16[768,1536]{1,0:T(8,128)(2,1)} %bitcast.127), channel_id=1, source_target_pairs={{0,1},{1,0},{2,3},{3,2},{4,5},{5,4},{6,7},{7,6},{8,9},{9,8},{10,11... | collective-permute-start | bytes 7077896 | tf_op jit(solution)/shard_map/ppermute | solution.py:47
  323.9 45.0 %collective-permute-start.65 = (bf16[3072,384]{1,0:T(8,128)(2,1)}, bf16[3072,384]{1,0:T(8,128)(2,1)}, u32[]{:S(2)}, u32[]{:S(2)}) collective-permute-start(bf16[3072,384]{1,0:T(8,128)(2,1)} %bitcast.142), channel_id=1, source_target_pairs={{0,1},{1,0},{2,3},{3,2},{4,5},{5,4},{6,7},{7,6},{8,9},{9,8},{10,11... | collective-permute-start | bytes 7077896 | tf_op jit(solution)/shard_map/ppermute | solution.py:47
  471.3 173.3 %collective-permute-start.118 = (bf16[3072,384]{1,0:T(8,128)(2,1)}, bf16[3072,384]{1,0:T(8,128)(2,1)}, u32[]{:S(2)}, u32[]{:S(2)}) collective-permute-start(bf16[3072,384]{1,0:T(8,128)(2,1)} %convolution_convert_fusion.1), channel_id=1, source_target_pairs={{0,1},{1,0},{2,3},{3,2},{4,5},{5,4},{6,7},{7,6},{8,9},{9,8},{10,11... | collective-permute-start | bytes 7077896 | tf_op jit(solution)/shard_map/ppermute | solution.py:47
  474.5 179.6 %collective-permute-start.125 = (bf16[3072,384]{1,0:T(8,128)(2,1)}, bf16[3072,384]{1,0:T(8,128)(2,1)}, u32[]{:S(2)}, u32[]{:S(2)}) collective-permute-start(bf16[3072,384]{1,0:T(8,128)(2,1)} %convolution_convert_fusion), channel_id=1, source_target_pairs={{0,1},{1,0},{2,3},{3,2},{4,5},{5,4},{6,7},{7,6},{8,9},{9,8},{10,11... | collective-permute-start | bytes 7077896 | tf_op jit(solution)/shard_map/ppermute | solution.py:47
  476.4 71.9 %collective-permute-start.90 = (bf16[768,384]{1,0:T(8,128)(2,1)}, bf16[768,384]{1,0:T(8,128)(2,1)}, u32[]{:S(2)}, u32[]{:S(2)}) collective-permute-start(bf16[768,384]{1,0:T(8,128)(2,1)} %convolution_convert_fusion.7), channel_id=1, source_target_pairs={{0,1},{1,0},{2,3},{3,2},{4,5},{5,4},{6,7},{7,6},{8,9},{9,8},{10,11... | collective-permute-start | bytes 1769480 | tf_op jit(solution)/shard_map/ppermute | solution.py:47
  545.0 71.9 %collective-permute-start.76 = (bf16[768,1152]{1,0:T(8,128)(2,1)}, bf16[768,1152]{1,0:T(8,128)(2,1)S(1)}, u32[]{:S(2)}, u32[]{:S(2)}) collective-permute-start(bf16[768,1152]{1,0:T(8,128)(2,1)} %convolution_convert_fusion.3), channel_id=1, source_target_pairs={{0,1},{1,0},{2,3},{3,2},{4,5},{5,4},{6,7},{7,6},{8,9},{9,8},{10,11... | collective-permute-start | bytes 5308424 | tf_op jit(solution)/shard_map/ppermute | solution.py:47
  548.4 70.9 %collective-permute-start.83 = (bf16[768,1152]{1,0:T(8,128)(2,1)S(1)}, bf16[768,1152]{1,0:T(8,128)(2,1)S(1)}, u32[]{:S(2)}, u32[]{:S(2)}) collective-permute-start(bf16[768,1152]{1,0:T(8,128)(2,1)S(1)} %copy-done.161), channel_id=1, source_target_pairs={{0,1},{1,0},{2,3},{3,2},{4,5},{5,4},{6,7},{7,6},{8,9},{9,8},{10,11... | collective-permute-start | bytes 5308424 | tf_op jit(solution)/shard_map/ppermute | solution.py:47
  616.9 47.3 %collective-permute-start.104 = (bf16[768,1536]{1,0:T(8,128)(2,1)}, bf16[768,1536]{1,0:T(8,128)(2,1)}, u32[]{:S(2)}, u32[]{:S(2)}) collective-permute-start(bf16[768,1536]{1,0:T(8,128)(2,1)} %convolution_convert_fusion.5), channel_id=1, source_target_pairs={{0,1},{1,0},{2,3},{3,2},{4,5},{5,4},{6,7},{7,6},{8,9},{9,8},{10,11... | collective-permute-start | bytes 7077896 | tf_op jit(solution)/shard_map/ppermute | solution.py:47
  643.2 40.1 %collective-permute-start.78 = (bf16[4,96,576]{2,1,0:T(8,128)(2,1)}, bf16[4,96,576]{2,1,0:T(8,128)(2,1)}, u32[]{:S(2)}, u32[]{:S(2)}) collective-permute-start(bf16[4,96,576]{2,1,0:T(8,128)(2,1)} %add_convert_fusion.21), channel_id=1, source_target_pairs={{0,4},{4,0},{8,12},{12,8},{16,20},{20,16},{24,28},{28,24},{1,5},{5... | collective-permute-start | bytes 1327112 | tf_op jit(solution)/shard_map/ppermute | solution.py:50
  644.6 41.1 %collective-permute-start.85 = (bf16[4,96,576]{2,1,0:T(8,128)(2,1)}, bf16[4,96,576]{2,1,0:T(8,128)(2,1)}, u32[]{:S(2)}, u32[]{:S(2)}) collective-permute-start(bf16[4,96,576]{2,1,0:T(8,128)(2,1)} %add_convert_fusion.19), channel_id=1, source_target_pairs={{0,4},{4,0},{8,12},{12,8},{16,20},{20,16},{24,28},{28,24},{1,5},{5... | collective-permute-start | bytes 1327112 | tf_op jit(solution)/shard_map/ppermute | solution.py:50
  654.1 47.2 %collective-permute-start.119 = (bf16[4,384,192]{1,2,0:T(8,128)(2,1)}, bf16[4,384,192]{1,2,0:T(8,128)(2,1)S(1)}, u32[]{:S(2)}, u32[]{:S(2)}) collective-permute-start(bf16[4,384,192]{1,2,0:T(8,128)(2,1)} %slice.817), channel_id=1, source_target_pairs={{0,2},{1,3},{2,0},{3,1},{4,6},{5,7},{6,4},{7,5},{8,10},{9,11},{10,... | collective-permute-start | bytes 1769480 | tf_op jit(solution)/shard_map/ppermute | solution.py:47
  708.9 41.6 %collective-permute-start.113 = (bf16[4,96,768]{2,1,0:T(8,128)(2,1)S(1)}, bf16[4,96,768]{2,1,0:T(8,128)(2,1)S(1)}, u32[]{:S(2)}, u32[]{:S(2)}) collective-permute-start(bf16[4,96,768]{2,1,0:T(8,128)(2,1)S(1)} %add_convert_fusion.13), channel_id=1, source_target_pairs={{0,4},{4,0},{8,12},{12,8},{16,20},{20,16},{24,28},{28,24},{1,5},{5... | collective-permute-start | bytes 1769480 | tf_op jit(solution)/shard_map/ppermute | solution.py:50
  (279 other events, 3735.3 us)

commit v2 on v1

--- a/solution.py
+++ b/solution.py
@@ -3,6 +3,8 @@
 import jax
 import jax.numpy as jnp
 from jax import lax
+from jax.experimental import pallas as pl
+from jax.experimental.pallas import tpu as pltpu
 from jax.sharding import PartitionSpec as P
 
 HD = 64
@@ -11,6 +13,8 @@
 KEEP_RATE = 0.9
 EPSILON = 1e-06
 MASKED = -1e30
+GAIN_ONE, SHIFT_ONE, BIAS_QUERY, BIAS_VALUE, BIAS_PROJ, GAIN_TWO, SHIFT_TWO, BIAS_DOWN = range(8)
+MIB = 1024 * 1024
 ROOT_HALF = 0.7071067811865476
 ROOT_TWO_PI = 0.3989422804014327
 BF = jnp.bfloat16
@@ -52,97 +56,15 @@
     def ring_z(self, values):
         return lax.ppermute(values, "dp", [(i, (i + 2) % self.n_dp) for i in range(self.n_dp)])
 
-    def own_half(self, values, which, axis):
-        low, high = jnp.split(values, 2, axis=axis)
-        return jnp.where(which == 0, low, high)
-
-    def in_order(self, which, mine, other, axis):
-        return jnp.where(
-            which == 0,
-            jnp.concatenate([mine, other], axis=axis),
-            jnp.concatenate([other, mine], axis=axis),
-        )
-
-
-def gather_matrix(place, shard):
-    if not place.walked:
-        whole = lax.all_gather(shard, "dp", axis=0, tiled=True)
-        half = whole.shape[1] // 2
-        return (whole[:, :half], whole[:, half:])
-    rows, columns = shard.shape
-    blocks = [place.own_half(shard, place.core, 1)]
-    for _ in range(place.nz - 1):
-        blocks.append(place.ring_z(blocks[-1]))
-    halves = [place.own_half(block, place.y, 0) for block in blocks]
-    first = place.swap_x(halves[0])
-    rest = place.swap_x(jnp.stack(halves[1:]))
-    first_back = place.swap_seq(first, 2)
-    rest_back = place.swap_seq(rest, 2)
-    crossed = [place.in_order(place.y, first, first_back, 0)]
-    rest_all = place.in_order(place.y, rest, rest_back, 1)
-    crossed += [rest_all[i] for i in range(place.nz - 1)]
-    mine = jnp.zeros((place.nz, 2, rows, columns // 2), shard.dtype)
-    for step in range(place.nz):
-        at = (place.z - step) % place.nz
-        mine = lax.dynamic_update_slice(mine, blocks[step][None, None], (at, place.x, 0, 0))
-        mine = lax.dynamic_update_slice(mine, crossed[step][None, None], (at, 1 - place.x, 0, 0))
-    mine = mine.reshape(place.n_dp * rows, columns // 2)
-    return (mine, place.swap_seq(mine, 1))
-
-
-def times(place, values, halves):
-    low = dot_nn(values, halves[0])
-    high = dot_nn(values, halves[1])
-    if not place.walked:
-        return jnp.concatenate([low, high], axis=1)
-    return place.in_order(place.core, low, high, 1)
-
-
-def times_back(place, values, halves):
-    if not place.walked:
-        low, high = jnp.split(values, 2, axis=1)
-    else:
-        low = place.own_half(values, place.core, 1)
-        high = place.own_half(values, 1 - place.core, 1)
-    return dot_nt(low, halves[0]) + dot_nt(high, halves[1])
-
-
-def quarter(place, values, y, core):
-    pieces = jnp.split(values, 4, axis=1)
-    low = jnp.where(core == 0, pieces[0], pieces[1])
-    high = jnp.where(core == 0, pieces[2], pieces[3])
-    return jnp.where(y == 0, low, high)
-
-
-def reduce_matrix(place, acts, grads):
-    if not place.walked:
-        part = dot_tn(acts, grads).astype(BF)
-        part = lax.psum_scatter(part, "dp", scatter_dimension=0, tiled=True)
-        return lax.psum_scatter(part, "seq", scatter_dimension=1, tiled=True).astype(F32)
-    y, core, nz = place.y, place.core, place.nz
-    rows = acts.shape[1] // place.n_dp
-    wide = grads.shape[1] // 4
-    sent = jnp.concatenate([quarter(place, grads, y, 1 - core), quarter(place, grads, 1 - y, 1 - core)], 1)
-    kept = jnp.concatenate([quarter(place, grads, y, core), quarter(place, grads, 1 - y, core)], 1)
-    got = place.swap_seq(dot_tn(acts, sent).astype(BF), 1)
-    pair = (dot_tn(acts, kept) + got).astype(BF).reshape(nz, 2, rows, 2 * wide)
-    near = lax.dynamic_index_in_dim(pair, place.x, 1, keepdims=False)
-    far = lax.dynamic_index_in_dim(pair, 1 - place.x, 1, keepdims=False)
-    got = place.swap_seq(far[:, :, wide:], 2)
-    far = (far[:, :, :wide].astype(F32) + got).astype(BF)
-    got = place.swap_x(far)
-    near = jnp.concatenate(
-        [(near[:, :, :wide].astype(F32) + got).astype(BF), near[:, :, wide:]], axis=2
-    )
-
-    def block(step):
-        return lax.dynamic_index_in_dim(near, (place.z - step) % nz, 0, keepdims=False)
-
-    total = block(1)
-    for step in range(2, nz + 1):
-        total = (place.ring_z(total).astype(F32) + block(step)).astype(BF)
-    got = place.swap_seq(total[:, wide:], 2)
-    return total[:, :wide].astype(F32) + got
+
+def gather_matrix(shard):
+    return lax.all_gather(shard, "dp", axis=0, tiled=True)
+
+
+def reduce_matrix(acts, grads):
+    part = dot_tn(acts, grads).astype(BF)
+    part = lax.psum_scatter(part, "dp", scatter_dimension=0, tiled=True)
+    return lax.psum_scatter(part, "seq", scatter_dimension=1, tiled=True).astype(F32)
 
 
 def reduce_vectors(place, vectors):
@@ -229,22 +151,22 @@
     )
 
 
-def layer_forward(place, stream, vectors, matrices, keeps, key_ok):
+def layer_forward(stream, vectors, matrices, keeps, key_ok):
     gain_one, shift_one, bias_query, bias_value, bias_proj, gain_two, shift_two, bias_down, bias_up = vectors
     w_mixed, w_proj, w_up, w_down = matrices
     hat_one, scale_one = normalize(stream)
     normed_one = (hat_one * gain_one + shift_one).astype(BF)
     bias_mixed = jnp.concatenate([bias_query, jnp.zeros_like(bias_query), bias_value])
-    mixed = (times(place, normed_one, w_mixed) + bias_mixed).astype(BF)
+    mixed = (dot_nn(normed_one, w_mixed) + bias_mixed).astype(BF)
     attended, probs = attend(mixed, key_ok)
-    middle = stream + keeps[0] * (times(place, attended, w_proj) + bias_proj) / KEEP_RATE
+    middle = stream + keeps[0] * (dot_nn(attended, w_proj) + bias_proj) / KEEP_RATE
     hat_two, scale_two = normalize(middle)
     normed_two = (hat_two * gain_two + shift_two).astype(BF)
-    hidden_pre = times(place, normed_two, w_up) + bias_up
+    hidden_pre = dot_nn(normed_two, w_up) + bias_up
     share = 0.5 * (1.0 + lax.erf(hidden_pre * ROOT_HALF))
     hidden = (hidden_pre * share).astype(BF)
     slope = share + hidden_pre * jnp.exp(-0.5 * hidden_pre * hidden_pre) * ROOT_TWO_PI
-    output = middle + keeps[1] * (times(place, hidden, w_down) + bias_down) / KEEP_RATE
+    output = middle + keeps[1] * (dot_nn(hidden, w_down) + bias_down) / KEEP_RATE
     saved = (hat_one, scale_one, normed_one, mixed, probs, attended, hat_two, scale_two, normed_two, hidden, slope)
     return (output, saved)
 
@@ -255,20 +177,20 @@
     w_mixed, w_proj, w_up, w_down = matrices
     width = grad_stream.shape[1]
     grad_down = (keeps[1] * grad_stream / KEEP_RATE).astype(BF)
-    total_down = reduce_matrix(place, hidden, grad_down)
-    grad_up = (times_back(place, grad_down, w_down) * slope).astype(BF)
-    total_up = reduce_matrix(place, normed_two, grad_up)
+    total_down = reduce_matrix(hidden, grad_down)
+    grad_up = (dot_nt(grad_down, w_down) * slope).astype(BF)
+    total_up = reduce_matrix(normed_two, grad_up)
     back_two, grad_gain_two, grad_shift_two = normalize_back(
-        hat_two, scale_two, gain_two, times_back(place, grad_up, w_up)
+        hat_two, scale_two, gain_two, dot_nt(grad_up, w_up)
     )
     grad_middle = grad_stream + back_two
     grad_proj = (keeps[0] * grad_middle / KEEP_RATE).astype(BF)
-    total_proj = reduce_matrix(place, attended, grad_proj)
-    grad_attended = times_back(place, grad_proj, w_proj).astype(BF)
+    total_proj = reduce_matrix(attended, grad_proj)
+    grad_attended = dot_nt(grad_proj, w_proj).astype(BF)
     grad_mixed = attend_back(mixed, probs, grad_attended)
-    total_mixed = reduce_matrix(place, normed_one, grad_mixed)
+    total_mixed = reduce_matrix(normed_one, grad_mixed)
     back_one, grad_gain_one, grad_shift_one = normalize_back(
-        hat_one, scale_one, gain_one, times_back(place, grad_mixed, w_mixed)
+        hat_one, scale_one, gain_one, dot_nt(grad_mixed, w_mixed)
     )
     grad_input = grad_middle + back_one
     sum_mixed = jnp.sum(grad_mixed, axis=0, dtype=F32)
@@ -321,7 +243,8 @@
     return (own, stream[MOST : MOST + specials])
 
 
-def local(
+def local_plain(
+    place,
     patches,
     specials,
     lengths,
@@ -342,7 +265,6 @@
     cot_patches,
     cot_specials,
 ):
-    place = Place()
     count = patches.shape[0]
     special_count = specials.shape[0]
     images = lengths.shape[1]
@@ -362,7 +284,7 @@
     for layer in range(LAYERS):
         matrices.append(
             tuple(
-                gather_matrix(place, shard[layer])
+                gather_matrix(shard[layer])
                 for shard in (qkv_weight, proj_weight, fc1_weight, fc2_weight)
             )
         )
@@ -370,7 +292,7 @@
     saved = []
     for layer in range(LAYERS):
         stream, kept = layer_forward(
-            place, stream, vectors[layer], matrices[layer], keeps[2 * layer : 2 * layer + 2], key_ok
+            stream, vectors[layer], matrices[layer], keeps[2 * layer : 2 * layer + 2], key_ok
         )
         saved.append(kept)
     out_patches, out_specials = from_image(place, stream, halo, start, length, count, special_count)
@@ -406,6 +328,990 @@
     )
 
 
+def whole_vmem(count):
+    return [pl.BlockSpec(memory_space=pltpu.VMEM)] * count
+
+
+def in_smem(count):
+    return [pl.BlockSpec(memory_space=pltpu.SMEM)] * count
+
+
+def kernel_params(mib):
+    return pltpu.CompilerParams(vmem_limit_bytes=mib * MIB)
+
+
+def place_pieces(spot, parts, crossed, split, first, quarter):
+    z, x, y, core = (spot[i] for i in range(4))
+    steps = len(parts) // 2
+    for side in range(2):
+        at_core = core if side == 0 else 1 - core
+        for step in range(steps):
+            part = parts[side * steps + step]
+            at_z = lax.rem(z - step + steps, steps)
+            for far_x in range(2):
+                row = 2 * at_z + lax.rem(x + far_x, 2)
+                if crossed is not None:
+                    base = far_x * (first + 2 * quarter)
+                    for j in range(first):
+                        crossed[at_core, row, j] = part[base + j]
+                if split is not None:
+                    for far_y in range(2):
+                        base = first + far_y * (first + 2 * quarter) + far_x * quarter
+                        for j in range(quarter):
+                            split[at_core, row, lax.rem(y + far_y, 2) * quarter + j] = part[base + j]
+
+
+def flat(block):
+    return block.reshape(-1, block.shape[-1])
+
+
+def moments(values):
+    center = values - jnp.mean(values, axis=-1, keepdims=True)
+    scale = lax.rsqrt(jnp.mean(center * center, axis=-1, keepdims=True) + EPSILON)
+    return (center * scale, scale)
+
+
+def norm_back(hat, scale, gain, grad):
+    scaled = grad * gain
+    first = jnp.mean(scaled, axis=-1, keepdims=True)
+    second = jnp.mean(scaled * hat, axis=-1, keepdims=True)
+    return scale * (scaled - first - hat * second)
+
+
+def erf_of(values):
+    v = jnp.clip(values, -3.7439211627767994, 3.7439211627767994)
+    s = v * v
+    top = s * 0.00022905065861350646 + 0.0034082910107109506
+    top = top * s + 0.050955695062380861
+    top = top * s + 0.18520832239976145
+    top = top * s + 1.128379143519084
+    low = s * -1.1791602954361697e-7 + 0.000023547966471313185
+    low = low * s + 0.0010179625278914885
+    low = low * s + 0.014070470171167667
+    low = low * s + 0.11098505178285362
+    low = low * s + 0.49746925110067538
+    low = low * s + 1.0
+    return v * top / low
+
+
+def head_probs(queries, keys, blocked):
+    scores = dot_nt(queries, keys) * 0.125 + blocked
+    powers = jnp.exp(scores - jnp.max(scores, axis=1, keepdims=True))
+    return powers / jnp.sum(powers, axis=1, keepdims=True)
+
+
+def forward_attention_kernel(
+    spot, keep, stream, vectors, blocked, *refs
+):
+    parts, refs = refs[:8], refs[8:]
+    middle, normed_two, normed_one_t, normed_two_t, mixed, attended, attended_t, crossed, split = refs
+    place_pieces(spot, parts, crossed, split, 2, 1)
+    hat, _ = moments(stream[...])
+    normed = (hat * vectors[GAIN_ONE : GAIN_ONE + 1] + vectors[SHIFT_ONE : SHIFT_ONE + 1]).astype(BF)
+    normed_one_t[...] = normed.T
+    width = stream.shape[1]
+    half = width // 2
+    for core in range(2):
+        for j in range(3):
+            weight = crossed[core, :, j] if j < 2 else split[core, :, 0]
+            columns = pl.ds(j * width + core * half, half)
+            ahead = dot_nn(normed, flat(weight))
+            if j != 1:
+                row = BIAS_QUERY if j == 0 else BIAS_VALUE
+                ahead = ahead + vectors[row : row + 1, core * half : (core + 1) * half]
+            mixed[:, columns] = ahead.astype(BF)
+    lane = lax.broadcasted_iota(jnp.int32, (1, 2 * HD), 1)
+    for pair in range(width // (2 * HD)):
+        queries, keys, values = (
+            mixed[:, pl.ds(j * width + pair * 2 * HD, 2 * HD)] for j in range(3)
+        )
+        outs = []
+        for side in range(2):
+            mine = ((lane < HD) if side == 0 else (lane >= HD)).astype(F32).astype(BF)
+            probs = head_probs(queries * mine, keys, blocked[...])
+            outs.append(dot_nn(probs.astype(BF), values))
+        attended[:, pl.ds(pair * 2 * HD, 2 * HD)] = jnp.where(lane < HD, outs[0], outs[1]).astype(BF)
+    ahead = attended[...]
+    attended_t[...] = ahead.T
+    for core in range(2):
+        columns = pl.ds(core * half, half)
+        branch = dot_nn(ahead, flat(split[core, :, 1])) + vectors[BIAS_PROJ : BIAS_PROJ + 1, columns]
+        middle[:, columns] = stream[:, columns] + keep[0] * branch
+    hat, _ = moments(middle[...])
+    normed = (hat * vectors[GAIN_TWO : GAIN_TWO + 1] + vectors[SHIFT_TWO : SHIFT_TWO + 1]).astype(BF)
+    normed_two[...] = normed
+    normed_two_t[...] = normed.T
+
+
+def forward_attention(place, spot, keep, stream, vectors, parts, blocked):
+    rows, width = stream.shape
+    group = parts[0].shape[1:]
+    shapes = [
+        jax.ShapeDtypeStruct((rows, width), F32),
+        jax.ShapeDtypeStruct((rows, width), BF),
+        jax.ShapeDtypeStruct((width, rows), BF),
+        jax.ShapeDtypeStruct((width, rows), BF),
+        jax.ShapeDtypeStruct((rows, 3 * width), BF),
+        jax.ShapeDtypeStruct((rows, width), BF),
+        jax.ShapeDtypeStruct((width, rows), BF),
+    ]
+    return pl.pallas_call(
+        forward_attention_kernel,
+        in_specs=in_smem(2) + whole_vmem(3) + whole_vmem(8),
+        out_specs=whole_vmem(len(shapes)),
+        out_shape=shapes,
+        scratch_shapes=[
+            pltpu.VMEM((2, place.n_dp, 2) + group, BF),
+            pltpu.VMEM((2, place.n_dp, 2) + group, BF),
+        ],
+        compiler_params=kernel_params(14),
+        name="forward_attention",
+    )(spot, keep, stream, vectors, blocked, *parts)
+
+
+def forward_feed_kernel(spot, keep, middle, normed, bias_up, vectors, *refs):
+    parts, refs = refs[:8], refs[8:]
+    output, hidden, slope, crossed, split = refs
+    place_pieces(spot, parts, crossed, split, 4, 2)
+    values = normed[...]
+    half = values.shape[1] // 2
+    for core in range(2):
+        for j in range(4):
+            columns = pl.ds((core * 4 + j) * half, half)
+            pre = dot_nn(values, flat(crossed[core, :, j])) + bias_up[:, columns]
+            share = 0.5 + 0.5 * erf_of(pre * ROOT_HALF)
+            hidden[:, columns] = (pre * share).astype(BF)
+            slope[:, columns] = (share + pre * jnp.exp(-0.5 * pre * pre) * ROOT_TWO_PI).astype(BF)
+    ahead = hidden[...]
+    for core in range(2):
+        columns = pl.ds(core * half, half)
+        branch = dot_nn(ahead, flat(split[core])) + vectors[BIAS_DOWN : BIAS_DOWN + 1, columns]
+        output[:, columns] = middle[:, columns] + keep[0] * branch
+
+
+def forward_feed(place, spot, keep, middle, normed, bias_up, vectors, parts):
+    rows, width = middle.shape
+    group = parts[0].shape[1:]
+    shapes = [
+        jax.ShapeDtypeStruct((rows, width), F32),
+        jax.ShapeDtypeStruct((rows, 4 * width), BF),
+        jax.ShapeDtypeStruct((rows, 4 * width), BF),
+    ]
+    return pl.pallas_call(
+        forward_feed_kernel,
+        in_specs=in_smem(2) + whole_vmem(4) + whole_vmem(8),
+        out_specs=whole_vmem(len(shapes)),
+        out_shape=shapes,
+        scratch_shapes=[
+            pltpu.VMEM((2, place.n_dp, 4) + group, BF),
+            pltpu.VMEM((2, place.n_dp, 4) + group, BF),
+        ],
+        compiler_params=kernel_params(20),
+        name="forward_feed",
+    )(spot, keep, middle, normed, bias_up, vectors, *parts)
+
+
+def backward_feed_kernel(spot, keep, grad, slope, *refs):
+    parts, refs = refs[:8], refs[8:]
+    grad_down_t, grad_up, sum_down, sum_up, split = refs
+    place_pieces(spot, parts, None, split, 4, 2)
+    down = (keep[0] * grad[...]).astype(BF)
+    grad_down_t[...] = down.T
+    sum_down[...] = jnp.sum(down.astype(F32), axis=0, keepdims=True)
+    half = grad.shape[1] // 2
+    for row in range(split.shape[1]):
+        columns = pl.ds(row * half, half)
+        ahead = dot_nt(down[:, :half], flat(split[0, row])) + dot_nt(down[:, half:], flat(split[1, row]))
+        up = (ahead * slope[:, columns].astype(F32)).astype(BF)
+        grad_up[:, columns] = up
+        sum_up[:, columns] = jnp.sum(up.astype(F32), axis=0, keepdims=True)
+
+
+def backward_feed(place, spot, keep, grad, slope, parts):
+    rows, width = grad.shape
+    group = parts[0].shape[1:]
+    shapes = [
+        jax.ShapeDtypeStruct((width, rows), BF),
+        jax.ShapeDtypeStruct((rows, 4 * width), BF),
+        jax.ShapeDtypeStruct((1, width), F32),
+        jax.ShapeDtypeStruct((1, 4 * width), F32),
+    ]
+    return pl.pallas_call(
+        backward_feed_kernel,
+        in_specs=in_smem(2) + whole_vmem(2) + whole_vmem(8),
+        out_specs=whole_vmem(len(shapes)),
+        out_shape=shapes,
+        scratch_shapes=[
+            pltpu.VMEM((2, place.n_dp, 4) + group, BF),
+        ],
+        compiler_params=kernel_params(14),
+        name="backward_feed",
+    )(spot, keep, grad, slope, *parts)
+
+
+def backward_middle_kernel(spot, keep, grad, grad_up, middle, vectors, *refs):
+    parts, refs = refs[:8], refs[8:]
+    grad_middle, grad_proj, sum_proj, grad_gain, grad_shift, crossed = refs
+    place_pieces(spot, parts, crossed, None, 4, 2)
+    hat, scale = moments(middle[...])
+    half = grad.shape[1] // 2
+    total = jnp.zeros(grad.shape, F32)
+    for core in range(2):
+        for j in range(4):
+            total += dot_nt(grad_up[:, pl.ds((core * 4 + j) * half, half)], flat(crossed[core, :, j]))
+    grad_gain[...] = jnp.sum(total * hat, axis=0, keepdims=True)
+    grad_shift[...] = jnp.sum(total, axis=0, keepdims=True)
+    after = grad[...] + norm_back(hat, scale, vectors[GAIN_TWO : GAIN_TWO + 1], total)
+    grad_middle[...] = after
+    proj = (keep[0] * after).astype(BF)
+    grad_proj[...] = proj
+    sum_proj[...] = jnp.sum(proj.astype(F32), axis=0, keepdims=True)
+
+
+def backward_middle(place, spot, keep, grad, grad_up, middle, vectors, parts):
+    rows, width = grad.shape
+    group = parts[0].shape[1:]
+    shapes = [
+        jax.ShapeDtypeStruct((rows, width), F32),
+        jax.ShapeDtypeStruct((rows, width), BF),
+    ] + [jax.ShapeDtypeStruct((1, width), F32)] * 3
+    return pl.pallas_call(
+        backward_middle_kernel,
+        in_specs=in_smem(2) + whole_vmem(4) + whole_vmem(8),
+        out_specs=whole_vmem(len(shapes)),
+        out_shape=shapes,
+        scratch_shapes=[
+            pltpu.VMEM((2, place.n_dp, 4) + group, BF),
+        ],
+        compiler_params=kernel_params(14),
+        name="backward_middle",
+    )(spot, keep, grad, grad_up, middle, vectors, *parts)
+
+
+def backward_attention_kernel(spot, grad_middle, grad_proj, mixed, stream, vectors, blocked, *refs):
+    others, parts, refs = refs[:5], refs[5:13], refs[13:]
+    grad_stream, grad_mixed, sums, ahead, crossed, split = refs
+    sum_proj, gain_two, shift_two, sum_down, sum_up = others
+    place_pieces(spot, parts, crossed, split, 2, 1)
+    hat, scale = moments(stream[...])
+    width = stream.shape[1]
+    half = width // 2
+    proj = grad_proj[...]
+    ahead[...] = (
+        dot_nt(proj[:, :half], flat(split[0, :, 1])) + dot_nt(proj[:, half:], flat(split[1, :, 1]))
+    ).astype(BF)
+    lane = lax.broadcasted_iota(jnp.int32, (1, 2 * HD), 1)
+    for pair in range(width // (2 * HD)):
+        queries, keys, values = (
+            mixed[:, pl.ds(j * width + pair * 2 * HD, 2 * HD)] for j in range(3)
+        )
+        grads = ahead[:, pl.ds(pair * 2 * HD, 2 * HD)]
+        found = []
+        for side in range(2):
+            mine = ((lane < HD) if side == 0 else (lane >= HD)).astype(F32).astype(BF)
+            probs = head_probs(queries * mine, keys, blocked[...])
+            grad_probs = dot_nt(grads * mine, values)
+            inner = jnp.sum(probs * grad_probs, axis=1, keepdims=True)
+            grad_scores = (probs * (grad_probs - inner)).astype(BF)
+            found.append(
+                (
+                    dot_nn(grad_scores, keys) * 0.125,
+                    dot_tn(grad_scores, queries) * 0.125,
+                    dot_tn(probs.astype(BF), grads),
+                )
+            )
+        for j in range(3):
+            grad_mixed[:, pl.ds(j * width + pair * 2 * HD, 2 * HD)] = jnp.where(
+                lane < HD, found[0][j], found[1][j]
+            ).astype(BF)
+    total = jnp.zeros(stream.shape, F32)
+    for core in range(2):
+        for j in range(3):
+            weight = crossed[core, :, j] if j < 2 else split[core, :, 0]
+            total += dot_nt(grad_mixed[:, pl.ds(j * width + core * half, half)], flat(weight))
+
+    def put(row, values):
+        sums[row : row + 1, :] = values
+
+    put(GAIN_ONE, jnp.sum(total * hat, axis=0, keepdims=True))
+    put(SHIFT_ONE, jnp.sum(total, axis=0, keepdims=True))
+    put(BIAS_QUERY, jnp.sum(grad_mixed[:, :width].astype(F32), axis=0, keepdims=True))
+    put(BIAS_VALUE, jnp.sum(grad_mixed[:, 2 * width :].astype(F32), axis=0, keepdims=True))
+    put(BIAS_PROJ, sum_proj[...])
+    put(GAIN_TWO, gain_two[...])
+    put(SHIFT_TWO, shift_two[...])
+    put(BIAS_DOWN, sum_down[...])
+    for j in range(4):
+        put(BIAS_DOWN + 1 + j, sum_up[:, j * width : (j + 1) * width])
+    sums[BIAS_DOWN + 5 :, :] = jnp.zeros((sums.shape[0] - BIAS_DOWN - 5, width), F32)
+    grad_stream[...] = grad_middle[...] + norm_back(hat, scale, vectors[GAIN_ONE : GAIN_ONE + 1], total)
+
+
+def backward_attention(place, spot, grad_middle, grad_proj, mixed, stream, vectors, blocked, others, parts):
+    rows, width = stream.shape
+    group = parts[0].shape[1:]
+    shapes = [
+        jax.ShapeDtypeStruct((rows, width), F32),
+        jax.ShapeDtypeStruct((rows, 3 * width), BF),
+        jax.ShapeDtypeStruct((16, width), F32),
+    ]
+    return pl.pallas_call(
+        backward_attention_kernel,
+        in_specs=in_smem(1) + whole_vmem(6 + 5 + 8),
+        out_specs=whole_vmem(len(shapes)),
+        out_shape=shapes,
+        scratch_shapes=[
+            pltpu.VMEM((rows, width), BF),
+            pltpu.VMEM((2, place.n_dp, 2) + group, BF),
+            pltpu.VMEM((2, place.n_dp, 2) + group, BF),
+        ],
+        compiler_params=kernel_params(16),
+        name="backward_attention",
+    )(spot, grad_middle, grad_proj, mixed, stream, vectors, blocked, *others, *parts)
+
+
+def row_of(spot, step, far_x, steps):
+    return 2 * lax.rem(spot[0] - step + steps, steps) + lax.rem(spot[1] + far_x, 2)
+
+
+def feed_group(spot, core, part, far_y, j, normed_t, grad_up, grad_down_t, hidden, spare):
+    half = spare.shape[2]
+    column = 2 * lax.rem(spot[2] + far_y, 2) + core
+    if part == 0:
+        at = pl.multiple_of((column * 2 + j) * half, half)
+        out = dot_nn(normed_t[...], grad_up[:, pl.ds(at, half)])
+        spare[...] = out.reshape(spare.shape).astype(BF)
+    else:
+        rows = spare.shape[1]
+        at = pl.multiple_of((column * 2 + j) * rows, rows)
+        left = grad_down_t[pl.ds(at, rows), :]
+        for row in range(spare.shape[0]):
+            spare[row] = dot_nn(left, hidden[:, pl.ds(row * half, half)]).astype(BF)
+
+
+def attention_group(spot, core, part, far_y, j, normed_t, grad_mixed, attended_t, grad_proj, spare):
+    half = spare.shape[2]
+    column = 2 * lax.rem(spot[2] + far_y, 2) + core
+    if part == 0:
+        out = dot_nn(normed_t[...], grad_mixed[column, :, :half])
+    else:
+        out = dot_nn(normed_t[...], grad_mixed[column, :, half:]) + dot_nn(
+            attended_t[...], grad_proj[column]
+        )
+    spare[...] = out.reshape(spare.shape).astype(BF)
+
+
+def sent_kernel(fill, wide, steps, spot, *refs):
+    operands, out, spare = refs[:4], refs[4], refs[5]
+    for part in range(2):
+        for far_y in range(2):
+            for j in range(wide):
+                fill(spot, 1 - spot[3], part, far_y, j, *operands, spare)
+                for step in range(steps):
+                    for far_x in range(2):
+                        if part == 0:
+                            at = (far_x * 2 + far_y) * wide + j
+                        else:
+                            at = (4 + far_y * 2 + far_x) * wide + j
+                        out[step, at] = spare[row_of(spot, step, far_x, steps)]
+
+
+def kept_kernel(fill, wide, steps, spot, *refs):
+    operands, got, outs, spare = refs[:4], refs[4], refs[5 : 5 + 3 * steps], refs[5 + 3 * steps]
+    for part in range(2):
+        for far_y in range(2):
+            for j in range(wide):
+                fill(spot, spot[3], part, far_y, j, *operands, spare)
+                for step in range(steps):
+                    for far_x in range(2):
+                        if part == 0:
+                            at = (far_x * 2 + far_y) * wide + j
+                        else:
+                            at = (4 + far_y * 2 + far_x) * wide + j
+                        total = spare[row_of(spot, step, far_x, steps)].astype(F32) + got[step, at].astype(F32)
+                        total = total.astype(BF)
+                        across, aside, stays = outs[3 * step : 3 * step + 3]
+                        if part == 0:
+                            target, index = (across, far_y * wide + j) if far_x else (stays, far_y * wide + j)
+                        else:
+                            index = far_x * wide + j
+                            target, index = (aside, index) if far_y else (stays, 2 * wide + index)
+                        target[index] = total
+
+
+def sent_part(place, spot, fill, wide, operands):
+    rows, half = (operands[0].shape[0] // place.n_dp, operands[0].shape[0] // 2)
+    return pl.pallas_call(
+        partial(sent_kernel, fill, wide, place.nz),
+        in_specs=in_smem(1) + whole_vmem(4),
+        out_specs=whole_vmem(1)[0],
+        out_shape=jax.ShapeDtypeStruct((place.nz, 8 * wide, rows, half), BF),
+        scratch_shapes=[pltpu.VMEM((place.n_dp, rows, half), BF)],
+        compiler_params=kernel_params(10),
+        name="gradient_sent",
+    )(spot, *operands)
+
+
+def kept_part(place, spot, fill, wide, operands, got):
+    rows, half = (operands[0].shape[0] // place.n_dp, operands[0].shape[0] // 2)
+    shapes = [
+        jax.ShapeDtypeStruct((size * wide, rows, half), BF)
+        for _ in range(place.nz)
+        for size in (2, 2, 4)
+    ]
+    outs = pl.pallas_call(
+        partial(kept_kernel, fill, wide, place.nz),
+        in_specs=in_smem(1) + whole_vmem(5),
+        out_specs=whole_vmem(len(shapes)),
+        out_shape=shapes,
+        scratch_shapes=[pltpu.VMEM((place.n_dp, rows, half), BF)],
+        compiler_params=kernel_params(10),
+        name="gradient_kept",
+    )(spot, *operands, got)
+    return [outs[3 * step : 3 * step + 3] for step in range(place.nz)]
+
+
+def ring_kernel(stays, across, aside, *refs):
+    out = refs[-1]
+    count = across.shape[0]
+    for at in range(2 * count):
+        side = across[at] if at < count else aside[at - count]
+        total = stays[at].astype(F32) + side.astype(F32)
+        if len(refs) == 2:
+            total = total + refs[0][at].astype(F32)
+        out[at] = total.astype(BF)
+
+
+def ring_block(stays, across, aside, running):
+    operands = [stays, across, aside] + ([] if running is None else [running])
+    return pl.pallas_call(
+        ring_kernel,
+        in_specs=whole_vmem(len(operands)),
+        out_specs=whole_vmem(1)[0],
+        out_shape=jax.ShapeDtypeStruct(stays.shape, BF),
+        compiler_params=kernel_params(4),
+        name="ring_block",
+    )(*operands)
+
+
+def fence(trees):
+    flat = [list(tree.values()) if isinstance(tree, dict) else tree for tree in trees]
+    flat = lax.optimization_barrier(flat)
+    return [
+        dict(zip(tree, values)) if isinstance(tree, dict) else values
+        for tree, values in zip(trees, flat)
+    ]
+
+
+def pick(which, low, high):
+    return jnp.where(which == 0, low, high)
+
+
+def own_groups(place, qkv, proj, up, down):
+    rows, half = proj.shape[0], proj.shape[1] // 2
+    wide = 2 * half
+
+    def attention_groups(core):
+        parts = [qkv[:, j * wide + core * half : j * wide + (core + 1) * half] for j in range(3)]
+        return jnp.stack(parts + [proj[:, core * half : (core + 1) * half]])
+
+    def feed_groups(core):
+        parts = [up[:, (core * 4 + j) * half : (core * 4 + j + 1) * half] for j in range(4)]
+        return jnp.concatenate(
+            [jnp.stack(parts), down[:, core * half : (core + 1) * half].reshape(4, rows, half)]
+        )
+
+    return (
+        pick(place.core, attention_groups(0), attention_groups(1)),
+        pick(place.core, feed_groups(0), feed_groups(1)),
+    )
+
+
+class Gathered:
+    def __init__(self, own, place):
+        groups = own.shape[0]
+        self.first = groups // 2
+        self.quarter = groups // 4
+        self.own = own
+        self.mine = pick(
+            place.y,
+            own[self.first : self.first + self.quarter],
+            own[self.first + self.quarter :],
+        )
+        self.blocks = []
+        self.whole = []
+        self.mate = []
+
+    def begin(self, crossed):
+        self.blocks.append(jnp.concatenate([self.own[: self.first], self.mine, crossed]))
+
+    def parts(self):
+        return self.whole + self.mate
+
+
+class Reduced:
+    def __init__(self, place):
+        self.place = place
+        self.operands = None
+        self.sent = None
+        self.kept = None
+        self.sides = {}
+        self.running = None
+        self.last = None
+
+    def block(self, step):
+        return ring_block(self.kept[step][2], *self.sides[step], self.running)
+
+
+def gather_vectors_packed(place, vectors, bias_up):
+    rows, part = vectors[0].shape
+    packed = jnp.concatenate([jnp.stack(vectors, axis=1), bias_up.reshape(rows, -1, part)], axis=1)
+    spread = jnp.broadcast_to(packed[None], (place.n_dp,) + packed.shape)
+    spread = lax.all_to_all(spread, "dp", split_axis=0, concat_axis=0, tiled=True).astype(F32)
+    count = len(vectors)
+    return (
+        jnp.transpose(spread[:, :, :count], (1, 2, 0, 3)).reshape(rows, count, -1),
+        jnp.transpose(spread[:, :, count:], (1, 0, 2, 3)).reshape(rows, 1, -1),
+    )
+
+
+def image_kernel(frame, before, patches, after, specials, out, window):
+    halo, count = before.shape[0], patches.shape[0]
+    window[:halo] = before[...]
+    window[halo : halo + count] = patches[...]
+    window[halo + count : 2 * halo + count] = after[...]
+    spare = window.shape[0] - 2 * halo - count
+    window[2 * halo + count :] = jnp.zeros((spare, window.shape[1]), F32)
+    inside = lax.broadcasted_iota(jnp.int32, (MOST, 1), 0) < frame[1]
+    turned = pltpu.roll(window[...], lax.rem(window.shape[0] - frame[0], window.shape[0]), 0)
+    out[:MOST] = jnp.where(inside, turned[:MOST], 0.0)
+    last = out.shape[0] - MOST
+    out[MOST:] = jnp.zeros((last, out.shape[1]), F32)
+    out[MOST : MOST + specials.shape[0]] = specials[...]
+
+
+def take_image(place, frame, patches, specials, halo, rows):
+    count, width = patches.shape
+    before = shift_seq(place, patches[count - halo :], 1)
+    after = shift_seq(place, patches[:halo], -1)
+
+    def build(before, patches, after, specials):
+        return pl.pallas_call(
+            image_kernel,
+            in_specs=in_smem(1) + whole_vmem(4),
+            out_specs=whole_vmem(1)[0],
+            out_shape=jax.ShapeDtypeStruct((rows, width), F32),
+            scratch_shapes=[pltpu.VMEM((MOST + 2 * halo, width), F32)],
+            compiler_params=kernel_params(6),
+            name="take_image",
+        )(frame, before, patches, after, specials)
+
+    return (before, patches, after, specials), build
+
+
+def block_kernel(frame, stream, own, before, after, specials, window):
+    halo, count = before.shape[0], own.shape[0]
+    window[MOST:] = jnp.zeros((window.shape[0] - MOST, window.shape[1]), F32)
+    inside = lax.broadcasted_iota(jnp.int32, (MOST, 1), 0) < frame[1]
+    window[:MOST] = jnp.where(inside, stream[:MOST], 0.0)
+    window[...] = pltpu.roll(window[...], frame[0], 0)
+    before[...] = window[:halo]
+    own[...] = window[halo : halo + count]
+    after[...] = window[halo + count : 2 * halo + count]
+    specials[...] = stream[MOST : MOST + specials.shape[0]]
+
+
+def give_image(place, frame, stream, halo, count, special_count):
+    width = stream.shape[1]
+    own, before, after, specials = pl.pallas_call(
+        block_kernel,
+        in_specs=in_smem(1) + whole_vmem(1),
+        out_specs=whole_vmem(4),
+        out_shape=[
+            jax.ShapeDtypeStruct((size, width), F32) for size in (count, halo, halo, special_count)
+        ],
+        scratch_shapes=[pltpu.VMEM((MOST + 2 * halo, width), F32)],
+        compiler_params=kernel_params(6),
+        name="give_image",
+    )(frame, stream)
+    return (own, shift_seq(place, after, 1), shift_seq(place, before, -1), specials)
+
+
+def join_image(own, from_before, from_after, specials):
+    halo = from_before.shape[0]
+    blank = jnp.zeros((own.shape[0] - halo, own.shape[1]), own.dtype)
+    return (
+        own + jnp.concatenate([from_before, blank]) + jnp.concatenate([blank, from_after]),
+        specials,
+    )
+
+
+def finish_kernel(*refs):
+    inputs, (out_mixed, out_proj, out_up, out_down) = refs[:-4], refs[-4:]
+    layers = len(inputs) // 6
+    for layer in range(layers):
+        last, aside, across = inputs[6 * layer : 6 * layer + 3]
+        one = last[0].astype(F32) + aside[0].astype(F32)
+        two = last[2].astype(F32) + across[0].astype(F32)
+        cut = one.shape[1] // 2
+        out_mixed[layer] = jnp.concatenate([one, two[:, :cut]], axis=1)
+        out_proj[layer] = two[:, cut:]
+        last, aside, across = inputs[6 * layer + 3 : 6 * layer + 6]
+        half = last.shape[2]
+        for j in range(2):
+            out_up[layer, :, j * half : (j + 1) * half] = last[j].astype(F32) + aside[j].astype(F32)
+        downs = [last[4 + j].astype(F32) + across[j].astype(F32) for j in range(2)]
+        out_down[layer] = jnp.concatenate(downs, axis=0).T
+
+
+def finish(place, parts, rows, width):
+    shapes = [
+        jax.ShapeDtypeStruct((LAYERS, rows, columns), F32)
+        for rows, columns in (
+            (rows, 3 * width // 4),
+            (rows, width // 4),
+            (rows, width),
+            (4 * rows, width // 4),
+        )
+    ]
+    flat_parts = [array for layer in parts for array in layer]
+    return pl.pallas_call(
+        finish_kernel,
+        in_specs=whole_vmem(len(flat_parts)),
+        out_specs=whole_vmem(len(shapes)),
+        out_shape=shapes,
+        compiler_params=kernel_params(10),
+        name="finish",
+    )(*flat_parts)
+
+
+def local_walked(
+    place,
+    patches,
+    specials,
+    lengths,
+    keep_mask,
+    norm1_gain,
+    norm1_bias,
+    qkv_weight,
+    query_bias,
+    value_bias,
+    proj_weight,
+    proj_bias,
+    norm2_gain,
+    norm2_bias,
+    fc1_weight,
+    fc1_bias,
+    fc2_weight,
+    fc2_bias,
+    cot_patches,
+    cot_specials,
+):
+    count, width = patches.shape
+    special_count = specials.shape[0]
+    images = lengths.shape[1]
+    halo = (MOST - count) * (images // 2)
+    rows = -(-(MOST + special_count) // 16) * 16
+    nz = place.nz
+    part_rows = proj_weight.shape[1]
+    before = jnp.sum(jnp.where(jnp.arange(images) < place.seq, lengths[0], 0))
+    length = lax.dynamic_index_in_dim(lengths[0], place.seq, 0, keepdims=False)
+    frame = jnp.stack([before - place.seq * count + halo, length]).astype(jnp.int32)
+    keeps = lax.dynamic_index_in_dim(keep_mask[0], place.seq, 0, keepdims=False).astype(F32)
+    keeps = [keeps[i : i + 1] / KEEP_RATE for i in range(2 * LAYERS)]
+    row_ids = jnp.arange(rows, dtype=jnp.int32)
+    key_ok = (row_ids < length) | ((row_ids >= MOST) & (row_ids < MOST + special_count))
+    blocked = jnp.where(key_ok, 0.0, MASKED).astype(F32)[None]
+    spot = jnp.stack([place.z, place.x, place.y, place.core]).astype(jnp.int32)
+
+    units = []
+    for layer in range(LAYERS):
+        attention_own, feed_own = own_groups(
+            place, qkv_weight[layer], proj_weight[layer], fc1_weight[layer], fc2_weight[layer]
+        )
+        units.append(Gathered(attention_own, place))
+        units.append(Gathered(feed_own, place))
+
+    first_cross = place.swap_x(units[0].mine)
+    inputs = {
+        "later": [unit.mine for unit in units[1:]],
+        "own": [unit.own for unit in units[1:]],
+        "rows": (patches, specials),
+        "cots": (cot_patches, cot_specials),
+        "vectors": (norm1_gain, norm1_bias, query_bias, value_bias, proj_bias, norm2_gain, norm2_bias, fc2_bias),
+        "bias": fc1_bias,
+    }
+    first_cross, inputs = fence((first_cross, inputs))
+    units[0].begin(first_cross)
+    for unit, own in zip(units[1:], inputs.pop("own")):
+        unit.own = own
+
+    vectors, bias_up = (None, None)
+    streams = [None] * (LAYERS + 1)
+    middles, normed_one_ts, normed_two_ts, mixeds, attended_ts, hiddens, slopes = (
+        [None] * LAYERS for _ in range(7)
+    )
+    cores = []
+    carried = {}
+    grad = None
+    for slot in range(3 * len(units) + 2):
+        new = {}
+        index, step = divmod(slot, 3)
+        todo = []
+        if index < len(units):
+            new["z"] = place.ring_z(units[index].blocks[step])
+            todo.append((index, step))
+        if step == 0 and index > 0:
+            todo.append((index - 1, 3))
+        for which, at in todo:
+            unit = units[which]
+            new["x", which, at] = place.swap_x(unit.blocks[at][: unit.first])
+            new["y", which, at] = place.swap_seq(unit.blocks[at][unit.first :], 2)
+        for which, at in cores:
+            new["core", which, at] = place.swap_seq(units[which].whole[at], 1)
+        if slot == 0:
+            new["later"] = place.swap_x(jnp.concatenate(inputs["later"]))
+        if slot in (1, 4):
+            new["image"], build = take_image(place, frame, *inputs["rows" if slot == 1 else "cots"], halo, rows)
+        if slot == 2:
+            carried["stream"] = build(*image)
+        if slot == 5:
+            grad = build(*image)
+        if slot == 3:
+            new["vectors"] = gather_vectors_packed(place, inputs["vectors"], inputs["bias"])
+        if slot in (5, 11):
+            layer = slot // 6
+            new["forward"] = forward_attention(
+                place, spot, keeps[2 * layer], carried["stream"], vectors[layer], units[2 * layer].parts(), blocked
+            )
+        if slot == 9:
+            new["feed"] = forward_feed(
+                place, spot, keeps[1], carried["middle"], carried["normed"], bias_up[0], vectors[0], units[1].parts()
+            )
+        after = (slot + 1) // 3
+        if slot % 3 == 2 and after < len(units):
+            carried["begin"] = units[after].blocks[0]
+        gate = inputs if slot < 4 else {}
+        new, carried, gate = fence((new, carried, gate))
+        inputs.update(gate)
+        if "begin" in carried:
+            units[after].blocks[0] = carried.pop("begin")
+        if "image" in new:
+            image = new["image"]
+        if "vectors" in new:
+            vectors, bias_up = new["vectors"]
+        if "later" in new:
+            at = 0
+            for unit in units[1:]:
+                unit.begin(new["later"][at : at + unit.quarter])
+                at += unit.quarter
+        if "z" in new:
+            units[index].blocks.append(new["z"])
+        for which, at in cores:
+            units[which].mate.append(new["core", which, at])
+        cores = todo
+        for which, at in todo:
+            unit = units[which]
+            unit.whole.append(
+                jnp.concatenate([unit.blocks[at], new["x", which, at], new["y", which, at]])
+            )
+        if "forward" in new:
+            streams[layer] = carried.pop("stream")
+            middle, normed, normed_one_ts[layer], normed_two_ts[layer], mixeds[layer], _, attended_ts[layer] = new["forward"]
+            middles[layer] = middle
+            carried["middle"], carried["normed"] = middle, normed
+        if "feed" in new:
+            carried["stream"], hiddens[0], slopes[0] = new["feed"]
+            del carried["middle"], carried["normed"]
+    streams[LAYERS], hiddens[1], slopes[1] = forward_feed(
+        place, spot, keeps[3], carried["middle"], carried["normed"], bias_up[1], vectors[1], units[3].parts()
+    )
+
+    reduces = [Reduced(place) for _ in range(2 * LAYERS)]
+    lasts = [None] * (2 * LAYERS)
+    back = [{} for _ in range(LAYERS)]
+
+    def feed_back(layer, grad):
+        found = back[layer]
+        found["down_t"], found["up"], found["sum_down"], found["sum_up"] = backward_feed(
+            place, spot, keeps[2 * layer + 1], grad, slopes[layer], units[2 * layer + 1].parts()
+        )
+
+    def feed_sent(layer):
+        unit = reduces[2 * (LAYERS - 1 - layer)]
+        unit.operands = (normed_two_ts[layer], back[layer]["up"], back[layer]["down_t"], hiddens[layer])
+        unit.sent = sent_part(place, spot, feed_group, 2, unit.operands)
+
+    def middle_back(layer, grad):
+        found = back[layer]
+        found["middle"], found["proj"], found["sum_proj"], found["gain"], found["shift"] = backward_middle(
+            place, spot, keeps[2 * layer], grad, found["up"], middles[layer], vectors[layer], units[2 * layer + 1].parts()
+        )
+
+    def attention_back(layer):
+        found = back[layer]
+        others = [found[name] for name in ("sum_proj", "gain", "shift", "sum_down", "sum_up")]
+        found["grad"], found["mixed"], found["sums"] = backward_attention(
+            place, spot, found["middle"], found["proj"], mixeds[layer], streams[layer], vectors[layer], blocked, others, units[2 * layer].parts()
+        )
+
+    def attention_sent(layer):
+        found = back[layer]
+        wide = 3 * width // 4
+        cut = width // 4
+        mixed = jnp.stack(
+            [jnp.pad(found["mixed"][:, i * wide : (i + 1) * wide], ((0, 0), (0, cut))) for i in range(4)]
+        )
+        proj = jnp.stack([jnp.pad(found["proj"][:, i * cut : (i + 1) * cut], ((0, 0), (cut, 0))) for i in range(4)])
+        unit = reduces[2 * (LAYERS - 1 - layer) + 1]
+        unit.operands = (normed_one_ts[layer], mixed, attended_ts[layer], proj)
+        unit.sent = sent_part(place, spot, attention_group, 1, unit.operands)
+
+    feed_back(1, grad)
+    feed_sent(1)
+    back[1], back_sent, output = fence((back[1], [reduces[0].sent], streams[LAYERS]))
+    reduces[0].sent = back_sent[0]
+    final_slot = 3 * len(reduces)
+    outs = {}
+    total = None
+    ringing = None
+    for slot in range(-2, final_slot + 1):
+        new = {}
+        for which, unit in enumerate(reduces):
+            at = slot - 3 * which
+            fill, wide = (attention_group, 1) if which % 2 else (feed_group, 2)
+            if at == -2:
+                new["core", which] = place.swap_seq(unit.sent, 1)
+            if at == -1:
+                unit.kept = kept_part(place, spot, fill, wide, unit.operands, unit.got)
+            if -1 <= at <= 2:
+                step = (at + 2) % nz
+                new["side", which] = (
+                    place.swap_x(unit.kept[step][0]),
+                    place.swap_seq(unit.kept[step][1], 2),
+                )
+            if 0 <= at <= 2:
+                new["z", which] = place.ring_z(unit.block(at + 1))
+            if at == 3:
+                last = unit.block(0)
+                part = last.shape[0] // 4
+                lasts[which] = [
+                    last,
+                    place.swap_seq(last[part : 2 * part], 2),
+                    place.swap_x(last[3 * part :]),
+                ]
+                if which < len(reduces) - 1:
+                    new["last", which] = lasts[which]
+        work = {}
+        if slot == -2:
+            middle_back(1, grad)
+            work["back", 1] = back[1]
+        if slot == -1:
+            attention_back(1)
+            work["back", 1] = back[1]
+        if slot == 0:
+            attention_sent(1)
+            work["sent", 1] = reduces[1].sent
+            feed_back(0, back[1]["grad"])
+            work["back", 0] = back[0]
+        if slot == 1:
+            feed_sent(0)
+            work["sent", 2] = reduces[2].sent
+            middle_back(0, back[1]["grad"])
+            work["back", 0] = back[0]
+        if slot == 2:
+            attention_back(0)
+            work["back", 0] = back[0]
+        if slot == 3:
+            attention_sent(0)
+            work["sent", 3] = reduces[3].sent
+            new["give", "out"] = give_image(place, frame, output, halo, count, special_count)
+            total = jnp.concatenate([back[layer]["sums"] for layer in range(LAYERS)])
+            new["total"] = total + place.swap_seq(total, 1)
+        if slot == 4:
+            new["give", "back"] = give_image(place, frame, back[0]["grad"], halo, count, special_count)
+            new["total"] = total + place.swap_seq(total, 2)
+        if slot == 5:
+            new["total"] = total + place.swap_x(total)
+            outs["out"] = join_image(*outs["out"])
+            outs["back"] = join_image(*outs["back"])
+        if slot in (6, 7, 8):
+            ringing = place.ring_z(total if slot == 6 else ringing)
+            new["ringing"] = ringing
+        pending = {}
+        for which, unit in enumerate(reduces):
+            at = slot + 1 - 3 * which
+            if at == -2:
+                pending["sent", which] = unit.sent
+            if 0 <= at <= 2:
+                pending["kept", which] = unit.kept[(at + 2) % nz]
+        if slot == -1:
+            pending["output"] = output
+        for key in list(work):
+            pending.pop(key, None)
+        new, work, pending = fence((new, work, pending))
+        for found in (work, pending):
+            for key, value in found.items():
+                if key[0] == "sent":
+                    reduces[key[1]].sent = value
+                if key[0] == "kept":
+                    reduces[key[1]].kept[(slot + 1 - 3 * key[1] + 2) % nz] = value
+                if key[0] == "back":
+                    back[key[1]] = value
+        output = pending.get("output", output)
+        for which, unit in enumerate(reduces):
+            at = slot - 3 * which
+            if at == -2:
+                unit.got = new["core", which]
+            if -1 <= at <= 2:
+                unit.sides[(at + 2) % nz] = new["side", which]
+            if 0 <= at <= 2:
+                unit.running = new["z", which]
+            if at == 3 and ("last", which) in new:
+                lasts[which] = new["last", which]
+        if "total" in new:
+            total = new["total"]
+        if "ringing" in new:
+            ringing = new["ringing"]
+            summed = ringing + (total if slot == 6 else summed)
+        for name in ("out", "back"):
+            if ("give", name) in new:
+                outs[name] = new["give", name]
+
+    wm, wp, wu, wd = finish(
+        place, [lasts[3] + lasts[2], lasts[1] + lasts[0]], part_rows, width
+    )
+    summed = summed.reshape(LAYERS, -1, place.n_dp, part_rows)
+    eight = lax.dynamic_index_in_dim(summed[:, :8], place.dp, 2, keepdims=False)
+    g1, s1, bq, bv, bp, g2, s2, bd = (eight[:, i] for i in range(8))
+    bu = summed[:, 8:12].reshape(LAYERS, place.n_dp, 4 * part_rows)
+    bu = lax.dynamic_index_in_dim(bu, place.dp, 1, keepdims=False)
+    return (
+        *outs["out"],
+        *outs["back"],
+        g1,
+        s1,
+        wm,
+        bq,
+        bv,
+        wp,
+        bp,
+        g2,
+        s2,
+        wu,
+        bu,
+        wd,
+        bd,
+    )
+
+
+def local(*args):
+    place = Place()
+    if place.walked:
+        return local_walked(place, *args)
+    return local_plain(place, *args)
+
+
 def solution(mesh):
     in_specs = (
         P(("dp", "seq"), None),

time: 830 us -> 497 us (0.60)
  matrix products: 144 us -> 0 us
  waiting for transfers between devices: 316 us -> 182 us
  Pallas kernels: 0 us -> 120 us
  other arithmetic: 106 us -> 8.64 us
  local copies, waits for them, and re-layouts: 114 us -> 45.5 us
    dot_general x60 -> x0, matrix products: 144 us -> none  [the longest x16 45.2 us: dot_nt(): lax.dot_general(left, right, (((1,), (1,)), ((), ())), preferred_element_...]
    pallas_call x0 -> x39, Pallas kernels: none -> 120 us  [the longest x2 25.7 us: backward_attention(): pl.pallas_call(backward_attention_kernel, in_specs=in_smem(1) + whole_vme...]
    ppermute x48 -> x27, waiting for transfers between devices: 181 us -> 74.2 us  [ring_z(): lax.ppermute(values, 'dp', [(i, (i + 2) % self.n_dp) for i in range(self....]
    dynamic_update_slice x50 -> x0, local copies, waits for them, and re-layouts: 40.8 us -> none  [the longest x24 18.9 us: gather_matrix(): lax.dynamic_update_slice(mine, blocks[step][None, None], (at, place.x, 0,...]
    select_n x36 -> x7, other arithmetic: 30.2 us -> 1.1 us  [the longest x1 0.65 us: local_walked(): blocked = jnp.where(key_ok, 0.0, MASKED).astype(F32)[None]]
    ppermute x48 -> x27, starting transfers between devices: 38.8 us -> 13 us  [ring_z(): lax.ppermute(values, 'dp', [(i, (i + 2) % self.n_dp) for i in range(self....]
    ppermute x24 -> x39, starting transfers between devices: 26.2 us -> 47.4 us  [swap_x(): return lax.ppermute(values, 'dp', [(i, i ^ 1) for i in range(self.n_dp)])]
    convert_element_type x52 -> x2, other arithmetic: 21.2 us -> 0.91 us  [the longest x1 0.87 us: local_walked(): lax.dynamic_index_in_dim(keep_mask[0], place.seq, 0, keepdims=False)]
  transfers between devices with their start and end apart: 135 -> 133, of which waited for: 70 -> 58; matrix products, arithmetic and copies ran while one was open for 31% -> 6% of each run, Pallas kernels for 0% -> 18%
where the time goes in v2:
time: 497 us; the launch traced here: 490 us
  waiting for transfers between devices  182 us (37%)
  starting transfers between devices  127 us (26%)
  Pallas kernels  120 us (24%)
  local copies, waits for them, and re-layouts  45.5 us (9%)
  other arithmetic  8.64 us (2%)
  between operations  6.72 us (1%)
    ppermute x27, waiting for transfers between devices, ring_z(): lax.ppermute(values, 'dp', [(i, (i + 2) % self.n_dp) for i in range(self....  74.2 us
    ppermute x58, waiting for transfers between devices, swap_seq(): lax.ppermute(values, 'seq', [(i, i ^ mask) for i in range(self.n_seq)])  66.5 us
    ppermute x39, starting transfers between devices, swap_x(): return lax.ppermute(values, 'dp', [(i, i ^ 1) for i in range(self.n_dp)])  47.4 us
    ppermute x58, starting transfers between devices, swap_seq(): lax.ppermute(values, 'seq', [(i, i ^ mask) for i in range(self.n_seq)])  45.6 us
    ppermute x39, waiting for transfers between devices, swap_x(): return lax.ppermute(values, 'dp', [(i, i ^ 1) for i in range(self.n_dp)])  36.1 us
    unnamed x273, local copies, waits for them, and re-layouts  25.7 us
    pallas_call x2, Pallas kernels, backward_attention(): pl.pallas_call(backward_attention_kernel, in_specs=in_smem(1) + whole_vme...  25.7 us
    pallas_call x4, Pallas kernels, kept_part(): pl.pallas_call(partial(kept_kernel, fill, wide, place.nz), in_specs=in_sm...  19.3 us
  transfers between devices with their start and end apart: 133, of which 58 were waited for; matrix products, arithmetic and copies ran while one was open for 6% of the time, Pallas kernels for 18%

profile of v2, /device:TPU:0, one launch (start us, length us, event | category | flops | bytes accessed | tf_op | source)
XLA Modules:
  0.0 490.1 jit_solution(10479030024960167510)
XLA Ops:
  17.5 5.1 %collective-permute-done.1 = bf16[4,96,384]{2,1,0:T(8,128)(2,1)S(1)} collective-permute-done((bf16[4,96,384]{2,1,0:T(8,128)(2,1)}, bf16[4,96,384]{2,1,0:T(8,128)(2,1)S(1)}, u32[]{:S(2)}, u32[]{:S(2)}) %collective-permute-start.1) | collective-permute-done | bytes 294944 | tf_op jit(solution)/shard_map/ppermute | solution.py:57
  52.6 5.9 %all-to-all-start = ((bf16[8,2,12,96]{3,1,2,0:T(2,128)(2,1)}), bf16[8,2,12,96]{3,1,2,0:T(2,128)(2,1)S(1)}, u32[]{:S(2)}, u32[]{:S(2)}) async-start(bf16[8,2,12,96]{3,1,2,0:T(2,128)(2,1)} %broadcast_in_dim.20), calls=%async_computation | async-start | bytes 98304 | tf_op jit(solution)/shard_map/all_to_all | solution.py:870
  64.6 5.5 %all-to-all-done = bf16[8,2,12,96]{3,1,2,0:T(2,128)(2,1)S(1)} async-done(((bf16[8,2,12,96]{3,1,2,0:T(2,128)(2,1)}), bf16[8,2,12,96]{3,1,2,0:T(2,128)(2,1)S(1)}, u32[]{:S(2)}, u32[]{:S(2)}) %all-to-all-start) | async-done | bytes 36896 | tf_op jit(solution)/shard_map/all_to_all | solution.py:870
  71.9 4.6 collective-permute-done.18
  91.3 7.0 %collective-permute-done.23 = bf16[4,96,384]{2,1,0:T(8,128)(2,1)S(1)} collective-permute-done((bf16[4,96,384]{2,1,0:T(8,128)(2,1)S(1)}, bf16[4,96,384]{2,1,0:T(8,128)(2,1)S(1)}, u32[]{:S(2)}, u32[]{:S(2)}) %collective-permute-start.23) | collective-permute-done | bytes 294944 | tf_op jit(solution)/shard_map/ppermute | solution.py:51
  105.3 9.1 %forward_attention.2 = (f32[288,768]{1,0:T(8,128)S(1)}, bf16[288,768]{1,0:T(8,128)(2,1)S(1)}, bf16[768,288]{1,0:T(8,128)(2,1)S(1)}, bf16[768,288]{1,0:T(8,128)(2...) custom-call(s32[4]{0:T(128)S(1)} %get-tuple-element.1015.spot, ...), custom_call_target="tpu_custom_call" | custom-call | tf_op jit(solution)/shard_map/forward_attention/pallas_call | solution.py:458
  128.5 6.1 %collective-permute-done.33 = bf16[2,96,384]{2,1,0:T(8,128)(2,1)S(1)} collective-permute-done((bf16[2,96,384]{2,1,0:T(8,128)(2,1)S(1)}, bf16[2,96,384]{2,1,0:T(8,128)(2,1)S(1)}, u32[]{:S(2)}, u32[]{:S(2)}) %collective-permute-start.33) | collective-permute-done | bytes 147488 | tf_op jit(solution)/shard_map/ppermute | solution.py:54
  165.9 8.7 %forward_feed.2 = (f32[288,768]{1,0:T(8,128)S(1)}, bf16[288,3072]{1,0:T(8,128)(2,1)S(1)}, bf16[288,3072]{1,0:T(8,128)(2,1)S(1)}) custom-call(s32[4]{0:T(128)S(1)} %get-tuple-element.1015.spot, f32[1]{0:T(128)} %bitcast.64.keep, f32[288,768]{1,0:T(8,128)S(1)} %get-tuple-element.541.middle, bf16[288,768]{1,0:T(8,128)(2,1)S(1)} %get-tuple-element.542.normed, ...), custom_call_target="tpu_custom_call" | custom-call | tf_op jit(solution)/shard_map/forward_feed/pallas_call | solution.py:500
  179.3 7.1 %collective-permute-done.55 = bf16[4,96,384]{2,1,0:T(8,128)(2,1)S(1)} collective-permute-done((bf16[4,96,384]{2,1,0:T(8,128)(2,1)S(1)}, bf16[4,96,384]{2,1,0:T(8,128)(2,1)S(1)}, u32[]{:S(2)}, u32[]{:S(2)}) %collective-permute-start.55) | collective-permute-done | bytes 294944 | tf_op jit(solution)/shard_map/ppermute | solution.py:51
  186.9 7.6 %collective-permute-done.53 = bf16[8,96,384]{2,1,0:T(8,128)(2,1)S(1)} collective-permute-done((bf16[8,96,384]{2,1,0:T(8,128)(2,1)S(1)}, bf16[8,96,384]{2,1,0:T(8,128)(2,1)S(1)}, u32[]{:S(2)}, u32[]{:S(2)}) %collective-permute-start.53) | collective-permute-done | bytes 589856 | tf_op jit(solution)/shard_map/ppermute | solution.py:57
  198.1 8.6 %forward_attention.3 = (f32[288,768]{1,0:T(8,128)S(1)}, bf16[288,768]{1,0:T(8,128)(2,1)S(1)}, bf16[768,288]{1,0:T(8,128)(2,1)S(1)}, bf16[768,288]{1,0:T(8,128)(2...) custom-call(s32[4]{0:T(128)S(1)} %get-tuple-element.1015.spot, ...), custom_call_target="tpu_custom_call" | custom-call | tf_op jit(solution)/shard_map/forward_attention/pallas_call | solution.py:458
  208.0 4.5 collective-permute-done.58
  215.2 7.0 %collective-permute-done.63 = bf16[4,96,384]{2,1,0:T(8,128)(2,1)S(1)} collective-permute-done((bf16[4,96,384]{2,1,0:T(8,128)(2,1)S(1)}, bf16[4,96,384]{2,1,0:T(8,128)(2,1)S(1)}, u32[]{:S(2)}, u32[]{:S(2)}) %collective-permute-start.63) | collective-permute-done | bytes 294944 | tf_op jit(solution)/shard_map/ppermute | solution.py:51
  225.5 8.9 %forward_feed.3 = (f32[288,768]{1,0:T(8,128)S(1)}, bf16[288,3072]{1,0:T(8,128)(2,1)S(1)}, bf16[288,3072]{1,0:T(8,128)(2,1)S(1)}) custom-call(s32[4]{0:T(128)S(1)} %get-tuple-element.1015.spot, f32[1]{0:T(128)} %bitcast.68.keep, f32[288,768]{1,0:T(8,128)S(1)} %get-tuple-element.585.middle, bf16[288,768]{1,0:T(8,128)(2,1)S(1)} %get-tuple-element.586.normed, ...), custom_call_target="tpu_custom_call" | custom-call | tf_op jit(solution)/shard_map/forward_feed/pallas_call | solution.py:500
  250.2 6.3 %gradient_kept.4 = (bf16[4,96,384]{2,1,0:T(8,128)(2,1)S(1)}, bf16[4,96,384]{2,1,0:T(8,128)(2,1)S(1)}, bf16[8,96,384]{2,1,0:T(8,128)(2,1)S(1)}, bf16[4,96,384]{2,...) custom-call(s32[4]{0:T(128)S(1)} %get-tuple-element.1015.spot, ...), custom_call_target="tpu_custom_call" | custom-call | tf_op jit(solution)/shard_map/gradient_kept/pallas_call | solution.py:762
  260.0 12.3 %backward_attention.2 = (f32[288,768]{1,0:T(8,128)S(1)}, bf16[288,2304]{1,0:T(8,128)(2,1)S(1)}, f32[16,768]{1,0:T(8,128)S(1)}) custom-call(s32[4]{0:T(128)S(1)} %get-tuple-element.1015.spot, f32[288,768]{1,0:T(8,128)S(1)} %get-tuple-element.611.grad_middle, bf16[288,768]{1,0:T(8,128)(2,1)S(1)} %get-tuple-element.634.grad_proj, ...), custom_call_target="tpu_custom_call" | custom-call | tf_op jit(solution)/shard_map/backward_attention/pallas_call | solution.py:658
  284.0 7.0 %collective-permute-done.71.refs_0_ = bf16[8,96,384]{2,1,0:T(8,128)(2,1)S(1)} collective-permute-done((bf16[8,96,384]{2,1,0:T(8,128)(2,1)S(1)}, bf16[8,96,384]{2,1,0:T(8,128)(2,1)S(1)}, u32[]{:S(2)}, u32[]{:S(2)}) %collective-permute-start.71) | collective-permute-done | bytes 589856 | tf_op jit(solution)/shard_map/ppermute | solution.py:57
  302.3 6.4 %collective-permute-done.74.refs_0_ = bf16[8,96,384]{2,1,0:T(8,128)(2,1)S(1)} collective-permute-done((bf16[8,96,384]{2,1,0:T(8,128)(2,1)S(1)}, bf16[8,96,384]{2,1,0:T(8,128)(2,1)S(1)}, u32[]{:S(2)}, u32[]{:S(2)}) %collective-permute-start.74) | collective-permute-done | bytes 589856 | tf_op jit(solution)/shard_map/ppermute | solution.py:57
  318.9 13.3 %backward_attention.3 = (f32[288,768]{1,0:T(8,128)S(1)}, bf16[288,2304]{1,0:T(8,128)(2,1)S(1)}, f32[16,768]{1,0:T(8,128)S(1)}) custom-call(s32[4]{0:T(128)S(1)} %get-tuple-element.1015.spot, f32[288,768]{1,0:T(8,128)S(1)} %get-tuple-element.676.grad_middle, bf16[288,768]{1,0:T(8,128)(2,1)S(1)} %get-tuple-element.708.grad_proj, ...), custom_call_target="tpu_custom_call" | custom-call | tf_op jit(solution)/shard_map/backward_attention/pallas_call | solution.py:658
  366.9 5.7 %gradient_kept.6 = (bf16[4,96,384]{2,1,0:T(8,128)(2,1)}, bf16[4,96,384]{2,1,0:T(8,128)(2,1)}, bf16[8,96,384]{2,1,0:T(8,128)(2,1)S(1)}, bf16[4,96,384]{2,1,0:T(8,...) custom-call(s32[4]{0:T(128)S(1)} %get-tuple-element.1015.spot, ...), custom_call_target="tpu_custom_call" | custom-call | tf_op jit(solution)/shard_map/gradient_kept/pallas_call | solution.py:762
  378.8 5.8 %collective-permute-done.101 = f32[32,768]{1,0:T(8,128)S(1)} collective-permute-done((f32[32,768]{1,0:T(8,128)S(1)}, f32[32,768]{1,0:T(8,128)S(1)}, u32[]{:S(2)}, u32[]{:S(2)}) %collective-permute-start.101) | collective-permute-done | bytes 98336 | tf_op jit(solution)/shard_map/ppermute | solution.py:54
  408.6 17.4 %collective-permute-done.112 = f32[32,768]{1,0:T(8,128)S(1)} collective-permute-done((f32[32,768]{1,0:T(8,128)S(1)}, f32[32,768]{1,0:T(8,128)S(1)}, u32[]{:S(2)}, u32[]{:S(2)}) %collective-permute-start.112) | collective-permute-done | bytes 98336 | tf_op jit(solution)/shard_map/ppermute | solution.py:57
  437.6 7.5 %collective-permute-done.118 = f32[32,768]{1,0:T(8,128)S(1)} collective-permute-done((f32[32,768]{1,0:T(8,128)S(1)}, f32[32,768]{1,0:T(8,128)S(1)}, u32[]{:S(2)}, u32[]{:S(2)}) %collective-permute-start.118) | collective-permute-done | bytes 98336 | tf_op jit(solution)/shard_map/ppermute | solution.py:57
  446.8 4.4 collective-permute-done.117.aside
  (681 shorter events, 301.7 us)
Async XLA Ops:
  51.7 24.7 %collective-permute-start.15 = (bf16[8,96,384]{2,1,0:T(8,128)(2,1)}, bf16[8,96,384]{2,1,0:T(8,128)(2,1)}, u32[]{:S(2)}, u32[]{:S(2)}) collective-permute-start(bf16[8,96,384]{2,1,0:T(8,128)(2,1)} %pad_maximum_fusion.4), channel_id=1, source_target_pairs={{0,8},{4,12},{8,16},{12,20},{16,24},{20,28},{24,0},{28,4},{1,9},{5... | collective-permute-start | bytes 1769480 | tf_op jit(solution)/shard_map/ppermute | solution.py:57
  52.6 17.5 %all-to-all-start = ((bf16[8,2,12,96]{3,1,2,0:T(2,128)(2,1)}), bf16[8,2,12,96]{3,1,2,0:T(2,128)(2,1)S(1)}, u32[]{:S(2)}, u32[]{:S(2)}) async-start(bf16[8,2,12,96]{3,1,2,0:T(2,128)(2,1)} %broadcast_in_dim.20), calls=%async_computation | async-start | bytes 98304 | tf_op jit(solution)/shard_map/all_to_all | solution.py:870
  58.6 17.9 %collective-permute-start.20 = (bf16[8,96,384]{2,1,0:T(8,128)(2,1)S(1)}, bf16[8,96,384]{2,1,0:T(8,128)(2,1)}, u32[]{:S(2)}, u32[]{:S(2)}) collective-permute-start(bf16[8,96,384]{2,1,0:T(8,128)(2,1)S(1)} %constant_dynamic-update-slice_fusion.28.refs_2_.refs_7_), channel_id=1, source_target_pairs={{0,1},{1,0},{2,3},{3,2},{4,5},{5,4},{6,7},{7,6},{8,9},{9,8},{10,11... | collective-permute-start | bytes 1769480 | tf_op jit(solution)/shard_map/ppermute | solution.py:51
  78.5 20.9 %collective-permute-start.24 = (bf16[16,96,384]{2,1,0:T(8,128)(2,1)S(1)}, bf16[16,96,384]{2,1,0:T(8,128)(2,1)S(1)}, u32[]{:S(2)}, u32[]{:S(2)}) collective-permute-start(bf16[16,96,384]{2,1,0:T(8,128)(2,1)S(1)} %constant_dynamic-update-slice_fusion.40.refs_0_), channel_id=1, source_target_pairs={{0,1},{1,0},{2,3},{3,2},{4,5},{5,4},{6,7},{7,6},{8,9},{9,8},{10,11... | collective-permute-start | bytes 3538952 | tf_op jit(solution)/shard_map/ppermute | solution.py:51
  81.4 17.9 %collective-permute-start.25 = (bf16[8,96,384]{2,1,0:T(8,128)(2,1)S(1)}, bf16[8,96,384]{2,1,0:T(8,128)(2,1)S(1)}, u32[]{:S(2)}, u32[]{:S(2)}) collective-permute-start(bf16[8,96,384]{2,1,0:T(8,128)(2,1)S(1)} %constant_dynamic-update-slice_fusion.43.refs_3_.refs_8_), channel_id=1, source_target_pairs={{0,1},{1,0},{2,3},{3,2},{4,5},{5,4},{6,7},{7,6},{8,9},{9,8},{10,11... | collective-permute-start | bytes 1769480 | tf_op jit(solution)/shard_map/ppermute | solution.py:51
  99.5 20.6 %collective-permute-start.31 = (bf16[16,96,384]{2,1,0:T(8,128)(2,1)S(1)}, bf16[16,96,384]{2,1,0:T(8,128)(2,1)S(1)}, u32[]{:S(2)}, u32[]{:S(2)}) collective-permute-start(bf16[16,96,384]{2,1,0:T(8,128)(2,1)S(1)} %constant_dynamic-update-slice_fusion.46.refs_1_), channel_id=1, source_target_pairs={{0,1},{1,0},{2,3},{3,2},{4,5},{5,4},{6,7},{7,6},{8,9},{9,8},{10,11... | collective-permute-start | bytes 3538952 | tf_op jit(solution)/shard_map/ppermute | solution.py:51
  102.5 17.6 %collective-permute-start.28 = (bf16[8,96,384]{2,1,0:T(8,128)(2,1)S(1)}, bf16[8,96,384]{2,1,0:T(8,128)(2,1)S(1)}, u32[]{:S(2)}, u32[]{:S(2)}) collective-permute-start(bf16[8,96,384]{2,1,0:T(8,128)(2,1)S(1)} %collective-permute-done.21), channel_id=1, source_target_pairs={{0,8},{4,12},{8,16},{12,20},{16,24},{20,28},{24,0},{28,4},{1,9},{5... | collective-permute-start | bytes 1769480 | tf_op jit(solution)/shard_map/ppermute | solution.py:57
  176.1 18.4 %collective-permute-start.56 = (bf16[16,96,384]{2,1,0:T(8,128)(2,1)S(1)}, bf16[16,96,384]{2,1,0:T(8,128)(2,1)S(1)}, u32[]{:S(2)}, u32[]{:S(2)}) collective-permute-start(bf16[16,96,384]{2,1,0:T(8,128)(2,1)S(1)} %constant_dynamic-update-slice_fusion.64.refs_0_), channel_id=1, source_target_pairs={{0,1},{1,0},{2,3},{3,2},{4,5},{5,4},{6,7},{7,6},{8,9},{9,8},{10,11... | collective-permute-start | bytes 3538952 | tf_op jit(solution)/shard_map/ppermute | solution.py:51
  176.8 17.7 %collective-permute-start.53 = (bf16[8,96,384]{2,1,0:T(8,128)(2,1)S(1)}, bf16[8,96,384]{2,1,0:T(8,128)(2,1)S(1)}, u32[]{:S(2)}, u32[]{:S(2)}) collective-permute-start(bf16[8,96,384]{2,1,0:T(8,128)(2,1)S(1)} %collective-permute-done.47), channel_id=1, source_target_pairs={{0,8},{4,12},{8,16},{12,20},{16,24},{20,28},{24,0},{28,4},{1,9},{5... | collective-permute-start | bytes 1769480 | tf_op jit(solution)/shard_map/ppermute | solution.py:57
  194.6 17.8 %collective-permute-start.61 = (bf16[16,96,384]{2,1,0:T(8,128)(2,1)S(1)}, bf16[16,96,384]{2,1,0:T(8,128)(2,1)S(1)}, u32[]{:S(2)}, u32[]{:S(2)}) collective-permute-start(bf16[16,96,384]{2,1,0:T(8,128)(2,1)S(1)} %constant_dynamic-update-slice_fusion.70.refs_1_), channel_id=1, source_target_pairs={{0,1},{1,0},{2,3},{3,2},{4,5},{5,4},{6,7},{7,6},{8,9},{9,8},{10,11... | collective-permute-start | bytes 3538952 | tf_op jit(solution)/shard_map/ppermute | solution.py:51
  194.7 17.7 %collective-permute-start.58 = (bf16[8,96,384]{2,1,0:T(8,128)(2,1)S(1)}, bf16[8,96,384]{2,1,0:T(8,128)(2,1)S(1)}, u32[]{:S(2)}, u32[]{:S(2)}) collective-permute-start(bf16[8,96,384]{2,1,0:T(8,128)(2,1)S(1)} %collective-permute-done.53), channel_id=1, source_target_pairs={{0,8},{4,12},{8,16},{12,20},{16,24},{20,28},{24,0},{28,4},{1,9},{5... | collective-permute-start | bytes 1769480 | tf_op jit(solution)/shard_map/ppermute | solution.py:57
  290.9 17.8 %collective-permute-start.75 = (bf16[4,8,96,384]{3,2,1,0:T(8,128)(2,1)S(1)}, bf16[4,8,96,384]{3,2,1,0:T(8,128)(2,1)S(1)}, u32[]{:S(2)}, u32[]{:S(2)}) collective-permute-start(bf16[4,8,96,384]{3,2,1,0:T(8,128)(2,1)S(1)} %gradient_sent.5), channel_id=1, source_target_pairs={{0,1},{1,0},{2,3},{3,2},{4,5},{5,4},{6,7},{7,6},{8,9},{9,8},{10,11... | collective-permute-start | bytes 7077896 | tf_op jit(solution)/shard_map/ppermute | solution.py:51
  291.2 17.6 %collective-permute-start.74 = (bf16[8,96,384]{2,1,0:T(8,128)(2,1)S(1)}, bf16[8,96,384]{2,1,0:T(8,128)(2,1)S(1)}, u32[]{:S(2)}, u32[]{:S(2)}) collective-permute-start(bf16[8,96,384]{2,1,0:T(8,128)(2,1)S(1)} %ring_block.17), channel_id=1, source_target_pairs={{0,8},{4,12},{8,16},{12,20},{16,24},{20,28},{24,0},{28,4},{1,9},{5... | collective-permute-start | bytes 1769480 | tf_op jit(solution)/shard_map/ppermute | solution.py:57
  309.0 25.9 %collective-permute-start.78 = (bf16[8,96,384]{2,1,0:T(8,128)(2,1)S(1)}, bf16[8,96,384]{2,1,0:T(8,128)(2,1)S(1)}, u32[]{:S(2)}, u32[]{:S(2)}) collective-permute-start(bf16[8,96,384]{2,1,0:T(8,128)(2,1)S(1)} %ring_block.18), channel_id=1, source_target_pairs={{0,8},{4,12},{8,16},{12,20},{16,24},{20,28},{24,0},{28,4},{1,9},{5... | collective-permute-start | bytes 1769480 | tf_op jit(solution)/shard_map/ppermute | solution.py:57
  309.7 25.2 %collective-permute-start.76 = (bf16[4,96,384]{2,1,0:T(8,128)(2,1)S(1)}, bf16[4,96,384]{2,1,0:T(8,128)(2,1)S(1)}, u32[]{:S(2)}, u32[]{:S(2)}) collective-permute-start(bf16[4,96,384]{2,1,0:T(8,128)(2,1)S(1)} %copy-done.67), channel_id=1, source_target_pairs={{0,4},{4,0},{8,12},{12,8},{16,20},{20,16},{24,28},{28,24},{1,5},{5... | collective-permute-start | bytes 884744 | tf_op jit(solution)/shard_map/ppermute | solution.py:54
  311.4 23.5 %collective-permute-start.77 = (bf16[4,96,384]{2,1,0:T(8,128)(2,1)S(1)}, bf16[4,96,384]{2,1,0:T(8,128)(2,1)S(1)}, u32[]{:S(2)}, u32[]{:S(2)}) collective-permute-start(bf16[4,96,384]{2,1,0:T(8,128)(2,1)S(1)} %copy-done.65), channel_id=1, source_target_pairs={{0,2},{1,3},{2,0},{3,1},{4,6},{5,7},{6,4},{7,5},{8,10},{9,11},{10,... | collective-permute-start | bytes 884744 | tf_op jit(solution)/shard_map/ppermute | solution.py:51
  406.0 20.0 %collective-permute-start.111 = (bf16[4,8,96,384]{3,2,1,0:T(8,128)(2,1)S(1)}, bf16[4,8,96,384]{3,2,1,0:T(8,128)(2,1)S(1)}, u32[]{:S(2)}, u32[]{:S(2)}) collective-permute-start(bf16[4,8,96,384]{3,2,1,0:T(8,128)(2,1)S(1)} %gradient_sent.7), channel_id=1, source_target_pairs={{0,1},{1,0},{2,3},{3,2},{4,5},{5,4},{6,7},{7,6},{8,9},{9,8},{10,11... | collective-permute-start | bytes 7077896 | tf_op jit(solution)/shard_map/ppermute | solution.py:51
  406.3 19.7 %collective-permute-start.110 = (bf16[8,96,384]{2,1,0:T(8,128)(2,1)S(1)}, bf16[8,96,384]{2,1,0:T(8,128)(2,1)S(1)}, u32[]{:S(2)}, u32[]{:S(2)}) collective-permute-start(bf16[8,96,384]{2,1,0:T(8,128)(2,1)S(1)} %ring_block.25), channel_id=1, source_target_pairs={{0,8},{4,12},{8,16},{12,20},{16,24},{20,28},{24,0},{28,4},{1,9},{5... | collective-permute-start | bytes 1769480 | tf_op jit(solution)/shard_map/ppermute | solution.py:57
  406.5 19.5 %collective-permute-start.108 = (bf16[4,96,384]{2,1,0:T(8,128)(2,1)S(1)}, bf16[4,96,384]{2,1,0:T(8,128)(2,1)S(1)}, u32[]{:S(2)}, u32[]{:S(2)}) collective-permute-start(bf16[4,96,384]{2,1,0:T(8,128)(2,1)S(1)} %get-tuple-element.764), channel_id=1, source_target_pairs={{0,4},{4,0},{8,12},{12,8},{16,20},{20,16},{24,28},{28,24},{1,5},{5... | collective-permute-start | bytes 884744 | tf_op jit(solution)/shard_map/ppermute | solution.py:54
  407.2 18.8 %collective-permute-start.109 = (bf16[4,96,384]{2,1,0:T(8,128)(2,1)S(1)}, bf16[4,96,384]{2,1,0:T(8,128)(2,1)S(1)}, u32[]{:S(2)}, u32[]{:S(2)}) collective-permute-start(bf16[4,96,384]{2,1,0:T(8,128)(2,1)S(1)} %get-tuple-element.765), channel_id=1, source_target_pairs={{0,2},{1,3},{2,0},{3,1},{4,6},{5,7},{6,4},{7,5},{8,10},{9,11},{10,... | collective-permute-start | bytes 884744 | tf_op jit(solution)/shard_map/ppermute | solution.py:51
  408.1 17.9 %collective-permute-start.112 = (f32[32,768]{1,0:T(8,128)S(1)}, f32[32,768]{1,0:T(8,128)S(1)}, u32[]{:S(2)}, u32[]{:S(2)}) collective-permute-start(f32[32,768]{1,0:T(8,128)S(1)} %collective-permute-done.107), channel_id=1, source_target_pairs={{0,8},{4,12},{8,16},{12,20},{16,24},{20,28},{24,0},{28,4},{1,9},{5... | collective-permute-start | bytes 294920 | tf_op jit(solution)/shard_map/ppermute | solution.py:57
  426.2 25.0 %collective-permute-start.115 = (bf16[8,96,384]{2,1,0:T(8,128)(2,1)S(1)}, bf16[8,96,384]{2,1,0:T(8,128)(2,1)S(1)}, u32[]{:S(2)}, u32[]{:S(2)}) collective-permute-start(bf16[8,96,384]{2,1,0:T(8,128)(2,1)S(1)} %ring_block.26), channel_id=1, source_target_pairs={{0,8},{4,12},{8,16},{12,20},{16,24},{20,28},{24,0},{28,4},{1,9},{5... | collective-permute-start | bytes 1769480 | tf_op jit(solution)/shard_map/ppermute | solution.py:57
  426.3 24.9 %collective-permute-start.113 = (bf16[4,96,384]{2,1,0:T(8,128)(2,1)}, bf16[4,96,384]{2,1,0:T(8,128)(2,1)}, u32[]{:S(2)}, u32[]{:S(2)}) collective-permute-start(bf16[4,96,384]{2,1,0:T(8,128)(2,1)} %get-tuple-element.775), channel_id=1, source_target_pairs={{0,4},{4,0},{8,12},{12,8},{16,20},{20,16},{24,28},{28,24},{1,5},{5... | collective-permute-start | bytes 884744 | tf_op jit(solution)/shard_map/ppermute | solution.py:54
  427.0 24.2 %collective-permute-start.114 = (bf16[4,96,384]{2,1,0:T(8,128)(2,1)}, bf16[4,96,384]{2,1,0:T(8,128)(2,1)}, u32[]{:S(2)}, u32[]{:S(2)}) collective-permute-start(bf16[4,96,384]{2,1,0:T(8,128)(2,1)} %get-tuple-element.776), channel_id=1, source_target_pairs={{0,2},{1,3},{2,0},{3,1},{4,6},{5,7},{6,4},{7,5},{8,10},{9,11},{10,... | collective-permute-start | bytes 884744 | tf_op jit(solution)/shard_map/ppermute | solution.py:51
  (222 other events, 1950.1 us)

commit v3 on v2

--- a/solution.py
+++ b/solution.py
@@ -14,6 +14,8 @@
 EPSILON = 1e-06
 MASKED = -1e30
 GAIN_ONE, SHIFT_ONE, BIAS_QUERY, BIAS_VALUE, BIAS_PROJ, GAIN_TWO, SHIFT_TWO, BIAS_DOWN = range(8)
+VECTOR_PIECES = 12
+EXTRA_ROWS = 16
 MIB = 1024 * 1024
 ROOT_HALF = 0.7071067811865476
 ROOT_TWO_PI = 0.3989422804014327
@@ -53,8 +55,8 @@
     def swap_x(self, values):
         return lax.ppermute(values, "dp", [(i, i ^ 1) for i in range(self.n_dp)])
 
-    def ring_z(self, values):
-        return lax.ppermute(values, "dp", [(i, (i + 2) % self.n_dp) for i in range(self.n_dp)])
+    def ring_z(self, values, by=1):
+        return lax.ppermute(values, "dp", [(i, (i + 2 * by) % self.n_dp) for i in range(self.n_dp)])
 
 
 def gather_matrix(shard):
@@ -340,25 +342,40 @@
     return pltpu.CompilerParams(vmem_limit_bytes=mib * MIB)
 
 
-def place_pieces(spot, parts, crossed, split, first, quarter):
+def place_pieces(spot, parts, chunks, crossed, split, extra, turned):
     z, x, y, core = (spot[i] for i in range(4))
-    steps = len(parts) // 2
+    steps = sum(len(chunk) for chunk in chunks)
+    first, rows = crossed.shape[2:4]
+    quarter = split.shape[2] // 2
+    more = 0 if extra is None else extra.shape[1]
+    wide, piece = first * rows + more, quarter * rows
+    block = wide + (piece if turned else 2 * piece)
+    spots = {
+        (0, 0): wide,
+        (1, 0): block + wide if turned else wide + piece,
+        (0, 1): 2 * wide + 2 * piece,
+        (1, 1): 2 * wide + 3 * piece,
+    }
     for side in range(2):
         at_core = core if side == 0 else 1 - core
         for step in range(steps):
-            part = parts[side * steps + step]
+            which = next(i for i, chunk in enumerate(chunks) if step in chunk)
+            part = parts[side * len(chunks) + which]
+            start = chunks[which].index(step) * (2 * wide + 4 * piece)
             at_z = lax.rem(z - step + steps, steps)
             for far_x in range(2):
                 row = 2 * at_z + lax.rem(x + far_x, 2)
-                if crossed is not None:
-                    base = far_x * (first + 2 * quarter)
-                    for j in range(first):
-                        crossed[at_core, row, j] = part[base + j]
-                if split is not None:
-                    for far_y in range(2):
-                        base = first + far_y * (first + 2 * quarter) + far_x * quarter
-                        for j in range(quarter):
-                            split[at_core, row, lax.rem(y + far_y, 2) * quarter + j] = part[base + j]
+                base = start + far_x * block
+                for j in range(first):
+                    crossed[at_core, row, j] = part[base + j * rows : base + (j + 1) * rows]
+                if extra is not None and side == 0:
+                    extra[row] = part[base + first * rows : base + wide]
+                for far_y in range(2):
+                    base = start + spots[far_x, far_y]
+                    for j in range(quarter):
+                        split[at_core, row, lax.rem(y + far_y, 2) * quarter + j] = part[
+                            base + j * rows : base + (j + 1) * rows
+                        ]
 
 
 def flat(block):
@@ -400,12 +417,21 @@
     return powers / jnp.sum(powers, axis=1, keepdims=True)
 
 
-def forward_attention_kernel(
-    spot, keep, stream, vectors, blocked, *refs
-):
-    parts, refs = refs[:8], refs[8:]
-    middle, normed_two, normed_one_t, normed_two_t, mixed, attended, attended_t, crossed, split = refs
-    place_pieces(spot, parts, crossed, split, 2, 1)
+def forward_attention_kernel(turned, chunks, spot, keep, stream, blocked, *refs):
+    parts, refs = refs[: 2 * len(chunks)], refs[2 * len(chunks) :]
+    middle, normed_two, normed_one_t, normed_two_t, mixed, attended, attended_t, crossed, split, vectors, bias_up, extra = refs
+    place_pieces(spot, parts, chunks, crossed, split, extra, turned)
+    rows = crossed.shape[3]
+    each = extra.shape[2] // rows
+    for row in range(extra.shape[0]):
+        block = extra[row].astype(F32)
+        for piece in range(VECTOR_PIECES):
+            values = block[piece // each : piece // each + 1, (piece % each) * rows : (piece % each + 1) * rows]
+            if piece < vectors.shape[0]:
+                vectors[piece : piece + 1, row * rows : (row + 1) * rows] = values
+            else:
+                column = (row * (VECTOR_PIECES - vectors.shape[0]) + piece - vectors.shape[0]) * rows
+                bias_up[:, column : column + rows] = values
     hat, _ = moments(stream[...])
     normed = (hat * vectors[GAIN_ONE : GAIN_ONE + 1] + vectors[SHIFT_ONE : SHIFT_ONE + 1]).astype(BF)
     normed_one_t[...] = normed.T
@@ -443,9 +469,10 @@
     normed_two_t[...] = normed.T
 
 
-def forward_attention(place, spot, keep, stream, vectors, parts, blocked):
+def forward_attention(place, spot, keep, stream, unit, blocked, extra_rows):
+    parts = unit.parts()
     rows, width = stream.shape
-    group = parts[0].shape[1:]
+    group = (width // place.n_dp, width // 2)
     shapes = [
         jax.ShapeDtypeStruct((rows, width), F32),
         jax.ShapeDtypeStruct((rows, width), BF),
@@ -454,25 +481,27 @@
         jax.ShapeDtypeStruct((rows, 3 * width), BF),
         jax.ShapeDtypeStruct((rows, width), BF),
         jax.ShapeDtypeStruct((width, rows), BF),
+    ] + [jax.ShapeDtypeStruct((2, place.n_dp, 2) + group, BF)] * 2
+    shapes += [
+        jax.ShapeDtypeStruct((BIAS_DOWN + 1, width), F32),
+        jax.ShapeDtypeStruct((1, 4 * width), F32),
     ]
     return pl.pallas_call(
-        forward_attention_kernel,
-        in_specs=in_smem(2) + whole_vmem(3) + whole_vmem(8),
+        partial(forward_attention_kernel, unit.turned, unit.chunks),
+        in_specs=in_smem(2) + whole_vmem(2 + len(parts)),
         out_specs=whole_vmem(len(shapes)),
         out_shape=shapes,
-        scratch_shapes=[
-            pltpu.VMEM((2, place.n_dp, 2) + group, BF),
-            pltpu.VMEM((2, place.n_dp, 2) + group, BF),
-        ],
-        compiler_params=kernel_params(14),
+        scratch_shapes=[pltpu.VMEM((place.n_dp, extra_rows, width // 2), BF)],
+        compiler_params=kernel_params(12),
+        cost_estimate=pl.CostEstimate(flops=0, bytes_accessed=0, transcendentals=0),
         name="forward_attention",
-    )(spot, keep, stream, vectors, blocked, *parts)
-
-
-def forward_feed_kernel(spot, keep, middle, normed, bias_up, vectors, *refs):
-    parts, refs = refs[:8], refs[8:]
-    output, hidden, slope, crossed, split = refs
-    place_pieces(spot, parts, crossed, split, 4, 2)
+    )(spot, keep, stream, blocked, *parts)
+
+
+def forward_up_kernel(turned, chunks, spot, normed, bias_up, *refs):
+    parts, refs = refs[: 2 * len(chunks)], refs[2 * len(chunks) :]
+    hidden, slope, crossed, split = refs
+    place_pieces(spot, parts, chunks, crossed, split, None, turned)
     values = normed[...]
     half = values.shape[1] // 2
     for core in range(2):
@@ -482,39 +511,46 @@
             share = 0.5 + 0.5 * erf_of(pre * ROOT_HALF)
             hidden[:, columns] = (pre * share).astype(BF)
             slope[:, columns] = (share + pre * jnp.exp(-0.5 * pre * pre) * ROOT_TWO_PI).astype(BF)
+
+
+def forward_up(place, spot, normed, bias_up, unit):
+    parts = unit.parts()
+    rows, width = normed.shape
+    group = (width // place.n_dp, width // 2)
+    return pl.pallas_call(
+        partial(forward_up_kernel, unit.turned, unit.chunks),
+        in_specs=in_smem(1) + whole_vmem(2 + len(parts)),
+        out_specs=whole_vmem(4),
+        out_shape=[jax.ShapeDtypeStruct((rows, 4 * width), BF)] * 2
+        + [jax.ShapeDtypeStruct((2, place.n_dp, 4) + group, BF)] * 2,
+        compiler_params=kernel_params(8),
+        cost_estimate=pl.CostEstimate(flops=0, bytes_accessed=0, transcendentals=0),
+        name="forward_up",
+    )(spot, normed, bias_up, *parts)
+
+
+def forward_down_kernel(keep, middle, hidden, vectors, split, output):
     ahead = hidden[...]
+    half = middle.shape[1] // 2
     for core in range(2):
         columns = pl.ds(core * half, half)
         branch = dot_nn(ahead, flat(split[core])) + vectors[BIAS_DOWN : BIAS_DOWN + 1, columns]
         output[:, columns] = middle[:, columns] + keep[0] * branch
 
 
-def forward_feed(place, spot, keep, middle, normed, bias_up, vectors, parts):
-    rows, width = middle.shape
-    group = parts[0].shape[1:]
-    shapes = [
-        jax.ShapeDtypeStruct((rows, width), F32),
-        jax.ShapeDtypeStruct((rows, 4 * width), BF),
-        jax.ShapeDtypeStruct((rows, 4 * width), BF),
-    ]
+def forward_down(keep, middle, hidden, vectors, split):
     return pl.pallas_call(
-        forward_feed_kernel,
-        in_specs=in_smem(2) + whole_vmem(4) + whole_vmem(8),
-        out_specs=whole_vmem(len(shapes)),
-        out_shape=shapes,
-        scratch_shapes=[
-            pltpu.VMEM((2, place.n_dp, 4) + group, BF),
-            pltpu.VMEM((2, place.n_dp, 4) + group, BF),
-        ],
-        compiler_params=kernel_params(20),
-        name="forward_feed",
-    )(spot, keep, middle, normed, bias_up, vectors, *parts)
-
-
-def backward_feed_kernel(spot, keep, grad, slope, *refs):
-    parts, refs = refs[:8], refs[8:]
-    grad_down_t, grad_up, sum_down, sum_up, split = refs
-    place_pieces(spot, parts, None, split, 4, 2)
+        forward_down_kernel,
+        in_specs=in_smem(1) + whole_vmem(4),
+        out_specs=whole_vmem(1)[0],
+        out_shape=jax.ShapeDtypeStruct(middle.shape, F32),
+        compiler_params=kernel_params(8),
+        cost_estimate=pl.CostEstimate(flops=0, bytes_accessed=0, transcendentals=0),
+        name="forward_down",
+    )(keep, middle, hidden, vectors, split)
+
+
+def backward_feed_kernel(keep, grad, slope, split, grad_down_t, grad_up, sum_down, sum_up):
     down = (keep[0] * grad[...]).astype(BF)
     grad_down_t[...] = down.T
     sum_down[...] = jnp.sum(down.astype(F32), axis=0, keepdims=True)
@@ -527,9 +563,8 @@
         sum_up[:, columns] = jnp.sum(up.astype(F32), axis=0, keepdims=True)
 
 
-def backward_feed(place, spot, keep, grad, slope, parts):
+def backward_feed(keep, grad, slope, split):
     rows, width = grad.shape
-    group = parts[0].shape[1:]
     shapes = [
         jax.ShapeDtypeStruct((width, rows), BF),
         jax.ShapeDtypeStruct((rows, 4 * width), BF),
@@ -538,21 +573,17 @@
     ]
     return pl.pallas_call(
         backward_feed_kernel,
-        in_specs=in_smem(2) + whole_vmem(2) + whole_vmem(8),
+        in_specs=in_smem(1) + whole_vmem(3),
         out_specs=whole_vmem(len(shapes)),
         out_shape=shapes,
-        scratch_shapes=[
-            pltpu.VMEM((2, place.n_dp, 4) + group, BF),
-        ],
-        compiler_params=kernel_params(14),
+        compiler_params=kernel_params(8),
+        cost_estimate=pl.CostEstimate(flops=0, bytes_accessed=0, transcendentals=0),
         name="backward_feed",
-    )(spot, keep, grad, slope, *parts)
-
-
-def backward_middle_kernel(spot, keep, grad, grad_up, middle, vectors, *refs):
-    parts, refs = refs[:8], refs[8:]
-    grad_middle, grad_proj, sum_proj, grad_gain, grad_shift, crossed = refs
-    place_pieces(spot, parts, crossed, None, 4, 2)
+    )(keep, grad, slope, split)
+
+
+def backward_middle_kernel(keep, grad, grad_up, middle, vectors, crossed, *refs):
+    grad_middle, grad_proj, sum_proj, grad_gain, grad_shift = refs
     hat, scale = moments(middle[...])
     half = grad.shape[1] // 2
     total = jnp.zeros(grad.shape, F32)
@@ -568,31 +599,52 @@
     sum_proj[...] = jnp.sum(proj.astype(F32), axis=0, keepdims=True)
 
 
-def backward_middle(place, spot, keep, grad, grad_up, middle, vectors, parts):
+def backward_middle(keep, grad, grad_up, middle, vectors, crossed):
     rows, width = grad.shape
-    group = parts[0].shape[1:]
     shapes = [
         jax.ShapeDtypeStruct((rows, width), F32),
         jax.ShapeDtypeStruct((rows, width), BF),
     ] + [jax.ShapeDtypeStruct((1, width), F32)] * 3
     return pl.pallas_call(
         backward_middle_kernel,
-        in_specs=in_smem(2) + whole_vmem(4) + whole_vmem(8),
+        in_specs=in_smem(1) + whole_vmem(5),
         out_specs=whole_vmem(len(shapes)),
         out_shape=shapes,
-        scratch_shapes=[
-            pltpu.VMEM((2, place.n_dp, 4) + group, BF),
-        ],
-        compiler_params=kernel_params(14),
+        compiler_params=kernel_params(10),
+        cost_estimate=pl.CostEstimate(flops=0, bytes_accessed=0, transcendentals=0),
         name="backward_middle",
-    )(spot, keep, grad, grad_up, middle, vectors, *parts)
-
-
-def backward_attention_kernel(spot, grad_middle, grad_proj, mixed, stream, vectors, blocked, *refs):
-    others, parts, refs = refs[:5], refs[5:13], refs[13:]
-    grad_stream, grad_mixed, sums, ahead, crossed, split = refs
+    )(keep, grad, grad_up, middle, vectors, crossed)
+
+
+def backward_feed_middle_kernel(keep_down, keep_up, grad, slope, split, middle, vectors, crossed, *refs):
+    backward_feed_kernel(keep_down, grad, slope, split, *refs[:4])
+    backward_middle_kernel(keep_up, grad, refs[1], middle, vectors, crossed, *refs[4:])
+
+
+def backward_feed_middle(keep_down, keep_up, grad, slope, split, middle, vectors, crossed):
+    rows, width = grad.shape
+    shapes = [
+        jax.ShapeDtypeStruct((width, rows), BF),
+        jax.ShapeDtypeStruct((rows, 4 * width), BF),
+        jax.ShapeDtypeStruct((1, width), F32),
+        jax.ShapeDtypeStruct((1, 4 * width), F32),
+        jax.ShapeDtypeStruct((rows, width), F32),
+        jax.ShapeDtypeStruct((rows, width), BF),
+    ] + [jax.ShapeDtypeStruct((1, width), F32)] * 3
+    return pl.pallas_call(
+        backward_feed_middle_kernel,
+        in_specs=in_smem(2) + whole_vmem(6),
+        out_specs=whole_vmem(len(shapes)),
+        out_shape=shapes,
+        compiler_params=kernel_params(12),
+        name="backward_feed_middle",
+    )(keep_down, keep_up, grad, slope, split, middle, vectors, crossed)
+
+
+def backward_attention_kernel(grad_middle, grad_proj, mixed, stream, vectors, blocked, *refs):
+    others, (crossed, split), refs = refs[:5], refs[5:7], refs[7:]
+    grad_stream, grad_mixed, sums, ahead = refs
     sum_proj, gain_two, shift_two, sum_down, sum_up = others
-    place_pieces(spot, parts, crossed, split, 2, 1)
     hat, scale = moments(stream[...])
     width = stream.shape[1]
     half = width // 2
@@ -647,9 +699,8 @@
     grad_stream[...] = grad_middle[...] + norm_back(hat, scale, vectors[GAIN_ONE : GAIN_ONE + 1], total)
 
 
-def backward_attention(place, spot, grad_middle, grad_proj, mixed, stream, vectors, blocked, others, parts):
+def backward_attention(grad_middle, grad_proj, mixed, stream, vectors, blocked, others, crossed, split):
     rows, width = stream.shape
-    group = parts[0].shape[1:]
     shapes = [
         jax.ShapeDtypeStruct((rows, width), F32),
         jax.ShapeDtypeStruct((rows, 3 * width), BF),
@@ -657,40 +708,40 @@
     ]
     return pl.pallas_call(
         backward_attention_kernel,
-        in_specs=in_smem(1) + whole_vmem(6 + 5 + 8),
+        in_specs=whole_vmem(6 + 5 + 2),
         out_specs=whole_vmem(len(shapes)),
         out_shape=shapes,
-        scratch_shapes=[
-            pltpu.VMEM((rows, width), BF),
-            pltpu.VMEM((2, place.n_dp, 2) + group, BF),
-            pltpu.VMEM((2, place.n_dp, 2) + group, BF),
-        ],
-        compiler_params=kernel_params(16),
+        scratch_shapes=[pltpu.VMEM((rows, width), BF)],
+        compiler_params=kernel_params(12),
+        cost_estimate=pl.CostEstimate(flops=0, bytes_accessed=0, transcendentals=0),
         name="backward_attention",
-    )(spot, grad_middle, grad_proj, mixed, stream, vectors, blocked, *others, *parts)
+    )(grad_middle, grad_proj, mixed, stream, vectors, blocked, *others, crossed, split)
 
 
 def row_of(spot, step, far_x, steps):
     return 2 * lax.rem(spot[0] - step + steps, steps) + lax.rem(spot[1] + far_x, 2)
 
 
-def feed_group(spot, core, part, far_y, j, normed_t, grad_up, grad_down_t, hidden, spare):
-    half = spare.shape[2]
+def feed_group(spot, core, part, far_y, at_z, normed_t, grad_up, grad_down_t, hidden, spare):
+    count, wide, rows, half = spare.shape
     column = 2 * lax.rem(spot[2] + far_y, 2) + core
     if part == 0:
-        at = pl.multiple_of((column * 2 + j) * half, half)
-        out = dot_nn(normed_t[...], grad_up[:, pl.ds(at, half)])
-        spare[...] = out.reshape(spare.shape).astype(BF)
+        left = normed_t[...] if at_z is None else normed_t[pl.ds(pl.multiple_of(at_z * 2 * rows, 2 * rows), 2 * rows), :]
+        for j in range(wide):
+            at = pl.multiple_of((column * wide + j) * half, half)
+            out = dot_nn(left, grad_up[:, pl.ds(at, half)])
+            spare[:, j] = out.reshape(count, rows, half).astype(BF)
     else:
-        rows = spare.shape[1]
-        at = pl.multiple_of((column * 2 + j) * rows, rows)
-        left = grad_down_t[pl.ds(at, rows), :]
-        for row in range(spare.shape[0]):
-            spare[row] = dot_nn(left, hidden[:, pl.ds(row * half, half)]).astype(BF)
-
-
-def attention_group(spot, core, part, far_y, j, normed_t, grad_mixed, attended_t, grad_proj, spare):
-    half = spare.shape[2]
+        at = pl.multiple_of(column * wide * rows, wide * rows)
+        left = grad_down_t[pl.ds(at, wide * rows), :]
+        for row in range(count):
+            columns = row * half if at_z is None else pl.multiple_of((at_z * 2 + row) * half, half)
+            out = dot_nn(left, hidden[:, pl.ds(columns, half)])
+            spare[row] = out.reshape(wide, rows, half).astype(BF)
+
+
+def attention_group(spot, core, part, far_y, at_z, normed_t, grad_mixed, attended_t, grad_proj, spare):
+    count, _, rows, half = spare.shape
     column = 2 * lax.rem(spot[2] + far_y, 2) + core
     if part == 0:
         out = dot_nn(normed_t[...], grad_mixed[column, :, :half])
@@ -698,77 +749,82 @@
         out = dot_nn(normed_t[...], grad_mixed[column, :, half:]) + dot_nn(
             attended_t[...], grad_proj[column]
         )
-    spare[...] = out.reshape(spare.shape).astype(BF)
-
-
-def sent_kernel(fill, wide, steps, spot, *refs):
-    operands, out, spare = refs[:4], refs[4], refs[5]
+    spare[:, 0] = out.reshape(count, rows, half).astype(BF)
+
+
+def each_group(fill, steps, ring, spot, core, operands, spare):
+    wide = spare.shape[1]
+    at_z = lax.rem(spot[0] - steps[0] + ring, ring) if len(steps) == 1 else None
     for part in range(2):
         for far_y in range(2):
-            for j in range(wide):
-                fill(spot, 1 - spot[3], part, far_y, j, *operands, spare)
-                for step in range(steps):
-                    for far_x in range(2):
-                        if part == 0:
-                            at = (far_x * 2 + far_y) * wide + j
-                        else:
-                            at = (4 + far_y * 2 + far_x) * wide + j
-                        out[step, at] = spare[row_of(spot, step, far_x, steps)]
-
-
-def kept_kernel(fill, wide, steps, spot, *refs):
-    operands, got, outs, spare = refs[:4], refs[4], refs[5 : 5 + 3 * steps], refs[5 + 3 * steps]
-    for part in range(2):
-        for far_y in range(2):
-            for j in range(wide):
-                fill(spot, spot[3], part, far_y, j, *operands, spare)
-                for step in range(steps):
-                    for far_x in range(2):
-                        if part == 0:
-                            at = (far_x * 2 + far_y) * wide + j
-                        else:
-                            at = (4 + far_y * 2 + far_x) * wide + j
-                        total = spare[row_of(spot, step, far_x, steps)].astype(F32) + got[step, at].astype(F32)
-                        total = total.astype(BF)
-                        across, aside, stays = outs[3 * step : 3 * step + 3]
-                        if part == 0:
-                            target, index = (across, far_y * wide + j) if far_x else (stays, far_y * wide + j)
-                        else:
-                            index = far_x * wide + j
-                            target, index = (aside, index) if far_y else (stays, 2 * wide + index)
-                        target[index] = total
-
-
-def sent_part(place, spot, fill, wide, operands):
+            fill(spot, core, part, far_y, at_z, *operands, spare)
+            for index, step in enumerate(steps):
+                for far_x in range(2):
+                    row = row_of(spot, step, far_x, ring) if at_z is None else lax.rem(spot[1] + far_x, 2)
+                    for j in range(wide):
+                        yield index, part, far_y, far_x, j, spare[row, j]
+
+
+def place_in(part, far_y, far_x, j, wide):
+    return (far_x * 2 + far_y) * wide + j if part == 0 else (4 + far_y * 2 + far_x) * wide + j
+
+
+def sent_kernel(fill, steps, ring, spot, *refs):
+    operands, out, spare = refs[:4], refs[4], refs[5]
+    for index, part, far_y, far_x, j, block in each_group(fill, steps, ring, spot, 1 - spot[3], operands, spare):
+        out[index, place_in(part, far_y, far_x, j, spare.shape[1])] = block
+
+
+def kept_kernel(fill, steps, ring, spot, *refs):
+    operands, got, outs, spare = refs[:4], refs[4], refs[5:-1], refs[-1]
+    wide = spare.shape[1]
+    for index, part, far_y, far_x, j, block in each_group(fill, steps, ring, spot, spot[3], operands, spare):
+        total = block.astype(F32) + got[index, place_in(part, far_y, far_x, j, wide)].astype(F32)
+        across, aside, stays = outs[3 * index : 3 * index + 3]
+        if part == 0:
+            at = far_y * wide + j
+            target = across if far_x else stays
+        else:
+            at = far_x * wide + j
+            target = aside if far_y else stays
+            at = at if far_y else 2 * wide + at
+        target[at] = total.astype(BF)
+
+
+def spare_shape(place, steps, wide, rows, half):
+    return pltpu.VMEM((2 if len(steps) == 1 else place.n_dp, wide, rows, half), BF)
+
+
+def sent_part(place, spot, fill, wide, steps, operands):
     rows, half = (operands[0].shape[0] // place.n_dp, operands[0].shape[0] // 2)
     return pl.pallas_call(
-        partial(sent_kernel, fill, wide, place.nz),
+        partial(sent_kernel, fill, steps, place.nz),
         in_specs=in_smem(1) + whole_vmem(4),
         out_specs=whole_vmem(1)[0],
-        out_shape=jax.ShapeDtypeStruct((place.nz, 8 * wide, rows, half), BF),
-        scratch_shapes=[pltpu.VMEM((place.n_dp, rows, half), BF)],
+        out_shape=jax.ShapeDtypeStruct((len(steps), 8 * wide, rows, half), BF),
+        scratch_shapes=[spare_shape(place, steps, wide, rows, half)],
         compiler_params=kernel_params(10),
+        cost_estimate=pl.CostEstimate(flops=0, bytes_accessed=0, transcendentals=0),
         name="gradient_sent",
     )(spot, *operands)
 
 
-def kept_part(place, spot, fill, wide, operands, got):
+def kept_part(place, spot, fill, wide, steps, operands, got):
     rows, half = (operands[0].shape[0] // place.n_dp, operands[0].shape[0] // 2)
     shapes = [
-        jax.ShapeDtypeStruct((size * wide, rows, half), BF)
-        for _ in range(place.nz)
-        for size in (2, 2, 4)
+        jax.ShapeDtypeStruct((size * wide, rows, half), BF) for _ in steps for size in (2, 2, 4)
     ]
     outs = pl.pallas_call(
-        partial(kept_kernel, fill, wide, place.nz),
+        partial(kept_kernel, fill, steps, place.nz),
         in_specs=in_smem(1) + whole_vmem(5),
         out_specs=whole_vmem(len(shapes)),
         out_shape=shapes,
-        scratch_shapes=[pltpu.VMEM((place.n_dp, rows, half), BF)],
+        scratch_shapes=[spare_shape(place, steps, wide, rows, half)],
         compiler_params=kernel_params(10),
+        cost_estimate=pl.CostEstimate(flops=0, bytes_accessed=0, transcendentals=0),
         name="gradient_kept",
     )(spot, *operands, got)
-    return [outs[3 * step : 3 * step + 3] for step in range(place.nz)]
+    return {step: list(outs[3 * i : 3 * i + 3]) for i, step in enumerate(steps)}
 
 
 def ring_kernel(stays, across, aside, *refs):
@@ -790,6 +846,7 @@
         out_specs=whole_vmem(1)[0],
         out_shape=jax.ShapeDtypeStruct(stays.shape, BF),
         compiler_params=kernel_params(4),
+        cost_estimate=pl.CostEstimate(flops=0, bytes_accessed=0, transcendentals=0),
         name="ring_block",
     )(*operands)
 
@@ -807,43 +864,68 @@
     return jnp.where(which == 0, low, high)
 
 
-def own_groups(place, qkv, proj, up, down):
-    rows, half = proj.shape[0], proj.shape[1] // 2
-    wide = 2 * half
-
-    def attention_groups(core):
-        parts = [qkv[:, j * wide + core * half : j * wide + (core + 1) * half] for j in range(3)]
+def attention_groups(place, qkv, proj):
+    half = proj.shape[1] // 2
+
+    def of(core):
+        parts = [qkv[:, (2 * j + core) * half : (2 * j + core + 1) * half] for j in range(3)]
         return jnp.stack(parts + [proj[:, core * half : (core + 1) * half]])
 
-    def feed_groups(core):
+    return pick(place.core, of(0), of(1))
+
+
+def feed_groups(place, up, down):
+    rows, half = up.shape[0], down.shape[1] // 2
+
+    def of(core):
         parts = [up[:, (core * 4 + j) * half : (core * 4 + j + 1) * half] for j in range(4)]
         return jnp.concatenate(
             [jnp.stack(parts), down[:, core * half : (core + 1) * half].reshape(4, rows, half)]
         )
 
-    return (
-        pick(place.core, attention_groups(0), attention_groups(1)),
-        pick(place.core, feed_groups(0), feed_groups(1)),
-    )
+    return pick(place.core, of(0), of(1))
 
 
 class Gathered:
-    def __init__(self, own, place):
-        groups = own.shape[0]
-        self.first = groups // 2
-        self.quarter = groups // 4
-        self.own = own
+    def __init__(self, place, own, extra, turned, chunks):
+        groups, rows, half = own.shape
+        self.turned = turned
+        self.chunks = chunks
+        self.first = jnp.concatenate([own[: groups // 2].reshape(-1, half)] + extra)
+        self.wide = self.first.shape[0]
         self.mine = pick(
             place.y,
-            own[self.first : self.first + self.quarter],
-            own[self.first + self.quarter :],
-        )
+            own[groups // 2 : groups // 2 + groups // 4],
+            own[groups // 2 + groups // 4 :],
+        ).reshape(-1, half)
         self.blocks = []
+        self.across = {}
+        self.aside = {}
         self.whole = []
         self.mate = []
+        if turned:
+            self.begin([])
 
     def begin(self, crossed):
-        self.blocks.append(jnp.concatenate([self.own[: self.first], self.mine, crossed]))
+        self.blocks.append(jnp.concatenate([self.first, self.mine] + crossed))
+
+    def over_x(self, step):
+        return self.blocks[step] if self.turned else self.blocks[step][: self.wide]
+
+    def over_y(self, step):
+        tails = [self.blocks[step][self.wide :]]
+        if self.turned:
+            tails.append(self.across[step][self.wide :])
+        return tails
+
+    def chunk(self, which, across, aside):
+        return jnp.concatenate(
+            [
+                piece
+                for step in self.chunks[which]
+                for piece in (self.blocks[step], across.get(step), aside.get(step))
+            ]
+        )
 
     def parts(self):
         return self.whole + self.mate
@@ -853,8 +935,7 @@
     def __init__(self, place):
         self.place = place
         self.operands = None
-        self.sent = None
-        self.kept = None
+        self.kept = {}
         self.sides = {}
         self.running = None
         self.last = None
@@ -863,16 +944,9 @@
         return ring_block(self.kept[step][2], *self.sides[step], self.running)
 
 
-def gather_vectors_packed(place, vectors, bias_up):
-    rows, part = vectors[0].shape
-    packed = jnp.concatenate([jnp.stack(vectors, axis=1), bias_up.reshape(rows, -1, part)], axis=1)
-    spread = jnp.broadcast_to(packed[None], (place.n_dp,) + packed.shape)
-    spread = lax.all_to_all(spread, "dp", split_axis=0, concat_axis=0, tiled=True).astype(F32)
-    count = len(vectors)
-    return (
-        jnp.transpose(spread[:, :, :count], (1, 2, 0, 3)).reshape(rows, count, -1),
-        jnp.transpose(spread[:, :, count:], (1, 0, 2, 3)).reshape(rows, 1, -1),
-    )
+def pack_vectors(vectors, bias_up, half, rows):
+    packed = jnp.concatenate(vectors + [bias_up]).reshape(-1, half)
+    return jnp.pad(packed, ((0, rows - packed.shape[0]), (0, 0)))
 
 
 def image_kernel(frame, before, patches, after, specials, out, window):
@@ -903,52 +977,74 @@
             out_shape=jax.ShapeDtypeStruct((rows, width), F32),
             scratch_shapes=[pltpu.VMEM((MOST + 2 * halo, width), F32)],
             compiler_params=kernel_params(6),
+        cost_estimate=pl.CostEstimate(flops=0, bytes_accessed=0, transcendentals=0),
             name="take_image",
         )(frame, before, patches, after, specials)
 
     return (before, patches, after, specials), build
 
 
-def block_kernel(frame, stream, own, before, after, specials, window):
-    halo, count = before.shape[0], own.shape[0]
-    window[MOST:] = jnp.zeros((window.shape[0] - MOST, window.shape[1]), F32)
-    inside = lax.broadcasted_iota(jnp.int32, (MOST, 1), 0) < frame[1]
-    window[:MOST] = jnp.where(inside, stream[:MOST], 0.0)
-    window[...] = pltpu.roll(window[...], frame[0], 0)
-    before[...] = window[:halo]
-    own[...] = window[halo : halo + count]
-    after[...] = window[halo + count : 2 * halo + count]
-    specials[...] = stream[MOST : MOST + specials.shape[0]]
-
-
-def give_image(place, frame, stream, halo, count, special_count):
-    width = stream.shape[1]
-    own, before, after, specials = pl.pallas_call(
+def block_kernel(frame, *refs):
+    streams, (before, after), owns, window = refs[:2], refs[2:4], refs[4:8], refs[8]
+    for at, stream in enumerate(streams):
+        own, specials = owns[2 * at : 2 * at + 2]
+        halo, count = before.shape[0] // 2, own.shape[0]
+        window[MOST:] = jnp.zeros((window.shape[0] - MOST, window.shape[1]), F32)
+        inside = lax.broadcasted_iota(jnp.int32, (MOST, 1), 0) < frame[1]
+        window[:MOST] = jnp.where(inside, stream[:MOST], 0.0)
+        window[...] = pltpu.roll(window[...], frame[0], 0)
+        before[at * halo : (at + 1) * halo] = window[:halo]
+        own[...] = window[halo : halo + count]
+        after[at * halo : (at + 1) * halo] = window[halo + count : 2 * halo + count]
+        specials[...] = stream[MOST : MOST + specials.shape[0]]
+
+
+def give_images(frame, streams, halo, count, special_count):
+    width = streams[0].shape[1]
+    return pl.pallas_call(
         block_kernel,
-        in_specs=in_smem(1) + whole_vmem(1),
-        out_specs=whole_vmem(4),
+        in_specs=in_smem(1) + whole_vmem(2),
+        out_specs=whole_vmem(6),
         out_shape=[
-            jax.ShapeDtypeStruct((size, width), F32) for size in (count, halo, halo, special_count)
+            jax.ShapeDtypeStruct((size, width), F32)
+            for size in (2 * halo, 2 * halo, count, special_count, count, special_count)
         ],
         scratch_shapes=[pltpu.VMEM((MOST + 2 * halo, width), F32)],
         compiler_params=kernel_params(6),
-        name="give_image",
-    )(frame, stream)
-    return (own, shift_seq(place, after, 1), shift_seq(place, before, -1), specials)
-
-
-def join_image(own, from_before, from_after, specials):
-    halo = from_before.shape[0]
-    blank = jnp.zeros((own.shape[0] - halo, own.shape[1]), own.dtype)
-    return (
-        own + jnp.concatenate([from_before, blank]) + jnp.concatenate([blank, from_after]),
-        specials,
-    )
+        cost_estimate=pl.CostEstimate(flops=0, bytes_accessed=0, transcendentals=0),
+        name="give_images",
+    )(frame, *streams)
 
 
 def finish_kernel(*refs):
-    inputs, (out_mixed, out_proj, out_up, out_down) = refs[:-4], refs[-4:]
-    layers = len(inputs) // 6
+    spot, refs = refs[0], refs[1:]
+    inputs, outs = refs[: 6 * LAYERS], refs[6 * LAYERS :]
+    sums, (own_one, own_two, from_before, from_after), outs = outs[:4], outs[4:8], outs[8:]
+    (out_mixed, out_proj, out_up, out_down), (image_one, image_two), out_rows = outs[:4], outs[4:6], outs[6:]
+    halo = from_before.shape[0] // 2
+    for at, (own, image) in enumerate(((own_one, image_one), (own_two, image_two))):
+        count = own.shape[0]
+        image[:halo] = own[:halo] + from_before[at * halo : (at + 1) * halo]
+        image[halo : count - halo] = own[halo : count - halo]
+        image[count - halo :] = own[count - halo :] + from_after[at * halo : (at + 1) * halo]
+    layers = LAYERS
+    total = sums[0][...]
+    for other in sums[1:]:
+        total = total + other[...]
+    place_dp = 2 * spot[0] + spot[1]
+    each, width = total.shape[0] // layers, total.shape[1]
+    part = out_rows[0].shape[1]
+    turned = pltpu.roll(total, lax.rem(width - place_dp * part, width), 1)
+    more = VECTOR_PIECES - BIAS_DOWN - 1
+    row_ids = lax.broadcasted_iota(jnp.int32, total.shape, 0)
+    half_turned = pltpu.roll(total, lax.rem(width - lax.rem(place_dp * more * part, width), width), 1)
+    for layer in range(layers):
+        for row in range(BIAS_DOWN + 1):
+            at = layer * each + row
+            out_rows[row][layer : layer + 1, :] = turned[at : at + 1, :part]
+        at = layer * each + BIAS_DOWN + 1 + place_dp * more * part // width
+        row = jnp.sum(jnp.where(row_ids == at, half_turned, 0.0), axis=0, keepdims=True)
+        out_rows[-1][layer : layer + 1, :] = row[:, : more * part]
     for layer in range(layers):
         last, aside, across = inputs[6 * layer : 6 * layer + 3]
         one = last[0].astype(F32) + aside[0].astype(F32)
@@ -961,28 +1057,34 @@
         for j in range(2):
             out_up[layer, :, j * half : (j + 1) * half] = last[j].astype(F32) + aside[j].astype(F32)
         downs = [last[4 + j].astype(F32) + across[j].astype(F32) for j in range(2)]
-        out_down[layer] = jnp.concatenate(downs, axis=0).T
-
-
-def finish(place, parts, rows, width):
+        for j in range(2):
+            out_down[layer, j * downs[j].shape[0] : (j + 1) * downs[j].shape[0]] = downs[j]
+
+
+def finish(place, spot, parts, sums, images, rows, width):
     shapes = [
         jax.ShapeDtypeStruct((LAYERS, rows, columns), F32)
         for rows, columns in (
             (rows, 3 * width // 4),
             (rows, width // 4),
             (rows, width),
-            (4 * rows, width // 4),
+            (width // 4, 4 * rows),
         )
     ]
-    flat_parts = [array for layer in parts for array in layer]
+    shapes += [jax.ShapeDtypeStruct(images[0].shape, F32)] * 2
+    more = VECTOR_PIECES - BIAS_DOWN - 1
+    shapes += [jax.ShapeDtypeStruct((LAYERS, rows), F32)] * (BIAS_DOWN + 1)
+    shapes += [jax.ShapeDtypeStruct((LAYERS, more * rows), F32)]
+    flat_parts = [array for layer in parts for array in layer] + sums + images
     return pl.pallas_call(
         finish_kernel,
-        in_specs=whole_vmem(len(flat_parts)),
+        in_specs=in_smem(1) + whole_vmem(len(flat_parts)),
         out_specs=whole_vmem(len(shapes)),
         out_shape=shapes,
         compiler_params=kernel_params(10),
+        cost_estimate=pl.CostEstimate(flops=0, bytes_accessed=0, transcendentals=0),
         name="finish",
-    )(*flat_parts)
+    )(spot, *flat_parts)
 
 
 def local_walked(
@@ -1013,6 +1115,7 @@
     halo = (MOST - count) * (images // 2)
     rows = -(-(MOST + special_count) // 16) * 16
     nz = place.nz
+    pairs = ((0, 1), (2, 3))
     part_rows = proj_weight.shape[1]
     before = jnp.sum(jnp.where(jnp.arange(images) < place.seq, lengths[0], 0))
     length = lax.dynamic_index_in_dim(lengths[0], place.seq, 0, keepdims=False)
@@ -1024,107 +1127,112 @@
     blocked = jnp.where(key_ok, 0.0, MASKED).astype(F32)[None]
     spot = jnp.stack([place.z, place.x, place.y, place.core]).astype(jnp.int32)
 
-    units = []
-    for layer in range(LAYERS):
-        attention_own, feed_own = own_groups(
-            place, qkv_weight[layer], proj_weight[layer], fc1_weight[layer], fc2_weight[layer]
-        )
-        units.append(Gathered(attention_own, place))
-        units.append(Gathered(feed_own, place))
-
-    first_cross = place.swap_x(units[0].mine)
+    shards = (norm1_gain, norm1_bias, query_bias, value_bias, proj_bias, norm2_gain, norm2_bias, fc2_bias)
+
+    def attention_unit(layer, qkv, proj):
+        extra = pack_vectors([shard[layer] for shard in shards], fc1_bias[layer], width // 2, EXTRA_ROWS)
+        return Gathered(place, attention_groups(place, qkv, proj), [extra], layer == 0, pairs)
+
+    units = [attention_unit(0, qkv_weight[0], proj_weight[0])]
+    image, build = take_image(place, frame, patches, specials, halo, rows)
     inputs = {
-        "later": [unit.mine for unit in units[1:]],
-        "own": [unit.own for unit in units[1:]],
-        "rows": (patches, specials),
+        "weights": (fc1_weight[0], fc2_weight[0], qkv_weight[1], proj_weight[1], fc1_weight[1], fc2_weight[1]),
         "cots": (cot_patches, cot_specials),
-        "vectors": (norm1_gain, norm1_bias, query_bias, value_bias, proj_bias, norm2_gain, norm2_bias, fc2_bias),
-        "bias": fc1_bias,
     }
-    first_cross, inputs = fence((first_cross, inputs))
-    units[0].begin(first_cross)
-    for unit, own in zip(units[1:], inputs.pop("own")):
-        unit.own = own
-
-    vectors, bias_up = (None, None)
+    vectors, bias_up = ([None] * LAYERS, [None] * LAYERS)
     streams = [None] * (LAYERS + 1)
     middles, normed_one_ts, normed_two_ts, mixeds, attended_ts, hiddens, slopes = (
         [None] * LAYERS for _ in range(7)
     )
-    cores = []
+    weights = [None] * (2 * LAYERS)
+    unit_count = 2 * LAYERS
+    last_slot = 3 * unit_count + 1
+    at_x, at_y = ([[] for _ in range(last_slot + 2)] for _ in range(2))
+    for which in range(unit_count):
+        for step in range(nz):
+            slot = 3 * which + step
+            at_x[slot].append((which, step))
+            at_y[slot + (which == 0)].append((which, step))
+    at_core = {4: [(0, 0)], 5: [(0, 1), (1, 0)], 7: [(1, 1)], 8: [(2, 0)], 10: [(2, 1)], 11: [(3, 0)], 12: [(3, 1)], 13: [(3, 2)]}
     carried = {}
     grad = None
-    for slot in range(3 * len(units) + 2):
+    for slot in range(last_slot + 1):
         new = {}
         index, step = divmod(slot, 3)
-        todo = []
-        if index < len(units):
+        if index < unit_count:
             new["z"] = place.ring_z(units[index].blocks[step])
-            todo.append((index, step))
-        if step == 0 and index > 0:
-            todo.append((index - 1, 3))
-        for which, at in todo:
-            unit = units[which]
-            new["x", which, at] = place.swap_x(unit.blocks[at][: unit.first])
-            new["y", which, at] = place.swap_seq(unit.blocks[at][unit.first :], 2)
-        for which, at in cores:
+        for which, at in at_x[slot]:
+            new["x", which, at] = place.swap_x(units[which].over_x(at))
+        for which, at in at_y[slot]:
+            tails = units[which].over_y(at)
+            new["y", which, at] = place.swap_seq(tails[0] if len(tails) == 1 else jnp.concatenate(tails), 2)
+        for which, at in at_core.get(slot, []):
             new["core", which, at] = place.swap_seq(units[which].whole[at], 1)
+        for which, at in at_y[slot]:
+            for index_of, chunk in enumerate(units[which].chunks):
+                if chunk[-1] == at:
+                    unit = units[which]
+                    across = {**unit.across, **{k[2]: v for k, v in new.items() if k[:2] == ("x", which)}}
+                    aside = {**unit.aside, **{k[2]: v for k, v in new.items() if k[:2] == ("y", which)}}
+                    new["chunk", which, index_of] = unit.chunk(index_of, across, aside)
+        later = {1: 1, 2: 2, 8: 3}.get(slot)
+        if later:
+            new["later"] = place.swap_x(units[later].mine)
         if slot == 0:
-            new["later"] = place.swap_x(jnp.concatenate(inputs["later"]))
-        if slot in (1, 4):
-            new["image"], build = take_image(place, frame, *inputs["rows" if slot == 1 else "cots"], halo, rows)
-        if slot == 2:
+            new["image"] = image
+        if slot == 5:
             carried["stream"] = build(*image)
-        if slot == 5:
+        if slot == 3 * unit_count:
+            new["image"], build = take_image(place, frame, *inputs["cots"], halo, rows)
+        if slot == 3 * unit_count + 1:
             grad = build(*image)
-        if slot == 3:
-            new["vectors"] = gather_vectors_packed(place, inputs["vectors"], inputs["bias"])
-        if slot in (5, 11):
-            layer = slot // 6
+        if slot in (9, 11):
+            layer = slot // 11
             new["forward"] = forward_attention(
-                place, spot, keeps[2 * layer], carried["stream"], vectors[layer], units[2 * layer].parts(), blocked
+                place, spot, keeps[2 * layer], carried["stream"], units[2 * layer], blocked, EXTRA_ROWS
             )
-        if slot == 9:
-            new["feed"] = forward_feed(
-                place, spot, keeps[1], carried["middle"], carried["normed"], bias_up[0], vectors[0], units[1].parts()
-            )
-        after = (slot + 1) // 3
-        if slot % 3 == 2 and after < len(units):
-            carried["begin"] = units[after].blocks[0]
-        gate = inputs if slot < 4 else {}
+        if slot == 10:
+            hidden, slope, crossed, split = forward_up(place, spot, carried["normed"], bias_up[0], units[1])
+            output = forward_down(keeps[1], carried["middle"], hidden, vectors[0], split)
+            new["feed"] = (output, hidden, slope, crossed, split)
+        if step == 2 and index + 1 < unit_count and units[index + 1].blocks:
+            carried["begin"] = units[index + 1].blocks[0]
+        gate = inputs if slot in (0, 3 * unit_count - 1) else {}
         new, carried, gate = fence((new, carried, gate))
         inputs.update(gate)
+        if slot == 0:
+            up_0, down_0, qkv_1, proj_1, up_1, down_1 = inputs.pop("weights")
+            units.append(Gathered(place, feed_groups(place, up_0, down_0), [], False, pairs))
+            units.append(attention_unit(1, qkv_1, proj_1))
+            units.append(Gathered(place, feed_groups(place, up_1, down_1), [], False, ((0, 1), (2,), (3,))))
         if "begin" in carried:
-            units[after].blocks[0] = carried.pop("begin")
+            units[index + 1].blocks[0] = carried.pop("begin")
         if "image" in new:
             image = new["image"]
-        if "vectors" in new:
-            vectors, bias_up = new["vectors"]
         if "later" in new:
-            at = 0
-            for unit in units[1:]:
-                unit.begin(new["later"][at : at + unit.quarter])
-                at += unit.quarter
+            units[later].begin([new["later"]])
         if "z" in new:
             units[index].blocks.append(new["z"])
-        for which, at in cores:
+        for which, at in at_core.get(slot, []):
             units[which].mate.append(new["core", which, at])
-        cores = todo
-        for which, at in todo:
-            unit = units[which]
-            unit.whole.append(
-                jnp.concatenate([unit.blocks[at], new["x", which, at], new["y", which, at]])
-            )
+        for which, at in at_x[slot]:
+            units[which].across[at] = new["x", which, at]
+        for which, at in at_y[slot]:
+            units[which].aside[at] = new["y", which, at]
+        for key in new:
+            if key[0] == "chunk":
+                units[key[1]].whole.append(new[key])
         if "forward" in new:
             streams[layer] = carried.pop("stream")
-            middle, normed, normed_one_ts[layer], normed_two_ts[layer], mixeds[layer], _, attended_ts[layer] = new["forward"]
+            middle, normed, normed_one_ts[layer], normed_two_ts[layer], mixeds[layer], _, attended_ts[layer], crossed, split, vectors[layer], bias_up[layer] = new["forward"]
+            weights[2 * layer] = [crossed, split]
             middles[layer] = middle
             carried["middle"], carried["normed"] = middle, normed
         if "feed" in new:
-            carried["stream"], hiddens[0], slopes[0] = new["feed"]
+            carried["stream"], hiddens[0], slopes[0], *weights[1] = new["feed"]
             del carried["middle"], carried["normed"]
-    streams[LAYERS], hiddens[1], slopes[1] = forward_feed(
-        place, spot, keeps[3], carried["middle"], carried["normed"], bias_up[1], vectors[1], units[3].parts()
+    hiddens[1], slopes[1], *weights[3] = forward_up(
+        place, spot, carried["normed"], bias_up[1], units[3]
     )
 
     reduces = [Reduced(place) for _ in range(2 * LAYERS)]
@@ -1134,28 +1242,28 @@
     def feed_back(layer, grad):
         found = back[layer]
         found["down_t"], found["up"], found["sum_down"], found["sum_up"] = backward_feed(
-            place, spot, keeps[2 * layer + 1], grad, slopes[layer], units[2 * layer + 1].parts()
+            keeps[2 * layer + 1], grad, slopes[layer], weights[2 * layer + 1][1]
         )
 
-    def feed_sent(layer):
-        unit = reduces[2 * (LAYERS - 1 - layer)]
-        unit.operands = (normed_two_ts[layer], back[layer]["up"], back[layer]["down_t"], hiddens[layer])
-        unit.sent = sent_part(place, spot, feed_group, 2, unit.operands)
+    def feed_operands(layer):
+        reduces[2 * (LAYERS - 1 - layer)].operands = (
+            normed_two_ts[layer], back[layer]["up"], back[layer]["down_t"], hiddens[layer]
+        )
 
     def middle_back(layer, grad):
         found = back[layer]
         found["middle"], found["proj"], found["sum_proj"], found["gain"], found["shift"] = backward_middle(
-            place, spot, keeps[2 * layer], grad, found["up"], middles[layer], vectors[layer], units[2 * layer + 1].parts()
+            keeps[2 * layer], grad, found["up"], middles[layer], vectors[layer], weights[2 * layer + 1][0]
         )
 
     def attention_back(layer):
         found = back[layer]
         others = [found[name] for name in ("sum_proj", "gain", "shift", "sum_down", "sum_up")]
         found["grad"], found["mixed"], found["sums"] = backward_attention(
-            place, spot, found["middle"], found["proj"], mixeds[layer], streams[layer], vectors[layer], blocked, others, units[2 * layer].parts()
+            found["middle"], found["proj"], mixeds[layer], streams[layer], vectors[layer], blocked, others, *weights[2 * layer]
         )
 
-    def attention_sent(layer):
+    def attention_operands(layer):
         found = back[layer]
         wide = 3 * width // 4
         cut = width // 4
@@ -1165,130 +1273,185 @@
         proj = jnp.stack([jnp.pad(found["proj"][:, i * cut : (i + 1) * cut], ((0, 0), (cut, 0))) for i in range(4)])
         unit = reduces[2 * (LAYERS - 1 - layer) + 1]
         unit.operands = (normed_one_ts[layer], mixed, attended_ts[layer], proj)
-        unit.sent = sent_part(place, spot, attention_group, 1, unit.operands)
+
+    fills = [(feed_group, 2), (attention_group, 1)] * LAYERS
+    all_steps = (1, 2, 3, 0)
+    cuts = [((1,), (2, 3, 0))] + [(all_steps,)] * (len(reduces) - 1)
+
+    def sent_cut(which, cut):
+        fill, wide = fills[which]
+        return sent_part(place, spot, fill, wide, cuts[which][cut], reduces[which].operands)
+
+    def keep_cut(which, cut, got):
+        fill, wide = fills[which]
+        unit = reduces[which]
+        unit.kept.update(kept_part(place, spot, fill, wide, cuts[which][cut], unit.operands, got))
 
     feed_back(1, grad)
-    feed_sent(1)
-    back[1], back_sent, output = fence((back[1], [reduces[0].sent], streams[LAYERS]))
-    reduces[0].sent = back_sent[0]
+    feed_operands(1)
+    sent = [sent_cut(0, 0), None]
+    back[1], sent = fence((back[1], sent[:1]))
     final_slot = 3 * len(reduces)
-    outs = {}
-    total = None
-    ringing = None
+    total = given = None
+    rung = []
+    got = {}
+    sending = {(0, 0): sent[0]}
     for slot in range(-2, final_slot + 1):
         new = {}
+        work = {}
         for which, unit in enumerate(reduces):
             at = slot - 3 * which
-            fill, wide = (attention_group, 1) if which % 2 else (feed_group, 2)
-            if at == -2:
-                new["core", which] = place.swap_seq(unit.sent, 1)
-            if at == -1:
-                unit.kept = kept_part(place, spot, fill, wide, unit.operands, unit.got)
+            if 0 <= at <= 2:
+                new["z", which] = place.ring_z(unit.block(at + 1))
+            if at == 3:
+                unit.last = unit.block(0)
+                work["last", which] = unit.last
+        for base, group in ((final_slot - 2, range(len(reduces) - 1)), (final_slot, [len(reduces) - 1])):
+            if slot == base:
+                ends = [reduces[which].last for which in group]
+                parts = [end.shape[0] // 4 for end in ends]
+                aside = place.swap_seq(
+                    jnp.concatenate([end[part : 2 * part] for end, part in zip(ends, parts)]), 2
+                )
+                across = place.swap_x(jnp.concatenate([end[3 * part :] for end, part in zip(ends, parts)]))
+                begins = 0
+                for which, end, part in zip(group, ends, parts):
+                    lasts[which] = [end, aside[begins : begins + part], across[begins : begins + part]]
+                    begins += part
+                if slot < final_slot:
+                    new["lasts"] = [lasts[which] for which in group]
+        if slot == -2:
+            sending[0, 1] = sent_cut(0, 1)
+            work["sending"] = sending[0, 1]
+        if slot == 0:
+            keep_cut(0, 1, got.pop((0, 1)))
+        if slot == -1:
+            keep_cut(0, 0, got.pop((0, 0)))
+        for which, base in ((1, 2), (2, 5), (3, 8)):
+            if slot == base:
+                keep_cut(which, 0, got.pop((which, 0)))
+        for key, base in (((0, 0), -2), ((0, 1), -1), ((2, 0), 4), ((3, 0), 6)):
+            if slot == base:
+                new["core", key] = place.swap_seq(sending.pop(key), 1)
+        for which, unit in enumerate(reduces):
+            at = slot - 3 * which
             if -1 <= at <= 2:
                 step = (at + 2) % nz
                 new["side", which] = (
                     place.swap_x(unit.kept[step][0]),
                     place.swap_seq(unit.kept[step][1], 2),
                 )
-            if 0 <= at <= 2:
-                new["z", which] = place.ring_z(unit.block(at + 1))
-            if at == 3:
-                last = unit.block(0)
-                part = last.shape[0] // 4
-                lasts[which] = [
-                    last,
-                    place.swap_seq(last[part : 2 * part], 2),
-                    place.swap_x(last[3 * part :]),
-                ]
-                if which < len(reduces) - 1:
-                    new["last", which] = lasts[which]
-        work = {}
-        if slot == -2:
+        if slot == 3:
+            feed_operands(0)
+            attention_operands(0)
+            work["sending"] = (sent_cut(2, 0), sent_cut(3, 0))
+        if slot == -1:
             middle_back(1, grad)
-            work["back", 1] = back[1]
-        if slot == -1:
+            streams[LAYERS] = forward_down(keeps[3], carried["middle"], hiddens[1], vectors[1], weights[3][1])
+            work["output"] = streams[LAYERS]
+        if slot == 0:
             attention_back(1)
-            work["back", 1] = back[1]
-        if slot == 0:
-            attention_sent(1)
-            work["sent", 1] = reduces[1].sent
-            feed_back(0, back[1]["grad"])
-            work["back", 0] = back[0]
         if slot == 1:
-            feed_sent(0)
-            work["sent", 2] = reduces[2].sent
-            middle_back(0, back[1]["grad"])
-            work["back", 0] = back[0]
+            attention_operands(1)
+            new["core", (1, 0)] = place.swap_seq(sent_cut(1, 0), 1)
+            names = ("down_t", "up", "sum_down", "sum_up", "middle", "proj", "sum_proj", "gain", "shift")
+            back[0] = dict(
+                zip(
+                    names,
+                    backward_feed_middle(
+                        keeps[1], keeps[0], back[1]["grad"], slopes[0], weights[1][1], middles[0], vectors[0], weights[1][0]
+                    ),
+                )
+            )
         if slot == 2:
             attention_back(0)
+        if slot in (-1, 0):
+            work["back", 1] = back[1]
+        if slot in (1, 2):
             work["back", 0] = back[0]
         if slot == 3:
-            attention_sent(0)
-            work["sent", 3] = reduces[3].sent
-            new["give", "out"] = give_image(place, frame, output, halo, count, special_count)
             total = jnp.concatenate([back[layer]["sums"] for layer in range(LAYERS)])
-            new["total"] = total + place.swap_seq(total, 1)
+            new["sum"] = place.swap_seq(total, 1)
         if slot == 4:
-            new["give", "back"] = give_image(place, frame, back[0]["grad"], halo, count, special_count)
-            new["total"] = total + place.swap_seq(total, 2)
-        if slot == 5:
-            new["total"] = total + place.swap_x(total)
-            outs["out"] = join_image(*outs["out"])
-            outs["back"] = join_image(*outs["back"])
-        if slot in (6, 7, 8):
-            ringing = place.ring_z(total if slot == 6 else ringing)
-            new["ringing"] = ringing
+            new["sum"] = place.swap_seq(total, 2)
+        if slot == 6:
+            new["sum"] = place.swap_x(total)
+        if slot in (7, 9):
+            new["ringing"] = [place.ring_z(total, by) for by in ((1,) if slot == 7 else (2, 3))]
+        if slot == final_slot - 2:
+            work["images"] = give_images(frame, given, halo, count, special_count)
+        if slot == final_slot - 1:
+            images_before, images_after, *owns = images
+            new["images"] = (shift_seq(place, images_after, 1), shift_seq(place, images_before, -1))
         pending = {}
         for which, unit in enumerate(reduces):
             at = slot + 1 - 3 * which
-            if at == -2:
-                pending["sent", which] = unit.sent
             if 0 <= at <= 2:
-                pending["kept", which] = unit.kept[(at + 2) % nz]
-        if slot == -1:
-            pending["output"] = output
-        for key in list(work):
-            pending.pop(key, None)
+                step = (at + 2) % nz
+                if step in unit.kept:
+                    pending["kept", which] = unit.kept[step]
+        if slot == final_slot - 3:
+            pending["give"] = [streams[LAYERS], back[0]["grad"]]
+        for key, base in (((3, 0), 5),):
+            if slot == base:
+                pending["sending", key] = sending[key]
+        for key, base in (((0, 1), 0), ((1, 0), 2), ((2, 0), 5), ((3, 0), 8)):
+            if slot == base - 1 and key in got:
+                pending["got", key] = got[key]
         new, work, pending = fence((new, work, pending))
-        for found in (work, pending):
-            for key, value in found.items():
-                if key[0] == "sent":
-                    reduces[key[1]].sent = value
-                if key[0] == "kept":
-                    reduces[key[1]].kept[(slot + 1 - 3 * key[1] + 2) % nz] = value
-                if key[0] == "back":
-                    back[key[1]] = value
-        output = pending.get("output", output)
-        for which, unit in enumerate(reduces):
-            at = slot - 3 * which
-            if at == -2:
-                unit.got = new["core", which]
-            if -1 <= at <= 2:
-                unit.sides[(at + 2) % nz] = new["side", which]
-            if 0 <= at <= 2:
-                unit.running = new["z", which]
-            if at == 3 and ("last", which) in new:
-                lasts[which] = new["last", which]
-        if "total" in new:
-            total = new["total"]
+        if "sending" in work:
+            if slot == 3:
+                sending[2, 0], sending[3, 0] = work.pop("sending")
+            else:
+                sending[0, 1] = work.pop("sending")
+        for key in [key for key in pending if key[0] == "sending"]:
+            sending[key[1]] = pending.pop(key)
+        if "output" in work:
+            streams[LAYERS] = work.pop("output")
+        for key, value in work.items():
+            if key[0] == "back":
+                back[key[1]] = value
+            if key[0] == "last":
+                reduces[key[1]].last = value
+            if key == "images":
+                images = value
+        if "give" in pending:
+            given = pending.pop("give")
+        for key in [key for key in pending if key[0] == "got"]:
+            got[key[1]] = pending.pop(key)
+        for key, value in pending.items():
+            reduces[key[1]].kept[(slot + 1 - 3 * key[1] + 2) % nz] = value
+        for key, value in new.items():
+            if key[0] == "core":
+                got[key[1]] = value
+            if key[0] == "z":
+                reduces[key[1]].running = value
+            if key[0] == "side":
+                reduces[key[1]].sides[(slot - 3 * key[1] + 2) % nz] = value
+        if "images" in new:
+            sides = new["images"]
+        if "lasts" in new:
+            lasts[: len(new["lasts"])] = new["lasts"]
+        if "sum" in new:
+            total = total + new["sum"]
         if "ringing" in new:
-            ringing = new["ringing"]
-            summed = ringing + (total if slot == 6 else summed)
-        for name in ("out", "back"):
-            if ("give", name) in new:
-                outs[name] = new["give", name]
-
-    wm, wp, wu, wd = finish(
-        place, [lasts[3] + lasts[2], lasts[1] + lasts[0]], part_rows, width
+            rung += new["ringing"]
+
+    wm, wp, wu, wd, out_patches, grad_patches, g1, s1, bq, bv, bp, g2, s2, bd, bu = finish(
+        place,
+        spot,
+        [lasts[3] + lasts[2], lasts[1] + lasts[0]],
+        [total] + rung,
+        [owns[0], owns[2], *sides],
+        part_rows,
+        width,
     )
-    summed = summed.reshape(LAYERS, -1, place.n_dp, part_rows)
-    eight = lax.dynamic_index_in_dim(summed[:, :8], place.dp, 2, keepdims=False)
-    g1, s1, bq, bv, bp, g2, s2, bd = (eight[:, i] for i in range(8))
-    bu = summed[:, 8:12].reshape(LAYERS, place.n_dp, 4 * part_rows)
-    bu = lax.dynamic_index_in_dim(bu, place.dp, 1, keepdims=False)
+    wd = jnp.transpose(wd, (0, 2, 1))
     return (
-        *outs["out"],
-        *outs["back"],
+        out_patches,
+        owns[1],
+        grad_patches,
+        owns[3],
         g1,
         s1,
         wm,

time: 497 us -> 451 us (0.907)
  waiting for transfers between devices: 182 us -> 148 us
  starting transfers between devices: 127 us -> 117 us
  local copies, waits for them, and re-layouts: 45.5 us -> 51.1 us
    ppermute x58 -> x50, waiting for transfers between devices: 66.5 us -> 42.4 us  [swap_seq(): lax.ppermute(values, 'seq', [(i, i ^ mask) for i in range(self.n_seq)])]
    ppermute x27, waiting for transfers between devices: 74.2 us -> 62.6 us  [ring_z(): lax.ppermute(values, 'dp', [(i, (i + 2 * by) % self.n_dp) for i in range(...]
    ppermute x27, starting transfers between devices: 13 us -> 23.6 us  [ring_z(): lax.ppermute(values, 'dp', [(i, (i + 2 * by) % self.n_dp) for i in range(...]
    ppermute x8 -> x6, starting transfers between devices: 15.1 us -> 8.64 us  [shift_seq(): lax.ppermute(values, 'seq', [(i, i + by) for i in range(count) if 0 <= i...]
    ppermute x39 -> x38, waiting for transfers between devices: 36.1 us -> 42.4 us  [swap_x(): return lax.ppermute(values, 'dp', [(i, i ^ 1) for i in range(self.n_dp)])]
    all_to_all x1 -> x0, starting transfers between devices: 5.92 us -> none  [gather_vectors_packed(): lax.all_to_all(spread, 'dp', split_axis=0, concat_axis=0, tiled=True)]
    ppermute x39 -> x38, starting transfers between devices: 47.4 us -> 41.6 us  [swap_x(): return lax.ppermute(values, 'dp', [(i, i ^ 1) for i in range(self.n_dp)])]
    all_to_all x1 -> x0, waiting for transfers between devices: 5.53 us -> none  [gather_vectors_packed(): lax.all_to_all(spread, 'dp', split_axis=0, concat_axis=0, tiled=True)]
  transfers between devices with their start and end apart: 133 -> 121, of which waited for: 58 -> 50; matrix products, arithmetic and copies ran while one was open for 6% -> 9% of each run, Pallas kernels for 18% -> 22%
where the time goes in v3:
time: 451 us; the launch traced here: 443 us
  waiting for transfers between devices  148 us (33%)
  starting transfers between devices  117 us (26%)
  Pallas kernels  116 us (26%)
  local copies, waits for them, and re-layouts  51.1 us (11%)
  between operations  6.08 us (1%)
  other arithmetic  5.61 us (1%)
    ppermute x27, waiting for transfers between devices, ring_z(): lax.ppermute(values, 'dp', [(i, (i + 2 * by) % self.n_dp) for i in range(...  62.6 us
    ppermute x50, starting transfers between devices, swap_seq(): lax.ppermute(values, 'seq', [(i, i ^ mask) for i in range(self.n_seq)])  43 us
    ppermute x38, waiting for transfers between devices, swap_x(): return lax.ppermute(values, 'dp', [(i, i ^ 1) for i in range(self.n_dp)])  42.4 us
    ppermute x50, waiting for transfers between devices, swap_seq(): lax.ppermute(values, 'seq', [(i, i ^ mask) for i in range(self.n_seq)])  42.4 us
    ppermute x38, starting transfers between devices, swap_x(): return lax.ppermute(values, 'dp', [(i, i ^ 1) for i in range(self.n_dp)])  41.6 us
    unnamed x134, local copies, waits for them, and re-layouts  26.2 us
    ppermute x27, starting transfers between devices, ring_z(): lax.ppermute(values, 'dp', [(i, (i + 2 * by) % self.n_dp) for i in range(...  23.6 us
    pallas_call x2, Pallas kernels, backward_attention(): pl.pallas_call(backward_attention_kernel, in_specs=whole_vmem(6 + 5 + 2),...  22.6 us
  transfers between devices with their start and end apart: 121, of which 50 were waited for; matrix products, arithmetic and copies ran while one was open for 9% of the time, Pallas kernels for 22%

profile of v3, /device:TPU:0, one launch (start us, length us, event | category | flops | bytes accessed | tf_op | source)
XLA Modules:
  0.0 443.5 jit_solution(16090716008081373593)
XLA Ops:
  45.9 7.6 %collective-permute-done.15 = bf16[192,384]{1,0:T(8,128)(2,1)S(1)} collective-permute-done((bf16[192,384]{1,0:T(8,128)(2,1)S(1)}, bf16[192,384]{1,0:T(8,128)(2,1)S(1)}, u32[]{:S(2)}, u32[]{:S(2)}) %collective-permute-start.15) | collective-permute-done | bytes 147488 | tf_op jit(solution)/shard_map/ppermute | solution.py:53
  63.3 6.6 %collective-permute-done.19 = bf16[192,384]{1,0:T(8,128)(2,1)S(1)} collective-permute-done((bf16[192,384]{1,0:T(8,128)(2,1)S(1)}, bf16[192,384]{1,0:T(8,128)(2,1)S(1)}, u32[]{:S(2)}, u32[]{:S(2)}) %collective-permute-start.19) | collective-permute-done | bytes 147488 | tf_op jit(solution)/shard_map/ppermute | solution.py:53
  80.9 6.0 %concatenate.97 = bf16[1152]{0:T(1024)(128)(2,1)S(1)} concatenate(bf16[96]{0:T(256)(128)(2,1)} %get-tuple-element.880, bf16[96]{0:T(256)(128)(2,1)} %get-tuple-element.869, bf16[96]{0:T(256)(128)(2,1)} %get-tuple-element.878, bf16[96]{0:T(256)(128)(2,1)} %get-tuple-element.865, bf16[96]{0:T(256)(128)(2,1)} %get-tuple-element.876, bf16[96]{0:T(256)(128)(2,1)} %get-tuple-element.861, ...), dimensions={0} | concatenate | bytes 4608 | tf_op jit(solution)/shard_map/concatenate | solution.py:948
  144.1 10.0 %forward_attention.2 = (f32[288,768]{1,0:T(8,128)S(1)}, bf16[288,768]{1,0:T(8,128)(2,1)S(1)}, bf16[768,288]{1,0:T(8,128)(2,1)S(1)}, bf16[768,288]{1,0:T(8,128)(2...) custom-call(s32[4]{0:T(128)S(1)} %pad_add_fusion.spot.refs_0_, ...), custom_call_target="tpu_custom_call" | custom-call | tf_op jit(solution)/shard_map/forward_attention/pallas_call | solution.py:489
  160.2 9.6 %forward_up.2 = (bf16[288,3072]{1,0:T(8,128)(2,1)S(1)}, bf16[288,3072]{1,0:T(8,128)(2,1)S(1)}, bf16[2,8,4,96,384]{4,3,2,1,0:T(8,128)(2,1)S(1)}, bf16[2,8,4,96,384]{4,3,2,1,0:T(8,128)(2,1)S(1)}) custom-call(s32[4]{0:T(128)S(1)} %pad_add_fusion.spot.refs_0_, bf16[288,768]{1,0:T(8,128)(2,1)S(1)} %get-tuple-element.453.normed, ...), custom_call_target="tpu_custom_call" | custom-call | tf_op jit(solution)/shard_map/forward_up/pallas_call | solution.py:520
  179.3 8.9 %forward_attention.3 = (f32[288,768]{1,0:T(8,128)S(1)}, bf16[288,768]{1,0:T(8,128)(2,1)S(1)}, bf16[768,288]{1,0:T(8,128)(2,1)S(1)}, bf16[768,288]{1,0:T(8,128)(2...) custom-call(s32[4]{0:T(128)S(1)} %pad_add_fusion.spot.refs_0_, ...), custom_call_target="tpu_custom_call" | custom-call | tf_op jit(solution)/shard_map/forward_attention/pallas_call | solution.py:489
  199.0 4.1 collective-permute-done.54
  208.3 7.0 %forward_up.3 = (bf16[288,3072]{1,0:T(8,128)(2,1)S(1)}, bf16[288,3072]{1,0:T(8,128)(2,1)S(1)}, bf16[2,8,4,96,384]{4,3,2,1,0:T(8,128)(2,1)S(1)}, bf16[2,8,4,96,384]{4,3,2,1,0:T(8,128)(2,1)S(1)}) custom-call(s32[4]{0:T(128)S(1)} %pad_add_fusion.spot.refs_0_, bf16[288,768]{1,0:T(8,128)(2,1)S(1)} %get-tuple-element.493.normed, ...), custom_call_target="tpu_custom_call" | custom-call | tf_op jit(solution)/shard_map/forward_up/pallas_call | solution.py:520
  220.0 4.3 gradient_sent.6
  236.0 4.6 %gradient_kept.6 = (bf16[4,96,384]{2,1,0:T(8,128)(2,1)S(1)}, bf16[4,96,384]{2,1,0:T(8,128)(2,1)S(1)}, bf16[8,96,384]{2,1,0:T(8,128)(2,1)S(1)}, bf16[4,96,384]{2,...) custom-call(s32[4]{0:T(128)S(1)} %pad_add_fusion.spot.refs_0_, ...), custom_call_target="tpu_custom_call" | custom-call | tf_op jit(solution)/shard_map/gradient_kept/pallas_call | solution.py:817
  242.9 11.4 %backward_attention.2 = (f32[288,768]{1,0:T(8,128)S(1)}, bf16[288,2304]{1,0:T(8,128)(2,1)S(1)}, f32[16,768]{1,0:T(8,128)S(1)}) custom-call(f32[288,768]{1,0:T(8,128)S(1)} %get-tuple-element.528.grad_middle, bf16[288,768]{1,0:T(8,128)(2,1)S(1)} %get-tuple-element.554.grad_proj, bf16[288,2304]{1,0:T(8,128)(2,1)S(1)} %get-tuple-element.530.mixed, ...), custom_call_target="tpu_custom_call" | custom-call | tf_op jit(solution)/shard_map/backward_attention/pallas_call | solution.py:709
  261.7 4.9 %backward_feed_middle.1 = (bf16[768,288]{1,0:T(8,128)(2,1)S(1)}, bf16[288,3072]{1,0:T(8,128)(2,1)S(1)}, f32[1,768]{1,0:T(1,128)S(1)}, f32[1,3072]{1,0:T(1,128)S(...) custom-call(f32[1]{0:T(128)} %bitcast.77.keep.keep_down, ...), custom_call_target="tpu_custom_call" | custom-call | tf_op jit(solution)/shard_map/backward_feed_middle/pallas_call | solution.py:634
  270.2 7.3 %collective-permute-done.67.refs_0_ = bf16[8,96,384]{2,1,0:T(8,128)(2,1)S(1)} collective-permute-done((bf16[8,96,384]{2,1,0:T(8,128)(2,1)S(1)}, bf16[8,96,384]{2,1,0:T(8,128)(2,1)S(1)}, u32[]{:S(2)}, u32[]{:S(2)}) %collective-permute-start.67) | collective-permute-done | bytes 589856 | tf_op jit(solution)/shard_map/ppermute | solution.py:59
  285.6 11.2 %backward_attention.3 = (f32[288,768]{1,0:T(8,128)S(1)}, bf16[288,2304]{1,0:T(8,128)(2,1)S(1)}, f32[16,768]{1,0:T(8,128)S(1)}) custom-call(f32[288,768]{1,0:T(8,128)S(1)} %get-tuple-element.581.grad_middle, bf16[288,768]{1,0:T(8,128)(2,1)S(1)} %get-tuple-element.616.grad_proj, bf16[288,2304]{1,0:T(8,128)(2,1)S(1)} %get-tuple-element.583.mixed, ...), custom_call_target="tpu_custom_call" | custom-call | tf_op jit(solution)/shard_map/backward_attention/pallas_call | solution.py:709
  304.2 4.1 gradient_sent.8
  315.1 5.7 %collective-permute-done.84 = f32[32,768]{1,0:T(8,128)S(1)} collective-permute-done((f32[32,768]{1,0:T(8,128)S(1)}, f32[32,768]{1,0:T(8,128)S(1)}, u32[]{:S(2)}, u32[]{:S(2)}) %collective-permute-start.84) | collective-permute-done | bytes 98336 | tf_op jit(solution)/shard_map/ppermute | solution.py:53
  323.3 4.9 %gradient_kept.8 = (bf16[4,96,384]{2,1,0:T(8,128)(2,1)S(1)}, bf16[4,96,384]{2,1,0:T(8,128)(2,1)S(1)}, bf16[8,96,384]{2,1,0:T(8,128)(2,1)S(1)}, bf16[4,96,384]{2,...) custom-call(s32[4]{0:T(128)S(1)} %pad_add_fusion.spot.refs_0_, ...), custom_call_target="tpu_custom_call" | custom-call | tf_op jit(solution)/shard_map/gradient_kept/pallas_call | solution.py:817
  332.3 6.8 %collective-permute-done.86.across = bf16[2,96,384]{2,1,0:T(8,128)(2,1)S(1)} collective-permute-done((bf16[2,96,384]{2,1,0:T(8,128)(2,1)S(1)}, bf16[2,96,384]{2,1,0:T(8,128)(2,1)S(1)}, u32[]{:S(2)}, u32[]{:S(2)}) %collective-permute-start.86) | collective-permute-done | bytes 147488 | tf_op jit(solution)/shard_map/ppermute | solution.py:56
  344.2 8.4 %collective-permute-done.94 = f32[32,768]{1,0:T(8,128)S(1)} collective-permute-done((f32[32,768]{1,0:T(8,128)S(1)}, f32[32,768]{1,0:T(8,128)S(1)}, u32[]{:S(2)}, u32[]{:S(2)}) %collective-permute-start.94) | collective-permute-done | bytes 98336 | tf_op jit(solution)/shard_map/ppermute | solution.py:56
  352.6 4.6 %collective-permute-done.90.refs_0_ = bf16[8,96,384]{2,1,0:T(8,128)(2,1)S(1)} collective-permute-done((bf16[8,96,384]{2,1,0:T(8,128)(2,1)S(1)}, bf16[8,96,384]{2,1,0:T(8,128)(2,1)S(1)}, u32[]{:S(2)}, u32[]{:S(2)}) %collective-permute-start.90) | collective-permute-done | bytes 589856 | tf_op jit(solution)/shard_map/ppermute | solution.py:59
  360.2 16.2 %collective-permute-done.98.refs_14_ = f32[32,768]{1,0:T(8,128)S(1)} collective-permute-done((f32[32,768]{1,0:T(8,128)S(1)}, f32[32,768]{1,0:T(8,128)S(1)}, u32[]{:S(2)}, u32[]{:S(2)}) %collective-permute-start.98) | collective-permute-done | bytes 98336 | tf_op jit(solution)/shard_map/ppermute | solution.py:59
  399.1 6.6 %collective-permute-done.107.refs_15_ = f32[32,768]{1,0:T(8,128)S(1)} collective-permute-done((f32[32,768]{1,0:T(8,128)S(1)}, f32[32,768]{1,0:T(8,128)S(1)}, u32[]{:S(2)}, u32[]{:S(2)}) %collective-permute-start.107) | collective-permute-done | bytes 98336 | tf_op jit(solution)/shard_map/ppermute | solution.py:59
  425.1 4.2 collective-permute-start.116
  430.1 5.9 %collective-permute-done.116.aside = bf16[2,96,384]{2,1,0:T(8,128)(2,1)S(1)} collective-permute-done((bf16[2,96,384]{2,1,0:T(8,128)(2,1)S(1)}, bf16[2,96,384]{2,1,0:T(8,128)(2,1)S(1)}, u32[]{:S(2)}, u32[]{:S(2)}) %collective-permute-start.116) | collective-permute-done | bytes 147488 | tf_op jit(solution)/shard_map/ppermute | solution.py:53
  (516 shorter events, 266.5 us)
Async XLA Ops:
  40.6 17.4 %collective-permute-start.12 = (bf16[768,384]{1,0:T(8,128)(2,1)S(1)}, bf16[768,384]{1,0:T(8,128)(2,1)S(1)}, u32[]{:S(2)}, u32[]{:S(2)}) collective-permute-start(bf16[768,384]{1,0:T(8,128)(2,1)S(1)} %pad_maximum_fusion.6), channel_id=1, source_target_pairs={{0,8},{4,12},{8,16},{12,20},{16,24},{20,28},{24,0},{28,4},{1,9},{5... | collective-permute-start | bytes 1769480 | tf_op jit(solution)/shard_map/ppermute | solution.py:59
  53.5 21.2 %collective-permute-start.21 = (bf16[1600,384]{1,0:T(8,128)(2,1)}, bf16[1600,384]{1,0:T(8,128)(2,1)S(1)}, u32[]{:S(2)}, u32[]{:S(2)}) collective-permute-start(bf16[1600,384]{1,0:T(8,128)(2,1)} %copy-done.10), channel_id=1, source_target_pairs={{0,1},{1,0},{2,3},{3,2},{4,5},{5,4},{6,7},{7,6},{8,9},{9,8},{10,11... | collective-permute-start | bytes 3686408 | tf_op jit(solution)/shard_map/ppermute | solution.py:53
  75.8 19.8 %collective-permute-start.26 = (bf16[3072,384]{1,0:T(8,128)(2,1)S(1)}, bf16[3072,384]{1,0:T(8,128)(2,1)}, u32[]{:S(2)}, u32[]{:S(2)}) collective-permute-start(bf16[3072,384]{1,0:T(8,128)(2,1)S(1)} %constant_dynamic-update-slice_fusion.34.refs_0_), channel_id=1, source_target_pairs={{0,1},{1,0},{2,3},{3,2},{4,5},{5,4},{6,7},{7,6},{8,9},{9,8},{10,11... | collective-permute-start | bytes 7077896 | tf_op jit(solution)/shard_map/ppermute | solution.py:53
  75.8 19.8 %collective-permute-start.25 = (bf16[1600,384]{1,0:T(8,128)(2,1)}, bf16[1600,384]{1,0:T(8,128)(2,1)}, u32[]{:S(2)}, u32[]{:S(2)}) collective-permute-start(bf16[1600,384]{1,0:T(8,128)(2,1)} %constant_dynamic-update-slice_fusion.28.refs_1_), channel_id=1, source_target_pairs={{0,1},{1,0},{2,3},{3,2},{4,5},{5,4},{6,7},{7,6},{8,9},{9,8},{10,11... | collective-permute-start | bytes 3686408 | tf_op jit(solution)/shard_map/ppermute | solution.py:53
  78.2 17.4 %collective-permute-start.22 = (bf16[768,384]{1,0:T(8,128)(2,1)}, bf16[768,384]{1,0:T(8,128)(2,1)}, u32[]{:S(2)}, u32[]{:S(2)}) collective-permute-start(bf16[768,384]{1,0:T(8,128)(2,1)} %collective-permute-done.17), channel_id=1, source_target_pairs={{0,8},{4,12},{8,16},{12,20},{16,24},{20,28},{24,0},{28,4},{1,9},{5... | collective-permute-start | bytes 1769480 | tf_op jit(solution)/shard_map/ppermute | solution.py:59
  109.6 17.5 %collective-permute-start.35 = (bf16[3072,384]{1,0:T(8,128)(2,1)}, bf16[3072,384]{1,0:T(8,128)(2,1)}, u32[]{:S(2)}, u32[]{:S(2)}) collective-permute-start(bf16[3072,384]{1,0:T(8,128)(2,1)} %constant_dynamic-update-slice_fusion.40.refs_1_), channel_id=1, source_target_pairs={{0,1},{1,0},{2,3},{3,2},{4,5},{5,4},{6,7},{7,6},{8,9},{9,8},{10,11... | collective-permute-start | bytes 7077896 | tf_op jit(solution)/shard_map/ppermute | solution.py:53
  135.1 20.6 %collective-permute-start.43 = (bf16[384,384]{1,0:T(8,128)(2,1)S(1)}, bf16[384,384]{1,0:T(8,128)(2,1)S(1)}, u32[]{:S(2)}, u32[]{:S(2)}) collective-permute-start(bf16[384,384]{1,0:T(8,128)(2,1)S(1)} %bitcast.173), channel_id=1, source_target_pairs={{0,4},{4,0},{8,12},{12,8},{16,20},{20,16},{24,28},{28,24},{1,5},{5... | collective-permute-start | bytes 884744 | tf_op jit(solution)/shard_map/ppermute | solution.py:56
  139.9 17.0 %collective-permute-start.41 = (bf16[768,384]{1,0:T(8,128)(2,1)S(1)}, bf16[768,384]{1,0:T(8,128)(2,1)S(1)}, u32[]{:S(2)}, u32[]{:S(2)}) collective-permute-start(bf16[768,384]{1,0:T(8,128)(2,1)S(1)} %pad_maximum_fusion.7), channel_id=1, source_target_pairs={{0,8},{4,12},{8,16},{12,20},{16,24},{20,28},{24,0},{28,4},{1,9},{5... | collective-permute-start | bytes 1769480 | tf_op jit(solution)/shard_map/ppermute | solution.py:59
  156.9 18.6 %collective-permute-start.49 = (bf16[1600,384]{1,0:T(8,128)(2,1)S(1)}, bf16[1600,384]{1,0:T(8,128)(2,1)S(1)}, u32[]{:S(2)}, u32[]{:S(2)}) collective-permute-start(bf16[1600,384]{1,0:T(8,128)(2,1)S(1)} %constant_dynamic-update-slice_fusion.52.refs_1_), channel_id=1, source_target_pairs={{0,1},{1,0},{2,3},{3,2},{4,5},{5,4},{6,7},{7,6},{8,9},{9,8},{10,11... | collective-permute-start | bytes 3686408 | tf_op jit(solution)/shard_map/ppermute | solution.py:53
  157.7 17.8 %collective-permute-start.46 = (bf16[768,384]{1,0:T(8,128)(2,1)S(1)}, bf16[768,384]{1,0:T(8,128)(2,1)S(1)}, u32[]{:S(2)}, u32[]{:S(2)}) collective-permute-start(bf16[768,384]{1,0:T(8,128)(2,1)S(1)} %collective-permute-done.41), channel_id=1, source_target_pairs={{0,8},{4,12},{8,16},{12,20},{16,24},{20,28},{24,0},{28,4},{1,9},{5... | collective-permute-start | bytes 1769480 | tf_op jit(solution)/shard_map/ppermute | solution.py:59
  175.5 18.0 %collective-permute-start.53 = (bf16[3072,384]{1,0:T(8,128)(2,1)S(1)}, bf16[3072,384]{1,0:T(8,128)(2,1)S(1)}, u32[]{:S(2)}, u32[]{:S(2)}) collective-permute-start(bf16[3072,384]{1,0:T(8,128)(2,1)S(1)} %constant_dynamic-update-slice_fusion.58.refs_0_), channel_id=1, source_target_pairs={{0,1},{1,0},{2,3},{3,2},{4,5},{5,4},{6,7},{7,6},{8,9},{9,8},{10,11... | collective-permute-start | bytes 7077896 | tf_op jit(solution)/shard_map/ppermute | solution.py:53
  175.5 18.0 %collective-permute-start.50 = (bf16[768,384]{1,0:T(8,128)(2,1)S(1)}, bf16[768,384]{1,0:T(8,128)(2,1)S(1)}, u32[]{:S(2)}, u32[]{:S(2)}) collective-permute-start(bf16[768,384]{1,0:T(8,128)(2,1)S(1)} %collective-permute-done.46), channel_id=1, source_target_pairs={{0,8},{4,12},{8,16},{12,20},{16,24},{20,28},{24,0},{28,4},{1,9},{5... | collective-permute-start | bytes 1769480 | tf_op jit(solution)/shard_map/ppermute | solution.py:59
  235.9 18.4 %collective-permute-start.64 = (bf16[8,96,384]{2,1,0:T(8,128)(2,1)S(1)}, bf16[8,96,384]{2,1,0:T(8,128)(2,1)S(1)}, u32[]{:S(2)}, u32[]{:S(2)}) collective-permute-start(bf16[8,96,384]{2,1,0:T(8,128)(2,1)S(1)} %ring_block.16), channel_id=1, source_target_pairs={{0,8},{4,12},{8,16},{12,20},{16,24},{20,28},{24,0},{28,4},{1,9},{5... | collective-permute-start | bytes 1769480 | tf_op jit(solution)/shard_map/ppermute | solution.py:59
  259.5 18.1 %collective-permute-start.70 = (bf16[4,8,96,384]{3,2,1,0:T(8,128)(2,1)S(1)}, bf16[4,8,96,384]{3,2,1,0:T(8,128)(2,1)S(1)}, u32[]{:S(2)}, u32[]{:S(2)}) collective-permute-start(bf16[4,8,96,384]{3,2,1,0:T(8,128)(2,1)S(1)} %gradient_sent.7), channel_id=1, source_target_pairs={{0,1},{1,0},{2,3},{3,2},{4,5},{5,4},{6,7},{7,6},{8,9},{9,8},{10,11... | collective-permute-start | bytes 7077896 | tf_op jit(solution)/shard_map/ppermute | solution.py:53
  259.8 17.8 %collective-permute-start.67 = (bf16[8,96,384]{2,1,0:T(8,128)(2,1)S(1)}, bf16[8,96,384]{2,1,0:T(8,128)(2,1)S(1)}, u32[]{:S(2)}, u32[]{:S(2)}) collective-permute-start(bf16[8,96,384]{2,1,0:T(8,128)(2,1)S(1)} %ring_block.17), channel_id=1, source_target_pairs={{0,8},{4,12},{8,16},{12,20},{16,24},{20,28},{24,0},{28,4},{1,9},{5... | collective-permute-start | bytes 1769480 | tf_op jit(solution)/shard_map/ppermute | solution.py:59
  277.8 19.1 %collective-permute-start.71 = (bf16[8,96,384]{2,1,0:T(8,128)(2,1)S(1)}, bf16[8,96,384]{2,1,0:T(8,128)(2,1)S(1)}, u32[]{:S(2)}, u32[]{:S(2)}) collective-permute-start(bf16[8,96,384]{2,1,0:T(8,128)(2,1)S(1)} %ring_block.18), channel_id=1, source_target_pairs={{0,8},{4,12},{8,16},{12,20},{16,24},{20,28},{24,0},{28,4},{1,9},{5... | collective-permute-start | bytes 1769480 | tf_op jit(solution)/shard_map/ppermute | solution.py:59
  278.1 18.8 %collective-permute-start.72 = (bf16[4,96,384]{2,1,0:T(8,128)(2,1)S(1)}, bf16[4,96,384]{2,1,0:T(8,128)(2,1)S(1)}, u32[]{:S(2)}, u32[]{:S(2)}) collective-permute-start(bf16[4,96,384]{2,1,0:T(8,128)(2,1)S(1)} %get-tuple-element.574), channel_id=1, source_target_pairs={{0,4},{4,0},{8,12},{12,8},{16,20},{20,16},{24,28},{28,24},{1,5},{5... | collective-permute-start | bytes 884744 | tf_op jit(solution)/shard_map/ppermute | solution.py:56
  279.4 17.5 %collective-permute-start.73 = (bf16[4,96,384]{2,1,0:T(8,128)(2,1)S(1)}, bf16[4,96,384]{2,1,0:T(8,128)(2,1)S(1)}, u32[]{:S(2)}, u32[]{:S(2)}) collective-permute-start(bf16[4,96,384]{2,1,0:T(8,128)(2,1)S(1)} %get-tuple-element.575), channel_id=1, source_target_pairs={{0,2},{1,3},{2,0},{3,1},{4,6},{5,7},{6,4},{7,5},{8,10},{9,11},{10,... | collective-permute-start | bytes 884744 | tf_op jit(solution)/shard_map/ppermute | solution.py:53
  321.4 18.0 %collective-permute-start.85 = (bf16[4,96,384]{2,1,0:T(8,128)(2,1)S(1)}, bf16[4,96,384]{2,1,0:T(8,128)(2,1)S(1)}, u32[]{:S(2)}, u32[]{:S(2)}) collective-permute-start(bf16[4,96,384]{2,1,0:T(8,128)(2,1)S(1)} %ring_block.22), channel_id=1, source_target_pairs={{0,8},{4,12},{8,16},{12,20},{16,24},{20,28},{24,0},{28,4},{1,9},{5... | collective-permute-start | bytes 884744 | tf_op jit(solution)/shard_map/ppermute | solution.py:59
  339.4 17.8 %collective-permute-start.91 = (bf16[4,8,96,384]{3,2,1,0:T(8,128)(2,1)S(1)}, bf16[4,8,96,384]{3,2,1,0:T(8,128)(2,1)S(1)}, u32[]{:S(2)}, u32[]{:S(2)}) collective-permute-start(bf16[4,8,96,384]{3,2,1,0:T(8,128)(2,1)S(1)} %gradient_sent.9), channel_id=1, source_target_pairs={{0,1},{1,0},{2,3},{3,2},{4,5},{5,4},{6,7},{7,6},{8,9},{9,8},{10,11... | collective-permute-start | bytes 7077896 | tf_op jit(solution)/shard_map/ppermute | solution.py:53
  339.6 17.6 %collective-permute-start.90 = (bf16[8,96,384]{2,1,0:T(8,128)(2,1)S(1)}, bf16[8,96,384]{2,1,0:T(8,128)(2,1)S(1)}, u32[]{:S(2)}, u32[]{:S(2)}) collective-permute-start(bf16[8,96,384]{2,1,0:T(8,128)(2,1)S(1)} %ring_block.23), channel_id=1, source_target_pairs={{0,8},{4,12},{8,16},{12,20},{16,24},{20,28},{24,0},{28,4},{1,9},{5... | collective-permute-start | bytes 1769480 | tf_op jit(solution)/shard_map/ppermute | solution.py:59
  357.4 18.9 %collective-permute-start.95 = (bf16[8,96,384]{2,1,0:T(8,128)(2,1)S(1)}, bf16[8,96,384]{2,1,0:T(8,128)(2,1)S(1)}, u32[]{:S(2)}, u32[]{:S(2)}) collective-permute-start(bf16[8,96,384]{2,1,0:T(8,128)(2,1)S(1)} %ring_block.25), channel_id=1, source_target_pairs={{0,8},{4,12},{8,16},{12,20},{16,24},{20,28},{24,0},{28,4},{1,9},{5... | collective-permute-start | bytes 1769480 | tf_op jit(solution)/shard_map/ppermute | solution.py:59
  357.5 18.8 %collective-permute-start.96 = (bf16[4,96,384]{2,1,0:T(8,128)(2,1)S(1)}, bf16[4,96,384]{2,1,0:T(8,128)(2,1)S(1)}, u32[]{:S(2)}, u32[]{:S(2)}) collective-permute-start(bf16[4,96,384]{2,1,0:T(8,128)(2,1)S(1)} %get-tuple-element.662), channel_id=1, source_target_pairs={{0,4},{4,0},{8,12},{12,8},{16,20},{20,16},{24,28},{28,24},{1,5},{5... | collective-permute-start | bytes 884744 | tf_op jit(solution)/shard_map/ppermute | solution.py:56
  359.0 17.3 %collective-permute-start.97 = (bf16[4,96,384]{2,1,0:T(8,128)(2,1)S(1)}, bf16[4,96,384]{2,1,0:T(8,128)(2,1)S(1)}, u32[]{:S(2)}, u32[]{:S(2)}) collective-permute-start(bf16[4,96,384]{2,1,0:T(8,128)(2,1)S(1)} %get-tuple-element.663), channel_id=1, source_target_pairs={{0,2},{1,3},{2,0},{3,1},{4,6},{5,7},{6,4},{7,5},{8,10},{9,11},{10,... | collective-permute-start | bytes 884744 | tf_op jit(solution)/shard_map/ppermute | solution.py:53
  (142 other events, 1236.0 us)

commit v4 on v3

--- a/solution.py
+++ b/solution.py
@@ -378,6 +378,23 @@
                         ]
 
 
+def keep_factor(spot, keep_mask, branch):
+    return keep_mask[spot[4], branch].astype(F32) * (1.0 / KEEP_RATE)
+
+
+def key_block(spot, lengths, rows, special_count):
+    ids = lax.broadcasted_iota(jnp.int32, (1, rows), 1)
+    inside = (ids < lengths[0, spot[4]]) | ((ids >= MOST) & (ids < MOST + special_count))
+    return jnp.where(inside, 0.0, MASKED).astype(F32)
+
+
+def image_frame(spot, lengths, count, halo):
+    before = jnp.int32(0)
+    for image in range(lengths.shape[1]):
+        before = before + jnp.where(image < spot[4], lengths[0, image], 0)
+    return before - spot[4] * count + halo, lengths[0, spot[4]]
+
+
 def flat(block):
     return block.reshape(-1, block.shape[-1])
 
@@ -417,16 +434,17 @@
     return powers / jnp.sum(powers, axis=1, keepdims=True)
 
 
-def forward_attention_kernel(turned, chunks, spot, keep, stream, blocked, *refs):
+def forward_attention_kernel(turned, chunks, branch, special_count, spot, lengths, keep_mask, stream, *refs):
+    keep = keep_factor(spot, keep_mask, branch)
+    blocked = key_block(spot, lengths, stream.shape[0], special_count)
     parts, refs = refs[: 2 * len(chunks)], refs[2 * len(chunks) :]
     middle, normed_two, normed_one_t, normed_two_t, mixed, attended, attended_t, crossed, split, vectors, bias_up, extra = refs
     place_pieces(spot, parts, chunks, crossed, split, extra, turned)
     rows = crossed.shape[3]
-    each = extra.shape[2] // rows
     for row in range(extra.shape[0]):
         block = extra[row].astype(F32)
         for piece in range(VECTOR_PIECES):
-            values = block[piece // each : piece // each + 1, (piece % each) * rows : (piece % each + 1) * rows]
+            values = block[piece : piece + 1, :rows]
             if piece < vectors.shape[0]:
                 vectors[piece : piece + 1, row * rows : (row + 1) * rows] = values
             else:
@@ -454,22 +472,22 @@
         outs = []
         for side in range(2):
             mine = ((lane < HD) if side == 0 else (lane >= HD)).astype(F32).astype(BF)
-            probs = head_probs(queries * mine, keys, blocked[...])
+            probs = head_probs(queries * mine, keys, blocked)
             outs.append(dot_nn(probs.astype(BF), values))
         attended[:, pl.ds(pair * 2 * HD, 2 * HD)] = jnp.where(lane < HD, outs[0], outs[1]).astype(BF)
     ahead = attended[...]
     attended_t[...] = ahead.T
     for core in range(2):
         columns = pl.ds(core * half, half)
-        branch = dot_nn(ahead, flat(split[core, :, 1])) + vectors[BIAS_PROJ : BIAS_PROJ + 1, columns]
-        middle[:, columns] = stream[:, columns] + keep[0] * branch
+        added = dot_nn(ahead, flat(split[core, :, 1])) + vectors[BIAS_PROJ : BIAS_PROJ + 1, columns]
+        middle[:, columns] = stream[:, columns] + keep * added
     hat, _ = moments(middle[...])
     normed = (hat * vectors[GAIN_TWO : GAIN_TWO + 1] + vectors[SHIFT_TWO : SHIFT_TWO + 1]).astype(BF)
     normed_two[...] = normed
     normed_two_t[...] = normed.T
 
 
-def forward_attention(place, spot, keep, stream, unit, blocked, extra_rows):
+def forward_attention(place, where, branch, special_count, stream, unit, extra_rows):
     parts = unit.parts()
     rows, width = stream.shape
     group = (width // place.n_dp, width // 2)
@@ -487,15 +505,15 @@
         jax.ShapeDtypeStruct((1, 4 * width), F32),
     ]
     return pl.pallas_call(
-        partial(forward_attention_kernel, unit.turned, unit.chunks),
-        in_specs=in_smem(2) + whole_vmem(2 + len(parts)),
+        partial(forward_attention_kernel, unit.turned, unit.chunks, branch, special_count),
+        in_specs=in_smem(3) + whole_vmem(1 + len(parts)),
         out_specs=whole_vmem(len(shapes)),
         out_shape=shapes,
         scratch_shapes=[pltpu.VMEM((place.n_dp, extra_rows, width // 2), BF)],
         compiler_params=kernel_params(12),
         cost_estimate=pl.CostEstimate(flops=0, bytes_accessed=0, transcendentals=0),
         name="forward_attention",
-    )(spot, keep, stream, blocked, *parts)
+    )(*where, stream, *parts)
 
 
 def forward_up_kernel(turned, chunks, spot, normed, bias_up, *refs):
@@ -529,29 +547,31 @@
     )(spot, normed, bias_up, *parts)
 
 
-def forward_down_kernel(keep, middle, hidden, vectors, split, output):
+def forward_down_kernel(branch, spot, keep_mask, middle, hidden, vectors, split, output):
+    keep = keep_factor(spot, keep_mask, branch)
     ahead = hidden[...]
     half = middle.shape[1] // 2
     for core in range(2):
         columns = pl.ds(core * half, half)
-        branch = dot_nn(ahead, flat(split[core])) + vectors[BIAS_DOWN : BIAS_DOWN + 1, columns]
-        output[:, columns] = middle[:, columns] + keep[0] * branch
-
-
-def forward_down(keep, middle, hidden, vectors, split):
+        added = dot_nn(ahead, flat(split[core])) + vectors[BIAS_DOWN : BIAS_DOWN + 1, columns]
+        output[:, columns] = middle[:, columns] + keep * added
+
+
+def forward_down(where, branch, middle, hidden, vectors, split):
     return pl.pallas_call(
-        forward_down_kernel,
-        in_specs=in_smem(1) + whole_vmem(4),
+        partial(forward_down_kernel, branch),
+        in_specs=in_smem(2) + whole_vmem(4),
         out_specs=whole_vmem(1)[0],
         out_shape=jax.ShapeDtypeStruct(middle.shape, F32),
         compiler_params=kernel_params(8),
         cost_estimate=pl.CostEstimate(flops=0, bytes_accessed=0, transcendentals=0),
         name="forward_down",
-    )(keep, middle, hidden, vectors, split)
-
-
-def backward_feed_kernel(keep, grad, slope, split, grad_down_t, grad_up, sum_down, sum_up):
-    down = (keep[0] * grad[...]).astype(BF)
+    )(where[0], where[2], middle, hidden, vectors, split)
+
+
+def backward_feed_kernel(branch, spot, keep_mask, grad, slope, split, grad_down_t, grad_up, sum_down, sum_up):
+    keep = keep_factor(spot, keep_mask, branch)
+    down = (keep * grad[...]).astype(BF)
     grad_down_t[...] = down.T
     sum_down[...] = jnp.sum(down.astype(F32), axis=0, keepdims=True)
     half = grad.shape[1] // 2
@@ -563,7 +583,7 @@
         sum_up[:, columns] = jnp.sum(up.astype(F32), axis=0, keepdims=True)
 
 
-def backward_feed(keep, grad, slope, split):
+def backward_feed(where, branch, grad, slope, split):
     rows, width = grad.shape
     shapes = [
         jax.ShapeDtypeStruct((width, rows), BF),
@@ -572,17 +592,18 @@
         jax.ShapeDtypeStruct((1, 4 * width), F32),
     ]
     return pl.pallas_call(
-        backward_feed_kernel,
-        in_specs=in_smem(1) + whole_vmem(3),
+        partial(backward_feed_kernel, branch),
+        in_specs=in_smem(2) + whole_vmem(3),
         out_specs=whole_vmem(len(shapes)),
         out_shape=shapes,
         compiler_params=kernel_params(8),
         cost_estimate=pl.CostEstimate(flops=0, bytes_accessed=0, transcendentals=0),
         name="backward_feed",
-    )(keep, grad, slope, split)
-
-
-def backward_middle_kernel(keep, grad, grad_up, middle, vectors, crossed, *refs):
+    )(where[0], where[2], grad, slope, split)
+
+
+def backward_middle_kernel(branch, spot, keep_mask, grad, grad_up, middle, vectors, crossed, *refs):
+    keep = keep_factor(spot, keep_mask, branch)
     grad_middle, grad_proj, sum_proj, grad_gain, grad_shift = refs
     hat, scale = moments(middle[...])
     half = grad.shape[1] // 2
@@ -594,34 +615,34 @@
     grad_shift[...] = jnp.sum(total, axis=0, keepdims=True)
     after = grad[...] + norm_back(hat, scale, vectors[GAIN_TWO : GAIN_TWO + 1], total)
     grad_middle[...] = after
-    proj = (keep[0] * after).astype(BF)
+    proj = (keep * after).astype(BF)
     grad_proj[...] = proj
     sum_proj[...] = jnp.sum(proj.astype(F32), axis=0, keepdims=True)
 
 
-def backward_middle(keep, grad, grad_up, middle, vectors, crossed):
+def backward_middle(where, branch, grad, grad_up, middle, vectors, crossed):
     rows, width = grad.shape
     shapes = [
         jax.ShapeDtypeStruct((rows, width), F32),
         jax.ShapeDtypeStruct((rows, width), BF),
     ] + [jax.ShapeDtypeStruct((1, width), F32)] * 3
     return pl.pallas_call(
-        backward_middle_kernel,
-        in_specs=in_smem(1) + whole_vmem(5),
+        partial(backward_middle_kernel, branch),
+        in_specs=in_smem(2) + whole_vmem(5),
         out_specs=whole_vmem(len(shapes)),
         out_shape=shapes,
         compiler_params=kernel_params(10),
         cost_estimate=pl.CostEstimate(flops=0, bytes_accessed=0, transcendentals=0),
         name="backward_middle",
-    )(keep, grad, grad_up, middle, vectors, crossed)
-
-
-def backward_feed_middle_kernel(keep_down, keep_up, grad, slope, split, middle, vectors, crossed, *refs):
-    backward_feed_kernel(keep_down, grad, slope, split, *refs[:4])
-    backward_middle_kernel(keep_up, grad, refs[1], middle, vectors, crossed, *refs[4:])
-
-
-def backward_feed_middle(keep_down, keep_up, grad, slope, split, middle, vectors, crossed):
+    )(where[0], where[2], grad, grad_up, middle, vectors, crossed)
+
+
+def backward_feed_middle_kernel(branches, spot, keep_mask, grad, slope, split, middle, vectors, crossed, *refs):
+    backward_feed_kernel(branches[1], spot, keep_mask, grad, slope, split, *refs[:4])
+    backward_middle_kernel(branches[0], spot, keep_mask, grad, refs[1], middle, vectors, crossed, *refs[4:])
+
+
+def backward_feed_middle(where, branches, grad, slope, split, middle, vectors, crossed):
     rows, width = grad.shape
     shapes = [
         jax.ShapeDtypeStruct((width, rows), BF),
@@ -632,16 +653,17 @@
         jax.ShapeDtypeStruct((rows, width), BF),
     ] + [jax.ShapeDtypeStruct((1, width), F32)] * 3
     return pl.pallas_call(
-        backward_feed_middle_kernel,
+        partial(backward_feed_middle_kernel, branches),
         in_specs=in_smem(2) + whole_vmem(6),
         out_specs=whole_vmem(len(shapes)),
         out_shape=shapes,
         compiler_params=kernel_params(12),
         name="backward_feed_middle",
-    )(keep_down, keep_up, grad, slope, split, middle, vectors, crossed)
-
-
-def backward_attention_kernel(grad_middle, grad_proj, mixed, stream, vectors, blocked, *refs):
+    )(where[0], where[2], grad, slope, split, middle, vectors, crossed)
+
+
+def backward_attention_kernel(special_count, spot, lengths, grad_middle, grad_proj, mixed, stream, vectors, *refs):
+    blocked = key_block(spot, lengths, stream.shape[0], special_count)
     others, (crossed, split), refs = refs[:5], refs[5:7], refs[7:]
     grad_stream, grad_mixed, sums, ahead = refs
     sum_proj, gain_two, shift_two, sum_down, sum_up = others
@@ -661,7 +683,7 @@
         found = []
         for side in range(2):
             mine = ((lane < HD) if side == 0 else (lane >= HD)).astype(F32).astype(BF)
-            probs = head_probs(queries * mine, keys, blocked[...])
+            probs = head_probs(queries * mine, keys, blocked)
             grad_probs = dot_nt(grads * mine, values)
             inner = jnp.sum(probs * grad_probs, axis=1, keepdims=True)
             grad_scores = (probs * (grad_probs - inner)).astype(BF)
@@ -699,7 +721,7 @@
     grad_stream[...] = grad_middle[...] + norm_back(hat, scale, vectors[GAIN_ONE : GAIN_ONE + 1], total)
 
 
-def backward_attention(grad_middle, grad_proj, mixed, stream, vectors, blocked, others, crossed, split):
+def backward_attention(where, special_count, grad_middle, grad_proj, mixed, stream, vectors, others, crossed, split):
     rows, width = stream.shape
     shapes = [
         jax.ShapeDtypeStruct((rows, width), F32),
@@ -707,15 +729,15 @@
         jax.ShapeDtypeStruct((16, width), F32),
     ]
     return pl.pallas_call(
-        backward_attention_kernel,
-        in_specs=whole_vmem(6 + 5 + 2),
+        partial(backward_attention_kernel, special_count),
+        in_specs=in_smem(2) + whole_vmem(5 + 5 + 2),
         out_specs=whole_vmem(len(shapes)),
         out_shape=shapes,
         scratch_shapes=[pltpu.VMEM((rows, width), BF)],
         compiler_params=kernel_params(12),
         cost_estimate=pl.CostEstimate(flops=0, bytes_accessed=0, transcendentals=0),
         name="backward_attention",
-    )(grad_middle, grad_proj, mixed, stream, vectors, blocked, *others, crossed, split)
+    )(where[0], where[1], grad_middle, grad_proj, mixed, stream, vectors, *others, crossed, split)
 
 
 def row_of(spot, step, far_x, steps):
@@ -945,26 +967,28 @@
 
 
 def pack_vectors(vectors, bias_up, half, rows):
-    packed = jnp.concatenate(vectors + [bias_up]).reshape(-1, half)
-    return jnp.pad(packed, ((0, rows - packed.shape[0]), (0, 0)))
-
-
-def image_kernel(frame, before, patches, after, specials, out, window):
+    layers, part = vectors[0].shape
+    packed = jnp.concatenate([jnp.stack(vectors, axis=1), bias_up.reshape(layers, -1, part)], axis=1)
+    return jnp.pad(packed, ((0, 0), (0, rows - packed.shape[1]), (0, half - part)))
+
+
+def image_kernel(spot, lengths, before, patches, after, specials, out, window):
     halo, count = before.shape[0], patches.shape[0]
+    begin, length = image_frame(spot, lengths, count, halo)
     window[:halo] = before[...]
     window[halo : halo + count] = patches[...]
     window[halo + count : 2 * halo + count] = after[...]
     spare = window.shape[0] - 2 * halo - count
     window[2 * halo + count :] = jnp.zeros((spare, window.shape[1]), F32)
-    inside = lax.broadcasted_iota(jnp.int32, (MOST, 1), 0) < frame[1]
-    turned = pltpu.roll(window[...], lax.rem(window.shape[0] - frame[0], window.shape[0]), 0)
+    inside = lax.broadcasted_iota(jnp.int32, (MOST, 1), 0) < length
+    turned = pltpu.roll(window[...], lax.rem(window.shape[0] - begin, window.shape[0]), 0)
     out[:MOST] = jnp.where(inside, turned[:MOST], 0.0)
     last = out.shape[0] - MOST
     out[MOST:] = jnp.zeros((last, out.shape[1]), F32)
     out[MOST : MOST + specials.shape[0]] = specials[...]
 
 
-def take_image(place, frame, patches, specials, halo, rows):
+def take_image(place, where, patches, specials, halo, rows):
     count, width = patches.shape
     before = shift_seq(place, patches[count - halo :], 1)
     after = shift_seq(place, patches[:halo], -1)
@@ -972,38 +996,39 @@
     def build(before, patches, after, specials):
         return pl.pallas_call(
             image_kernel,
-            in_specs=in_smem(1) + whole_vmem(4),
+            in_specs=in_smem(2) + whole_vmem(4),
             out_specs=whole_vmem(1)[0],
             out_shape=jax.ShapeDtypeStruct((rows, width), F32),
             scratch_shapes=[pltpu.VMEM((MOST + 2 * halo, width), F32)],
             compiler_params=kernel_params(6),
         cost_estimate=pl.CostEstimate(flops=0, bytes_accessed=0, transcendentals=0),
             name="take_image",
-        )(frame, before, patches, after, specials)
+        )(where[0], where[1], before, patches, after, specials)
 
     return (before, patches, after, specials), build
 
 
-def block_kernel(frame, *refs):
+def block_kernel(spot, lengths, *refs):
     streams, (before, after), owns, window = refs[:2], refs[2:4], refs[4:8], refs[8]
     for at, stream in enumerate(streams):
         own, specials = owns[2 * at : 2 * at + 2]
         halo, count = before.shape[0] // 2, own.shape[0]
+        begin, length = image_frame(spot, lengths, count, halo)
         window[MOST:] = jnp.zeros((window.shape[0] - MOST, window.shape[1]), F32)
-        inside = lax.broadcasted_iota(jnp.int32, (MOST, 1), 0) < frame[1]
+        inside = lax.broadcasted_iota(jnp.int32, (MOST, 1), 0) < length
         window[:MOST] = jnp.where(inside, stream[:MOST], 0.0)
-        window[...] = pltpu.roll(window[...], frame[0], 0)
+        window[...] = pltpu.roll(window[...], begin, 0)
         before[at * halo : (at + 1) * halo] = window[:halo]
         own[...] = window[halo : halo + count]
         after[at * halo : (at + 1) * halo] = window[halo + count : 2 * halo + count]
         specials[...] = stream[MOST : MOST + specials.shape[0]]
 
 
-def give_images(frame, streams, halo, count, special_count):
+def give_images(where, streams, halo, count, special_count):
     width = streams[0].shape[1]
     return pl.pallas_call(
         block_kernel,
-        in_specs=in_smem(1) + whole_vmem(2),
+        in_specs=in_smem(2) + whole_vmem(2),
         out_specs=whole_vmem(6),
         out_shape=[
             jax.ShapeDtypeStruct((size, width), F32)
@@ -1013,7 +1038,7 @@
         compiler_params=kernel_params(6),
         cost_estimate=pl.CostEstimate(flops=0, bytes_accessed=0, transcendentals=0),
         name="give_images",
-    )(frame, *streams)
+    )(where[0], where[1], *streams)
 
 
 def finish_kernel(*refs):
@@ -1117,26 +1142,20 @@
     nz = place.nz
     pairs = ((0, 1), (2, 3))
     part_rows = proj_weight.shape[1]
-    before = jnp.sum(jnp.where(jnp.arange(images) < place.seq, lengths[0], 0))
-    length = lax.dynamic_index_in_dim(lengths[0], place.seq, 0, keepdims=False)
-    frame = jnp.stack([before - place.seq * count + halo, length]).astype(jnp.int32)
-    keeps = lax.dynamic_index_in_dim(keep_mask[0], place.seq, 0, keepdims=False).astype(F32)
-    keeps = [keeps[i : i + 1] / KEEP_RATE for i in range(2 * LAYERS)]
-    row_ids = jnp.arange(rows, dtype=jnp.int32)
-    key_ok = (row_ids < length) | ((row_ids >= MOST) & (row_ids < MOST + special_count))
-    blocked = jnp.where(key_ok, 0.0, MASKED).astype(F32)[None]
-    spot = jnp.stack([place.z, place.x, place.y, place.core]).astype(jnp.int32)
+    spot = jnp.stack([place.z, place.x, place.y, place.core, place.seq]).astype(jnp.int32)
+    where = (spot, lengths, keep_mask[0])
 
     shards = (norm1_gain, norm1_bias, query_bias, value_bias, proj_bias, norm2_gain, norm2_bias, fc2_bias)
 
-    def attention_unit(layer, qkv, proj):
-        extra = pack_vectors([shard[layer] for shard in shards], fc1_bias[layer], width // 2, EXTRA_ROWS)
+    extras = pack_vectors(list(shards), fc1_bias, width // 2, EXTRA_ROWS)
+
+    def attention_unit(layer, qkv, proj, extra):
         return Gathered(place, attention_groups(place, qkv, proj), [extra], layer == 0, pairs)
 
-    units = [attention_unit(0, qkv_weight[0], proj_weight[0])]
-    image, build = take_image(place, frame, patches, specials, halo, rows)
+    units = [attention_unit(0, qkv_weight[0], proj_weight[0], extras[0])]
+    image, build = take_image(place, where, patches, specials, halo, rows)
     inputs = {
-        "weights": (fc1_weight[0], fc2_weight[0], qkv_weight[1], proj_weight[1], fc1_weight[1], fc2_weight[1]),
+        "weights": (fc1_weight[0], fc2_weight[0], qkv_weight[1], proj_weight[1], extras[1], fc1_weight[1], fc2_weight[1]),
         "cots": (cot_patches, cot_specials),
     }
     vectors, bias_up = ([None] * LAYERS, [None] * LAYERS)
@@ -1175,7 +1194,7 @@
                     across = {**unit.across, **{k[2]: v for k, v in new.items() if k[:2] == ("x", which)}}
                     aside = {**unit.aside, **{k[2]: v for k, v in new.items() if k[:2] == ("y", which)}}
                     new["chunk", which, index_of] = unit.chunk(index_of, across, aside)
-        later = {1: 1, 2: 2, 8: 3}.get(slot)
+        later = {1: 1, 4: 2, 8: 3}.get(slot)
         if later:
             new["later"] = place.swap_x(units[later].mine)
         if slot == 0:
@@ -1183,28 +1202,38 @@
         if slot == 5:
             carried["stream"] = build(*image)
         if slot == 3 * unit_count:
-            new["image"], build = take_image(place, frame, *inputs["cots"], halo, rows)
+            new["image"], build = take_image(place, where, *inputs["cots"], halo, rows)
         if slot == 3 * unit_count + 1:
             grad = build(*image)
         if slot in (9, 11):
             layer = slot // 11
             new["forward"] = forward_attention(
-                place, spot, keeps[2 * layer], carried["stream"], units[2 * layer], blocked, EXTRA_ROWS
+                place, where, 2 * layer, special_count, carried["stream"], units[2 * layer], EXTRA_ROWS
             )
         if slot == 10:
             hidden, slope, crossed, split = forward_up(place, spot, carried["normed"], bias_up[0], units[1])
-            output = forward_down(keeps[1], carried["middle"], hidden, vectors[0], split)
+            output = forward_down(where, 1, carried["middle"], hidden, vectors[0], split)
             new["feed"] = (output, hidden, slope, crossed, split)
-        if step == 2 and index + 1 < unit_count and units[index + 1].blocks:
+        if slot in (3, 5):
+            names = [key for key in new if key[0] in ("x", "y")]
+            swapped, weights_1 = fence(([new[key] for key in names], weights_1))
+            new.update(zip(names, swapped))
+            if slot == 3:
+                unit = attention_unit(1, *weights_1[:3])
+            else:
+                unit = Gathered(place, feed_groups(place, *weights_1[3:]), [], False, ((0, 1), (2,), (3,)))
+            new["unit"] = (unit.first, unit.mine)
+        if step == 2 and index + 1 < len(units) and units[index + 1].blocks:
             carried["begin"] = units[index + 1].blocks[0]
         gate = inputs if slot in (0, 3 * unit_count - 1) else {}
         new, carried, gate = fence((new, carried, gate))
         inputs.update(gate)
         if slot == 0:
-            up_0, down_0, qkv_1, proj_1, up_1, down_1 = inputs.pop("weights")
+            up_0, down_0, *weights_1 = inputs.pop("weights")
             units.append(Gathered(place, feed_groups(place, up_0, down_0), [], False, pairs))
-            units.append(attention_unit(1, qkv_1, proj_1))
-            units.append(Gathered(place, feed_groups(place, up_1, down_1), [], False, ((0, 1), (2,), (3,))))
+        if "unit" in new:
+            unit.first, unit.mine = new["unit"]
+            units.append(unit)
         if "begin" in carried:
             units[index + 1].blocks[0] = carried.pop("begin")
         if "image" in new:
@@ -1242,7 +1271,7 @@
     def feed_back(layer, grad):
         found = back[layer]
         found["down_t"], found["up"], found["sum_down"], found["sum_up"] = backward_feed(
-            keeps[2 * layer + 1], grad, slopes[layer], weights[2 * layer + 1][1]
+            where, 2 * layer + 1, grad, slopes[layer], weights[2 * layer + 1][1]
         )
 
     def feed_operands(layer):
@@ -1253,14 +1282,14 @@
     def middle_back(layer, grad):
         found = back[layer]
         found["middle"], found["proj"], found["sum_proj"], found["gain"], found["shift"] = backward_middle(
-            keeps[2 * layer], grad, found["up"], middles[layer], vectors[layer], weights[2 * layer + 1][0]
+            where, 2 * layer, grad, found["up"], middles[layer], vectors[layer], weights[2 * layer + 1][0]
         )
 
     def attention_back(layer):
         found = back[layer]
         others = [found[name] for name in ("sum_proj", "gain", "shift", "sum_down", "sum_up")]
         found["grad"], found["mixed"], found["sums"] = backward_attention(
-            found["middle"], found["proj"], mixeds[layer], streams[layer], vectors[layer], blocked, others, *weights[2 * layer]
+            where, special_count, found["middle"], found["proj"], mixeds[layer], streams[layer], vectors[layer], others, *weights[2 * layer]
         )
 
     def attention_operands(layer):
@@ -1327,12 +1356,16 @@
             keep_cut(0, 1, got.pop((0, 1)))
         if slot == -1:
             keep_cut(0, 0, got.pop((0, 0)))
-        for which, base in ((1, 2), (2, 5), (3, 8)):
+        for which, base in ((2, 4), (3, 7)):
             if slot == base:
                 keep_cut(which, 0, got.pop((which, 0)))
-        for key, base in (((0, 0), -2), ((0, 1), -1), ((2, 0), 4), ((3, 0), 6)):
+                for step in all_steps:
+                    work["kept", which, step] = reduces[which].kept[step]
+        for key, base in (((0, 0), -2), ((0, 1), -1), ((1, 0), 2), ((2, 0), 3), ((3, 0), 6)):
             if slot == base:
                 new["core", key] = place.swap_seq(sending.pop(key), 1)
+        if slot == 2:
+            keep_cut(1, 0, new["core", (1, 0)])
         for which, unit in enumerate(reduces):
             at = slot - 3 * which
             if -1 <= at <= 2:
@@ -1342,27 +1375,27 @@
                     place.swap_seq(unit.kept[step][1], 2),
                 )
         if slot == 3:
-            feed_operands(0)
             attention_operands(0)
-            work["sending"] = (sent_cut(2, 0), sent_cut(3, 0))
+            work["sending"] = sent_cut(3, 0)
         if slot == -1:
             middle_back(1, grad)
-            streams[LAYERS] = forward_down(keeps[3], carried["middle"], hiddens[1], vectors[1], weights[3][1])
+            streams[LAYERS] = forward_down(where, 3, carried["middle"], hiddens[1], vectors[1], weights[3][1])
             work["output"] = streams[LAYERS]
         if slot == 0:
             attention_back(1)
         if slot == 1:
             attention_operands(1)
-            new["core", (1, 0)] = place.swap_seq(sent_cut(1, 0), 1)
             names = ("down_t", "up", "sum_down", "sum_up", "middle", "proj", "sum_proj", "gain", "shift")
             back[0] = dict(
                 zip(
                     names,
                     backward_feed_middle(
-                        keeps[1], keeps[0], back[1]["grad"], slopes[0], weights[1][1], middles[0], vectors[0], weights[1][0]
+                        where, (0, 1), back[1]["grad"], slopes[0], weights[1][1], middles[0], vectors[0], weights[1][0]
                     ),
                 )
             )
+            feed_operands(0)
+            work["sending"] = (sent_cut(1, 0), sent_cut(2, 0))
         if slot == 2:
             attention_back(0)
         if slot in (-1, 0):
@@ -1378,9 +1411,9 @@
             new["sum"] = place.swap_x(total)
         if slot in (7, 9):
             new["ringing"] = [place.ring_z(total, by) for by in ((1,) if slot == 7 else (2, 3))]
-        if slot == final_slot - 2:
-            work["images"] = give_images(frame, given, halo, count, special_count)
         if slot == final_slot - 1:
+            work["images"] = give_images(where, given, halo, count, special_count)
+        if slot == final_slot:
             images_before, images_after, *owns = images
             new["images"] = (shift_seq(place, images_after, 1), shift_seq(place, images_before, -1))
         pending = {}
@@ -1390,20 +1423,20 @@
                 step = (at + 2) % nz
                 if step in unit.kept:
                     pending["kept", which] = unit.kept[step]
-        if slot == final_slot - 3:
+        if slot == final_slot - 2:
             pending["give"] = [streams[LAYERS], back[0]["grad"]]
-        for key, base in (((3, 0), 5),):
+        for key, base in (((2, 0), 2), ((3, 0), 5)):
             if slot == base:
                 pending["sending", key] = sending[key]
-        for key, base in (((0, 1), 0), ((1, 0), 2), ((2, 0), 5), ((3, 0), 8)):
+        for key, base in (((0, 1), 0), ((2, 0), 4), ((3, 0), 7)):
             if slot == base - 1 and key in got:
                 pending["got", key] = got[key]
         new, work, pending = fence((new, work, pending))
         if "sending" in work:
-            if slot == 3:
-                sending[2, 0], sending[3, 0] = work.pop("sending")
+            if slot == 1:
+                sending[1, 0], sending[2, 0] = work.pop("sending")
             else:
-                sending[0, 1] = work.pop("sending")
+                sending[(0, 1) if slot == -2 else (3, 0)] = work.pop("sending")
         for key in [key for key in pending if key[0] == "sending"]:
             sending[key[1]] = pending.pop(key)
         if "output" in work:
@@ -1415,6 +1448,8 @@
                 reduces[key[1]].last = value
             if key == "images":
                 images = value
+            if key[0] == "kept":
+                reduces[key[1]].kept[key[2]] = value
         if "give" in pending:
             given = pending.pop("give")
         for key in [key for key in pending if key[0] == "got"]:

time: 451 us -> 427 us (0.947)
  local copies, waits for them, and re-layouts: 51.1 us -> 19.7 us
  waiting for transfers between devices: 148 us -> 160 us
    unnamed x134 -> x133, local copies, waits for them, and re-layouts: 26.2 us -> 10.4 us
    ppermute x38, waiting for transfers between devices: 42.4 us -> 57.7 us  [swap_x(): return lax.ppermute(values, 'dp', [(i, i ^ 1) for i in range(self.n_dp)])]
    concatenate x2 -> x1, local copies, waits for them, and re-layouts: 6.06 us -> 0.06 us  [pack_vectors(): jnp.concatenate([jnp.stack(vectors, axis=1), bias_up.reshape(layers, -1,...]
  transfers between devices with their start and end apart: 121 -> 121, of which waited for: 50 -> 51; matrix products, arithmetic and copies ran while one was open for 9% -> 3% of each run, Pallas kernels for 22% -> 24%
where the time goes in v4:
time: 427 us; the launch traced here: 420 us
  waiting for transfers between devices  160 us (37%)
  Pallas kernels  118 us (28%)
  starting transfers between devices  116 us (27%)
  local copies, waits for them, and re-layouts  19.7 us (5%)
    ppermute x27, waiting for transfers between devices, ring_z(): lax.ppermute(values, 'dp', [(i, (i + 2 * by) % self.n_dp) for i in range(...  60.7 us
    ppermute x38, waiting for transfers between devices, swap_x(): return lax.ppermute(values, 'dp', [(i, i ^ 1) for i in range(self.n_dp)])  57.7 us
    ppermute x50, starting transfers between devices, swap_seq(): lax.ppermute(values, 'seq', [(i, i ^ mask) for i in range(self.n_seq)])  46 us
    ppermute x38, starting transfers between devices, swap_x(): return lax.ppermute(values, 'dp', [(i, i ^ 1) for i in range(self.n_dp)])  39.5 us
    ppermute x50, waiting for transfers between devices, swap_seq(): lax.ppermute(values, 'seq', [(i, i ^ mask) for i in range(self.n_seq)])  39.2 us
    pallas_call x2, Pallas kernels, backward_attention(): pl.pallas_call(partial(backward_attention_kernel, special_count), in_spec...  23.7 us
    ppermute x27, starting transfers between devices, ring_z(): lax.ppermute(values, 'dp', [(i, (i + 2 * by) % self.n_dp) for i in range(...  21.9 us
    pallas_call x2, Pallas kernels, forward_attention(): pl.pallas_call(partial(forward_attention_kernel, unit.turned, unit.chunks...  18.4 us
  transfers between devices with their start and end apart: 121, of which 51 were waited for; matrix products, arithmetic and copies ran while one was open for 3% of the time, Pallas kernels for 24%

profile of v4, /device:TPU:0, one launch (start us, length us, event | category | flops | bytes accessed | tf_op | source)
XLA Modules:
  0.0 419.7 jit_solution(7947102703477413360)
XLA Ops:
  31.5 4.4 %collective-permute-done.10 = bf16[192,384]{1,0:T(8,128)(2,1)S(1)} collective-permute-done((bf16[192,384]{1,0:T(8,128)(2,1)S(1)}, bf16[192,384]{1,0:T(8,128)(2,1)S(1)}, u32[]{:S(2)}, u32[]{:S(2)}) %collective-permute-start.10) | collective-permute-done | bytes 147488 | tf_op jit(solution)/shard_map/ppermute | solution.py:53
  41.5 8.3 %collective-permute-done.14 = bf16[192,384]{1,0:T(8,128)(2,1)S(1)} collective-permute-done((bf16[192,384]{1,0:T(8,128)(2,1)S(1)}, bf16[192,384]{1,0:T(8,128)(2,1)S(1)}, u32[]{:S(2)}, u32[]{:S(2)}) %collective-permute-start.14) | collective-permute-done | bytes 147488 | tf_op jit(solution)/shard_map/ppermute | solution.py:53
  57.7 8.8 %collective-permute-done.18 = bf16[192,384]{1,0:T(8,128)(2,1)S(1)} collective-permute-done((bf16[192,384]{1,0:T(8,128)(2,1)S(1)}, bf16[192,384]{1,0:T(8,128)(2,1)S(1)}, u32[]{:S(2)}, u32[]{:S(2)}) %collective-permute-start.18) | collective-permute-done | bytes 147488 | tf_op jit(solution)/shard_map/ppermute | solution.py:53
  77.4 5.4 %collective-permute-done.23 = bf16[384,384]{1,0:T(8,128)(2,1)} collective-permute-done((bf16[384,384]{1,0:T(8,128)(2,1)}, bf16[384,384]{1,0:T(8,128)(2,1)}, u32[]{:S(2)}, u32[]{:S(2)}) %collective-permute-start.23) | collective-permute-done | bytes 294944 | tf_op jit(solution)/shard_map/ppermute | solution.py:56
  84.3 8.6 %collective-permute-done.22 = bf16[768,384]{1,0:T(8,128)(2,1)S(1)} collective-permute-done((bf16[768,384]{1,0:T(8,128)(2,1)S(1)}, bf16[768,384]{1,0:T(8,128)(2,1)S(1)}, u32[]{:S(2)}, u32[]{:S(2)}) %collective-permute-start.22) | collective-permute-done | bytes 589856 | tf_op jit(solution)/shard_map/ppermute | solution.py:59
  112.1 4.4 %collective-permute-done.32 = bf16[400,384]{1,0:T(8,128)(2,1)S(1)} collective-permute-done((bf16[400,384]{1,0:T(8,128)(2,1)S(1)}, bf16[400,384]{1,0:T(8,128)(2,1)S(1)}, u32[]{:S(2)}, u32[]{:S(2)}) %collective-permute-start.32) | collective-permute-done | bytes 307232 | tf_op jit(solution)/shard_map/ppermute | solution.py:59
  120.2 6.1 %collective-permute-done.40 = bf16[192,384]{1,0:T(8,128)(2,1)S(1)} collective-permute-done((bf16[192,384]{1,0:T(8,128)(2,1)S(1)}, bf16[192,384]{1,0:T(8,128)(2,1)S(1)}, u32[]{:S(2)}, u32[]{:S(2)}) %collective-permute-start.40) | collective-permute-done | bytes 147488 | tf_op jit(solution)/shard_map/ppermute | solution.py:56
  131.7 9.2 %forward_attention.2 = (f32[288,768]{1,0:T(8,128)S(1)}, bf16[288,768]{1,0:T(8,128)(2,1)S(1)}, bf16[768,288]{1,0:T(8,128)(2,1)S(1)}, bf16[768,288]{1,0:T(8,128)(2...) custom-call(s32[5]{0:T(128)S(1)} %stack.215.spot.refs_0_, ...), custom_call_target="tpu_custom_call" | custom-call | tf_op jit(solution)/shard_map/forward_attention/pallas_call | solution.py:507
  148.5 8.1 %forward_up.2 = (bf16[288,3072]{1,0:T(8,128)(2,1)S(1)}, bf16[288,3072]{1,0:T(8,128)(2,1)S(1)}, bf16[2,8,4,96,384]{4,3,2,1,0:T(8,128)(2,1)S(1)}, bf16[2,8,4,96,384]{4,3,2,1,0:T(8,128)(2,1)S(1)}) custom-call(s32[5]{0:T(128)S(1)} %stack.215.spot.refs_0_, bf16[288,768]{1,0:T(8,128)(2,1)S(1)} %get-tuple-element.508.normed, ...), custom_call_target="tpu_custom_call" | custom-call | tf_op jit(solution)/shard_map/forward_up/pallas_call | solution.py:538
  166.4 9.2 %forward_attention.3 = (f32[288,768]{1,0:T(8,128)S(1)}, bf16[288,768]{1,0:T(8,128)(2,1)S(1)}, bf16[768,288]{1,0:T(8,128)(2,1)S(1)}, bf16[768,288]{1,0:T(8,128)(2...) custom-call(s32[5]{0:T(128)S(1)} %stack.215.spot.refs_0_, ...), custom_call_target="tpu_custom_call" | custom-call | tf_op jit(solution)/shard_map/forward_attention/pallas_call | solution.py:507
  195.2 7.0 %forward_up.3 = (bf16[288,3072]{1,0:T(8,128)(2,1)S(1)}, bf16[288,3072]{1,0:T(8,128)(2,1)S(1)}, bf16[2,8,4,96,384]{4,3,2,1,0:T(8,128)(2,1)S(1)}, bf16[2,8,4,96,384]{4,3,2,1,0:T(8,128)(2,1)S(1)}) custom-call(s32[5]{0:T(128)S(1)} %stack.215.spot.refs_0_, bf16[288,768]{1,0:T(8,128)(2,1)S(1)} %get-tuple-element.548.normed, ...), custom_call_target="tpu_custom_call" | custom-call | tf_op jit(solution)/shard_map/forward_up/pallas_call | solution.py:538
  224.2 4.6 %gradient_kept.6 = (bf16[4,96,384]{2,1,0:T(8,128)(2,1)S(1)}, bf16[4,96,384]{2,1,0:T(8,128)(2,1)S(1)}, bf16[8,96,384]{2,1,0:T(8,128)(2,1)S(1)}, bf16[4,96,384]{2,...) custom-call(s32[5]{0:T(128)S(1)} %stack.215.spot.refs_0_, ...), custom_call_target="tpu_custom_call" | custom-call | tf_op jit(solution)/shard_map/gradient_kept/pallas_call | solution.py:839
  231.8 11.9 %backward_attention.2 = (f32[288,768]{1,0:T(8,128)S(1)}, bf16[288,2304]{1,0:T(8,128)(2,1)S(1)}, f32[16,768]{1,0:T(8,128)S(1)}) custom-call(s32[5]{0:T(128)S(1)} %stack.215.spot.refs_0_, s32[1,4]{1,0:T(1,128)S(1)} %copy-done.19, f32[288,768]{1,0:T(8,128)S(1)} %get-tuple-element.583.grad_middle, bf16[288,768]{1,0:T(8,128)(2,1)S(1)} %get-tuple-element.609.grad_proj, ...), custom_call_target="tpu_custom_call" | custom-call | tf_op jit(solution)/shard_map/backward_attention/pallas_call | solution.py:731
  247.0 5.5 %backward_feed_middle.1 = (bf16[768,288]{1,0:T(8,128)(2,1)S(1)}, bf16[288,3072]{1,0:T(8,128)(2,1)S(1)}, f32[1,768]{1,0:T(1,128)S(1)}, f32[1,3072]{1,0:T(1,128)S(...) custom-call(s32[5]{0:T(128)S(1)} %stack.215.spot.refs_0_, ...), custom_call_target="tpu_custom_call" | custom-call | tf_op jit(solution)/shard_map/backward_feed_middle/pallas_call | solution.py:655
  271.1 11.7 %backward_attention.3 = (f32[288,768]{1,0:T(8,128)S(1)}, bf16[288,2304]{1,0:T(8,128)(2,1)S(1)}, f32[16,768]{1,0:T(8,128)S(1)}) custom-call(s32[5]{0:T(128)S(1)} %stack.215.spot.refs_0_, s32[1,4]{1,0:T(1,128)S(1)} %copy-done.19, f32[288,768]{1,0:T(8,128)S(1)} %get-tuple-element.637.grad_middle, bf16[288,768]{1,0:T(8,128)(2,1)S(1)} %get-tuple-element.670.grad_proj, ...), custom_call_target="tpu_custom_call" | custom-call | tf_op jit(solution)/shard_map/backward_attention/pallas_call | solution.py:731
  298.5 4.9 %gradient_kept.8 = (bf16[4,96,384]{2,1,0:T(8,128)(2,1)S(1)}, bf16[4,96,384]{2,1,0:T(8,128)(2,1)S(1)}, bf16[8,96,384]{2,1,0:T(8,128)(2,1)S(1)}, bf16[4,96,384]{2,...) custom-call(s32[5]{0:T(128)S(1)} %stack.215.spot.refs_0_, ...), custom_call_target="tpu_custom_call" | custom-call | tf_op jit(solution)/shard_map/gradient_kept/pallas_call | solution.py:839
  310.1 6.2 %collective-permute-done.86.across = bf16[2,96,384]{2,1,0:T(8,128)(2,1)S(1)} collective-permute-done((bf16[2,96,384]{2,1,0:T(8,128)(2,1)S(1)}, bf16[2,96,384]{2,1,0:T(8,128)(2,1)S(1)}, u32[]{:S(2)}, u32[]{:S(2)}) %collective-permute-start.86) | collective-permute-done | bytes 147488 | tf_op jit(solution)/shard_map/ppermute | solution.py:56
  320.3 8.7 %collective-permute-done.94 = f32[32,768]{1,0:T(8,128)S(1)} collective-permute-done((f32[32,768]{1,0:T(8,128)S(1)}, f32[32,768]{1,0:T(8,128)S(1)}, u32[]{:S(2)}, u32[]{:S(2)}) %collective-permute-start.94) | collective-permute-done | bytes 98336 | tf_op jit(solution)/shard_map/ppermute | solution.py:56
  329.0 5.7 %collective-permute-done.90.refs_0_ = bf16[8,96,384]{2,1,0:T(8,128)(2,1)S(1)} collective-permute-done((bf16[8,96,384]{2,1,0:T(8,128)(2,1)S(1)}, bf16[8,96,384]{2,1,0:T(8,128)(2,1)S(1)}, u32[]{:S(2)}, u32[]{:S(2)}) %collective-permute-start.90) | collective-permute-done | bytes 589856 | tf_op jit(solution)/shard_map/ppermute | solution.py:59
  340.6 13.3 %collective-permute-done.98.refs_14_ = f32[32,768]{1,0:T(8,128)S(1)} collective-permute-done((f32[32,768]{1,0:T(8,128)S(1)}, f32[32,768]{1,0:T(8,128)S(1)}, u32[]{:S(2)}, u32[]{:S(2)}) %collective-permute-start.98) | collective-permute-done | bytes 98336 | tf_op jit(solution)/shard_map/ppermute | solution.py:59
  358.3 6.8 %collective-permute-done.102.across = bf16[2,96,384]{2,1,0:T(8,128)(2,1)S(1)} collective-permute-done((bf16[2,96,384]{2,1,0:T(8,128)(2,1)S(1)}, bf16[2,96,384]{2,1,0:T(8,128)(2,1)S(1)}, u32[]{:S(2)}, u32[]{:S(2)}) %collective-permute-start.102) | collective-permute-done | bytes 147488 | tf_op jit(solution)/shard_map/ppermute | solution.py:56
  375.9 7.3 %collective-permute-done.107.refs_15_ = f32[32,768]{1,0:T(8,128)S(1)} collective-permute-done((f32[32,768]{1,0:T(8,128)S(1)}, f32[32,768]{1,0:T(8,128)S(1)}, u32[]{:S(2)}, u32[]{:S(2)}) %collective-permute-start.107) | collective-permute-done | bytes 98336 | tf_op jit(solution)/shard_map/ppermute | solution.py:59
  389.4 4.3 %collective-permute-done.111 = bf16[5,96,384]{2,1,0:T(8,128)(2,1)S(1)} collective-permute-done((bf16[5,96,384]{2,1,0:T(8,128)(2,1)S(1)}, bf16[5,96,384]{2,1,0:T(8,128)(2,1)S(1)}, u32[]{:S(2)}, u32[]{:S(2)}) %collective-permute-start.111) | collective-permute-done | bytes 368672 | tf_op jit(solution)/shard_map/ppermute | solution.py:56
  412.4 4.6 %collective-permute-done.117.refs_2_ = bf16[1,96,384]{2,1,0:T(8,128)(2,1)S(1)} collective-permute-done((bf16[1,96,384]{2,1,0:T(8,128)(2,1)S(1)}, bf16[1,96,384]{2,1,0:T(8,128)(2,1)S(1)}, u32[]{:S(2)}, u32[]{:S(2)}) %collective-permute-start.117) | collective-permute-done | bytes 73760 | tf_op jit(solution)/shard_map/ppermute | solution.py:53
  (510 shorter events, 241.6 us)
Async XLA Ops:
  37.1 17.4 %collective-permute-start.11 = (bf16[768,384]{1,0:T(8,128)(2,1)S(1)}, bf16[768,384]{1,0:T(8,128)(2,1)S(1)}, u32[]{:S(2)}, u32[]{:S(2)}) collective-permute-start(bf16[768,384]{1,0:T(8,128)(2,1)S(1)} %pad_maximum_fusion.6), channel_id=1, source_target_pairs={{0,8},{4,12},{8,16},{12,20},{16,24},{20,28},{24,0},{28,4},{1,9},{5... | collective-permute-start | bytes 1769480 | tf_op jit(solution)/shard_map/ppermute | solution.py:59
  49.9 21.3 %collective-permute-start.20 = (bf16[1600,384]{1,0:T(8,128)(2,1)}, bf16[1600,384]{1,0:T(8,128)(2,1)S(1)}, u32[]{:S(2)}, u32[]{:S(2)}) collective-permute-start(bf16[1600,384]{1,0:T(8,128)(2,1)} %copy-done.12), channel_id=1, source_target_pairs={{0,1},{1,0},{2,3},{3,2},{4,5},{5,4},{6,7},{7,6},{8,9},{9,8},{10,11... | collective-permute-start | bytes 3686408 | tf_op jit(solution)/shard_map/ppermute | solution.py:53
  54.6 16.6 %collective-permute-start.16 = (bf16[768,384]{1,0:T(8,128)(2,1)S(1)}, bf16[768,384]{1,0:T(8,128)(2,1)S(1)}, u32[]{:S(2)}, u32[]{:S(2)}) collective-permute-start(bf16[768,384]{1,0:T(8,128)(2,1)S(1)} %collective-permute-done.11), channel_id=1, source_target_pairs={{0,8},{4,12},{8,16},{12,20},{16,24},{20,28},{24,0},{28,4},{1,9},{5... | collective-permute-start | bytes 1769480 | tf_op jit(solution)/shard_map/ppermute | solution.py:59
  72.2 20.6 %collective-permute-start.26 = (bf16[3072,384]{1,0:T(8,128)(2,1)S(1)}, bf16[3072,384]{1,0:T(8,128)(2,1)}, u32[]{:S(2)}, u32[]{:S(2)}) collective-permute-start(bf16[3072,384]{1,0:T(8,128)(2,1)S(1)} %constant_dynamic-update-slice_fusion.24.refs_0_), channel_id=1, source_target_pairs={{0,1},{1,0},{2,3},{3,2},{4,5},{5,4},{6,7},{7,6},{8,9},{9,8},{10,11... | collective-permute-start | bytes 7077896 | tf_op jit(solution)/shard_map/ppermute | solution.py:53
  75.9 16.9 %collective-permute-start.22 = (bf16[768,384]{1,0:T(8,128)(2,1)S(1)}, bf16[768,384]{1,0:T(8,128)(2,1)S(1)}, u32[]{:S(2)}, u32[]{:S(2)}) collective-permute-start(bf16[768,384]{1,0:T(8,128)(2,1)S(1)} %copy-done.23), channel_id=1, source_target_pairs={{0,8},{4,12},{8,16},{12,20},{16,24},{20,28},{24,0},{28,4},{1,9},{5... | collective-permute-start | bytes 1769480 | tf_op jit(solution)/shard_map/ppermute | solution.py:59
  76.3 16.5 %collective-permute-start.25 = (bf16[1600,384]{1,0:T(8,128)(2,1)S(1)}, bf16[1600,384]{1,0:T(8,128)(2,1)S(1)}, u32[]{:S(2)}, u32[]{:S(2)}) collective-permute-start(bf16[1600,384]{1,0:T(8,128)(2,1)S(1)} %copy-done.11), channel_id=1, source_target_pairs={{0,1},{1,0},{2,3},{3,2},{4,5},{5,4},{6,7},{7,6},{8,9},{9,8},{10,11... | collective-permute-start | bytes 3686408 | tf_op jit(solution)/shard_map/ppermute | solution.py:53
  126.3 16.0 %collective-permute-start.43 = (bf16[384,384]{1,0:T(8,128)(2,1)S(1)}, bf16[384,384]{1,0:T(8,128)(2,1)S(1)}, u32[]{:S(2)}, u32[]{:S(2)}) collective-permute-start(bf16[384,384]{1,0:T(8,128)(2,1)S(1)} %bitcast.155), channel_id=1, source_target_pairs={{0,4},{4,0},{8,12},{12,8},{16,20},{20,16},{24,28},{28,24},{1,5},{5... | collective-permute-start | bytes 884744 | tf_op jit(solution)/shard_map/ppermute | solution.py:56
  128.1 17.0 %collective-permute-start.41 = (bf16[768,384]{1,0:T(8,128)(2,1)S(1)}, bf16[768,384]{1,0:T(8,128)(2,1)S(1)}, u32[]{:S(2)}, u32[]{:S(2)}) collective-permute-start(bf16[768,384]{1,0:T(8,128)(2,1)S(1)} %pad_maximum_fusion.7), channel_id=1, source_target_pairs={{0,8},{4,12},{8,16},{12,20},{16,24},{20,28},{24,0},{28,4},{1,9},{5... | collective-permute-start | bytes 1769480 | tf_op jit(solution)/shard_map/ppermute | solution.py:59
  145.1 18.0 %collective-permute-start.49 = (bf16[1600,384]{1,0:T(8,128)(2,1)S(1)}, bf16[1600,384]{1,0:T(8,128)(2,1)S(1)}, u32[]{:S(2)}, u32[]{:S(2)}) collective-permute-start(bf16[1600,384]{1,0:T(8,128)(2,1)S(1)} %constant_dynamic-update-slice_fusion.52.refs_1_), channel_id=1, source_target_pairs={{0,1},{1,0},{2,3},{3,2},{4,5},{5,4},{6,7},{7,6},{8,9},{9,8},{10,11... | collective-permute-start | bytes 3686408 | tf_op jit(solution)/shard_map/ppermute | solution.py:53
  145.2 17.8 %collective-permute-start.46 = (bf16[768,384]{1,0:T(8,128)(2,1)S(1)}, bf16[768,384]{1,0:T(8,128)(2,1)S(1)}, u32[]{:S(2)}, u32[]{:S(2)}) collective-permute-start(bf16[768,384]{1,0:T(8,128)(2,1)S(1)} %collective-permute-done.41), channel_id=1, source_target_pairs={{0,8},{4,12},{8,16},{12,20},{16,24},{20,28},{24,0},{28,4},{1,9},{5... | collective-permute-start | bytes 1769480 | tf_op jit(solution)/shard_map/ppermute | solution.py:59
  163.1 18.0 %collective-permute-start.53 = (bf16[3072,384]{1,0:T(8,128)(2,1)S(1)}, bf16[3072,384]{1,0:T(8,128)(2,1)S(1)}, u32[]{:S(2)}, u32[]{:S(2)}) collective-permute-start(bf16[3072,384]{1,0:T(8,128)(2,1)S(1)} %constant_dynamic-update-slice_fusion.58.refs_0_), channel_id=1, source_target_pairs={{0,1},{1,0},{2,3},{3,2},{4,5},{5,4},{6,7},{7,6},{8,9},{9,8},{10,11... | collective-permute-start | bytes 7077896 | tf_op jit(solution)/shard_map/ppermute | solution.py:53
  163.1 18.0 %collective-permute-start.50 = (bf16[768,384]{1,0:T(8,128)(2,1)S(1)}, bf16[768,384]{1,0:T(8,128)(2,1)S(1)}, u32[]{:S(2)}, u32[]{:S(2)}) collective-permute-start(bf16[768,384]{1,0:T(8,128)(2,1)S(1)} %collective-permute-done.46), channel_id=1, source_target_pairs={{0,8},{4,12},{8,16},{12,20},{16,24},{20,28},{24,0},{28,4},{1,9},{5... | collective-permute-start | bytes 1769480 | tf_op jit(solution)/shard_map/ppermute | solution.py:59
  224.1 19.7 %collective-permute-start.64 = (bf16[8,96,384]{2,1,0:T(8,128)(2,1)S(1)}, bf16[8,96,384]{2,1,0:T(8,128)(2,1)S(1)}, u32[]{:S(2)}, u32[]{:S(2)}) collective-permute-start(bf16[8,96,384]{2,1,0:T(8,128)(2,1)S(1)} %ring_block.16), channel_id=1, source_target_pairs={{0,8},{4,12},{8,16},{12,20},{16,24},{20,28},{24,0},{28,4},{1,9},{5... | collective-permute-start | bytes 1769480 | tf_op jit(solution)/shard_map/ppermute | solution.py:59
  245.5 15.5 %collective-permute-start.67 = (bf16[8,96,384]{2,1,0:T(8,128)(2,1)S(1)}, bf16[8,96,384]{2,1,0:T(8,128)(2,1)S(1)}, u32[]{:S(2)}, u32[]{:S(2)}) collective-permute-start(bf16[8,96,384]{2,1,0:T(8,128)(2,1)S(1)} %ring_block.17), channel_id=1, source_target_pairs={{0,8},{4,12},{8,16},{12,20},{16,24},{20,28},{24,0},{28,4},{1,9},{5... | collective-permute-start | bytes 1769480 | tf_op jit(solution)/shard_map/ppermute | solution.py:59
  261.3 21.5 %collective-permute-start.70 = (bf16[8,96,384]{2,1,0:T(8,128)(2,1)S(1)}, bf16[8,96,384]{2,1,0:T(8,128)(2,1)S(1)}, u32[]{:S(2)}, u32[]{:S(2)}) collective-permute-start(bf16[8,96,384]{2,1,0:T(8,128)(2,1)S(1)} %ring_block.18), channel_id=1, source_target_pairs={{0,8},{4,12},{8,16},{12,20},{16,24},{20,28},{24,0},{28,4},{1,9},{5... | collective-permute-start | bytes 1769480 | tf_op jit(solution)/shard_map/ppermute | solution.py:59
  262.8 20.1 %collective-permute-start.72 = (bf16[4,96,384]{2,1,0:T(8,128)(2,1)S(1)}, bf16[4,96,384]{2,1,0:T(8,128)(2,1)S(1)}, u32[]{:S(2)}, u32[]{:S(2)}) collective-permute-start(bf16[4,96,384]{2,1,0:T(8,128)(2,1)S(1)} %get-tuple-element.632), channel_id=1, source_target_pairs={{0,4},{4,0},{8,12},{12,8},{16,20},{20,16},{24,28},{28,24},{1,5},{5... | collective-permute-start | bytes 884744 | tf_op jit(solution)/shard_map/ppermute | solution.py:56
  263.5 19.3 %collective-permute-start.73 = (bf16[4,96,384]{2,1,0:T(8,128)(2,1)S(1)}, bf16[4,96,384]{2,1,0:T(8,128)(2,1)S(1)}, u32[]{:S(2)}, u32[]{:S(2)}) collective-permute-start(bf16[4,96,384]{2,1,0:T(8,128)(2,1)S(1)} %get-tuple-element.633), channel_id=1, source_target_pairs={{0,2},{1,3},{2,0},{3,1},{4,6},{5,7},{6,4},{7,5},{8,10},{9,11},{10,... | collective-permute-start | bytes 884744 | tf_op jit(solution)/shard_map/ppermute | solution.py:53
  316.9 17.8 %collective-permute-start.91 = (bf16[4,8,96,384]{3,2,1,0:T(8,128)(2,1)S(1)}, bf16[4,8,96,384]{3,2,1,0:T(8,128)(2,1)S(1)}, u32[]{:S(2)}, u32[]{:S(2)}) collective-permute-start(bf16[4,8,96,384]{3,2,1,0:T(8,128)(2,1)S(1)} %gradient_sent.9), channel_id=1, source_target_pairs={{0,1},{1,0},{2,3},{3,2},{4,5},{5,4},{6,7},{7,6},{8,9},{9,8},{10,11... | collective-permute-start | bytes 7077896 | tf_op jit(solution)/shard_map/ppermute | solution.py:53
  317.1 17.6 %collective-permute-start.90 = (bf16[8,96,384]{2,1,0:T(8,128)(2,1)S(1)}, bf16[8,96,384]{2,1,0:T(8,128)(2,1)S(1)}, u32[]{:S(2)}, u32[]{:S(2)}) collective-permute-start(bf16[8,96,384]{2,1,0:T(8,128)(2,1)S(1)} %ring_block.23), channel_id=1, source_target_pairs={{0,8},{4,12},{8,16},{12,20},{16,24},{20,28},{24,0},{28,4},{1,9},{5... | collective-permute-start | bytes 1769480 | tf_op jit(solution)/shard_map/ppermute | solution.py:59
  335.0 18.9 %collective-permute-start.95 = (bf16[8,96,384]{2,1,0:T(8,128)(2,1)S(1)}, bf16[8,96,384]{2,1,0:T(8,128)(2,1)S(1)}, u32[]{:S(2)}, u32[]{:S(2)}) collective-permute-start(bf16[8,96,384]{2,1,0:T(8,128)(2,1)S(1)} %ring_block.25), channel_id=1, source_target_pairs={{0,8},{4,12},{8,16},{12,20},{16,24},{20,28},{24,0},{28,4},{1,9},{5... | collective-permute-start | bytes 1769480 | tf_op jit(solution)/shard_map/ppermute | solution.py:59
  335.0 18.8 %collective-permute-start.96 = (bf16[4,96,384]{2,1,0:T(8,128)(2,1)S(1)}, bf16[4,96,384]{2,1,0:T(8,128)(2,1)S(1)}, u32[]{:S(2)}, u32[]{:S(2)}) collective-permute-start(bf16[4,96,384]{2,1,0:T(8,128)(2,1)S(1)} %get-tuple-element.727), channel_id=1, source_target_pairs={{0,4},{4,0},{8,12},{12,8},{16,20},{20,16},{24,28},{28,24},{1,5},{5... | collective-permute-start | bytes 884744 | tf_op jit(solution)/shard_map/ppermute | solution.py:56
  336.3 17.6 %collective-permute-start.97 = (bf16[4,96,384]{2,1,0:T(8,128)(2,1)S(1)}, bf16[4,96,384]{2,1,0:T(8,128)(2,1)S(1)}, u32[]{:S(2)}, u32[]{:S(2)}) collective-permute-start(bf16[4,96,384]{2,1,0:T(8,128)(2,1)S(1)} %get-tuple-element.728), channel_id=1, source_target_pairs={{0,2},{1,3},{2,0},{3,1},{4,6},{5,7},{6,4},{7,5},{8,10},{9,11},{10,... | collective-permute-start | bytes 884744 | tf_op jit(solution)/shard_map/ppermute | solution.py:53
  336.6 17.3 %collective-permute-start.98 = (f32[32,768]{1,0:T(8,128)S(1)}, f32[32,768]{1,0:T(8,128)S(1)}, u32[]{:S(2)}, u32[]{:S(2)}) collective-permute-start(f32[32,768]{1,0:T(8,128)S(1)} %add.52.refs_13_), channel_id=1, source_target_pairs={{0,8},{4,12},{8,16},{12,20},{16,24},{20,28},{24,0},{28,4},{1,9},{5... | collective-permute-start | bytes 294920 | tf_op jit(solution)/shard_map/ppermute | solution.py:59
  354.1 15.9 %collective-permute-start.99 = (bf16[8,96,384]{2,1,0:T(8,128)(2,1)S(1)}, bf16[8,96,384]{2,1,0:T(8,128)(2,1)S(1)}, u32[]{:S(2)}, u32[]{:S(2)}) collective-permute-start(bf16[8,96,384]{2,1,0:T(8,128)(2,1)S(1)} %ring_block.26), channel_id=1, source_target_pairs={{0,8},{4,12},{8,16},{12,20},{16,24},{20,28},{24,0},{28,4},{1,9},{5... | collective-permute-start | bytes 1769480 | tf_op jit(solution)/shard_map/ppermute | solution.py:59
  (140 other events, 1136.8 us)

commit v5 on v4

--- a/solution.py
+++ b/solution.py
@@ -378,21 +378,24 @@
                         ]
 
 
-def keep_factor(spot, keep_mask, branch):
-    return keep_mask[spot[4], branch].astype(F32) * (1.0 / KEEP_RATE)
-
-
-def key_block(spot, lengths, rows, special_count):
+SPOT = 5
+
+
+def keep_factor(spot, images, branch):
+    return spot[SPOT + images + spot[4] * 2 * LAYERS + branch].astype(F32) * (1.0 / KEEP_RATE)
+
+
+def key_block(spot, rows, special_count):
     ids = lax.broadcasted_iota(jnp.int32, (1, rows), 1)
-    inside = (ids < lengths[0, spot[4]]) | ((ids >= MOST) & (ids < MOST + special_count))
+    inside = (ids < spot[SPOT + spot[4]]) | ((ids >= MOST) & (ids < MOST + special_count))
     return jnp.where(inside, 0.0, MASKED).astype(F32)
 
 
-def image_frame(spot, lengths, count, halo):
+def image_frame(spot, images, count, halo):
     before = jnp.int32(0)
-    for image in range(lengths.shape[1]):
-        before = before + jnp.where(image < spot[4], lengths[0, image], 0)
-    return before - spot[4] * count + halo, lengths[0, spot[4]]
+    for image in range(images):
+        before = before + jnp.where(image < spot[4], spot[SPOT + image], 0)
+    return before - spot[4] * count + halo, spot[SPOT + spot[4]]
 
 
 def flat(block):
@@ -429,14 +432,14 @@
 
 
 def head_probs(queries, keys, blocked):
-    scores = dot_nt(queries, keys) * 0.125 + blocked
+    scores = dot_nt(queries, keys) + blocked
     powers = jnp.exp(scores - jnp.max(scores, axis=1, keepdims=True))
-    return powers / jnp.sum(powers, axis=1, keepdims=True)
-
-
-def forward_attention_kernel(turned, chunks, branch, special_count, spot, lengths, keep_mask, stream, *refs):
-    keep = keep_factor(spot, keep_mask, branch)
-    blocked = key_block(spot, lengths, stream.shape[0], special_count)
+    return powers * (1.0 / jnp.sum(powers, axis=1, keepdims=True))
+
+
+def forward_attention_kernel(turned, chunks, images, branch, special_count, spot, stream, *refs):
+    keep = keep_factor(spot, images, branch)
+    blocked = key_block(spot, stream.shape[0], special_count)
     parts, refs = refs[: 2 * len(chunks)], refs[2 * len(chunks) :]
     middle, normed_two, normed_one_t, normed_two_t, mixed, attended, attended_t, crossed, split, vectors, bias_up, extra = refs
     place_pieces(spot, parts, chunks, crossed, split, extra, turned)
@@ -472,7 +475,7 @@
         outs = []
         for side in range(2):
             mine = ((lane < HD) if side == 0 else (lane >= HD)).astype(F32).astype(BF)
-            probs = head_probs(queries * mine, keys, blocked)
+            probs = head_probs(queries * (mine * 0.125), keys, blocked)
             outs.append(dot_nn(probs.astype(BF), values))
         attended[:, pl.ds(pair * 2 * HD, 2 * HD)] = jnp.where(lane < HD, outs[0], outs[1]).astype(BF)
     ahead = attended[...]
@@ -487,7 +490,7 @@
     normed_two_t[...] = normed.T
 
 
-def forward_attention(place, where, branch, special_count, stream, unit, extra_rows):
+def forward_attention(place, spot, branch, special_count, stream, unit, extra_rows):
     parts = unit.parts()
     rows, width = stream.shape
     group = (width // place.n_dp, width // 2)
@@ -505,15 +508,15 @@
         jax.ShapeDtypeStruct((1, 4 * width), F32),
     ]
     return pl.pallas_call(
-        partial(forward_attention_kernel, unit.turned, unit.chunks, branch, special_count),
-        in_specs=in_smem(3) + whole_vmem(1 + len(parts)),
+        partial(forward_attention_kernel, unit.turned, unit.chunks, place.n_seq, branch, special_count),
+        in_specs=in_smem(1) + whole_vmem(1 + len(parts)),
         out_specs=whole_vmem(len(shapes)),
         out_shape=shapes,
         scratch_shapes=[pltpu.VMEM((place.n_dp, extra_rows, width // 2), BF)],
         compiler_params=kernel_params(12),
         cost_estimate=pl.CostEstimate(flops=0, bytes_accessed=0, transcendentals=0),
         name="forward_attention",
-    )(*where, stream, *parts)
+    )(spot, stream, *parts)
 
 
 def forward_up_kernel(turned, chunks, spot, normed, bias_up, *refs):
@@ -547,8 +550,8 @@
     )(spot, normed, bias_up, *parts)
 
 
-def forward_down_kernel(branch, spot, keep_mask, middle, hidden, vectors, split, output):
-    keep = keep_factor(spot, keep_mask, branch)
+def forward_down_kernel(images, branch, spot, middle, hidden, vectors, split, output):
+    keep = keep_factor(spot, images, branch)
     ahead = hidden[...]
     half = middle.shape[1] // 2
     for core in range(2):
@@ -557,20 +560,20 @@
         output[:, columns] = middle[:, columns] + keep * added
 
 
-def forward_down(where, branch, middle, hidden, vectors, split):
+def forward_down(place, spot, branch, middle, hidden, vectors, split):
     return pl.pallas_call(
-        partial(forward_down_kernel, branch),
-        in_specs=in_smem(2) + whole_vmem(4),
+        partial(forward_down_kernel, place.n_seq, branch),
+        in_specs=in_smem(1) + whole_vmem(4),
         out_specs=whole_vmem(1)[0],
         out_shape=jax.ShapeDtypeStruct(middle.shape, F32),
         compiler_params=kernel_params(8),
         cost_estimate=pl.CostEstimate(flops=0, bytes_accessed=0, transcendentals=0),
         name="forward_down",
-    )(where[0], where[2], middle, hidden, vectors, split)
-
-
-def backward_feed_kernel(branch, spot, keep_mask, grad, slope, split, grad_down_t, grad_up, sum_down, sum_up):
-    keep = keep_factor(spot, keep_mask, branch)
+    )(spot, middle, hidden, vectors, split)
+
+
+def backward_feed_kernel(images, branch, spot, grad, slope, split, grad_down_t, grad_up, sum_down, sum_up):
+    keep = keep_factor(spot, images, branch)
     down = (keep * grad[...]).astype(BF)
     grad_down_t[...] = down.T
     sum_down[...] = jnp.sum(down.astype(F32), axis=0, keepdims=True)
@@ -583,7 +586,7 @@
         sum_up[:, columns] = jnp.sum(up.astype(F32), axis=0, keepdims=True)
 
 
-def backward_feed(where, branch, grad, slope, split):
+def backward_feed(place, spot, branch, grad, slope, split):
     rows, width = grad.shape
     shapes = [
         jax.ShapeDtypeStruct((width, rows), BF),
@@ -592,18 +595,18 @@
         jax.ShapeDtypeStruct((1, 4 * width), F32),
     ]
     return pl.pallas_call(
-        partial(backward_feed_kernel, branch),
-        in_specs=in_smem(2) + whole_vmem(3),
+        partial(backward_feed_kernel, place.n_seq, branch),
+        in_specs=in_smem(1) + whole_vmem(3),
         out_specs=whole_vmem(len(shapes)),
         out_shape=shapes,
         compiler_params=kernel_params(8),
         cost_estimate=pl.CostEstimate(flops=0, bytes_accessed=0, transcendentals=0),
         name="backward_feed",
-    )(where[0], where[2], grad, slope, split)
-
-
-def backward_middle_kernel(branch, spot, keep_mask, grad, grad_up, middle, vectors, crossed, *refs):
-    keep = keep_factor(spot, keep_mask, branch)
+    )(spot, grad, slope, split)
+
+
+def backward_middle_kernel(images, branch, spot, grad, grad_up, middle, vectors, crossed, *refs):
+    keep = keep_factor(spot, images, branch)
     grad_middle, grad_proj, sum_proj, grad_gain, grad_shift = refs
     hat, scale = moments(middle[...])
     half = grad.shape[1] // 2
@@ -620,29 +623,29 @@
     sum_proj[...] = jnp.sum(proj.astype(F32), axis=0, keepdims=True)
 
 
-def backward_middle(where, branch, grad, grad_up, middle, vectors, crossed):
+def backward_middle(place, spot, branch, grad, grad_up, middle, vectors, crossed):
     rows, width = grad.shape
     shapes = [
         jax.ShapeDtypeStruct((rows, width), F32),
         jax.ShapeDtypeStruct((rows, width), BF),
     ] + [jax.ShapeDtypeStruct((1, width), F32)] * 3
     return pl.pallas_call(
-        partial(backward_middle_kernel, branch),
-        in_specs=in_smem(2) + whole_vmem(5),
+        partial(backward_middle_kernel, place.n_seq, branch),
+        in_specs=in_smem(1) + whole_vmem(5),
         out_specs=whole_vmem(len(shapes)),
         out_shape=shapes,
         compiler_params=kernel_params(10),
         cost_estimate=pl.CostEstimate(flops=0, bytes_accessed=0, transcendentals=0),
         name="backward_middle",
-    )(where[0], where[2], grad, grad_up, middle, vectors, crossed)
-
-
-def backward_feed_middle_kernel(branches, spot, keep_mask, grad, slope, split, middle, vectors, crossed, *refs):
-    backward_feed_kernel(branches[1], spot, keep_mask, grad, slope, split, *refs[:4])
-    backward_middle_kernel(branches[0], spot, keep_mask, grad, refs[1], middle, vectors, crossed, *refs[4:])
-
-
-def backward_feed_middle(where, branches, grad, slope, split, middle, vectors, crossed):
+    )(spot, grad, grad_up, middle, vectors, crossed)
+
+
+def backward_feed_middle_kernel(images, branches, spot, grad, slope, split, middle, vectors, crossed, *refs):
+    backward_feed_kernel(images, branches[1], spot, grad, slope, split, *refs[:4])
+    backward_middle_kernel(images, branches[0], spot, grad, refs[1], middle, vectors, crossed, *refs[4:])
+
+
+def backward_feed_middle(place, spot, branches, grad, slope, split, middle, vectors, crossed):
     rows, width = grad.shape
     shapes = [
         jax.ShapeDtypeStruct((width, rows), BF),
@@ -653,17 +656,17 @@
         jax.ShapeDtypeStruct((rows, width), BF),
     ] + [jax.ShapeDtypeStruct((1, width), F32)] * 3
     return pl.pallas_call(
-        partial(backward_feed_middle_kernel, branches),
-        in_specs=in_smem(2) + whole_vmem(6),
+        partial(backward_feed_middle_kernel, place.n_seq, branches),
+        in_specs=in_smem(1) + whole_vmem(6),
         out_specs=whole_vmem(len(shapes)),
         out_shape=shapes,
         compiler_params=kernel_params(12),
         name="backward_feed_middle",
-    )(where[0], where[2], grad, slope, split, middle, vectors, crossed)
-
-
-def backward_attention_kernel(special_count, spot, lengths, grad_middle, grad_proj, mixed, stream, vectors, *refs):
-    blocked = key_block(spot, lengths, stream.shape[0], special_count)
+    )(spot, grad, slope, split, middle, vectors, crossed)
+
+
+def backward_attention_kernel(special_count, spot, grad_middle, grad_proj, mixed, stream, vectors, *refs):
+    blocked = key_block(spot, stream.shape[0], special_count)
     others, (crossed, split), refs = refs[:5], refs[5:7], refs[7:]
     grad_stream, grad_mixed, sums, ahead = refs
     sum_proj, gain_two, shift_two, sum_down, sum_up = others
@@ -683,7 +686,7 @@
         found = []
         for side in range(2):
             mine = ((lane < HD) if side == 0 else (lane >= HD)).astype(F32).astype(BF)
-            probs = head_probs(queries * mine, keys, blocked)
+            probs = head_probs(queries * (mine * 0.125), keys, blocked)
             grad_probs = dot_nt(grads * mine, values)
             inner = jnp.sum(probs * grad_probs, axis=1, keepdims=True)
             grad_scores = (probs * (grad_probs - inner)).astype(BF)
@@ -721,7 +724,7 @@
     grad_stream[...] = grad_middle[...] + norm_back(hat, scale, vectors[GAIN_ONE : GAIN_ONE + 1], total)
 
 
-def backward_attention(where, special_count, grad_middle, grad_proj, mixed, stream, vectors, others, crossed, split):
+def backward_attention(spot, special_count, grad_middle, grad_proj, mixed, stream, vectors, others, crossed, split):
     rows, width = stream.shape
     shapes = [
         jax.ShapeDtypeStruct((rows, width), F32),
@@ -730,14 +733,14 @@
     ]
     return pl.pallas_call(
         partial(backward_attention_kernel, special_count),
-        in_specs=in_smem(2) + whole_vmem(5 + 5 + 2),
+        in_specs=in_smem(1) + whole_vmem(5 + 5 + 2),
         out_specs=whole_vmem(len(shapes)),
         out_shape=shapes,
         scratch_shapes=[pltpu.VMEM((rows, width), BF)],
         compiler_params=kernel_params(12),
         cost_estimate=pl.CostEstimate(flops=0, bytes_accessed=0, transcendentals=0),
         name="backward_attention",
-    )(where[0], where[1], grad_middle, grad_proj, mixed, stream, vectors, *others, crossed, split)
+    )(spot, grad_middle, grad_proj, mixed, stream, vectors, *others, crossed, split)
 
 
 def row_of(spot, step, far_x, steps):
@@ -972,9 +975,9 @@
     return jnp.pad(packed, ((0, 0), (0, rows - packed.shape[1]), (0, half - part)))
 
 
-def image_kernel(spot, lengths, before, patches, after, specials, out, window):
+def image_kernel(images, spot, before, patches, after, specials, out, window):
     halo, count = before.shape[0], patches.shape[0]
-    begin, length = image_frame(spot, lengths, count, halo)
+    begin, length = image_frame(spot, images, count, halo)
     window[:halo] = before[...]
     window[halo : halo + count] = patches[...]
     window[halo + count : 2 * halo + count] = after[...]
@@ -988,32 +991,32 @@
     out[MOST : MOST + specials.shape[0]] = specials[...]
 
 
-def take_image(place, where, patches, specials, halo, rows):
+def take_image(place, spot, patches, specials, halo, rows):
     count, width = patches.shape
     before = shift_seq(place, patches[count - halo :], 1)
     after = shift_seq(place, patches[:halo], -1)
 
     def build(before, patches, after, specials):
         return pl.pallas_call(
-            image_kernel,
-            in_specs=in_smem(2) + whole_vmem(4),
+            partial(image_kernel, place.n_seq),
+            in_specs=in_smem(1) + whole_vmem(4),
             out_specs=whole_vmem(1)[0],
             out_shape=jax.ShapeDtypeStruct((rows, width), F32),
             scratch_shapes=[pltpu.VMEM((MOST + 2 * halo, width), F32)],
             compiler_params=kernel_params(6),
         cost_estimate=pl.CostEstimate(flops=0, bytes_accessed=0, transcendentals=0),
             name="take_image",
-        )(where[0], where[1], before, patches, after, specials)
+        )(spot, before, patches, after, specials)
 
     return (before, patches, after, specials), build
 
 
-def block_kernel(spot, lengths, *refs):
+def block_kernel(images, spot, *refs):
     streams, (before, after), owns, window = refs[:2], refs[2:4], refs[4:8], refs[8]
     for at, stream in enumerate(streams):
         own, specials = owns[2 * at : 2 * at + 2]
         halo, count = before.shape[0] // 2, own.shape[0]
-        begin, length = image_frame(spot, lengths, count, halo)
+        begin, length = image_frame(spot, images, count, halo)
         window[MOST:] = jnp.zeros((window.shape[0] - MOST, window.shape[1]), F32)
         inside = lax.broadcasted_iota(jnp.int32, (MOST, 1), 0) < length
         window[:MOST] = jnp.where(inside, stream[:MOST], 0.0)
@@ -1024,11 +1027,11 @@
         specials[...] = stream[MOST : MOST + specials.shape[0]]
 
 
-def give_images(where, streams, halo, count, special_count):
+def give_images(place, spot, streams, halo, count, special_count):
     width = streams[0].shape[1]
     return pl.pallas_call(
-        block_kernel,
-        in_specs=in_smem(2) + whole_vmem(2),
+        partial(block_kernel, place.n_seq),
+        in_specs=in_smem(1) + whole_vmem(2),
         out_specs=whole_vmem(6),
         out_shape=[
             jax.ShapeDtypeStruct((size, width), F32)
@@ -1038,7 +1041,7 @@
         compiler_params=kernel_params(6),
         cost_estimate=pl.CostEstimate(flops=0, bytes_accessed=0, transcendentals=0),
         name="give_images",
-    )(where[0], where[1], *streams)
+    )(spot, *streams)
 
 
 def finish_kernel(*refs):
@@ -1143,7 +1146,7 @@
     pairs = ((0, 1), (2, 3))
     part_rows = proj_weight.shape[1]
     spot = jnp.stack([place.z, place.x, place.y, place.core, place.seq]).astype(jnp.int32)
-    where = (spot, lengths, keep_mask[0])
+    spot = jnp.concatenate([spot, lengths.reshape(-1), keep_mask.reshape(-1)])
 
     shards = (norm1_gain, norm1_bias, query_bias, value_bias, proj_bias, norm2_gain, norm2_bias, fc2_bias)
 
@@ -1153,7 +1156,7 @@
         return Gathered(place, attention_groups(place, qkv, proj), [extra], layer == 0, pairs)
 
     units = [attention_unit(0, qkv_weight[0], proj_weight[0], extras[0])]
-    image, build = take_image(place, where, patches, specials, halo, rows)
+    image, build = take_image(place, spot, patches, specials, halo, rows)
     inputs = {
         "weights": (fc1_weight[0], fc2_weight[0], qkv_weight[1], proj_weight[1], extras[1], fc1_weight[1], fc2_weight[1]),
         "cots": (cot_patches, cot_specials),
@@ -1202,17 +1205,17 @@
         if slot == 5:
             carried["stream"] = build(*image)
         if slot == 3 * unit_count:
-            new["image"], build = take_image(place, where, *inputs["cots"], halo, rows)
+            new["image"], build = take_image(place, spot, *inputs["cots"], halo, rows)
         if slot == 3 * unit_count + 1:
             grad = build(*image)
         if slot in (9, 11):
             layer = slot // 11
             new["forward"] = forward_attention(
-                place, where, 2 * layer, special_count, carried["stream"], units[2 * layer], EXTRA_ROWS
+                place, spot, 2 * layer, special_count, carried["stream"], units[2 * layer], EXTRA_ROWS
             )
         if slot == 10:
             hidden, slope, crossed, split = forward_up(place, spot, carried["normed"], bias_up[0], units[1])
-            output = forward_down(where, 1, carried["middle"], hidden, vectors[0], split)
+            output = forward_down(place, spot, 1, carried["middle"], hidden, vectors[0], split)
             new["feed"] = (output, hidden, slope, crossed, split)
         if slot in (3, 5):
             names = [key for key in new if key[0] in ("x", "y")]
@@ -1271,7 +1274,7 @@
     def feed_back(layer, grad):
         found = back[layer]
         found["down_t"], found["up"], found["sum_down"], found["sum_up"] = backward_feed(
-            where, 2 * layer + 1, grad, slopes[layer], weights[2 * layer + 1][1]
+            place, spot, 2 * layer + 1, grad, slopes[layer], weights[2 * layer + 1][1]
         )
 
     def feed_operands(layer):
@@ -1282,14 +1285,14 @@
     def middle_back(layer, grad):
         found = back[layer]
         found["middle"], found["proj"], found["sum_proj"], found["gain"], found["shift"] = backward_middle(
-            where, 2 * layer, grad, found["up"], middles[layer], vectors[layer], weights[2 * layer + 1][0]
+            place, spot, 2 * layer, grad, found["up"], middles[layer], vectors[layer], weights[2 * layer + 1][0]
         )
 
     def attention_back(layer):
         found = back[layer]
         others = [found[name] for name in ("sum_proj", "gain", "shift", "sum_down", "sum_up")]
         found["grad"], found["mixed"], found["sums"] = backward_attention(
-            where, special_count, found["middle"], found["proj"], mixeds[layer], streams[layer], vectors[layer], others, *weights[2 * layer]
+            spot, special_count, found["middle"], found["proj"], mixeds[layer], streams[layer], vectors[layer], others, *weights[2 * layer]
         )
 
     def attention_operands(layer):
@@ -1352,8 +1355,6 @@
         if slot == -2:
             sending[0, 1] = sent_cut(0, 1)
             work["sending"] = sending[0, 1]
-        if slot == 0:
-            keep_cut(0, 1, got.pop((0, 1)))
         if slot == -1:
             keep_cut(0, 0, got.pop((0, 0)))
         for which, base in ((2, 4), (3, 7)):
@@ -1364,6 +1365,10 @@
         for key, base in (((0, 0), -2), ((0, 1), -1), ((1, 0), 2), ((2, 0), 3), ((3, 0), 6)):
             if slot == base:
                 new["core", key] = place.swap_seq(sending.pop(key), 1)
+        if slot == -1:
+            keep_cut(0, 1, new["core", (0, 1)])
+            for step in cuts[0][1]:
+                work["kept", 0, step] = reduces[0].kept[step]
         if slot == 2:
             keep_cut(1, 0, new["core", (1, 0)])
         for which, unit in enumerate(reduces):
@@ -1379,7 +1384,8 @@
             work["sending"] = sent_cut(3, 0)
         if slot == -1:
             middle_back(1, grad)
-            streams[LAYERS] = forward_down(where, 3, carried["middle"], hiddens[1], vectors[1], weights[3][1])
+        if slot == 4:
+            streams[LAYERS] = forward_down(place, spot, 3, carried["middle"], hiddens[1], vectors[1], weights[3][1])
             work["output"] = streams[LAYERS]
         if slot == 0:
             attention_back(1)
@@ -1390,7 +1396,7 @@
                 zip(
                     names,
                     backward_feed_middle(
-                        where, (0, 1), back[1]["grad"], slopes[0], weights[1][1], middles[0], vectors[0], weights[1][0]
+                        place, spot, (0, 1), back[1]["grad"], slopes[0], weights[1][1], middles[0], vectors[0], weights[1][0]
                     ),
                 )
             )
@@ -1409,26 +1415,30 @@
             new["sum"] = place.swap_seq(total, 2)
         if slot == 6:
             new["sum"] = place.swap_x(total)
-        if slot in (7, 9):
-            new["ringing"] = [place.ring_z(total, by) for by in ((1,) if slot == 7 else (2, 3))]
+        if slot in (7, 9, 11):
+            new["ringing"] = [place.ring_z(total if slot == 7 else rung[-1])]
+        if slot == final_slot - 4:
+            work["images"] = give_images(place, spot, given, halo, count, special_count)
+        if slot == final_slot - 3:
+            images_before, images_after, *owns = images
+            new["image_down"] = shift_seq(place, images_before, -1)
         if slot == final_slot - 1:
-            work["images"] = give_images(where, given, halo, count, special_count)
-        if slot == final_slot:
-            images_before, images_after, *owns = images
-            new["images"] = (shift_seq(place, images_after, 1), shift_seq(place, images_before, -1))
+            new["image_up"] = shift_seq(place, images_after, 1)
         pending = {}
+        if slot == final_slot - 2:
+            pending["after"] = images_after
         for which, unit in enumerate(reduces):
             at = slot + 1 - 3 * which
             if 0 <= at <= 2:
                 step = (at + 2) % nz
-                if step in unit.kept:
+                if step in unit.kept and ("kept", which, step) not in work:
                     pending["kept", which] = unit.kept[step]
-        if slot == final_slot - 2:
+        if slot == final_slot - 5:
             pending["give"] = [streams[LAYERS], back[0]["grad"]]
         for key, base in (((2, 0), 2), ((3, 0), 5)):
             if slot == base:
                 pending["sending", key] = sending[key]
-        for key, base in (((0, 1), 0), ((2, 0), 4), ((3, 0), 7)):
+        for key, base in (((2, 0), 4), ((3, 0), 7)):
             if slot == base - 1 and key in got:
                 pending["got", key] = got[key]
         new, work, pending = fence((new, work, pending))
@@ -1452,6 +1462,8 @@
                 reduces[key[1]].kept[key[2]] = value
         if "give" in pending:
             given = pending.pop("give")
+        if "after" in pending:
+            images_after = pending.pop("after")
         for key in [key for key in pending if key[0] == "got"]:
             got[key[1]] = pending.pop(key)
         for key, value in pending.items():
@@ -1463,8 +1475,10 @@
                 reduces[key[1]].running = value
             if key[0] == "side":
                 reduces[key[1]].sides[(slot - 3 * key[1] + 2) % nz] = value
-        if "images" in new:
-            sides = new["images"]
+        if "image_down" in new:
+            image_down = new["image_down"]
+        if "image_up" in new:
+            sides = (new["image_up"], image_down)
         if "lasts" in new:
             lasts[: len(new["lasts"])] = new["lasts"]
         if "sum" in new:

time: 427 us -> 419 us (0.981)
    ppermute x27, starting transfers between devices: 21.9 us -> 17.4 us  [ring_z(): lax.ppermute(values, 'dp', [(i, (i + 2 * by) % self.n_dp) for i in range(...]
  transfers between devices with their start and end apart: 121 -> 121, of which waited for: 51 -> 50; matrix products, arithmetic and copies ran while one was open for 3% -> 3% of each run, Pallas kernels for 24% -> 25%
where the time goes in v5:
time: 419 us; the launch traced here: 412 us
  waiting for transfers between devices  156 us (37%)
  Pallas kernels  117 us (28%)
  starting transfers between devices  113 us (27%)
  local copies, waits for them, and re-layouts  18.6 us (4%)
    ppermute x27, waiting for transfers between devices, ring_z(): lax.ppermute(values, 'dp', [(i, (i + 2 * by) % self.n_dp) for i in range(...  63.2 us
    ppermute x38, waiting for transfers between devices, swap_x(): return lax.ppermute(values, 'dp', [(i, i ^ 1) for i in range(self.n_dp)])  54.8 us
    ppermute x50, starting transfers between devices, swap_seq(): lax.ppermute(values, 'seq', [(i, i ^ mask) for i in range(self.n_seq)])  43.8 us
    ppermute x38, starting transfers between devices, swap_x(): return lax.ppermute(values, 'dp', [(i, i ^ 1) for i in range(self.n_dp)])  43.1 us
    ppermute x50, waiting for transfers between devices, swap_seq(): lax.ppermute(values, 'seq', [(i, i ^ mask) for i in range(self.n_seq)])  36.3 us
    pallas_call x2, Pallas kernels, backward_attention(): pl.pallas_call(partial(backward_attention_kernel, special_count), in_spec...  23.5 us
    pallas_call x2, Pallas kernels, forward_attention(): pl.pallas_call(partial(forward_attention_kernel, unit.turned, unit.chunks...  18.3 us
    pallas_call x5, Pallas kernels, kept_part(): pl.pallas_call(partial(kept_kernel, fill, steps, place.nz), in_specs=in_s...  17.9 us
  transfers between devices with their start and end apart: 121, of which 50 were waited for; matrix products, arithmetic and copies ran while one was open for 3% of the time, Pallas kernels for 25%

profile of v5, /device:TPU:0, one launch (start us, length us, event | category | flops | bytes accessed | tf_op | source)
XLA Modules:
  0.0 411.9 jit_solution(1721777483539969666)
XLA Ops:
  31.5 4.4 %collective-permute-done.10 = bf16[192,384]{1,0:T(8,128)(2,1)S(1)} collective-permute-done((bf16[192,384]{1,0:T(8,128)(2,1)S(1)}, bf16[192,384]{1,0:T(8,128)(2,1)S(1)}, u32[]{:S(2)}, u32[]{:S(2)}) %collective-permute-start.10) | collective-permute-done | bytes 147488 | tf_op jit(solution)/shard_map/ppermute | solution.py:53
  41.5 8.3 %collective-permute-done.14 = bf16[192,384]{1,0:T(8,128)(2,1)S(1)} collective-permute-done((bf16[192,384]{1,0:T(8,128)(2,1)S(1)}, bf16[192,384]{1,0:T(8,128)(2,1)S(1)}, u32[]{:S(2)}, u32[]{:S(2)}) %collective-permute-start.14) | collective-permute-done | bytes 147488 | tf_op jit(solution)/shard_map/ppermute | solution.py:53
  57.7 8.7 %collective-permute-done.18 = bf16[192,384]{1,0:T(8,128)(2,1)S(1)} collective-permute-done((bf16[192,384]{1,0:T(8,128)(2,1)S(1)}, bf16[192,384]{1,0:T(8,128)(2,1)S(1)}, u32[]{:S(2)}, u32[]{:S(2)}) %collective-permute-start.18) | collective-permute-done | bytes 147488 | tf_op jit(solution)/shard_map/ppermute | solution.py:53
  77.5 5.4 %collective-permute-done.23 = bf16[384,384]{1,0:T(8,128)(2,1)} collective-permute-done((bf16[384,384]{1,0:T(8,128)(2,1)}, bf16[384,384]{1,0:T(8,128)(2,1)}, u32[]{:S(2)}, u32[]{:S(2)}) %collective-permute-start.23) | collective-permute-done | bytes 294944 | tf_op jit(solution)/shard_map/ppermute | solution.py:56
  84.3 8.6 %collective-permute-done.22 = bf16[768,384]{1,0:T(8,128)(2,1)S(1)} collective-permute-done((bf16[768,384]{1,0:T(8,128)(2,1)S(1)}, bf16[768,384]{1,0:T(8,128)(2,1)S(1)}, u32[]{:S(2)}, u32[]{:S(2)}) %collective-permute-start.22) | collective-permute-done | bytes 589856 | tf_op jit(solution)/shard_map/ppermute | solution.py:59
  112.1 4.4 %collective-permute-done.32 = bf16[400,384]{1,0:T(8,128)(2,1)S(1)} collective-permute-done((bf16[400,384]{1,0:T(8,128)(2,1)S(1)}, bf16[400,384]{1,0:T(8,128)(2,1)S(1)}, u32[]{:S(2)}, u32[]{:S(2)}) %collective-permute-start.32) | collective-permute-done | bytes 307232 | tf_op jit(solution)/shard_map/ppermute | solution.py:59
  120.3 6.1 %collective-permute-done.40 = bf16[192,384]{1,0:T(8,128)(2,1)S(1)} collective-permute-done((bf16[192,384]{1,0:T(8,128)(2,1)S(1)}, bf16[192,384]{1,0:T(8,128)(2,1)S(1)}, u32[]{:S(2)}, u32[]{:S(2)}) %collective-permute-start.40) | collective-permute-done | bytes 147488 | tf_op jit(solution)/shard_map/ppermute | solution.py:56
  132.0 9.2 %forward_attention.2 = (f32[288,768]{1,0:T(8,128)S(1)}, bf16[288,768]{1,0:T(8,128)(2,1)S(1)}, bf16[768,288]{1,0:T(8,128)(2,1)S(1)}, bf16[768,288]{1,0:T(8,128)(2...) custom-call(s32[25]{0:T(128)S(1)} %concatenate.86.spot.refs_0_, ...), custom_call_target="tpu_custom_call" | custom-call | tf_op jit(solution)/shard_map/forward_attention/pallas_call | solution.py:510
  148.8 8.2 %forward_up.2 = (bf16[288,3072]{1,0:T(8,128)(2,1)S(1)}, bf16[288,3072]{1,0:T(8,128)(2,1)S(1)}, bf16[2,8,4,96,384]{4,3,2,1,0:T(8,128)(2,1)S(1)}, bf16[2,8,4,96,384]{4,3,2,1,0:T(8,128)(2,1)S(1)}) custom-call(s32[25]{0:T(128)S(1)} %concatenate.86.spot.refs_0_, bf16[288,768]{1,0:T(8,128)(2,1)S(1)} %get-tuple-element.517.normed, ...), custom_call_target="tpu_custom_call" | custom-call | tf_op jit(solution)/shard_map/forward_up/pallas_call | solution.py:541
  166.4 9.1 %forward_attention.3 = (f32[288,768]{1,0:T(8,128)S(1)}, bf16[288,768]{1,0:T(8,128)(2,1)S(1)}, bf16[768,288]{1,0:T(8,128)(2,1)S(1)}, bf16[768,288]{1,0:T(8,128)(2...) custom-call(s32[25]{0:T(128)S(1)} %concatenate.86.spot.refs_0_, ...), custom_call_target="tpu_custom_call" | custom-call | tf_op jit(solution)/shard_map/forward_attention/pallas_call | solution.py:510
  195.2 7.0 %forward_up.3 = (bf16[288,3072]{1,0:T(8,128)(2,1)S(1)}, bf16[288,3072]{1,0:T(8,128)(2,1)S(1)}, bf16[2,8,4,96,384]{4,3,2,1,0:T(8,128)(2,1)S(1)}, bf16[2,8,4,96,384]{4,3,2,1,0:T(8,128)(2,1)S(1)}) custom-call(s32[25]{0:T(128)S(1)} %concatenate.86.spot.refs_0_, bf16[288,768]{1,0:T(8,128)(2,1)S(1)} %get-tuple-element.557.normed, ...), custom_call_target="tpu_custom_call" | custom-call | tf_op jit(solution)/shard_map/forward_up/pallas_call | solution.py:541
  207.4 4.4 %gradient_sent.6 = bf16[3,16,96,384]{3,2,1,0:T(8,128)(2,1)S(1)} custom-call(s32[25]{0:T(128)S(1)} %concatenate.86.spot.refs_0_, bf16[768,288]{1,0:T(8,128)(2,1)S(1)} %get-tuple-element.543.refs_0_, bf16[288,3072]{1,0:T(8,128)(2,1)S(1)} %get-tuple-element.584.refs_1_.grad_up, bf16[768,288]{1,0:T(8,128)(2,1)S(1)} %get-tuple-element.565.refs_2_, ...), custom_call_target="tpu_custom_call" | custom-call | tf_op jit(solution)/shard_map/gradient_sent/pallas_call | solution.py:825
  220.0 4.6 %gradient_kept.6 = (bf16[4,96,384]{2,1,0:T(8,128)(2,1)S(1)}, bf16[4,96,384]{2,1,0:T(8,128)(2,1)S(1)}, bf16[8,96,384]{2,1,0:T(8,128)(2,1)S(1)}, bf16[4,96,384]{2,...) custom-call(s32[25]{0:T(128)S(1)} %concatenate.86.spot.refs_0_, ...), custom_call_target="tpu_custom_call" | custom-call | tf_op jit(solution)/shard_map/gradient_kept/pallas_call | solution.py:842
  227.4 11.7 %backward_attention.2 = (f32[288,768]{1,0:T(8,128)S(1)}, bf16[288,2304]{1,0:T(8,128)(2,1)S(1)}, f32[16,768]{1,0:T(8,128)S(1)}) custom-call(s32[25]{0:T(128)S(1)} %concatenate.86.spot.refs_0_, f32[288,768]{1,0:T(8,128)S(1)} %get-tuple-element.599.grad_middle, bf16[288,768]{1,0:T(8,128)(2,1)S(1)} %get-tuple-element.625.grad_proj, ...), custom_call_target="tpu_custom_call" | custom-call | tf_op jit(solution)/shard_map/backward_attention/pallas_call | solution.py:734
  245.7 5.4 %backward_feed_middle.1 = (bf16[768,288]{1,0:T(8,128)(2,1)S(1)}, bf16[288,3072]{1,0:T(8,128)(2,1)S(1)}, f32[1,768]{1,0:T(1,128)S(1)}, f32[1,3072]{1,0:T(1,128)S(...) custom-call(s32[25]{0:T(128)S(1)} %concatenate.86.spot.refs_0_, ...), custom_call_target="tpu_custom_call" | custom-call | tf_op jit(solution)/shard_map/backward_feed_middle/pallas_call | solution.py:658
  269.0 11.7 %backward_attention.3 = (f32[288,768]{1,0:T(8,128)S(1)}, bf16[288,2304]{1,0:T(8,128)(2,1)S(1)}, f32[16,768]{1,0:T(8,128)S(1)}) custom-call(s32[25]{0:T(128)S(1)} %concatenate.86.spot.refs_0_, f32[288,768]{1,0:T(8,128)S(1)} %get-tuple-element.653.grad_middle, bf16[288,768]{1,0:T(8,128)(2,1)S(1)} %get-tuple-element.686.grad_proj, ...), custom_call_target="tpu_custom_call" | custom-call | tf_op jit(solution)/shard_map/backward_attention/pallas_call | solution.py:734
  299.0 4.9 %gradient_kept.8 = (bf16[4,96,384]{2,1,0:T(8,128)(2,1)S(1)}, bf16[4,96,384]{2,1,0:T(8,128)(2,1)S(1)}, bf16[8,96,384]{2,1,0:T(8,128)(2,1)S(1)}, bf16[4,96,384]{2,...) custom-call(s32[25]{0:T(128)S(1)} %concatenate.86.spot.refs_0_, ...), custom_call_target="tpu_custom_call" | custom-call | tf_op jit(solution)/shard_map/gradient_kept/pallas_call | solution.py:842
  308.8 6.1 %collective-permute-done.86.across = bf16[2,96,384]{2,1,0:T(8,128)(2,1)S(1)} collective-permute-done((bf16[2,96,384]{2,1,0:T(8,128)(2,1)S(1)}, bf16[2,96,384]{2,1,0:T(8,128)(2,1)S(1)}, u32[]{:S(2)}, u32[]{:S(2)}) %collective-permute-start.86) | collective-permute-done | bytes 147488 | tf_op jit(solution)/shard_map/ppermute | solution.py:56
  320.6 8.1 %collective-permute-done.94 = f32[32,768]{1,0:T(8,128)S(1)} collective-permute-done((f32[32,768]{1,0:T(8,128)S(1)}, f32[32,768]{1,0:T(8,128)S(1)}, u32[]{:S(2)}, u32[]{:S(2)}) %collective-permute-start.94) | collective-permute-done | bytes 98336 | tf_op jit(solution)/shard_map/ppermute | solution.py:56
  328.7 4.4 %collective-permute-done.90.refs_0_ = bf16[8,96,384]{2,1,0:T(8,128)(2,1)S(1)} collective-permute-done((bf16[8,96,384]{2,1,0:T(8,128)(2,1)S(1)}, bf16[8,96,384]{2,1,0:T(8,128)(2,1)S(1)}, u32[]{:S(2)}, u32[]{:S(2)}) %collective-permute-start.90) | collective-permute-done | bytes 589856 | tf_op jit(solution)/shard_map/ppermute | solution.py:59
  341.2 11.1 %collective-permute-done.98.refs_14_ = f32[32,768]{1,0:T(8,128)S(1)} collective-permute-done((f32[32,768]{1,0:T(8,128)S(1)}, f32[32,768]{1,0:T(8,128)S(1)}, u32[]{:S(2)}, u32[]{:S(2)}) %collective-permute-start.98) | collective-permute-done | bytes 98336 | tf_op jit(solution)/shard_map/ppermute | solution.py:59
  359.3 4.3 %collective-permute-done.102.across = bf16[2,96,384]{2,1,0:T(8,128)(2,1)S(1)} collective-permute-done((bf16[2,96,384]{2,1,0:T(8,128)(2,1)S(1)}, bf16[2,96,384]{2,1,0:T(8,128)(2,1)S(1)}, u32[]{:S(2)}, u32[]{:S(2)}) %collective-permute-start.102) | collective-permute-done | bytes 147488 | tf_op jit(solution)/shard_map/ppermute | solution.py:56
  373.0 6.3 %collective-permute-done.107.refs_15_ = f32[32,768]{1,0:T(8,128)S(1)} collective-permute-done((f32[32,768]{1,0:T(8,128)S(1)}, f32[32,768]{1,0:T(8,128)S(1)}, u32[]{:S(2)}, u32[]{:S(2)}) %collective-permute-start.107) | collective-permute-done | bytes 98336 | tf_op jit(solution)/shard_map/ppermute | solution.py:59
  384.3 6.2 %collective-permute-done.111 = bf16[5,96,384]{2,1,0:T(8,128)(2,1)S(1)} collective-permute-done((bf16[5,96,384]{2,1,0:T(8,128)(2,1)S(1)}, bf16[5,96,384]{2,1,0:T(8,128)(2,1)S(1)}, u32[]{:S(2)}, u32[]{:S(2)}) %collective-permute-start.111) | collective-permute-done | bytes 368672 | tf_op jit(solution)/shard_map/ppermute | solution.py:56
  (511 shorter events, 240.2 us)
Async XLA Ops:
  37.1 17.4 %collective-permute-start.11 = (bf16[768,384]{1,0:T(8,128)(2,1)S(1)}, bf16[768,384]{1,0:T(8,128)(2,1)S(1)}, u32[]{:S(2)}, u32[]{:S(2)}) collective-permute-start(bf16[768,384]{1,0:T(8,128)(2,1)S(1)} %pad_maximum_fusion.6), channel_id=1, source_target_pairs={{0,8},{4,12},{8,16},{12,20},{16,24},{20,28},{24,0},{28,4},{1,9},{5... | collective-permute-start | bytes 1769480 | tf_op jit(solution)/shard_map/ppermute | solution.py:59
  49.9 21.3 %collective-permute-start.20 = (bf16[1600,384]{1,0:T(8,128)(2,1)}, bf16[1600,384]{1,0:T(8,128)(2,1)S(1)}, u32[]{:S(2)}, u32[]{:S(2)}) collective-permute-start(bf16[1600,384]{1,0:T(8,128)(2,1)} %copy-done.12), channel_id=1, source_target_pairs={{0,1},{1,0},{2,3},{3,2},{4,5},{5,4},{6,7},{7,6},{8,9},{9,8},{10,11... | collective-permute-start | bytes 3686408 | tf_op jit(solution)/shard_map/ppermute | solution.py:53
  54.6 16.6 %collective-permute-start.16 = (bf16[768,384]{1,0:T(8,128)(2,1)S(1)}, bf16[768,384]{1,0:T(8,128)(2,1)S(1)}, u32[]{:S(2)}, u32[]{:S(2)}) collective-permute-start(bf16[768,384]{1,0:T(8,128)(2,1)S(1)} %collective-permute-done.11), channel_id=1, source_target_pairs={{0,8},{4,12},{8,16},{12,20},{16,24},{20,28},{24,0},{28,4},{1,9},{5... | collective-permute-start | bytes 1769480 | tf_op jit(solution)/shard_map/ppermute | solution.py:59
  72.2 20.7 %collective-permute-start.26 = (bf16[3072,384]{1,0:T(8,128)(2,1)S(1)}, bf16[3072,384]{1,0:T(8,128)(2,1)}, u32[]{:S(2)}, u32[]{:S(2)}) collective-permute-start(bf16[3072,384]{1,0:T(8,128)(2,1)S(1)} %constant_dynamic-update-slice_fusion.24.refs_0_), channel_id=1, source_target_pairs={{0,1},{1,0},{2,3},{3,2},{4,5},{5,4},{6,7},{7,6},{8,9},{9,8},{10,11... | collective-permute-start | bytes 7077896 | tf_op jit(solution)/shard_map/ppermute | solution.py:53
  76.0 16.9 %collective-permute-start.22 = (bf16[768,384]{1,0:T(8,128)(2,1)S(1)}, bf16[768,384]{1,0:T(8,128)(2,1)S(1)}, u32[]{:S(2)}, u32[]{:S(2)}) collective-permute-start(bf16[768,384]{1,0:T(8,128)(2,1)S(1)} %copy-done.21), channel_id=1, source_target_pairs={{0,8},{4,12},{8,16},{12,20},{16,24},{20,28},{24,0},{28,4},{1,9},{5... | collective-permute-start | bytes 1769480 | tf_op jit(solution)/shard_map/ppermute | solution.py:59
  76.4 16.5 %collective-permute-start.25 = (bf16[1600,384]{1,0:T(8,128)(2,1)S(1)}, bf16[1600,384]{1,0:T(8,128)(2,1)S(1)}, u32[]{:S(2)}, u32[]{:S(2)}) collective-permute-start(bf16[1600,384]{1,0:T(8,128)(2,1)S(1)} %copy-done.11), channel_id=1, source_target_pairs={{0,1},{1,0},{2,3},{3,2},{4,5},{5,4},{6,7},{7,6},{8,9},{9,8},{10,11... | collective-permute-start | bytes 3686408 | tf_op jit(solution)/shard_map/ppermute | solution.py:53
  126.4 16.3 %collective-permute-start.43 = (bf16[384,384]{1,0:T(8,128)(2,1)S(1)}, bf16[384,384]{1,0:T(8,128)(2,1)S(1)}, u32[]{:S(2)}, u32[]{:S(2)}) collective-permute-start(bf16[384,384]{1,0:T(8,128)(2,1)S(1)} %bitcast.148), channel_id=1, source_target_pairs={{0,4},{4,0},{8,12},{12,8},{16,20},{20,16},{24,28},{28,24},{1,5},{5... | collective-permute-start | bytes 884744 | tf_op jit(solution)/shard_map/ppermute | solution.py:56
  128.2 17.3 %collective-permute-start.41 = (bf16[768,384]{1,0:T(8,128)(2,1)S(1)}, bf16[768,384]{1,0:T(8,128)(2,1)S(1)}, u32[]{:S(2)}, u32[]{:S(2)}) collective-permute-start(bf16[768,384]{1,0:T(8,128)(2,1)S(1)} %pad_maximum_fusion.7), channel_id=1, source_target_pairs={{0,8},{4,12},{8,16},{12,20},{16,24},{20,28},{24,0},{28,4},{1,9},{5... | collective-permute-start | bytes 1769480 | tf_op jit(solution)/shard_map/ppermute | solution.py:59
  145.5 17.9 %collective-permute-start.49 = (bf16[1600,384]{1,0:T(8,128)(2,1)S(1)}, bf16[1600,384]{1,0:T(8,128)(2,1)S(1)}, u32[]{:S(2)}, u32[]{:S(2)}) collective-permute-start(bf16[1600,384]{1,0:T(8,128)(2,1)S(1)} %constant_dynamic-update-slice_fusion.52.refs_1_), channel_id=1, source_target_pairs={{0,1},{1,0},{2,3},{3,2},{4,5},{5,4},{6,7},{7,6},{8,9},{9,8},{10,11... | collective-permute-start | bytes 3686408 | tf_op jit(solution)/shard_map/ppermute | solution.py:53
  145.6 17.8 %collective-permute-start.46 = (bf16[768,384]{1,0:T(8,128)(2,1)S(1)}, bf16[768,384]{1,0:T(8,128)(2,1)S(1)}, u32[]{:S(2)}, u32[]{:S(2)}) collective-permute-start(bf16[768,384]{1,0:T(8,128)(2,1)S(1)} %collective-permute-done.41), channel_id=1, source_target_pairs={{0,8},{4,12},{8,16},{12,20},{16,24},{20,28},{24,0},{28,4},{1,9},{5... | collective-permute-start | bytes 1769480 | tf_op jit(solution)/shard_map/ppermute | solution.py:59
  163.4 17.7 %collective-permute-start.53 = (bf16[3072,384]{1,0:T(8,128)(2,1)S(1)}, bf16[3072,384]{1,0:T(8,128)(2,1)S(1)}, u32[]{:S(2)}, u32[]{:S(2)}) collective-permute-start(bf16[3072,384]{1,0:T(8,128)(2,1)S(1)} %constant_dynamic-update-slice_fusion.58.refs_0_), channel_id=1, source_target_pairs={{0,1},{1,0},{2,3},{3,2},{4,5},{5,4},{6,7},{7,6},{8,9},{9,8},{10,11... | collective-permute-start | bytes 7077896 | tf_op jit(solution)/shard_map/ppermute | solution.py:53
  163.4 17.7 %collective-permute-start.50 = (bf16[768,384]{1,0:T(8,128)(2,1)S(1)}, bf16[768,384]{1,0:T(8,128)(2,1)S(1)}, u32[]{:S(2)}, u32[]{:S(2)}) collective-permute-start(bf16[768,384]{1,0:T(8,128)(2,1)S(1)} %collective-permute-done.46), channel_id=1, source_target_pairs={{0,8},{4,12},{8,16},{12,20},{16,24},{20,28},{24,0},{28,4},{1,9},{5... | collective-permute-start | bytes 1769480 | tf_op jit(solution)/shard_map/ppermute | solution.py:59
  224.8 16.8 %collective-permute-start.64 = (bf16[8,96,384]{2,1,0:T(8,128)(2,1)S(1)}, bf16[8,96,384]{2,1,0:T(8,128)(2,1)S(1)}, u32[]{:S(2)}, u32[]{:S(2)}) collective-permute-start(bf16[8,96,384]{2,1,0:T(8,128)(2,1)S(1)} %ring_block.16), channel_id=1, source_target_pairs={{0,8},{4,12},{8,16},{12,20},{16,24},{20,28},{24,0},{28,4},{1,9},{5... | collective-permute-start | bytes 1769480 | tf_op jit(solution)/shard_map/ppermute | solution.py:59
  243.3 16.0 %collective-permute-start.67 = (bf16[8,96,384]{2,1,0:T(8,128)(2,1)S(1)}, bf16[8,96,384]{2,1,0:T(8,128)(2,1)S(1)}, u32[]{:S(2)}, u32[]{:S(2)}) collective-permute-start(bf16[8,96,384]{2,1,0:T(8,128)(2,1)S(1)} %ring_block.17), channel_id=1, source_target_pairs={{0,8},{4,12},{8,16},{12,20},{16,24},{20,28},{24,0},{28,4},{1,9},{5... | collective-permute-start | bytes 1769480 | tf_op jit(solution)/shard_map/ppermute | solution.py:59
  259.5 21.3 %collective-permute-start.70 = (bf16[8,96,384]{2,1,0:T(8,128)(2,1)S(1)}, bf16[8,96,384]{2,1,0:T(8,128)(2,1)S(1)}, u32[]{:S(2)}, u32[]{:S(2)}) collective-permute-start(bf16[8,96,384]{2,1,0:T(8,128)(2,1)S(1)} %ring_block.18), channel_id=1, source_target_pairs={{0,8},{4,12},{8,16},{12,20},{16,24},{20,28},{24,0},{28,4},{1,9},{5... | collective-permute-start | bytes 1769480 | tf_op jit(solution)/shard_map/ppermute | solution.py:59
  260.0 20.8 %collective-permute-start.72 = (bf16[4,96,384]{2,1,0:T(8,128)(2,1)S(1)}, bf16[4,96,384]{2,1,0:T(8,128)(2,1)S(1)}, u32[]{:S(2)}, u32[]{:S(2)}) collective-permute-start(bf16[4,96,384]{2,1,0:T(8,128)(2,1)S(1)} %get-tuple-element.648), channel_id=1, source_target_pairs={{0,4},{4,0},{8,12},{12,8},{16,20},{20,16},{24,28},{28,24},{1,5},{5... | collective-permute-start | bytes 884744 | tf_op jit(solution)/shard_map/ppermute | solution.py:56
  261.3 19.4 %collective-permute-start.73 = (bf16[4,96,384]{2,1,0:T(8,128)(2,1)S(1)}, bf16[4,96,384]{2,1,0:T(8,128)(2,1)S(1)}, u32[]{:S(2)}, u32[]{:S(2)}) collective-permute-start(bf16[4,96,384]{2,1,0:T(8,128)(2,1)S(1)} %get-tuple-element.649), channel_id=1, source_target_pairs={{0,2},{1,3},{2,0},{3,1},{4,6},{5,7},{6,4},{7,5},{8,10},{9,11},{10,... | collective-permute-start | bytes 884744 | tf_op jit(solution)/shard_map/ppermute | solution.py:53
  315.4 17.8 %collective-permute-start.91 = (bf16[4,8,96,384]{3,2,1,0:T(8,128)(2,1)S(1)}, bf16[4,8,96,384]{3,2,1,0:T(8,128)(2,1)S(1)}, u32[]{:S(2)}, u32[]{:S(2)}) collective-permute-start(bf16[4,8,96,384]{3,2,1,0:T(8,128)(2,1)S(1)} %gradient_sent.9), channel_id=1, source_target_pairs={{0,1},{1,0},{2,3},{3,2},{4,5},{5,4},{6,7},{7,6},{8,9},{9,8},{10,11... | collective-permute-start | bytes 7077896 | tf_op jit(solution)/shard_map/ppermute | solution.py:53
  315.6 17.6 %collective-permute-start.90 = (bf16[8,96,384]{2,1,0:T(8,128)(2,1)S(1)}, bf16[8,96,384]{2,1,0:T(8,128)(2,1)S(1)}, u32[]{:S(2)}, u32[]{:S(2)}) collective-permute-start(bf16[8,96,384]{2,1,0:T(8,128)(2,1)S(1)} %ring_block.23), channel_id=1, source_target_pairs={{0,8},{4,12},{8,16},{12,20},{16,24},{20,28},{24,0},{28,4},{1,9},{5... | collective-permute-start | bytes 1769480 | tf_op jit(solution)/shard_map/ppermute | solution.py:59
  333.4 18.9 %collective-permute-start.95 = (bf16[8,96,384]{2,1,0:T(8,128)(2,1)S(1)}, bf16[8,96,384]{2,1,0:T(8,128)(2,1)S(1)}, u32[]{:S(2)}, u32[]{:S(2)}) collective-permute-start(bf16[8,96,384]{2,1,0:T(8,128)(2,1)S(1)} %ring_block.25), channel_id=1, source_target_pairs={{0,8},{4,12},{8,16},{12,20},{16,24},{20,28},{24,0},{28,4},{1,9},{5... | collective-permute-start | bytes 1769480 | tf_op jit(solution)/shard_map/ppermute | solution.py:59
  333.5 18.8 %collective-permute-start.96 = (bf16[4,96,384]{2,1,0:T(8,128)(2,1)S(1)}, bf16[4,96,384]{2,1,0:T(8,128)(2,1)S(1)}, u32[]{:S(2)}, u32[]{:S(2)}) collective-permute-start(bf16[4,96,384]{2,1,0:T(8,128)(2,1)S(1)} %get-tuple-element.744), channel_id=1, source_target_pairs={{0,4},{4,0},{8,12},{12,8},{16,20},{20,16},{24,28},{28,24},{1,5},{5... | collective-permute-start | bytes 884744 | tf_op jit(solution)/shard_map/ppermute | solution.py:56
  334.8 17.5 %collective-permute-start.97 = (bf16[4,96,384]{2,1,0:T(8,128)(2,1)S(1)}, bf16[4,96,384]{2,1,0:T(8,128)(2,1)S(1)}, u32[]{:S(2)}, u32[]{:S(2)}) collective-permute-start(bf16[4,96,384]{2,1,0:T(8,128)(2,1)S(1)} %get-tuple-element.745), channel_id=1, source_target_pairs={{0,2},{1,3},{2,0},{3,1},{4,6},{5,7},{6,4},{7,5},{8,10},{9,11},{10,... | collective-permute-start | bytes 884744 | tf_op jit(solution)/shard_map/ppermute | solution.py:53
  335.6 16.7 %collective-permute-start.98 = (f32[32,768]{1,0:T(8,128)S(1)}, f32[32,768]{1,0:T(8,128)S(1)}, u32[]{:S(2)}, u32[]{:S(2)}) collective-permute-start(f32[32,768]{1,0:T(8,128)S(1)} %add.52.refs_13_), channel_id=1, source_target_pairs={{0,8},{4,12},{8,16},{12,20},{16,24},{20,28},{24,0},{28,4},{1,9},{5... | collective-permute-start | bytes 294920 | tf_op jit(solution)/shard_map/ppermute | solution.py:59
  352.5 15.9 %collective-permute-start.99 = (bf16[8,96,384]{2,1,0:T(8,128)(2,1)S(1)}, bf16[8,96,384]{2,1,0:T(8,128)(2,1)S(1)}, u32[]{:S(2)}, u32[]{:S(2)}) collective-permute-start(bf16[8,96,384]{2,1,0:T(8,128)(2,1)S(1)} %ring_block.26), channel_id=1, source_target_pairs={{0,8},{4,12},{8,16},{12,20},{16,24},{20,28},{24,0},{28,4},{1,9},{5... | collective-permute-start | bytes 1769480 | tf_op jit(solution)/shard_map/ppermute | solution.py:59
  (140 other events, 1151.5 us)

commit v6 on v5

--- a/solution.py
+++ b/solution.py
@@ -515,7 +515,6 @@
         scratch_shapes=[pltpu.VMEM((place.n_dp, extra_rows, width // 2), BF)],
         compiler_params=kernel_params(12),
         cost_estimate=pl.CostEstimate(flops=0, bytes_accessed=0, transcendentals=0),
-        name="forward_attention",
     )(spot, stream, *parts)
 
 
@@ -546,7 +545,6 @@
         + [jax.ShapeDtypeStruct((2, place.n_dp, 4) + group, BF)] * 2,
         compiler_params=kernel_params(8),
         cost_estimate=pl.CostEstimate(flops=0, bytes_accessed=0, transcendentals=0),
-        name="forward_up",
     )(spot, normed, bias_up, *parts)
 
 
@@ -568,7 +566,6 @@
         out_shape=jax.ShapeDtypeStruct(middle.shape, F32),
         compiler_params=kernel_params(8),
         cost_estimate=pl.CostEstimate(flops=0, bytes_accessed=0, transcendentals=0),
-        name="forward_down",
     )(spot, middle, hidden, vectors, split)
 
 
@@ -601,7 +598,6 @@
         out_shape=shapes,
         compiler_params=kernel_params(8),
         cost_estimate=pl.CostEstimate(flops=0, bytes_accessed=0, transcendentals=0),
-        name="backward_feed",
     )(spot, grad, slope, split)
 
 
@@ -636,7 +632,6 @@
         out_shape=shapes,
         compiler_params=kernel_params(10),
         cost_estimate=pl.CostEstimate(flops=0, bytes_accessed=0, transcendentals=0),
-        name="backward_middle",
     )(spot, grad, grad_up, middle, vectors, crossed)
 
 
@@ -661,7 +656,6 @@
         out_specs=whole_vmem(len(shapes)),
         out_shape=shapes,
         compiler_params=kernel_params(12),
-        name="backward_feed_middle",
     )(spot, grad, slope, split, middle, vectors, crossed)
 
 
@@ -739,7 +733,6 @@
         scratch_shapes=[pltpu.VMEM((rows, width), BF)],
         compiler_params=kernel_params(12),
         cost_estimate=pl.CostEstimate(flops=0, bytes_accessed=0, transcendentals=0),
-        name="backward_attention",
     )(spot, grad_middle, grad_proj, mixed, stream, vectors, *others, crossed, split)
 
 
@@ -830,7 +823,6 @@
         scratch_shapes=[spare_shape(place, steps, wide, rows, half)],
         compiler_params=kernel_params(10),
         cost_estimate=pl.CostEstimate(flops=0, bytes_accessed=0, transcendentals=0),
-        name="gradient_sent",
     )(spot, *operands)
 
 
@@ -847,7 +839,6 @@
         scratch_shapes=[spare_shape(place, steps, wide, rows, half)],
         compiler_params=kernel_params(10),
         cost_estimate=pl.CostEstimate(flops=0, bytes_accessed=0, transcendentals=0),
-        name="gradient_kept",
     )(spot, *operands, got)
     return {step: list(outs[3 * i : 3 * i + 3]) for i, step in enumerate(steps)}
 
@@ -872,7 +863,6 @@
         out_shape=jax.ShapeDtypeStruct(stays.shape, BF),
         compiler_params=kernel_params(4),
         cost_estimate=pl.CostEstimate(flops=0, bytes_accessed=0, transcendentals=0),
-        name="ring_block",
     )(*operands)
 
 
@@ -1005,7 +995,6 @@
             scratch_shapes=[pltpu.VMEM((MOST + 2 * halo, width), F32)],
             compiler_params=kernel_params(6),
         cost_estimate=pl.CostEstimate(flops=0, bytes_accessed=0, transcendentals=0),
-            name="take_image",
         )(spot, before, patches, after, specials)
 
     return (before, patches, after, specials), build
@@ -1040,67 +1029,74 @@
         scratch_shapes=[pltpu.VMEM((MOST + 2 * halo, width), F32)],
         compiler_params=kernel_params(6),
         cost_estimate=pl.CostEstimate(flops=0, bytes_accessed=0, transcendentals=0),
-        name="give_images",
     )(spot, *streams)
 
 
-def finish_kernel(*refs):
-    spot, refs = refs[0], refs[1:]
-    inputs, outs = refs[: 6 * LAYERS], refs[6 * LAYERS :]
-    sums, (own_one, own_two, from_before, from_after), outs = outs[:4], outs[4:8], outs[8:]
-    (out_mixed, out_proj, out_up, out_down), (image_one, image_two), out_rows = outs[:4], outs[4:6], outs[6:]
+def finish_attention_kernel(*refs):
+    inputs, (out_mixed, out_proj) = refs[:-2], refs[-2:]
+    for layer in range(LAYERS):
+        last, aside, across = inputs[3 * layer : 3 * layer + 3]
+        one = last[0].astype(F32) + aside[0].astype(F32)
+        two = last[2].astype(F32) + across[0].astype(F32)
+        cut = one.shape[1] // 2
+        out_mixed[layer] = jnp.concatenate([one, two[:, :cut]], axis=1)
+        out_proj[layer] = two[:, cut:]
+
+
+def finish_attention(parts, rows, width):
+    flat_parts = [array for layer in parts for array in layer]
+    return pl.pallas_call(
+        finish_attention_kernel,
+        in_specs=whole_vmem(len(flat_parts)),
+        out_specs=whole_vmem(2),
+        out_shape=[
+            jax.ShapeDtypeStruct((LAYERS, rows, columns), F32) for columns in (3 * width // 4, width // 4)
+        ],
+        compiler_params=kernel_params(6),
+    )(*flat_parts)
+
+
+def finish_kernel(spot, *refs):
+    inputs, refs = refs[: 3 * LAYERS], refs[3 * LAYERS :]
+    sums, (own_one, own_two, from_before, from_after), refs = refs[:4], refs[4:8], refs[8:]
+    (out_up, out_down, image_one, image_two), out_rows = refs[:4], refs[4:]
     halo = from_before.shape[0] // 2
     for at, (own, image) in enumerate(((own_one, image_one), (own_two, image_two))):
         count = own.shape[0]
         image[:halo] = own[:halo] + from_before[at * halo : (at + 1) * halo]
         image[halo : count - halo] = own[halo : count - halo]
         image[count - halo :] = own[count - halo :] + from_after[at * halo : (at + 1) * halo]
-    layers = LAYERS
     total = sums[0][...]
     for other in sums[1:]:
         total = total + other[...]
     place_dp = 2 * spot[0] + spot[1]
-    each, width = total.shape[0] // layers, total.shape[1]
+    each, width = total.shape[0] // LAYERS, total.shape[1]
     part = out_rows[0].shape[1]
     turned = pltpu.roll(total, lax.rem(width - place_dp * part, width), 1)
     more = VECTOR_PIECES - BIAS_DOWN - 1
     row_ids = lax.broadcasted_iota(jnp.int32, total.shape, 0)
     half_turned = pltpu.roll(total, lax.rem(width - lax.rem(place_dp * more * part, width), width), 1)
-    for layer in range(layers):
+    for layer in range(LAYERS):
         for row in range(BIAS_DOWN + 1):
             at = layer * each + row
             out_rows[row][layer : layer + 1, :] = turned[at : at + 1, :part]
         at = layer * each + BIAS_DOWN + 1 + place_dp * more * part // width
         row = jnp.sum(jnp.where(row_ids == at, half_turned, 0.0), axis=0, keepdims=True)
         out_rows[-1][layer : layer + 1, :] = row[:, : more * part]
-    for layer in range(layers):
-        last, aside, across = inputs[6 * layer : 6 * layer + 3]
-        one = last[0].astype(F32) + aside[0].astype(F32)
-        two = last[2].astype(F32) + across[0].astype(F32)
-        cut = one.shape[1] // 2
-        out_mixed[layer] = jnp.concatenate([one, two[:, :cut]], axis=1)
-        out_proj[layer] = two[:, cut:]
-        last, aside, across = inputs[6 * layer + 3 : 6 * layer + 6]
-        half = last.shape[2]
+        last, aside, across = inputs[3 * layer : 3 * layer + 3]
+        rows, half = last.shape[1:]
         for j in range(2):
             out_up[layer, :, j * half : (j + 1) * half] = last[j].astype(F32) + aside[j].astype(F32)
-        downs = [last[4 + j].astype(F32) + across[j].astype(F32) for j in range(2)]
-        for j in range(2):
-            out_down[layer, j * downs[j].shape[0] : (j + 1) * downs[j].shape[0]] = downs[j]
-
-
-def finish(place, spot, parts, sums, images, rows, width):
+            out_down[layer, j * rows : (j + 1) * rows] = last[4 + j].astype(F32) + across[j].astype(F32)
+
+
+def finish(spot, parts, sums, images, rows, width):
+    more = VECTOR_PIECES - BIAS_DOWN - 1
     shapes = [
-        jax.ShapeDtypeStruct((LAYERS, rows, columns), F32)
-        for rows, columns in (
-            (rows, 3 * width // 4),
-            (rows, width // 4),
-            (rows, width),
-            (width // 4, 4 * rows),
-        )
+        jax.ShapeDtypeStruct((LAYERS, rows, width), F32),
+        jax.ShapeDtypeStruct((LAYERS, width // 4, 4 * rows), F32),
     ]
     shapes += [jax.ShapeDtypeStruct(images[0].shape, F32)] * 2
-    more = VECTOR_PIECES - BIAS_DOWN - 1
     shapes += [jax.ShapeDtypeStruct((LAYERS, rows), F32)] * (BIAS_DOWN + 1)
     shapes += [jax.ShapeDtypeStruct((LAYERS, more * rows), F32)]
     flat_parts = [array for layer in parts for array in layer] + sums + images
@@ -1110,8 +1106,6 @@
         out_specs=whole_vmem(len(shapes)),
         out_shape=shapes,
         compiler_params=kernel_params(10),
-        cost_estimate=pl.CostEstimate(flops=0, bytes_accessed=0, transcendentals=0),
-        name="finish",
     )(spot, *flat_parts)
 
 
@@ -1202,7 +1196,7 @@
             new["later"] = place.swap_x(units[later].mine)
         if slot == 0:
             new["image"] = image
-        if slot == 5:
+        if slot == 4:
             carried["stream"] = build(*image)
         if slot == 3 * unit_count:
             new["image"], build = take_image(place, spot, *inputs["cots"], halo, rows)
@@ -1325,6 +1319,7 @@
     back[1], sent = fence((back[1], sent[:1]))
     final_slot = 3 * len(reduces)
     total = given = None
+    first_last = []
     rung = []
     got = {}
     sending = {(0, 0): sent[0]}
@@ -1338,7 +1333,14 @@
             if at == 3:
                 unit.last = unit.block(0)
                 work["last", which] = unit.last
-        for base, group in ((final_slot - 2, range(len(reduces) - 1)), (final_slot, [len(reduces) - 1])):
+        if slot in (4, 7):
+            end = reduces[0].last
+            part = end.shape[0] // 4
+            if slot == 4:
+                new["last"] = place.swap_seq(end[part : 2 * part], 2)
+            else:
+                new["last"] = place.swap_x(end[3 * part :])
+        for base, group in ((final_slot - 2, range(1, len(reduces) - 1)), (final_slot, [len(reduces) - 1])):
             if slot == base:
                 ends = [reduces[which].last for which in group]
                 parts = [end.shape[0] // 4 for end in ends]
@@ -1480,21 +1482,24 @@
         if "image_up" in new:
             sides = (new["image_up"], image_down)
         if "lasts" in new:
-            lasts[: len(new["lasts"])] = new["lasts"]
+            lasts[1 : 1 + len(new["lasts"])] = new["lasts"]
+        if "last" in new:
+            first_last.append(new["last"])
+            lasts[0] = [reduces[0].last] + first_last
         if "sum" in new:
             total = total + new["sum"]
         if "ringing" in new:
             rung += new["ringing"]
 
-    wm, wp, wu, wd, out_patches, grad_patches, g1, s1, bq, bv, bp, g2, s2, bd, bu = finish(
-        place,
+    wu, wd, out_patches, grad_patches, g1, s1, bq, bv, bp, g2, s2, bd, bu = finish(
         spot,
-        [lasts[3] + lasts[2], lasts[1] + lasts[0]],
+        [lasts[2], lasts[0]],
         [total] + rung,
         [owns[0], owns[2], *sides],
         part_rows,
         width,
     )
+    wm, wp = finish_attention([lasts[3], lasts[1]], part_rows, width)
     wd = jnp.transpose(wd, (0, 2, 1))
     return (
         out_patches,

time: 419 us -> 415 us (level)
  waiting for transfers between devices: 156 us -> 151 us
    ppermute x50 -> x51, waiting for transfers between devices: 36.3 us -> 28.2 us  [swap_seq(): lax.ppermute(values, 'seq', [(i, i ^ mask) for i in range(self.n_seq)])]
    ppermute x38 -> x39, waiting for transfers between devices: 54.8 us -> 57.4 us  [swap_x(): return lax.ppermute(values, 'dp', [(i, i ^ 1) for i in range(self.n_dp)])]
    ppermute x38 -> x39, starting transfers between devices: 43.1 us -> 40.7 us  [swap_x(): return lax.ppermute(values, 'dp', [(i, i ^ 1) for i in range(self.n_dp)])]
    unnamed x133 -> x121, local copies, waits for them, and re-layouts: 9.21 us -> 10.6 us
    ppermute x50 -> x51, starting transfers between devices: 43.8 us -> 42.9 us  [swap_seq(): lax.ppermute(values, 'seq', [(i, i ^ mask) for i in range(self.n_seq)])]
  transfers between devices with their start and end apart: 121 -> 123, of which waited for: 50 -> 48; matrix products, arithmetic and copies ran while one was open for 3% -> 4% of each run, Pallas kernels for 25% -> 25%
where the time goes in v6:
time: 415 us; the launch traced here: 408 us
  waiting for transfers between devices  151 us (36%)
  Pallas kernels  116 us (28%)
  starting transfers between devices  113 us (27%)
  local copies, waits for them, and re-layouts  21.2 us (5%)
    ppermute x27, waiting for transfers between devices, ring_z(): lax.ppermute(values, 'dp', [(i, (i + 2 * by) % self.n_dp) for i in range(...  63.7 us
    ppermute x39, waiting for transfers between devices, swap_x(): return lax.ppermute(values, 'dp', [(i, i ^ 1) for i in range(self.n_dp)])  57.4 us
    ppermute x51, starting transfers between devices, swap_seq(): lax.ppermute(values, 'seq', [(i, i ^ mask) for i in range(self.n_seq)])  42.9 us
    ppermute x39, starting transfers between devices, swap_x(): return lax.ppermute(values, 'dp', [(i, i ^ 1) for i in range(self.n_dp)])  40.7 us
    ppermute x51, waiting for transfers between devices, swap_seq(): lax.ppermute(values, 'seq', [(i, i ^ mask) for i in range(self.n_seq)])  28.2 us
    pallas_call x2, Pallas kernels, backward_attention(): pl.pallas_call(partial(backward_attention_kernel, special_count), in_spec...  23.4 us
    ppermute x27, starting transfers between devices, ring_z(): lax.ppermute(values, 'dp', [(i, (i + 2 * by) % self.n_dp) for i in range(...  20.9 us
    pallas_call x2, Pallas kernels, forward_attention(): pl.pallas_call(partial(forward_attention_kernel, unit.turned, unit.chunks...  18.2 us
  transfers between devices with their start and end apart: 123, of which 48 were waited for; matrix products, arithmetic and copies ran while one was open for 4% of the time, Pallas kernels for 25%

profile of v6, /device:TPU:0, one launch (start us, length us, event | category | flops | bytes accessed | tf_op | source)
XLA Modules:
  0.0 408.4 jit_solution(5674277143361696300)
XLA Ops:
  42.9 8.2 %collective-permute-done.14 = bf16[192,384]{1,0:T(8,128)(2,1)S(1)} collective-permute-done((bf16[192,384]{1,0:T(8,128)(2,1)S(1)}, bf16[192,384]{1,0:T(8,128)(2,1)S(1)}, u32[]{:S(2)}, u32[]{:S(2)}) %collective-permute-start.14) | collective-permute-done | bytes 147488 | tf_op jit(solution)/shard_map/ppermute | solution.py:53
  58.9 7.6 %collective-permute-done.18 = bf16[192,384]{1,0:T(8,128)(2,1)S(1)} collective-permute-done((bf16[192,384]{1,0:T(8,128)(2,1)S(1)}, bf16[192,384]{1,0:T(8,128)(2,1)S(1)}, u32[]{:S(2)}, u32[]{:S(2)}) %collective-permute-start.18) | collective-permute-done | bytes 147488 | tf_op jit(solution)/shard_map/ppermute | solution.py:53
  74.5 6.2 %collective-permute-done.23 = bf16[384,384]{1,0:T(8,128)(2,1)S(1)} collective-permute-done((bf16[384,384]{1,0:T(8,128)(2,1)S(1)}, bf16[384,384]{1,0:T(8,128)(2,1)S(1)}, u32[]{:S(2)}, u32[]{:S(2)}) %collective-permute-start.23) | collective-permute-done | bytes 294944 | tf_op jit(solution)/shard_map/ppermute | solution.py:56
  82.1 8.4 %collective-permute-done.22 = bf16[768,384]{1,0:T(8,128)(2,1)S(1)} collective-permute-done((bf16[768,384]{1,0:T(8,128)(2,1)S(1)}, bf16[768,384]{1,0:T(8,128)(2,1)S(1)}, u32[]{:S(2)}, u32[]{:S(2)}) %collective-permute-start.22) | collective-permute-done | bytes 589856 | tf_op jit(solution)/shard_map/ppermute | solution.py:59
  95.0 5.4 %collective-permute-done.28 = bf16[384,384]{1,0:T(8,128)(2,1)S(1)} collective-permute-done((bf16[384,384]{1,0:T(8,128)(2,1)S(1)}, bf16[384,384]{1,0:T(8,128)(2,1)S(1)}, u32[]{:S(2)}, u32[]{:S(2)}) %collective-permute-start.28) | collective-permute-done | bytes 294944 | tf_op jit(solution)/shard_map/ppermute | solution.py:56
  105.0 4.6 %collective-permute-done.33 = bf16[208,384]{1,0:T(8,128)(2,1)S(1)} collective-permute-done((bf16[208,384]{1,0:T(8,128)(2,1)S(1)}, bf16[208,384]{1,0:T(8,128)(2,1)S(1)}, u32[]{:S(2)}, u32[]{:S(2)}) %collective-permute-start.33) | collective-permute-done | bytes 159776 | tf_op jit(solution)/shard_map/ppermute | solution.py:56
  109.9 4.6 %collective-permute-done.32 = bf16[400,384]{1,0:T(8,128)(2,1)S(1)} collective-permute-done((bf16[400,384]{1,0:T(8,128)(2,1)S(1)}, bf16[400,384]{1,0:T(8,128)(2,1)S(1)}, u32[]{:S(2)}, u32[]{:S(2)}) %collective-permute-start.32) | collective-permute-done | bytes 307232 | tf_op jit(solution)/shard_map/ppermute | solution.py:59
  117.3 6.9 %collective-permute-done.40 = bf16[192,384]{1,0:T(8,128)(2,1)S(1)} collective-permute-done((bf16[192,384]{1,0:T(8,128)(2,1)S(1)}, bf16[192,384]{1,0:T(8,128)(2,1)S(1)}, u32[]{:S(2)}, u32[]{:S(2)}) %collective-permute-start.40) | collective-permute-done | bytes 147488 | tf_op jit(solution)/shard_map/ppermute | solution.py:56
  129.8 9.1 %shard_map.315 = (f32[288,768]{1,0:T(8,128)S(1)}, bf16[288,768]{1,0:T(8,128)(2,1)S(1)}, bf16[768,288]{1,0:T(8,128)(2,1)S(1)}, bf16[768,288]{1,0:T(8,128)(2,1)S(1...) custom-call(s32[25]{0:T(128)S(1)} %concatenate.86.spot, ...), custom_call_target="tpu_custom_call" | custom-call | tf_op jit(solution)/shard_map/pallas_call | solution.py:510
  145.8 7.0 %shard_map.316 = (bf16[288,3072]{1,0:T(8,128)(2,1)S(1)}, bf16[288,3072]{1,0:T(8,128)(2,1)S(1)}, bf16[2,8,4,96,384]{4,3,2,1,0:T(8,128)(2,1)S(1)}, bf16[2,8,4,96,384]{4,3,2,1,0:T(8,128)(2,1)S(1)}) custom-call(s32[25]{0:T(128)S(1)} %concatenate.86.spot, bf16[288,768]{1,0:T(8,128)(2,1)S(1)} %get-tuple-element.518.normed, ...), custom_call_target="tpu_custom_call" | custom-call | tf_op jit(solution)/shard_map/pallas_call | solution.py:540
  155.6 5.7 %collective-permute-done.46 = bf16[768,384]{1,0:T(8,128)(2,1)S(1)} collective-permute-done((bf16[768,384]{1,0:T(8,128)(2,1)S(1)}, bf16[768,384]{1,0:T(8,128)(2,1)S(1)}, u32[]{:S(2)}, u32[]{:S(2)}) %collective-permute-start.46) | collective-permute-done | bytes 589856 | tf_op jit(solution)/shard_map/ppermute | solution.py:59
  163.4 9.1 %shard_map.318 = (f32[288,768]{1,0:T(8,128)S(1)}, bf16[288,768]{1,0:T(8,128)(2,1)S(1)}, bf16[768,288]{1,0:T(8,128)(2,1)S(1)}, bf16[768,288]{1,0:T(8,128)(2,1)S(1...) custom-call(s32[25]{0:T(128)S(1)} %concatenate.86.spot, ...), custom_call_target="tpu_custom_call" | custom-call | tf_op jit(solution)/shard_map/pallas_call | solution.py:510
  193.0 7.0 %shard_map.320 = (bf16[288,3072]{1,0:T(8,128)(2,1)S(1)}, bf16[288,3072]{1,0:T(8,128)(2,1)S(1)}, bf16[2,8,4,96,384]{4,3,2,1,0:T(8,128)(2,1)S(1)}, bf16[2,8,4,96,384]{4,3,2,1,0:T(8,128)(2,1)S(1)}) custom-call(s32[25]{0:T(128)S(1)} %concatenate.86.spot, bf16[288,768]{1,0:T(8,128)(2,1)S(1)} %get-tuple-element.558.normed, ...), custom_call_target="tpu_custom_call" | custom-call | tf_op jit(solution)/shard_map/pallas_call | solution.py:540
  216.9 4.6 %shard_map.325 = (bf16[4,96,384]{2,1,0:T(8,128)(2,1)S(1)}, bf16[4,96,384]{2,1,0:T(8,128)(2,1)S(1)}, bf16[8,96,384]{2,1,0:T(8,128)(2,1)S(1)}, bf16[4,96,384]{2,1,...) custom-call(s32[25]{0:T(128)S(1)} %concatenate.86.spot, ...), custom_call_target="tpu_custom_call" | custom-call | tf_op jit(solution)/shard_map/pallas_call | solution.py:834
  224.3 11.7 %shard_map.328 = (f32[288,768]{1,0:T(8,128)S(1)}, bf16[288,2304]{1,0:T(8,128)(2,1)S(1)}, f32[16,768]{1,0:T(8,128)S(1)}) custom-call(s32[25]{0:T(128)S(1)} %concatenate.86.spot, f32[288,768]{1,0:T(8,128)S(1)} %get-tuple-element.600.grad_middle, bf16[288,768]{1,0:T(8,128)(2,1)S(1)} %get-tuple-element.626.grad_proj, bf16[288,2304]{1,0:T(8,128)(2,1)S(1)} %copy-done.13, ...), custom_call_target="tpu_custom_call" | custom-call | tf_op jit(solution)/shard_map/pallas_call | solution.py:728
  242.8 5.3 %shard_map.331 = (bf16[768,288]{1,0:T(8,128)(2,1)S(1)}, bf16[288,3072]{1,0:T(8,128)(2,1)S(1)}, f32[1,768]{1,0:T(1,128)S(1)}, f32[1,3072]{1,0:T(1,128)S(1)}, f32[...) custom-call(s32[25]{0:T(128)S(1)} %concatenate.86.spot, ...), custom_call_target="tpu_custom_call" | custom-call | tf_op jit(solution)/shard_map/pallas_call | solution.py:653
  265.8 11.7 %shard_map.335 = (f32[288,768]{1,0:T(8,128)S(1)}, bf16[288,2304]{1,0:T(8,128)(2,1)S(1)}, f32[16,768]{1,0:T(8,128)S(1)}) custom-call(s32[25]{0:T(128)S(1)} %concatenate.86.spot, f32[288,768]{1,0:T(8,128)S(1)} %get-tuple-element.654.grad_middle, bf16[288,768]{1,0:T(8,128)(2,1)S(1)} %get-tuple-element.687.grad_proj, ...), custom_call_target="tpu_custom_call" | custom-call | tf_op jit(solution)/shard_map/pallas_call | solution.py:728
  296.4 4.8 %shard_map.340 = (bf16[4,96,384]{2,1,0:T(8,128)(2,1)S(1)}, bf16[4,96,384]{2,1,0:T(8,128)(2,1)S(1)}, bf16[8,96,384]{2,1,0:T(8,128)(2,1)S(1)}, bf16[4,96,384]{2,1,...) custom-call(s32[25]{0:T(128)S(1)} %concatenate.86.spot, ...), custom_call_target="tpu_custom_call" | custom-call | tf_op jit(solution)/shard_map/pallas_call | solution.py:834
  306.7 5.5 %collective-permute-done.87.across = bf16[2,96,384]{2,1,0:T(8,128)(2,1)S(1)} collective-permute-done((bf16[2,96,384]{2,1,0:T(8,128)(2,1)S(1)}, bf16[2,96,384]{2,1,0:T(8,128)(2,1)S(1)}, u32[]{:S(2)}, u32[]{:S(2)}) %collective-permute-start.87) | collective-permute-done | bytes 147488 | tf_op jit(solution)/shard_map/ppermute | solution.py:56
  318.3 8.1 %collective-permute-done.95 = f32[32,768]{1,0:T(8,128)S(1)} collective-permute-done((f32[32,768]{1,0:T(8,128)S(1)}, f32[32,768]{1,0:T(8,128)S(1)}, u32[]{:S(2)}, u32[]{:S(2)}) %collective-permute-start.95) | collective-permute-done | bytes 98336 | tf_op jit(solution)/shard_map/ppermute | solution.py:56
  326.4 4.6 %collective-permute-done.91.refs_0_ = bf16[8,96,384]{2,1,0:T(8,128)(2,1)S(1)} collective-permute-done((bf16[8,96,384]{2,1,0:T(8,128)(2,1)S(1)}, bf16[8,96,384]{2,1,0:T(8,128)(2,1)S(1)}, u32[]{:S(2)}, u32[]{:S(2)}) %collective-permute-start.91) | collective-permute-done | bytes 589856 | tf_op jit(solution)/shard_map/ppermute | solution.py:59
  343.1 7.0 %collective-permute-done.100.refs_7_ = f32[32,768]{1,0:T(8,128)S(1)} collective-permute-done((f32[32,768]{1,0:T(8,128)S(1)}, f32[32,768]{1,0:T(8,128)S(1)}, u32[]{:S(2)}, u32[]{:S(2)}) %collective-permute-start.100) | collective-permute-done | bytes 98336 | tf_op jit(solution)/shard_map/ppermute | solution.py:59
  370.7 6.4 %collective-permute-done.109.refs_8_ = f32[32,768]{1,0:T(8,128)S(1)} collective-permute-done((f32[32,768]{1,0:T(8,128)S(1)}, f32[32,768]{1,0:T(8,128)S(1)}, u32[]{:S(2)}, u32[]{:S(2)}) %collective-permute-start.109) | collective-permute-done | bytes 98336 | tf_op jit(solution)/shard_map/ppermute | solution.py:59
  395.3 5.7 %collective-permute-done.119.refs_9_ = f32[32,768]{1,0:T(8,128)S(1)} collective-permute-done((f32[32,768]{1,0:T(8,128)S(1)}, f32[32,768]{1,0:T(8,128)S(1)}, u32[]{:S(2)}, u32[]{:S(2)}) %collective-permute-start.119) | collective-permute-done | bytes 98336 | tf_op jit(solution)/shard_map/ppermute | solution.py:59
  (505 shorter events, 239.9 us)
Async XLA Ops:
  38.2 16.9 %collective-permute-start.11 = (bf16[768,384]{1,0:T(8,128)(2,1)S(1)}, bf16[768,384]{1,0:T(8,128)(2,1)S(1)}, u32[]{:S(2)}, u32[]{:S(2)}) collective-permute-start(bf16[768,384]{1,0:T(8,128)(2,1)S(1)} %pad_maximum_fusion.6), channel_id=1, source_target_pairs={{0,8},{4,12},{8,16},{12,20},{16,24},{20,28},{24,0},{28,4},{1,9},{5... | collective-permute-start | bytes 1769480 | tf_op jit(solution)/shard_map/ppermute | solution.py:59
  51.1 20.0 %collective-permute-start.20 = (bf16[1600,384]{1,0:T(8,128)(2,1)S(1)}, bf16[1600,384]{1,0:T(8,128)(2,1)S(1)}, u32[]{:S(2)}, u32[]{:S(2)}) collective-permute-start(bf16[1600,384]{1,0:T(8,128)(2,1)S(1)} %constant_dynamic-update-slice_fusion.10.refs_0_), channel_id=1, source_target_pairs={{0,1},{1,0},{2,3},{3,2},{4,5},{5,4},{6,7},{7,6},{8,9},{9,8},{10,11... | collective-permute-start | bytes 3686408 | tf_op jit(solution)/shard_map/ppermute | solution.py:53
  55.1 16.0 %collective-permute-start.16 = (bf16[768,384]{1,0:T(8,128)(2,1)S(1)}, bf16[768,384]{1,0:T(8,128)(2,1)S(1)}, u32[]{:S(2)}, u32[]{:S(2)}) collective-permute-start(bf16[768,384]{1,0:T(8,128)(2,1)S(1)} %collective-permute-done.11), channel_id=1, source_target_pairs={{0,8},{4,12},{8,16},{12,20},{16,24},{20,28},{24,0},{28,4},{1,9},{5... | collective-permute-start | bytes 1769480 | tf_op jit(solution)/shard_map/ppermute | solution.py:59
  71.1 19.4 %collective-permute-start.26 = (bf16[3072,384]{1,0:T(8,128)(2,1)S(1)}, bf16[3072,384]{1,0:T(8,128)(2,1)S(1)}, u32[]{:S(2)}, u32[]{:S(2)}) collective-permute-start(bf16[3072,384]{1,0:T(8,128)(2,1)S(1)} %constant_dynamic-update-slice_fusion.24.refs_0_), channel_id=1, source_target_pairs={{0,1},{1,0},{2,3},{3,2},{4,5},{5,4},{6,7},{7,6},{8,9},{9,8},{10,11... | collective-permute-start | bytes 7077896 | tf_op jit(solution)/shard_map/ppermute | solution.py:53
  73.6 17.0 %collective-permute-start.22 = (bf16[768,384]{1,0:T(8,128)(2,1)S(1)}, bf16[768,384]{1,0:T(8,128)(2,1)S(1)}, u32[]{:S(2)}, u32[]{:S(2)}) collective-permute-start(bf16[768,384]{1,0:T(8,128)(2,1)S(1)} %collective-permute-done.16), channel_id=1, source_target_pairs={{0,8},{4,12},{8,16},{12,20},{16,24},{20,28},{24,0},{28,4},{1,9},{5... | collective-permute-start | bytes 1769480 | tf_op jit(solution)/shard_map/ppermute | solution.py:59
  74.3 16.2 %collective-permute-start.25 = (bf16[1600,384]{1,0:T(8,128)(2,1)S(1)}, bf16[1600,384]{1,0:T(8,128)(2,1)S(1)}, u32[]{:S(2)}, u32[]{:S(2)}) collective-permute-start(bf16[1600,384]{1,0:T(8,128)(2,1)S(1)} %constant_dynamic-update-slice_fusion.18.refs_1_), channel_id=1, source_target_pairs={{0,1},{1,0},{2,3},{3,2},{4,5},{5,4},{6,7},{7,6},{8,9},{9,8},{10,11... | collective-permute-start | bytes 3686408 | tf_op jit(solution)/shard_map/ppermute | solution.py:53
  124.3 16.1 %collective-permute-start.43 = (bf16[384,384]{1,0:T(8,128)(2,1)S(1)}, bf16[384,384]{1,0:T(8,128)(2,1)S(1)}, u32[]{:S(2)}, u32[]{:S(2)}) collective-permute-start(bf16[384,384]{1,0:T(8,128)(2,1)S(1)} %bitcast.148), channel_id=1, source_target_pairs={{0,4},{4,0},{8,12},{12,8},{16,20},{20,16},{24,28},{28,24},{1,5},{5... | collective-permute-start | bytes 884744 | tf_op jit(solution)/shard_map/ppermute | solution.py:56
  126.1 17.3 %collective-permute-start.41 = (bf16[768,384]{1,0:T(8,128)(2,1)S(1)}, bf16[768,384]{1,0:T(8,128)(2,1)S(1)}, u32[]{:S(2)}, u32[]{:S(2)}) collective-permute-start(bf16[768,384]{1,0:T(8,128)(2,1)S(1)} %pad_maximum_fusion.7), channel_id=1, source_target_pairs={{0,8},{4,12},{8,16},{12,20},{16,24},{20,28},{24,0},{28,4},{1,9},{5... | collective-permute-start | bytes 1769480 | tf_op jit(solution)/shard_map/ppermute | solution.py:59
  143.4 17.9 %collective-permute-start.49 = (bf16[1600,384]{1,0:T(8,128)(2,1)S(1)}, bf16[1600,384]{1,0:T(8,128)(2,1)S(1)}, u32[]{:S(2)}, u32[]{:S(2)}) collective-permute-start(bf16[1600,384]{1,0:T(8,128)(2,1)S(1)} %constant_dynamic-update-slice_fusion.52.refs_1_), channel_id=1, source_target_pairs={{0,1},{1,0},{2,3},{3,2},{4,5},{5,4},{6,7},{7,6},{8,9},{9,8},{10,11... | collective-permute-start | bytes 3686408 | tf_op jit(solution)/shard_map/ppermute | solution.py:53
  143.5 17.8 %collective-permute-start.46 = (bf16[768,384]{1,0:T(8,128)(2,1)S(1)}, bf16[768,384]{1,0:T(8,128)(2,1)S(1)}, u32[]{:S(2)}, u32[]{:S(2)}) collective-permute-start(bf16[768,384]{1,0:T(8,128)(2,1)S(1)} %collective-permute-done.41), channel_id=1, source_target_pairs={{0,8},{4,12},{8,16},{12,20},{16,24},{20,28},{24,0},{28,4},{1,9},{5... | collective-permute-start | bytes 1769480 | tf_op jit(solution)/shard_map/ppermute | solution.py:59
  161.3 17.7 %collective-permute-start.53 = (bf16[3072,384]{1,0:T(8,128)(2,1)S(1)}, bf16[3072,384]{1,0:T(8,128)(2,1)S(1)}, u32[]{:S(2)}, u32[]{:S(2)}) collective-permute-start(bf16[3072,384]{1,0:T(8,128)(2,1)S(1)} %constant_dynamic-update-slice_fusion.58.refs_0_), channel_id=1, source_target_pairs={{0,1},{1,0},{2,3},{3,2},{4,5},{5,4},{6,7},{7,6},{8,9},{9,8},{10,11... | collective-permute-start | bytes 7077896 | tf_op jit(solution)/shard_map/ppermute | solution.py:53
  161.3 17.7 %collective-permute-start.50 = (bf16[768,384]{1,0:T(8,128)(2,1)S(1)}, bf16[768,384]{1,0:T(8,128)(2,1)S(1)}, u32[]{:S(2)}, u32[]{:S(2)}) collective-permute-start(bf16[768,384]{1,0:T(8,128)(2,1)S(1)} %collective-permute-done.46), channel_id=1, source_target_pairs={{0,8},{4,12},{8,16},{12,20},{16,24},{20,28},{24,0},{28,4},{1,9},{5... | collective-permute-start | bytes 1769480 | tf_op jit(solution)/shard_map/ppermute | solution.py:59
  221.9 16.6 %collective-permute-start.64 = (bf16[8,96,384]{2,1,0:T(8,128)(2,1)S(1)}, bf16[8,96,384]{2,1,0:T(8,128)(2,1)S(1)}, u32[]{:S(2)}, u32[]{:S(2)}) collective-permute-start(bf16[8,96,384]{2,1,0:T(8,128)(2,1)S(1)} %shard_map.327), channel_id=1, source_target_pairs={{0,8},{4,12},{8,16},{12,20},{16,24},{20,28},{24,0},{28,4},{1,9},{5... | collective-permute-start | bytes 1769480 | tf_op jit(solution)/shard_map/ppermute | solution.py:59
  240.2 15.7 %collective-permute-start.67 = (bf16[8,96,384]{2,1,0:T(8,128)(2,1)S(1)}, bf16[8,96,384]{2,1,0:T(8,128)(2,1)S(1)}, u32[]{:S(2)}, u32[]{:S(2)}) collective-permute-start(bf16[8,96,384]{2,1,0:T(8,128)(2,1)S(1)} %shard_map.329), channel_id=1, source_target_pairs={{0,8},{4,12},{8,16},{12,20},{16,24},{20,28},{24,0},{28,4},{1,9},{5... | collective-permute-start | bytes 1769480 | tf_op jit(solution)/shard_map/ppermute | solution.py:59
  256.1 21.4 %collective-permute-start.70 = (bf16[8,96,384]{2,1,0:T(8,128)(2,1)S(1)}, bf16[8,96,384]{2,1,0:T(8,128)(2,1)S(1)}, u32[]{:S(2)}, u32[]{:S(2)}) collective-permute-start(bf16[8,96,384]{2,1,0:T(8,128)(2,1)S(1)} %shard_map.333), channel_id=1, source_target_pairs={{0,8},{4,12},{8,16},{12,20},{16,24},{20,28},{24,0},{28,4},{1,9},{5... | collective-permute-start | bytes 1769480 | tf_op jit(solution)/shard_map/ppermute | solution.py:59
  256.6 20.9 %collective-permute-start.72 = (bf16[4,96,384]{2,1,0:T(8,128)(2,1)S(1)}, bf16[4,96,384]{2,1,0:T(8,128)(2,1)S(1)}, u32[]{:S(2)}, u32[]{:S(2)}) collective-permute-start(bf16[4,96,384]{2,1,0:T(8,128)(2,1)S(1)} %get-tuple-element.649), channel_id=1, source_target_pairs={{0,4},{4,0},{8,12},{12,8},{16,20},{20,16},{24,28},{28,24},{1,5},{5... | collective-permute-start | bytes 884744 | tf_op jit(solution)/shard_map/ppermute | solution.py:56
  258.2 19.3 %collective-permute-start.73 = (bf16[4,96,384]{2,1,0:T(8,128)(2,1)S(1)}, bf16[4,96,384]{2,1,0:T(8,128)(2,1)S(1)}, u32[]{:S(2)}, u32[]{:S(2)}) collective-permute-start(bf16[4,96,384]{2,1,0:T(8,128)(2,1)S(1)} %get-tuple-element.650), channel_id=1, source_target_pairs={{0,2},{1,3},{2,0},{3,1},{4,6},{5,7},{6,4},{7,5},{8,10},{9,11},{10,... | collective-permute-start | bytes 884744 | tf_op jit(solution)/shard_map/ppermute | solution.py:53
  313.2 17.8 %collective-permute-start.92 = (bf16[4,8,96,384]{3,2,1,0:T(8,128)(2,1)S(1)}, bf16[4,8,96,384]{3,2,1,0:T(8,128)(2,1)S(1)}, u32[]{:S(2)}, u32[]{:S(2)}) collective-permute-start(bf16[4,8,96,384]{3,2,1,0:T(8,128)(2,1)S(1)} %shard_map.338), channel_id=1, source_target_pairs={{0,1},{1,0},{2,3},{3,2},{4,5},{5,4},{6,7},{7,6},{8,9},{9,8},{10,11... | collective-permute-start | bytes 7077896 | tf_op jit(solution)/shard_map/ppermute | solution.py:53
  313.4 17.6 %collective-permute-start.91 = (bf16[8,96,384]{2,1,0:T(8,128)(2,1)S(1)}, bf16[8,96,384]{2,1,0:T(8,128)(2,1)S(1)}, u32[]{:S(2)}, u32[]{:S(2)}) collective-permute-start(bf16[8,96,384]{2,1,0:T(8,128)(2,1)S(1)} %shard_map.343), channel_id=1, source_target_pairs={{0,8},{4,12},{8,16},{12,20},{16,24},{20,28},{24,0},{28,4},{1,9},{5... | collective-permute-start | bytes 1769480 | tf_op jit(solution)/shard_map/ppermute | solution.py:59
  331.2 18.9 %collective-permute-start.96 = (bf16[8,96,384]{2,1,0:T(8,128)(2,1)S(1)}, bf16[8,96,384]{2,1,0:T(8,128)(2,1)S(1)}, u32[]{:S(2)}, u32[]{:S(2)}) collective-permute-start(bf16[8,96,384]{2,1,0:T(8,128)(2,1)S(1)} %shard_map.345), channel_id=1, source_target_pairs={{0,8},{4,12},{8,16},{12,20},{16,24},{20,28},{24,0},{28,4},{1,9},{5... | collective-permute-start | bytes 1769480 | tf_op jit(solution)/shard_map/ppermute | solution.py:59
  331.3 18.8 %collective-permute-start.98 = (bf16[4,96,384]{2,1,0:T(8,128)(2,1)S(1)}, bf16[4,96,384]{2,1,0:T(8,128)(2,1)S(1)}, u32[]{:S(2)}, u32[]{:S(2)}) collective-permute-start(bf16[4,96,384]{2,1,0:T(8,128)(2,1)S(1)} %get-tuple-element.746), channel_id=1, source_target_pairs={{0,4},{4,0},{8,12},{12,8},{16,20},{20,16},{24,28},{28,24},{1,5},{5... | collective-permute-start | bytes 884744 | tf_op jit(solution)/shard_map/ppermute | solution.py:56
  332.1 18.0 %collective-permute-start.99 = (bf16[4,96,384]{2,1,0:T(8,128)(2,1)S(1)}, bf16[4,96,384]{2,1,0:T(8,128)(2,1)S(1)}, u32[]{:S(2)}, u32[]{:S(2)}) collective-permute-start(bf16[4,96,384]{2,1,0:T(8,128)(2,1)S(1)} %get-tuple-element.747), channel_id=1, source_target_pairs={{0,2},{1,3},{2,0},{3,1},{4,6},{5,7},{6,4},{7,5},{8,10},{9,11},{10,... | collective-permute-start | bytes 884744 | tf_op jit(solution)/shard_map/ppermute | solution.py:53
  334.1 16.0 %collective-permute-start.100 = (f32[32,768]{1,0:T(8,128)S(1)}, f32[32,768]{1,0:T(8,128)S(1)}, u32[]{:S(2)}, u32[]{:S(2)}) collective-permute-start(f32[32,768]{1,0:T(8,128)S(1)} %add.52.refs_6_), channel_id=1, source_target_pairs={{0,8},{4,12},{8,16},{12,20},{16,24},{20,28},{24,0},{28,4},{1,9},{5... | collective-permute-start | bytes 294920 | tf_op jit(solution)/shard_map/ppermute | solution.py:59
  350.3 15.9 %collective-permute-start.101 = (bf16[8,96,384]{2,1,0:T(8,128)(2,1)S(1)}, bf16[8,96,384]{2,1,0:T(8,128)(2,1)S(1)}, u32[]{:S(2)}, u32[]{:S(2)}) collective-permute-start(bf16[8,96,384]{2,1,0:T(8,128)(2,1)S(1)} %shard_map.347), channel_id=1, source_target_pairs={{0,8},{4,12},{8,16},{12,20},{16,24},{20,28},{24,0},{28,4},{1,9},{5... | collective-permute-start | bytes 1769480 | tf_op jit(solution)/shard_map/ppermute | solution.py:59
  (137 other events, 1109.7 us)

commit v7 on v6

--- a/solution.py
+++ b/solution.py
@@ -599,6 +599,35 @@
         compiler_params=kernel_params(8),
         cost_estimate=pl.CostEstimate(flops=0, bytes_accessed=0, transcendentals=0),
     )(spot, grad, slope, split)
+
+
+def forward_up_back_kernel(turned, chunks, images, branch, spot, normed, bias_up, grad, *refs):
+    parts, refs = refs[: 2 * len(chunks)], refs[2 * len(chunks) :]
+    hidden, crossed, split, backs, slope = refs[0], refs[1], refs[2], refs[3:7], refs[7]
+    forward_up_kernel(turned, chunks, spot, normed, bias_up, *parts, hidden, slope, crossed, split)
+    backward_feed_kernel(images, branch, spot, grad, slope, split, *backs)
+
+
+def forward_up_back(place, spot, branch, normed, bias_up, unit, grad):
+    parts = unit.parts()
+    rows, width = normed.shape
+    group = (width // place.n_dp, width // 2)
+    shapes = [jax.ShapeDtypeStruct((rows, 4 * width), BF)]
+    shapes += [jax.ShapeDtypeStruct((2, place.n_dp, 4) + group, BF)] * 2
+    shapes += [
+        jax.ShapeDtypeStruct((width, rows), BF),
+        jax.ShapeDtypeStruct((rows, 4 * width), BF),
+        jax.ShapeDtypeStruct((1, width), F32),
+        jax.ShapeDtypeStruct((1, 4 * width), F32),
+    ]
+    return pl.pallas_call(
+        partial(forward_up_back_kernel, unit.turned, unit.chunks, place.n_seq, branch),
+        in_specs=in_smem(1) + whole_vmem(3 + len(parts)),
+        out_specs=whole_vmem(len(shapes)),
+        out_shape=shapes,
+        scratch_shapes=[pltpu.VMEM((rows, 4 * width), BF)],
+        compiler_params=kernel_params(12),
+    )(spot, normed, bias_up, grad, *parts)
 
 
 def backward_middle_kernel(images, branch, spot, grad, grad_up, middle, vectors, crossed, *refs):
@@ -1257,19 +1286,12 @@
         if "feed" in new:
             carried["stream"], hiddens[0], slopes[0], *weights[1] = new["feed"]
             del carried["middle"], carried["normed"]
-    hiddens[1], slopes[1], *weights[3] = forward_up(
-        place, spot, carried["normed"], bias_up[1], units[3]
-    )
+    hiddens[1], *found_1 = forward_up_back(place, spot, 3, carried["normed"], bias_up[1], units[3], grad)
+    weights[3] = found_1[:2]
 
     reduces = [Reduced(place) for _ in range(2 * LAYERS)]
     lasts = [None] * (2 * LAYERS)
     back = [{} for _ in range(LAYERS)]
-
-    def feed_back(layer, grad):
-        found = back[layer]
-        found["down_t"], found["up"], found["sum_down"], found["sum_up"] = backward_feed(
-            place, spot, 2 * layer + 1, grad, slopes[layer], weights[2 * layer + 1][1]
-        )
 
     def feed_operands(layer):
         reduces[2 * (LAYERS - 1 - layer)].operands = (
@@ -1313,7 +1335,8 @@
         unit = reduces[which]
         unit.kept.update(kept_part(place, spot, fill, wide, cuts[which][cut], unit.operands, got))
 
-    feed_back(1, grad)
+    found = back[1]
+    found["down_t"], found["up"], found["sum_down"], found["sum_up"] = found_1[2:]
     feed_operands(1)
     sent = [sent_cut(0, 0), None]
     back[1], sent = fence((back[1], sent[:1]))

time: 415 us -> 423 us (1.019)
  local copies, waits for them, and re-layouts: 21.2 us -> 26.6 us
    ppermute x27, waiting for transfers between devices: 63.7 us -> 72.6 us  [ring_z(): lax.ppermute(values, 'dp', [(i, (i + 2 * by) % self.n_dp) for i in range(...]
    ppermute x27, starting transfers between devices: 20.9 us -> 13.5 us  [ring_z(): lax.ppermute(values, 'dp', [(i, (i + 2 * by) % self.n_dp) for i in range(...]
    pallas_call x2 -> x1, Pallas kernels: 14 us -> 6.98 us  [forward_up(): pl.pallas_call(partial(forward_up_kernel, unit.turned, unit.chunks), in_s...]
    pallas_call x1, Pallas kernels: 3 us -> 9.18 us  [forward_up_back(): pl.pallas_call(partial(forward_up_back_kernel, unit.turned, unit.chunks,...]
    another operation x8, local copies, waits for them, and re-layouts: 0.04 us -> 5.26 us  [pack_vectors(): jnp.stack(vectors, axis=1)]
    ppermute x39, waiting for transfers between devices: 57.4 us -> 52.6 us  [swap_x(): return lax.ppermute(values, 'dp', [(i, i ^ 1) for i in range(self.n_dp)])]
    unnamed x121 -> x107, local copies, waits for them, and re-layouts: 10.6 us -> 9.41 us
  transfers between devices with their start and end apart: 123 -> 123, of which waited for: 48 -> 47; matrix products, arithmetic and copies ran while one was open for 4% -> 3% of each run, Pallas kernels for 25% -> 25%
where the time goes in v7:
time: 423 us; the launch traced here: 416 us
  waiting for transfers between devices  154 us (36%)
  Pallas kernels  116 us (27%)
  starting transfers between devices  112 us (26%)
  local copies, waits for them, and re-layouts  26.6 us (6%)
    ppermute x27, waiting for transfers between devices, ring_z(): lax.ppermute(values, 'dp', [(i, (i + 2 * by) % self.n_dp) for i in range(...  72.6 us
    ppermute x39, waiting for transfers between devices, swap_x(): return lax.ppermute(values, 'dp', [(i, i ^ 1) for i in range(self.n_dp)])  52.6 us
    ppermute x51, starting transfers between devices, swap_seq(): lax.ppermute(values, 'seq', [(i, i ^ mask) for i in range(self.n_seq)])  44.7 us
    ppermute x39, starting transfers between devices, swap_x(): return lax.ppermute(values, 'dp', [(i, i ^ 1) for i in range(self.n_dp)])  42.7 us
    ppermute x51, waiting for transfers between devices, swap_seq(): lax.ppermute(values, 'seq', [(i, i ^ mask) for i in range(self.n_seq)])  29.1 us
    pallas_call x2, Pallas kernels, backward_attention(): pl.pallas_call(partial(backward_attention_kernel, special_count), in_spec...  23.5 us
    pallas_call x5, Pallas kernels, kept_part(): pl.pallas_call(partial(kept_kernel, fill, steps, place.nz), in_specs=in_s...  18.4 us
    pallas_call x2, Pallas kernels, forward_attention(): pl.pallas_call(partial(forward_attention_kernel, unit.turned, unit.chunks...  18.2 us
  transfers between devices with their start and end apart: 123, of which 47 were waited for; matrix products, arithmetic and copies ran while one was open for 3% of the time, Pallas kernels for 25%

profile of v7, /device:TPU:0, one launch (start us, length us, event | category | flops | bytes accessed | tf_op | source)
XLA Modules:
  0.0 415.7 jit_solution(1799432571086019498)
XLA Ops:
  56.3 8.5 %collective-permute-done.11 = bf16[768,384]{1,0:T(8,128)(2,1)S(1)} collective-permute-done((bf16[768,384]{1,0:T(8,128)(2,1)S(1)}, bf16[768,384]{1,0:T(8,128)(2,1)S(1)}, u32[]{:S(2)}, u32[]{:S(2)}) %collective-permute-start.11) | collective-permute-done | bytes 589856 | tf_op jit(solution)/shard_map/ppermute | solution.py:59
  79.1 7.3 %collective-permute-done.24 = bf16[384,384]{1,0:T(8,128)(2,1)S(1)} collective-permute-done((bf16[384,384]{1,0:T(8,128)(2,1)S(1)}, bf16[384,384]{1,0:T(8,128)(2,1)S(1)}, u32[]{:S(2)}, u32[]{:S(2)}) %collective-permute-start.24) | collective-permute-done | bytes 294944 | tf_op jit(solution)/shard_map/ppermute | solution.py:53
  88.3 7.7 %collective-permute-done.22 = bf16[768,384]{1,0:T(8,128)(2,1)S(1)} collective-permute-done((bf16[768,384]{1,0:T(8,128)(2,1)S(1)}, bf16[768,384]{1,0:T(8,128)(2,1)S(1)}, u32[]{:S(2)}, u32[]{:S(2)}) %collective-permute-start.22) | collective-permute-done | bytes 589856 | tf_op jit(solution)/shard_map/ppermute | solution.py:59
  100.5 7.9 %collective-permute-done.28 = bf16[384,384]{1,0:T(8,128)(2,1)S(1)} collective-permute-done((bf16[384,384]{1,0:T(8,128)(2,1)S(1)}, bf16[384,384]{1,0:T(8,128)(2,1)S(1)}, u32[]{:S(2)}, u32[]{:S(2)}) %collective-permute-start.28) | collective-permute-done | bytes 294944 | tf_op jit(solution)/shard_map/ppermute | solution.py:56
  111.7 4.7 %collective-permute-done.33 = bf16[208,384]{1,0:T(8,128)(2,1)S(1)} collective-permute-done((bf16[208,384]{1,0:T(8,128)(2,1)S(1)}, bf16[208,384]{1,0:T(8,128)(2,1)S(1)}, u32[]{:S(2)}, u32[]{:S(2)}) %collective-permute-start.33) | collective-permute-done | bytes 159776 | tf_op jit(solution)/shard_map/ppermute | solution.py:56
  123.8 6.3 %collective-permute-done.40 = bf16[192,384]{1,0:T(8,128)(2,1)S(1)} collective-permute-done((bf16[192,384]{1,0:T(8,128)(2,1)S(1)}, bf16[192,384]{1,0:T(8,128)(2,1)S(1)}, u32[]{:S(2)}, u32[]{:S(2)}) %collective-permute-start.40) | collective-permute-done | bytes 147488 | tf_op jit(solution)/shard_map/ppermute | solution.py:56
  136.1 9.1 %shard_map.315 = (f32[288,768]{1,0:T(8,128)S(1)}, bf16[288,768]{1,0:T(8,128)(2,1)S(1)}, bf16[768,288]{1,0:T(8,128)(2,1)S(1)}, bf16[768,288]{1,0:T(8,128)(2,1)S(1...) custom-call(s32[25]{0:T(128)S(1)} %concatenate.86.spot, ...), custom_call_target="tpu_custom_call" | custom-call | tf_op jit(solution)/shard_map/pallas_call | solution.py:510
  152.5 7.0 %shard_map.316 = (bf16[288,3072]{1,0:T(8,128)(2,1)S(1)}, bf16[288,3072]{1,0:T(8,128)(2,1)S(1)}, bf16[2,8,4,96,384]{4,3,2,1,0:T(8,128)(2,1)S(1)}, bf16[2,8,4,96,384]{4,3,2,1,0:T(8,128)(2,1)S(1)}) custom-call(s32[25]{0:T(128)S(1)} %concatenate.86.spot, bf16[288,768]{1,0:T(8,128)(2,1)S(1)} %get-tuple-element.517.normed, ...), custom_call_target="tpu_custom_call" | custom-call | tf_op jit(solution)/shard_map/pallas_call | solution.py:540
  162.2 4.9 %collective-permute-done.46 = bf16[768,384]{1,0:T(8,128)(2,1)S(1)} collective-permute-done((bf16[768,384]{1,0:T(8,128)(2,1)S(1)}, bf16[768,384]{1,0:T(8,128)(2,1)S(1)}, u32[]{:S(2)}, u32[]{:S(2)}) %collective-permute-start.46) | collective-permute-done | bytes 589856 | tf_op jit(solution)/shard_map/ppermute | solution.py:59
  170.1 9.1 %shard_map.318 = (f32[288,768]{1,0:T(8,128)S(1)}, bf16[288,768]{1,0:T(8,128)(2,1)S(1)}, bf16[768,288]{1,0:T(8,128)(2,1)S(1)}, bf16[768,288]{1,0:T(8,128)(2,1)S(1...) custom-call(s32[25]{0:T(128)S(1)} %concatenate.86.spot, ...), custom_call_target="tpu_custom_call" | custom-call | tf_op jit(solution)/shard_map/pallas_call | solution.py:510
  198.4 9.2 %shard_map.320 = (bf16[288,3072]{1,0:T(8,128)(2,1)S(1)}, bf16[2,8,4,96,384]{4,3,2,1,0:T(8,128)(2,1)S(1)}, bf16[2,8,4,96,384]{4,3,2,1,0:T(8,128)(2,1)S(1)}, bf16[...) custom-call(s32[25]{0:T(128)S(1)} %concatenate.86.spot, ...), custom_call_target="tpu_custom_call" | custom-call | tf_op jit(solution)/shard_map/pallas_call | solution.py:623
  209.6 4.3 %shard_map.322 = bf16[3,16,96,384]{3,2,1,0:T(8,128)(2,1)S(1)} custom-call(s32[25]{0:T(128)S(1)} %concatenate.86.spot, bf16[768,288]{1,0:T(8,128)(2,1)S(1)} %get-tuple-element.543.refs_0_, bf16[288,3072]{1,0:T(8,128)(2,1)S(1)} %get-tuple-element.582.refs_1_.grad_up, bf16[768,288]{1,0:T(8,128)(2,1)S(1)} %get-tuple-element.563.refs_2_, ...), custom_call_target="tpu_custom_call" | custom-call | tf_op jit(solution)/shard_map/pallas_call | solution.py:847
  222.2 5.1 %shard_map.324 = (bf16[4,96,384]{2,1,0:T(8,128)(2,1)S(1)}, bf16[4,96,384]{2,1,0:T(8,128)(2,1)S(1)}, bf16[8,96,384]{2,1,0:T(8,128)(2,1)S(1)}, bf16[4,96,384]{2,1,...) custom-call(s32[25]{0:T(128)S(1)} %concatenate.86.spot, ...), custom_call_target="tpu_custom_call" | custom-call | tf_op jit(solution)/shard_map/pallas_call | solution.py:863
  229.4 11.7 %shard_map.327 = (f32[288,768]{1,0:T(8,128)S(1)}, bf16[288,2304]{1,0:T(8,128)(2,1)S(1)}, f32[16,768]{1,0:T(8,128)S(1)}) custom-call(s32[25]{0:T(128)S(1)} %concatenate.86.spot, f32[288,768]{1,0:T(8,128)S(1)} %get-tuple-element.597.grad_middle, bf16[288,768]{1,0:T(8,128)(2,1)S(1)} %get-tuple-element.623.grad_proj, bf16[288,2304]{1,0:T(8,128)(2,1)S(1)} %copy-done.13, ...), custom_call_target="tpu_custom_call" | custom-call | tf_op jit(solution)/shard_map/pallas_call | solution.py:757
  248.4 5.4 %shard_map.330 = (bf16[768,288]{1,0:T(8,128)(2,1)S(1)}, bf16[288,3072]{1,0:T(8,128)(2,1)S(1)}, f32[1,768]{1,0:T(1,128)S(1)}, f32[1,3072]{1,0:T(1,128)S(1)}, f32[...) custom-call(s32[25]{0:T(128)S(1)} %concatenate.86.spot, ...), custom_call_target="tpu_custom_call" | custom-call | tf_op jit(solution)/shard_map/pallas_call | solution.py:682
  272.8 11.7 %shard_map.334 = (f32[288,768]{1,0:T(8,128)S(1)}, bf16[288,2304]{1,0:T(8,128)(2,1)S(1)}, f32[16,768]{1,0:T(8,128)S(1)}) custom-call(s32[25]{0:T(128)S(1)} %concatenate.86.spot, f32[288,768]{1,0:T(8,128)S(1)} %get-tuple-element.651.grad_middle, bf16[288,768]{1,0:T(8,128)(2,1)S(1)} %get-tuple-element.684.grad_proj, ...), custom_call_target="tpu_custom_call" | custom-call | tf_op jit(solution)/shard_map/pallas_call | solution.py:757
  292.8 5.0 %collective-permute-done.76.refs_0_ = bf16[4,96,384]{2,1,0:T(8,128)(2,1)S(1)} collective-permute-done((bf16[4,96,384]{2,1,0:T(8,128)(2,1)S(1)}, bf16[4,96,384]{2,1,0:T(8,128)(2,1)S(1)}, u32[]{:S(2)}, u32[]{:S(2)}) %collective-permute-start.76) | collective-permute-done | bytes 294944 | tf_op jit(solution)/shard_map/ppermute | solution.py:59
  304.8 4.8 %shard_map.339 = (bf16[4,96,384]{2,1,0:T(8,128)(2,1)S(1)}, bf16[4,96,384]{2,1,0:T(8,128)(2,1)S(1)}, bf16[8,96,384]{2,1,0:T(8,128)(2,1)S(1)}, bf16[4,96,384]{2,1,...) custom-call(s32[25]{0:T(128)S(1)} %concatenate.86.spot, ...), custom_call_target="tpu_custom_call" | custom-call | tf_op jit(solution)/shard_map/pallas_call | solution.py:863
  314.0 5.5 %collective-permute-done.87.across = bf16[2,96,384]{2,1,0:T(8,128)(2,1)S(1)} collective-permute-done((bf16[2,96,384]{2,1,0:T(8,128)(2,1)S(1)}, bf16[2,96,384]{2,1,0:T(8,128)(2,1)S(1)}, u32[]{:S(2)}, u32[]{:S(2)}) %collective-permute-start.87) | collective-permute-done | bytes 147488 | tf_op jit(solution)/shard_map/ppermute | solution.py:56
  324.5 7.9 %collective-permute-done.95 = f32[32,768]{1,0:T(8,128)S(1)} collective-permute-done((f32[32,768]{1,0:T(8,128)S(1)}, f32[32,768]{1,0:T(8,128)S(1)}, u32[]{:S(2)}, u32[]{:S(2)}) %collective-permute-start.95) | collective-permute-done | bytes 98336 | tf_op jit(solution)/shard_map/ppermute | solution.py:56
  332.4 5.7 %collective-permute-done.91.refs_0_ = bf16[8,96,384]{2,1,0:T(8,128)(2,1)S(1)} collective-permute-done((bf16[8,96,384]{2,1,0:T(8,128)(2,1)S(1)}, bf16[8,96,384]{2,1,0:T(8,128)(2,1)S(1)}, u32[]{:S(2)}, u32[]{:S(2)}) %collective-permute-start.91) | collective-permute-done | bytes 589856 | tf_op jit(solution)/shard_map/ppermute | solution.py:59
  350.3 7.0 %collective-permute-done.100.refs_7_ = f32[32,768]{1,0:T(8,128)S(1)} collective-permute-done((f32[32,768]{1,0:T(8,128)S(1)}, f32[32,768]{1,0:T(8,128)S(1)}, u32[]{:S(2)}, u32[]{:S(2)}) %collective-permute-start.100) | collective-permute-done | bytes 98336 | tf_op jit(solution)/shard_map/ppermute | solution.py:59
  377.8 6.5 %collective-permute-done.109.refs_8_ = f32[32,768]{1,0:T(8,128)S(1)} collective-permute-done((f32[32,768]{1,0:T(8,128)S(1)}, f32[32,768]{1,0:T(8,128)S(1)}, u32[]{:S(2)}, u32[]{:S(2)}) %collective-permute-start.109) | collective-permute-done | bytes 98336 | tf_op jit(solution)/shard_map/ppermute | solution.py:59
  403.3 5.7 %collective-permute-done.119.refs_9_ = f32[32,768]{1,0:T(8,128)S(1)} collective-permute-done((f32[32,768]{1,0:T(8,128)S(1)}, f32[32,768]{1,0:T(8,128)S(1)}, u32[]{:S(2)}, u32[]{:S(2)}) %collective-permute-start.119) | collective-permute-done | bytes 98336 | tf_op jit(solution)/shard_map/ppermute | solution.py:59
  (490 shorter events, 244.7 us)
Async XLA Ops:
  54.9 21.7 %collective-permute-start.20 = (bf16[1600,384]{1,0:T(8,128)(2,1)S(1)}, bf16[1600,384]{1,0:T(8,128)(2,1)S(1)}, u32[]{:S(2)}, u32[]{:S(2)}) collective-permute-start(bf16[1600,384]{1,0:T(8,128)(2,1)S(1)} %constant_dynamic-update-slice_fusion.10.refs_0_), channel_id=1, source_target_pairs={{0,1},{1,0},{2,3},{3,2},{4,5},{5,4},{6,7},{7,6},{8,9},{9,8},{10,11... | collective-permute-start | bytes 3686408 | tf_op jit(solution)/shard_map/ppermute | solution.py:53
  76.6 19.4 %collective-permute-start.26 = (bf16[3072,384]{1,0:T(8,128)(2,1)S(1)}, bf16[3072,384]{1,0:T(8,128)(2,1)S(1)}, u32[]{:S(2)}, u32[]{:S(2)}) collective-permute-start(bf16[3072,384]{1,0:T(8,128)(2,1)S(1)} %constant_dynamic-update-slice_fusion.24.refs_0_), channel_id=1, source_target_pairs={{0,1},{1,0},{2,3},{3,2},{4,5},{5,4},{6,7},{7,6},{8,9},{9,8},{10,11... | collective-permute-start | bytes 7077896 | tf_op jit(solution)/shard_map/ppermute | solution.py:53
  78.7 17.3 %collective-permute-start.22 = (bf16[768,384]{1,0:T(8,128)(2,1)S(1)}, bf16[768,384]{1,0:T(8,128)(2,1)S(1)}, u32[]{:S(2)}, u32[]{:S(2)}) collective-permute-start(bf16[768,384]{1,0:T(8,128)(2,1)S(1)} %collective-permute-done.16), channel_id=1, source_target_pairs={{0,8},{4,12},{8,16},{12,20},{16,24},{20,28},{24,0},{28,4},{1,9},{5... | collective-permute-start | bytes 1769480 | tf_op jit(solution)/shard_map/ppermute | solution.py:59
  78.7 17.3 %collective-permute-start.25 = (bf16[1600,384]{1,0:T(8,128)(2,1)S(1)}, bf16[1600,384]{1,0:T(8,128)(2,1)S(1)}, u32[]{:S(2)}, u32[]{:S(2)}) collective-permute-start(bf16[1600,384]{1,0:T(8,128)(2,1)S(1)} %constant_dynamic-update-slice_fusion.18.refs_1_), channel_id=1, source_target_pairs={{0,1},{1,0},{2,3},{3,2},{4,5},{5,4},{6,7},{7,6},{8,9},{9,8},{10,11... | collective-permute-start | bytes 3686408 | tf_op jit(solution)/shard_map/ppermute | solution.py:53
  130.1 16.6 %collective-permute-start.43 = (bf16[384,384]{1,0:T(8,128)(2,1)S(1)}, bf16[384,384]{1,0:T(8,128)(2,1)S(1)}, u32[]{:S(2)}, u32[]{:S(2)}) collective-permute-start(bf16[384,384]{1,0:T(8,128)(2,1)S(1)} %bitcast.148), channel_id=1, source_target_pairs={{0,4},{4,0},{8,12},{12,8},{16,20},{20,16},{24,28},{28,24},{1,5},{5... | collective-permute-start | bytes 884744 | tf_op jit(solution)/shard_map/ppermute | solution.py:56
  131.9 17.3 %collective-permute-start.41 = (bf16[768,384]{1,0:T(8,128)(2,1)S(1)}, bf16[768,384]{1,0:T(8,128)(2,1)S(1)}, u32[]{:S(2)}, u32[]{:S(2)}) collective-permute-start(bf16[768,384]{1,0:T(8,128)(2,1)S(1)} %pad_maximum_fusion.7), channel_id=1, source_target_pairs={{0,8},{4,12},{8,16},{12,20},{16,24},{20,28},{24,0},{28,4},{1,9},{5... | collective-permute-start | bytes 1769480 | tf_op jit(solution)/shard_map/ppermute | solution.py:59
  149.2 17.9 %collective-permute-start.49 = (bf16[1600,384]{1,0:T(8,128)(2,1)S(1)}, bf16[1600,384]{1,0:T(8,128)(2,1)S(1)}, u32[]{:S(2)}, u32[]{:S(2)}) collective-permute-start(bf16[1600,384]{1,0:T(8,128)(2,1)S(1)} %constant_dynamic-update-slice_fusion.52.refs_1_), channel_id=1, source_target_pairs={{0,1},{1,0},{2,3},{3,2},{4,5},{5,4},{6,7},{7,6},{8,9},{9,8},{10,11... | collective-permute-start | bytes 3686408 | tf_op jit(solution)/shard_map/ppermute | solution.py:53
  149.3 17.8 %collective-permute-start.46 = (bf16[768,384]{1,0:T(8,128)(2,1)S(1)}, bf16[768,384]{1,0:T(8,128)(2,1)S(1)}, u32[]{:S(2)}, u32[]{:S(2)}) collective-permute-start(bf16[768,384]{1,0:T(8,128)(2,1)S(1)} %collective-permute-done.41), channel_id=1, source_target_pairs={{0,8},{4,12},{8,16},{12,20},{16,24},{20,28},{24,0},{28,4},{1,9},{5... | collective-permute-start | bytes 1769480 | tf_op jit(solution)/shard_map/ppermute | solution.py:59
  167.1 17.7 %collective-permute-start.53 = (bf16[3072,384]{1,0:T(8,128)(2,1)S(1)}, bf16[3072,384]{1,0:T(8,128)(2,1)S(1)}, u32[]{:S(2)}, u32[]{:S(2)}) collective-permute-start(bf16[3072,384]{1,0:T(8,128)(2,1)S(1)} %constant_dynamic-update-slice_fusion.58.refs_0_), channel_id=1, source_target_pairs={{0,1},{1,0},{2,3},{3,2},{4,5},{5,4},{6,7},{7,6},{8,9},{9,8},{10,11... | collective-permute-start | bytes 7077896 | tf_op jit(solution)/shard_map/ppermute | solution.py:53
  167.1 17.7 %collective-permute-start.50 = (bf16[768,384]{1,0:T(8,128)(2,1)S(1)}, bf16[768,384]{1,0:T(8,128)(2,1)S(1)}, u32[]{:S(2)}, u32[]{:S(2)}) collective-permute-start(bf16[768,384]{1,0:T(8,128)(2,1)S(1)} %collective-permute-done.46), channel_id=1, source_target_pairs={{0,8},{4,12},{8,16},{12,20},{16,24},{20,28},{24,0},{28,4},{1,9},{5... | collective-permute-start | bytes 1769480 | tf_op jit(solution)/shard_map/ppermute | solution.py:59
  227.4 16.9 %collective-permute-start.64 = (bf16[8,96,384]{2,1,0:T(8,128)(2,1)S(1)}, bf16[8,96,384]{2,1,0:T(8,128)(2,1)S(1)}, u32[]{:S(2)}, u32[]{:S(2)}) collective-permute-start(bf16[8,96,384]{2,1,0:T(8,128)(2,1)S(1)} %shard_map.326), channel_id=1, source_target_pairs={{0,8},{4,12},{8,16},{12,20},{16,24},{20,28},{24,0},{28,4},{1,9},{5... | collective-permute-start | bytes 1769480 | tf_op jit(solution)/shard_map/ppermute | solution.py:59
  244.3 17.0 %collective-permute-start.68 = (bf16[4,96,384]{2,1,0:T(8,128)(2,1)}, bf16[4,96,384]{2,1,0:T(8,128)(2,1)S(1)}, u32[]{:S(2)}, u32[]{:S(2)}) collective-permute-start(bf16[4,96,384]{2,1,0:T(8,128)(2,1)} %get-tuple-element.618), channel_id=1, source_target_pairs={{0,4},{4,0},{8,12},{12,8},{16,20},{20,16},{24,28},{28,24},{1,5},{5... | collective-permute-start | bytes 884744 | tf_op jit(solution)/shard_map/ppermute | solution.py:56
  245.3 16.0 %collective-permute-start.69 = (bf16[4,96,384]{2,1,0:T(8,128)(2,1)S(1)}, bf16[4,96,384]{2,1,0:T(8,128)(2,1)S(1)}, u32[]{:S(2)}, u32[]{:S(2)}) collective-permute-start(bf16[4,96,384]{2,1,0:T(8,128)(2,1)S(1)} %get-tuple-element.619), channel_id=1, source_target_pairs={{0,2},{1,3},{2,0},{3,1},{4,6},{5,7},{6,4},{7,5},{8,10},{9,11},{10,... | collective-permute-start | bytes 884744 | tf_op jit(solution)/shard_map/ppermute | solution.py:53
  247.2 15.6 %collective-permute-start.67 = (bf16[8,96,384]{2,1,0:T(8,128)(2,1)S(1)}, bf16[8,96,384]{2,1,0:T(8,128)(2,1)S(1)}, u32[]{:S(2)}, u32[]{:S(2)}) collective-permute-start(bf16[8,96,384]{2,1,0:T(8,128)(2,1)S(1)} %shard_map.328), channel_id=1, source_target_pairs={{0,8},{4,12},{8,16},{12,20},{16,24},{20,28},{24,0},{28,4},{1,9},{5... | collective-permute-start | bytes 1769480 | tf_op jit(solution)/shard_map/ppermute | solution.py:59
  263.0 21.6 %collective-permute-start.70 = (bf16[8,96,384]{2,1,0:T(8,128)(2,1)S(1)}, bf16[8,96,384]{2,1,0:T(8,128)(2,1)S(1)}, u32[]{:S(2)}, u32[]{:S(2)}) collective-permute-start(bf16[8,96,384]{2,1,0:T(8,128)(2,1)S(1)} %shard_map.332), channel_id=1, source_target_pairs={{0,8},{4,12},{8,16},{12,20},{16,24},{20,28},{24,0},{28,4},{1,9},{5... | collective-permute-start | bytes 1769480 | tf_op jit(solution)/shard_map/ppermute | solution.py:59
  263.5 21.1 %collective-permute-start.72 = (bf16[4,96,384]{2,1,0:T(8,128)(2,1)}, bf16[4,96,384]{2,1,0:T(8,128)(2,1)S(1)}, u32[]{:S(2)}, u32[]{:S(2)}) collective-permute-start(bf16[4,96,384]{2,1,0:T(8,128)(2,1)} %get-tuple-element.646), channel_id=1, source_target_pairs={{0,4},{4,0},{8,12},{12,8},{16,20},{20,16},{24,28},{28,24},{1,5},{5... | collective-permute-start | bytes 884744 | tf_op jit(solution)/shard_map/ppermute | solution.py:56
  264.6 20.0 %collective-permute-start.73 = (bf16[4,96,384]{2,1,0:T(8,128)(2,1)}, bf16[4,96,384]{2,1,0:T(8,128)(2,1)S(1)}, u32[]{:S(2)}, u32[]{:S(2)}) collective-permute-start(bf16[4,96,384]{2,1,0:T(8,128)(2,1)} %get-tuple-element.647), channel_id=1, source_target_pairs={{0,2},{1,3},{2,0},{3,1},{4,6},{5,7},{6,4},{7,5},{8,10},{9,11},{10,... | collective-permute-start | bytes 884744 | tf_op jit(solution)/shard_map/ppermute | solution.py:53
  320.3 17.8 %collective-permute-start.92 = (bf16[4,8,96,384]{3,2,1,0:T(8,128)(2,1)S(1)}, bf16[4,8,96,384]{3,2,1,0:T(8,128)(2,1)S(1)}, u32[]{:S(2)}, u32[]{:S(2)}) collective-permute-start(bf16[4,8,96,384]{3,2,1,0:T(8,128)(2,1)S(1)} %shard_map.337), channel_id=1, source_target_pairs={{0,1},{1,0},{2,3},{3,2},{4,5},{5,4},{6,7},{7,6},{8,9},{9,8},{10,11... | collective-permute-start | bytes 7077896 | tf_op jit(solution)/shard_map/ppermute | solution.py:53
  320.5 17.6 %collective-permute-start.91 = (bf16[8,96,384]{2,1,0:T(8,128)(2,1)S(1)}, bf16[8,96,384]{2,1,0:T(8,128)(2,1)S(1)}, u32[]{:S(2)}, u32[]{:S(2)}) collective-permute-start(bf16[8,96,384]{2,1,0:T(8,128)(2,1)S(1)} %shard_map.342), channel_id=1, source_target_pairs={{0,8},{4,12},{8,16},{12,20},{16,24},{20,28},{24,0},{28,4},{1,9},{5... | collective-permute-start | bytes 1769480 | tf_op jit(solution)/shard_map/ppermute | solution.py:59
  338.4 18.9 %collective-permute-start.96 = (bf16[8,96,384]{2,1,0:T(8,128)(2,1)S(1)}, bf16[8,96,384]{2,1,0:T(8,128)(2,1)S(1)}, u32[]{:S(2)}, u32[]{:S(2)}) collective-permute-start(bf16[8,96,384]{2,1,0:T(8,128)(2,1)S(1)} %shard_map.344), channel_id=1, source_target_pairs={{0,8},{4,12},{8,16},{12,20},{16,24},{20,28},{24,0},{28,4},{1,9},{5... | collective-permute-start | bytes 1769480 | tf_op jit(solution)/shard_map/ppermute | solution.py:59
  338.4 18.8 %collective-permute-start.98 = (bf16[4,96,384]{2,1,0:T(8,128)(2,1)S(1)}, bf16[4,96,384]{2,1,0:T(8,128)(2,1)S(1)}, u32[]{:S(2)}, u32[]{:S(2)}) collective-permute-start(bf16[4,96,384]{2,1,0:T(8,128)(2,1)S(1)} %get-tuple-element.744), channel_id=1, source_target_pairs={{0,4},{4,0},{8,12},{12,8},{16,20},{20,16},{24,28},{28,24},{1,5},{5... | collective-permute-start | bytes 884744 | tf_op jit(solution)/shard_map/ppermute | solution.py:56
  339.5 17.8 %collective-permute-start.99 = (bf16[4,96,384]{2,1,0:T(8,128)(2,1)S(1)}, bf16[4,96,384]{2,1,0:T(8,128)(2,1)S(1)}, u32[]{:S(2)}, u32[]{:S(2)}) collective-permute-start(bf16[4,96,384]{2,1,0:T(8,128)(2,1)S(1)} %get-tuple-element.745), channel_id=1, source_target_pairs={{0,2},{1,3},{2,0},{3,1},{4,6},{5,7},{6,4},{7,5},{8,10},{9,11},{10,... | collective-permute-start | bytes 884744 | tf_op jit(solution)/shard_map/ppermute | solution.py:53
  341.4 15.9 %collective-permute-start.100 = (f32[32,768]{1,0:T(8,128)S(1)}, f32[32,768]{1,0:T(8,128)S(1)}, u32[]{:S(2)}, u32[]{:S(2)}) collective-permute-start(f32[32,768]{1,0:T(8,128)S(1)} %add.52.refs_6_), channel_id=1, source_target_pairs={{0,8},{4,12},{8,16},{12,20},{16,24},{20,28},{24,0},{28,4},{1,9},{5... | collective-permute-start | bytes 294920 | tf_op jit(solution)/shard_map/ppermute | solution.py:59
  357.5 15.9 %collective-permute-start.101 = (bf16[8,96,384]{2,1,0:T(8,128)(2,1)S(1)}, bf16[8,96,384]{2,1,0:T(8,128)(2,1)S(1)}, u32[]{:S(2)}, u32[]{:S(2)}) collective-permute-start(bf16[8,96,384]{2,1,0:T(8,128)(2,1)S(1)} %shard_map.346), channel_id=1, source_target_pairs={{0,8},{4,12},{8,16},{12,20},{16,24},{20,28},{24,0},{28,4},{1,9},{5... | collective-permute-start | bytes 1769480 | tf_op jit(solution)/shard_map/ppermute | solution.py:59
  (130 other events, 1103.7 us)
